TPU v7x, 32 devices: a whole 2x2x4 slice. The times are simulated.
32 devices in a mesh: section: 2 (over core), fsdp: 8 (over z, y), dp: 2 (over x).
Axes of the slice: x: 2, y: 2, z: 4, core: 2. Of those that a mesh axis runs over, the one named last changes fastest.
Arguments:
- inputs: bfloat16 [4096, 1536], P(('fsdp', 'dp')), may hold values from -6 to 6
- seq_lengths: int32 [32, 3], P(('fsdp', 'dp')), may hold values from 1 to 64, 128 in all within a row
- norm_gain: float32 [2, 1536], P('section'), may hold values from 0.5 to 1.5
- in_w: bfloat16 [2, 1536, 6448], P('section', 'fsdp'), may hold values from -0.15625 to 0.15625
- conv_w: float32 [2, 4, 3328], P('section'), may hold values from -3 to 3
- conv_b: float32 [2, 3328], P('section'), may hold values from -1.5 to 1.5
- dt_bias: float32 [2, 48], P('section'), may hold values from -4 to -1
- a_log: float32 [2, 48], P('section'), may hold values from -2 to 1
- skip: float32 [2, 48], P('section'), may hold values from 0.5 to 1.5
- out_gain: float32 [2, 3072], P('section'), may hold values from 0.5 to 1.5
- out_w: bfloat16 [2, 3072, 1536], P('section', 'fsdp'), may hold values from -0.109375 to 0.109375
- cotangent: bfloat16 [4096, 1536], P(('fsdp', 'dp')), may hold values from -6 to 6
Outputs:
- phase_out: bfloat16 [2, 4096, 1536], P('section', ('fsdp', 'dp'))
- input_grad: bfloat16 [2, 4096, 1536], P('section', ('fsdp', 'dp'))
- grad_norm_gain: float32 [2, 1536], P('section')
- grad_in_w: float32 [2, 1536, 6448], P('section', 'fsdp')
- grad_conv_w: float32 [2, 4, 3328], P('section')
- grad_conv_b: float32 [2, 3328], P('section')
- grad_dt_bias: float32 [2, 48], P('section')
- grad_a_log: float32 [2, 48], P('section')
- grad_skip: float32 [2, 48], P('section')
- grad_out_gain: float32 [2, 3072], P('section')
- grad_out_w: float32 [2, 3072, 1536], P('section', 'fsdp')
Inputs may be any that keep to these rules, and one draw needn't show every extreme that they name: `seq_lengths`: each row sums to 128; the largest entry of every row is exactly 64.
All inputs are finite; a program needn't handle non-finite values.
Results may differ from a plain program's by a relative error of at most 0.02.
The roundings to bfloat16 on the way count: a program that leaves them out, or rounds other values in their place, can miss the bound.
Values may be sent and summed in bfloat16 or wider, within the bound.
No kernel may reach another device: no remote copies, remote signals or barrier semaphores. Data moves between devices by JAX's collectives and lax.ppermute only.
A program may use at most 448 MiB of HBM per device.

v0:
```python
import jax
import jax.numpy as jnp
from jax import lax
from jax.sharding import PartitionSpec as P


def passed_along(x, axis, by):
    devices = lax.axis_size(axis)
    pairs = [(i, i + by) for i in range(devices) if 0 <= i + by < devices]
    return lax.ppermute(x, axis, pairs)


def round_keep(value):
    rounded = lax.optimization_barrier(value.astype(jnp.bfloat16)).astype(jnp.float32)
    return value + lax.stop_gradient(rounded - value)


def segment_of(seq_lengths, length):
    ends = jnp.cumsum(seq_lengths)
    positions = jnp.arange(length, dtype=jnp.int32)
    return jnp.sum((positions[:, None] >= ends[None, :]).astype(jnp.int32), axis=1)


def rms_scale(resid, gain):
    return resid * lax.rsqrt(jnp.mean(resid * resid, axis=-1, keepdims=True) + 1e-05) * gain


def core(projected, segment_ids, smalls):
    conv_w, conv_b, dt_bias, a_log, skip, out_gain = smalls
    length = projected.shape[0]
    inner = out_gain.shape[0]
    heads = a_log.shape[0]
    width_conv = conv_b.shape[0]
    state = (width_conv - inner) // 2
    head_dim = inner // heads
    taps = conv_w.shape[0]
    gate_part = projected[:, :inner]
    conv_in = projected[:, inner : inner + width_conv]
    step_raw = projected[:, inner + width_conv :]
    padded = jnp.pad(conv_in, ((taps - 1, 0), (0, 0)))
    seg_pad = jnp.concatenate([jnp.full((taps - 1,), -1, jnp.int32), segment_ids])
    mixed = conv_b + conv_w[taps - 1] * conv_in
    for back in range(1, taps):
        begin = taps - 1 - back
        same = (seg_pad[begin : begin + length] == segment_ids)[:, None]
        mixed = mixed + conv_w[taps - 1 - back] * jnp.where(
            same, padded[begin : begin + length], 0.0
        )
    activated = jax.nn.silu(mixed)
    values = activated[:, :inner]
    in_state = activated[:, inner : inner + state]
    out_state = activated[:, inner + state :]
    step = jax.nn.softplus(step_raw + dt_bias)
    log_decay = jnp.cumsum(-jnp.exp(a_log) * step, axis=0)
    positions = jnp.arange(length, dtype=jnp.int32)
    allowed = (positions[:, None] >= positions[None, :]) & (
        segment_ids[:, None] == segment_ids[None, :]
    )
    allowed = allowed[:, :, None]
    gap = log_decay[:, None, :] - log_decay[None, :, :]
    decay = jnp.where(allowed, jnp.exp(jnp.where(allowed, gap, -60.0)), 0.0)
    intersection = jnp.dot(round_keep(out_state), round_keep(in_state).T)
    weights = round_keep(intersection[:, :, None] * decay * step[None, :, :])
    head_values = values.reshape(length, heads, head_dim)
    carried = jnp.einsum("ijh,jhp->ihp", weights, round_keep(head_values))
    outputs = (carried + skip[:, None] * head_values).reshape(length, inner)
    gated = outputs * jax.nn.silu(gate_part)
    return gated * lax.rsqrt(jnp.mean(gated * gated, axis=-1, keepdims=True) + 1e-05) * out_gain


def forward(resid, segment_ids, in_weight, out_weight, smalls):
    scaled = rms_scale(resid, smalls[0])
    projected = jnp.dot(scaled.astype(jnp.bfloat16), in_weight, preferred_element_type=jnp.float32)
    normed = core(projected, segment_ids, smalls[1:])
    branch = jnp.dot(normed.astype(jnp.bfloat16), out_weight, preferred_element_type=jnp.float32)
    return resid + branch


def backward(resid, segment_ids, in_weight, out_weight, smalls, grad):
    scaled, pull_norm = jax.vjp(rms_scale, resid, smalls[0])
    scaled_low = scaled.astype(jnp.bfloat16)
    projected = jnp.dot(scaled_low, in_weight, preferred_element_type=jnp.float32)
    normed, pull_core = jax.vjp(lambda p, s: core(p, segment_ids, s), projected, smalls[1:])
    grad_low = grad.astype(jnp.bfloat16)
    d_out_w = jnp.dot(normed.astype(jnp.bfloat16).T, grad_low, preferred_element_type=jnp.float32)
    d_normed = jnp.dot(grad_low, out_weight.T, preferred_element_type=jnp.float32)
    d_proj, d_smalls = pull_core(d_normed)
    d_proj_low = d_proj.astype(jnp.bfloat16)
    d_in_w = jnp.dot(scaled_low.T, d_proj_low, preferred_element_type=jnp.float32)
    d_scaled = jnp.dot(d_proj_low, in_weight.T, preferred_element_type=jnp.float32)
    d_resid, d_gain = pull_norm(d_scaled)
    deltas = (d_gain, d_in_w) + tuple(d_smalls) + (d_out_w,)
    return (grad + d_resid, deltas)


def body(
    inputs,
    seq_lengths,
    norm_gain,
    in_w,
    conv_w,
    conv_b,
    dt_bias,
    a_log,
    skip,
    out_gain,
    out_w,
    cotangent,
):
    phase_idx = lax.axis_index("section")
    micro = seq_lengths.shape[0]
    width = inputs.shape[1]
    rows = inputs.shape[0] // micro
    x_blocks = inputs.reshape(micro, rows, width)
    cot_blocks = cotangent.reshape(micro, rows, width)
    smalls = tuple((p[0] for p in (norm_gain, conv_w, conv_b, dt_bias, a_log, skip, out_gain)))
    small_slots = (0, 2, 3, 4, 5, 6, 7)
    kept_pair = (
        lax.all_gather(in_w, "fsdp", axis=1, tiled=True),
        lax.all_gather(out_w, "fsdp", axis=1, tiled=True),
    )
    input_store = jnp.zeros((micro, rows, width), jnp.float32)
    output_store = jnp.zeros((micro, rows, width), jnp.bfloat16)
    received = jnp.zeros((rows, width), jnp.bfloat16)
    for moment in range(micro + 1):
        pair = kept_pair
        own_micro = moment - phase_idx
        valid = (own_micro >= 0) & (own_micro < micro)
        position = jnp.clip(own_micro, 0, micro - 1)
        own_x = lax.dynamic_index_in_dim(x_blocks, position, 0, keepdims=False).astype(jnp.float32)
        phase_input = jnp.where(phase_idx == 0, own_x, received.astype(jnp.float32))
        segment_ids = segment_of(
            lax.dynamic_index_in_dim(seq_lengths, position, 0, keepdims=False), rows
        )
        produced = forward(phase_input, segment_ids, pair[0][0], pair[1][0], smalls).astype(
            jnp.bfloat16
        )
        input_store = jnp.where(
            valid,
            lax.dynamic_update_index_in_dim(input_store, phase_input, position, 0),
            input_store,
        )
        output_store = jnp.where(
            valid,
            lax.dynamic_update_index_in_dim(output_store, produced, position, 0),
            output_store,
        )
        received = passed_along(produced, "section", 1)
    grad_store = jnp.zeros((micro, rows, width), jnp.bfloat16)
    returned = jnp.zeros((rows, width), jnp.bfloat16)
    acc_shards = (jnp.zeros(in_w.shape, jnp.float32), jnp.zeros(out_w.shape, jnp.float32))
    acc_small = tuple((jnp.zeros(p.shape, jnp.float32) for p in smalls))
    for moment in range(micro + 1):
        pair = kept_pair
        own_micro = moment - (1 - phase_idx)
        valid = (own_micro >= 0) & (own_micro < micro)
        position = jnp.clip(own_micro, 0, micro - 1)
        own_cot = lax.dynamic_index_in_dim(cot_blocks, position, 0, keepdims=False).astype(
            jnp.float32
        )
        grad_in = jnp.where(phase_idx == 1, own_cot, returned.astype(jnp.float32)) * valid.astype(
            jnp.float32
        )
        phase_input = lax.dynamic_index_in_dim(input_store, position, 0, keepdims=False)
        segment_ids = segment_of(
            lax.dynamic_index_in_dim(seq_lengths, position, 0, keepdims=False), rows
        )
        input_delta, param_delta = backward(
            phase_input, segment_ids, pair[0][0], pair[1][0], smalls, grad_in
        )
        sent_grad = input_delta.astype(jnp.bfloat16)
        grad_store = jnp.where(
            valid, lax.dynamic_update_index_in_dim(grad_store, sent_grad, position, 0), grad_store
        )
        shard_pair = (
            lax.psum_scatter(
                param_delta[1][None].astype(jnp.bfloat16), "fsdp", scatter_dimension=1, tiled=True
            ).astype(jnp.float32),
            lax.psum_scatter(
                param_delta[8][None].astype(jnp.bfloat16), "fsdp", scatter_dimension=1, tiled=True
            ).astype(jnp.float32),
        )
        acc_shards = (acc_shards[0] + shard_pair[0], acc_shards[1] + shard_pair[1])
        acc_small = tuple((a + param_delta[k] for a, k in zip(acc_small, small_slots)))
        returned = passed_along(sent_grad, "section", -1)
    small_terms = tuple((a[None] for a in acc_small))
    owned_total = (
        lax.psum(acc_shards[0].astype(jnp.bfloat16), "dp").astype(jnp.float32),
        lax.psum(acc_shards[1].astype(jnp.bfloat16), "dp").astype(jnp.float32),
    )
    small_total = lax.psum(small_terms, ("fsdp", "dp"))
    phase_out = output_store.reshape(1, micro * rows, width)
    input_grad = grad_store.reshape(1, micro * rows, width)
    return (
        phase_out,
        input_grad,
        small_total[0],
        owned_total[0],
        small_total[1],
        small_total[2],
        small_total[3],
        small_total[4],
        small_total[5],
        small_total[6],
        owned_total[1],
    )


def solution(mesh):
    return jax.shard_map(
        body,
        mesh=mesh,
        in_specs=(
            P(("fsdp", "dp"), None),
            P(("fsdp", "dp"), None),
            P("section", None),
            P("section", "fsdp", None),
            P("section", None, None),
            P("section", None),
            P("section", None),
            P("section", None),
            P("section", None),
            P("section", None),
            P("section", "fsdp", None),
            P(("fsdp", "dp"), None),
        ),
        out_specs=(
            P("section", ("fsdp", "dp"), None),
            P("section", ("fsdp", "dp"), None),
            P("section", None),
            P("section", "fsdp", None),
            P("section", None, None),
            P("section", None),
            P("section", None),
            P("section", None),
            P("section", None),
            P("section", None),
            P("section", "fsdp", None),
        ),
        check_vma=False,
    )
```

profile of v0, /device:TPU:0, one launch (start us, length us, event | category | flops | bytes accessed | tf_op | source)
XLA Modules:
  0.0 2380.5 jit_solution(1858187396040455460)
XLA Ops:
  11.6 385.3 %all-gather.3.cloned.1.call-done = bf16[1,1536,6448]{2,1,0:T(8,128)(2,1)} async-done(((bf16[1,192,6448]{2,1,0:T(8,128)(2,1)}), bf16[1,1536,6448]{2,1,0:T(8,128)(2,1)}) %all-gather.3.cloned.1.call-update) | async-done | bytes 19808272 | tf_op jit(solution)/shard_map/all_gather | solution.py:119
  396.9 12.4 fusion.19
  409.5 4.4 divide_multiply_fusion.2
  420.8 116.4 %all-gather.5.cloned.1.call-done = bf16[1,3072,1536]{2,1,0:T(8,128)(2,1)} async-done(((bf16[1,384,1536]{2,1,0:T(8,128)(2,1)}), bf16[1,3072,1536]{2,1,0:T(8,128)(2,1)}) %all-gather.5.cloned.1.call-update) | async-done | bytes 9437200 | tf_op jit(solution)/shard_map/all_gather | solution.py:120
  537.2 5.3 bitcast_dynamic-update-slice_fusion.1
  545.4 12.4 fusion.17
  559.7 4.4 divide_multiply_fusion.1
  578.5 12.5 fusion.13
  592.8 5.3 fusion.140
  608.0 5.5 fusion.21
  615.3 7.7 multiply_reduce_fusion.17
  623.1 5.2 multiply_reduce_fusion.20
  628.2 3.3 fusion.142
  636.3 4.0 bitcast_add_fusion.4
  640.8 5.2 fusion.418
  648.2 2.8 fusion.137
  651.0 12.5 multiply_reduce_fusion.32
  663.5 12.7 fusion.9
  676.5 5.9 fusion.139
  697.1 5.6 fusion.22
  707.4 14.5 fusion.15
  721.9 2.9 slice.343
  724.9 3.4 multiply_reduce_fusion.16
  728.4 5.0 multiply_reduce_fusion.19
  733.5 3.3 fusion.144
  741.6 3.9 bitcast_add_fusion.2
  746.0 5.4 fusion.417
  753.5 2.9 fusion.136
  756.4 12.4 multiply_reduce_fusion.31
  769.3 12.5 fusion.5
  784.5 12.5 fusion.138
  808.8 5.5 fusion.23
  815.1 12.0 fusion
  827.1 85.1 %copy.149 = bf16[1,1536,6448]{2,0,1:T(2,128)(2,1)} copy(bf16[1,1536,6448]{1,2,0:T(8,128)(2,1)} %fusion) | data formatting | bytes 39616512
  912.2 27.5 %copy.163 = bf16[1536,1,6448]{2,0,1:T(8,128)(2,1)} copy(bf16[1536,1,6448]{2,1,0:T(2,128)(2,1)} %bitcast.399) | data formatting | bytes 39616512
  939.8 12.3 fusion.1
  952.0 85.3 %copy.151 = bf16[1,1536,6448]{2,0,1:T(2,128)(2,1)} copy(bf16[1,1536,6448]{1,2,0:T(8,128)(2,1)} %fusion.1) | data formatting | bytes 39616512
  1037.3 27.5 %copy.162 = bf16[1536,1,6448]{2,0,1:T(8,128)(2,1)} copy(bf16[1536,1,6448]{2,1,0:T(2,128)(2,1)} %bitcast.400) | data formatting | bytes 39616512
  1064.9 7.4 multiply_reduce_fusion.15
  1072.3 4.6 multiply_reduce_fusion.18
  1076.9 3.3 fusion.146
  1085.2 4.0 bitcast_add_fusion
  1089.6 4.6 fusion.419
  1099.5 10.7 fusion.2
  1110.3 85.5 %copy.153 = bf16[1,1536,6448]{2,0,1:T(2,128)(2,1)} copy(bf16[1,1536,6448]{1,2,0:T(8,128)(2,1)} %fusion.2) | data formatting | bytes 39616512
  1195.8 27.6 %copy.161 = bf16[1536,1,6448]{2,0,1:T(8,128)(2,1)} copy(bf16[1536,1,6448]{2,1,0:T(2,128)(2,1)} %bitcast.401) | data formatting | bytes 39616512
  1228.9 3.4 add_convert_fusion.4
  1232.3 209.6 %reduce-scatter.19.cloned.1.call-done = bf16[192,6448]{1,0:T(8,128)(2,1)} async-done(((bf16[1536,6448]{1,0:T(8,128)(2,1)}), bf16[192,6448]{1,0:T(8,128)(2,1)}) %reduce-scatter.19.cloned.1.call-update) | async-done | bytes 2476048
  1441.9 5.7 reshape_bitcast_fusion.2
  1447.6 11.7 copy.150
  1459.4 316.8 %reduce-scatter.21.cloned.1.call-done = bf16[192,6448]{1,0:T(8,128)(2,1)} async-done(((bf16[1536,6448]{1,0:T(8,128)(2,1)}), bf16[192,6448]{1,0:T(8,128)(2,1)}) %reduce-scatter.21.cloned.1.call-update) | async-done | bytes 2476048
  1776.2 5.7 reshape_bitcast_fusion.1
  1781.9 11.8 copy.152
  1793.7 317.4 %reduce-scatter.23.cloned.1.call-done = bf16[192,6448]{1,0:T(8,128)(2,1)} async-done(((bf16[1536,6448]{1,0:T(8,128)(2,1)}), bf16[192,6448]{1,0:T(8,128)(2,1)}) %reduce-scatter.23.cloned.1.call-update) | async-done | bytes 2476048
  2111.1 5.7 reshape_bitcast_fusion
  2116.8 11.6 copy.154
  2128.4 6.9 add_convert_fusion
  2135.4 12.2 multiply_reduce_fusion.30
  2151.4 4.0 bitcast_add_fusion.6
  2155.5 3.2 multiply_reduce_fusion.27
  2161.8 6.6 fusion.90
  2170.5 78.5 %all-reduce.58.cloned.1.call-done = (bf16[1,192,6448]{1,2,0:T(8,128)(2,1)}, bf16[1,384,1536]{2,1,0:T(8,128)(2,1)}) async-done(((bf16[1,192,6448]{1,2,0:T(8,128)(2,1)}, bf16[1,384,1536]{2,1,0:T(8,128)(2,1)}), (bf16[1,192,6448]{1,2,0:T(8,128)(2,1)}, bf16[1,384,1536]{2,1,0:T(8,128)(2,1)})) %all-reduce.58.cloned.1.call-update) | async-done | bytes 3655696 | tf_op jit(solution)/shard_map/psum | solution.py:188
  2249.0 5.2 copy.139
  2255.9 108.5 %all-reduce.56.cloned.1.call-done = (f32[1,1536]{1,0:T(1,128)}, f32[1,4,3328]{2,1,0:T(4,128)}, f32[1,3328]{1,0:T(1,128)}, f32[1,48]{1,0:T(1,128)}, f32[1,48]{1,0...) async-done(((f32[1,1536]{1,0:T(1,128)}, f32[1,4,3328]{2,1,0:T(4,128)}, f32[1,3328]{1,0:T(1,128)}, f32[1,48]{1,0:T(1,128)}, f32[1,48]{1,0:T(1,128)}, ...) | async-done | bytes 85584 | tf_op jit(solution)/shard_map/psum | solution.py:191
  (574 shorter events, 128.1 us)
Async XLA Ops:
  7.2 389.7 %all-gather.3.cloned.1.call-start = ((), (), s32[]{:S(2)}) async-start(), calls=%async_computation.6 | async-start | bytes 22560768 | tf_op jit(solution)/shard_map/all_gather | solution.py:119
  8.0 529.2 %all-gather.5.cloned.1.call-start = ((), (), s32[]{:S(2)}) async-start(), calls=%async_computation.7 | async-start | bytes 10616832 | tf_op jit(solution)/shard_map/all_gather | solution.py:120
  8.7 1220.1 %reduce-scatter.13.cloned.1.call-start = ((), (), s32[]{:S(2)}) async-start(), calls=%async_computation.8 | async-start | bytes 10616832 | tf_op jit(solution)/shard_map/reduce_scatter | solution.py:179
  8.9 550.8 %copy-start.76 = (f32[3328]{0:T(1024)}, f32[3328]{0:T(1024)S(1)}, u32[]{:S(2)}) copy-start(f32[3328]{0:T(1024)S(1)} %reduce.6) | copy-start | bytes 39940
  10.5 547.5 %copy-start.115 = (f32[48]{0:T(128)}, f32[48]{0:T(128)S(1)}, u32[]{:S(2)}) copy-start(f32[48]{0:T(128)S(1)} %negate_bitcast_fusion) | copy-start | bytes 580
  409.4 5.8 copy-start.31
  418.8 118.5 %copy-start.54 = (f32[1,3072]{1,0:T(1,128)S(1)}, f32[1,3072]{1,0:T(1,128)}, u32[]{:S(2)}) copy-start(f32[1,3072]{1,0:T(1,128)} %param.22) | copy-start | bytes 36868
  542.5 2.7 collective-permute-start
  574.6 3.6 collective-permute-start.1
  578.2 129.2 %copy-start.33 = (bf16[128,1536]{1,0:T(8,128)(2,1)}, bf16[128,1536]{1,0:T(8,128)(2,1)S(1)}, u32[]{:S(2)}) copy-start(bf16[128,1536]{1,0:T(8,128)(2,1)S(1)} %collective-permute-done.1) | copy-start | bytes 1179652
  578.5 110.2 %copy-start.124 = (f32[128]{0:T(128)}, f32[128]{0:T(128)S(1)}, u32[]{:S(2)}) copy-start(f32[128]{0:T(128)S(1)} %fusion.390) | copy-start | bytes 1540
  591.7 6.3 copy-start.27
  613.5 615.3 %reduce-scatter.15.cloned.1.call-start = ((), (), s32[]{:S(2)}) async-start(), calls=%async_computation.9 | async-start | bytes 10616832 | tf_op jit(solution)/shard_map/reduce_scatter | solution.py:179
  615.1 61.3 %copy-start.135 = (pred[128]{0:T(512)(128)(4,1)}, pred[128]{0:T(512)(128)(4,1)S(1)}, u32[]{:S(2)}) copy-start(pred[128]{0:T(512)(128)(4,1)S(1)} %get-tuple-element.207) | copy-start | bytes 388
  615.1 61.3 %copy-start.137 = (pred[128]{0:T(512)(128)(4,1)}, pred[128]{0:T(512)(128)(4,1)S(1)}, u32[]{:S(2)}) copy-start(pred[128]{0:T(512)(128)(4,1)S(1)} %get-tuple-element.208) | copy-start | bytes 388
  615.2 61.3 %copy-start.139 = (pred[128]{0:T(512)(128)(4,1)}, pred[128]{0:T(512)(128)(4,1)S(1)}, u32[]{:S(2)}) copy-start(pred[128]{0:T(512)(128)(4,1)S(1)} %get-tuple-element.209) | copy-start | bytes 388
  615.2 76.4 %copy-start.102 = (pred[128,128]{1,0:T(8,128)(4,1)}, pred[128,128]{1,0:T(8,128)(4,1)S(1)}, u32[]{:S(2)}) copy-start(pred[128,128]{1,0:T(8,128)(4,1)S(1)} %fusion.316) | copy-start | bytes 49156
  615.3 7.8 copy-start.5
  615.3 7.7 copy-start.23
  615.3 7.7 copy-start.44
  623.0 5.2 copy-start.51
  623.0 5.2 copy-start.75
  634.3 16.7 copy-start.89
  663.5 12.8 copy-start.158
  663.5 12.8 copy-start.126
  676.3 7.4 copy-start.8
  676.4 5.9 copy-start.25
  684.1 7.6 copy-start.85
  684.4 7.3 copy-start.87
  686.5 5.2 copy-start.83
  690.4 5.6 collective-permute-start.2
  696.0 6.7 copy-start.160
  696.0 6.7 copy-start.142
  696.0 6.7 copy-start.55
  702.8 22.0 slice-start.3
  702.8 526.1 %reduce-scatter.17.cloned.1.call-start = ((), (), s32[]{:S(2)}) async-start(), calls=%async_computation.10 | async-start | bytes 10616832 | tf_op jit(solution)/shard_map/reduce_scatter | solution.py:179
  707.4 17.4 slice-start.4
  707.4 17.4 slice-start.5
  728.3 5.0 copy-start.47
  728.3 5.0 copy-start.73
  728.3 5.0 copy-start.84
  733.4 6.1 copy-start.82
  733.4 7.1 copy-start.80
  733.5 8.1 copy-start.169
  769.3 12.5 copy-start.122
  797.2 6.2 copy-start.48
  802.1 5.5 collective-permute-start.3
  814.4 627.6 %reduce-scatter.19.cloned.1.call-start = ((), (), s32[]{:S(2)}) async-start(), calls=%async_computation.11 | async-start | bytes 22560768
  939.7 836.5 %reduce-scatter.21.cloned.1.call-start = ((), (), s32[]{:S(2)}) async-start(), calls=%async_computation.12 | async-start | bytes 22560768
  1064.8 1046.2 %reduce-scatter.23.cloned.1.call-start = ((), (), s32[]{:S(2)}) async-start(), calls=%async_computation.13 | async-start | bytes 22560768
  1064.9 7.4 copy-start.1
  1064.9 7.4 copy-start.19
  1064.9 7.4 copy-start.40
  1076.9 6.6 copy-start.114
  1076.9 6.6 copy-start.118
  1076.9 8.2 copy-start.101
  1076.9 8.2 copy-start.170
  1223.4 1025.6 %all-reduce.58.cloned.1.call-start = ((), (), s32[]{:S(2)}) async-start(), calls=%async_computation.15 | async-start | bytes 8962048 | tf_op jit(solution)/shard_map/psum | solution.py:188
  2135.3 229.1 %all-reduce.56.cloned.1.call-start = ((), (), s32[]{:S(2)}) async-start(), calls=%async_computation.14 | async-start | bytes 173056 | tf_op jit(solution)/shard_map/psum | solution.py:191
  2155.4 6.3 copy-start.13
  2155.4 6.3 copy-start.34
  2161.7 6.7 copy-start.17
  2161.7 6.6 copy-start.59
  2249.0 5.2 copy-start.69
  (127 other events, 343.5 us)
Sparse Core Ops, SparseCore 0:
  9.6 387.2 all-gather.2
  399.1 138.0 all-gather.4
  613.6 162.1 reduce-scatter.12
  779.3 162.5 reduce-scatter.14
  945.4 162.5 reduce-scatter.16
  1111.8 330.1 reduce-scatter.18
  1445.9 330.2 reduce-scatter.20
  1780.1 330.8 reduce-scatter.22
  2135.4 113.5 all-reduce.57
  2257.6 106.7 all-reduce.55
where the time goes:
time: 2400 us; the launch traced here: 2380 us
  waiting for transfers between devices  1540 us (64%)
  local copies, waits for them, and re-layouts  440 us (18%)
  matrix products  243 us (10%)
  other arithmetic  138 us (6%)
    unnamed x13, waiting for transfers between devices  845 us
    unnamed x374, local copies, waits for them, and re-layouts  421 us
    all_gather x1, waiting for transfers between devices, body(): lax.all_gather(in_w, 'fsdp', axis=1, tiled=True)  385 us
    all_gather x1, waiting for transfers between devices, body(): lax.all_gather(out_w, 'fsdp', axis=1, tiled=True)  116 us
    psum x1, waiting for transfers between devices, body(): small_total = lax.psum(small_terms, ('fsdp', 'dp'))  108 us
    psum x1, waiting for transfers between devices, body(): lax.psum(acc_shards[0].astype(jnp.bfloat16), 'dp').astype(jnp.float32)  78.5 us
  transfers between devices with their start and end apart: 14, of which 9 were waited for; matrix products, arithmetic and copies ran while one was open for 30% of the time, Pallas kernels for 0%

commit v1 on v0

v1 whole, which is shorter than its diff:
```python
import functools

import jax
import jax.numpy as jnp
from jax import lax
from jax.experimental import pallas as pl
from jax.experimental.pallas import tpu as pltpu
from jax.sharding import PartitionSpec as P

F32 = jnp.float32
BF16 = jnp.bfloat16
LANES = 128
HALF = 64
VMEM_LIMIT = 40 * 1024 * 1024


def dot(a, b, dims=((1,), (0,)), precision=None):
    return lax.dot_general(a, b, (dims, ((), ())), precision=precision, preferred_element_type=F32)


def dot_exact(a, b, dims=((1,), (0,))):
    return dot(a, b, dims, lax.Precision.HIGHEST)


def silu_parts(x):
    gate = 1.0 / (1.0 + jnp.exp(-x))
    return gate, x * gate


def softplus(x):
    return jnp.maximum(x, 0.0) + jnp.log1p(jnp.exp(-jnp.abs(x)))


def conv_mixed(conv_in, aux, conv_w, conv_b):
    taps = conv_w.shape[0]
    mixed = conv_b + conv_w[taps - 1 : taps] * conv_in
    shifted = []
    for back in range(1, taps):
        moved = pltpu.roll(conv_in, back, 0) * aux[:, back : back + 1]
        shifted.append(moved)
        mixed = mixed + conv_w[taps - 1 - back : taps - back] * moved
    return mixed, shifted


def conv_back(d_mixed, conv_in, shifted, aux, conv_w):
    taps = conv_w.shape[0]
    rows = d_mixed.shape[0]
    d_in = conv_w[taps - 1 : taps] * d_mixed
    d_w = [None] * taps
    d_w[taps - 1] = jnp.sum(d_mixed * conv_in, axis=0, keepdims=True)
    for back in range(1, taps):
        ahead = pltpu.roll(d_mixed, rows - back, 0) * aux[:, taps - 1 + back : taps + back]
        d_in = d_in + conv_w[taps - 1 - back : taps - back] * ahead
        d_w[taps - 1 - back] = jnp.sum(d_mixed * shifted[back - 1], axis=0, keepdims=True)
    return d_in, d_w, jnp.sum(d_mixed, axis=0, keepdims=True)


def decays(last, dt_bias, neg_rate, aux, seg_row):
    rows = last.shape[0]
    step = softplus(last + dt_bias)
    row = lax.broadcasted_iota(jnp.int32, (rows, rows), 0)
    col = lax.broadcasted_iota(jnp.int32, (rows, rows), 1)
    lower = row >= col
    log_decay = dot_exact(lower.astype(F32), neg_rate * step)
    allowed = lower & (aux[:, 0:1] == seg_row)
    return step, log_decay, allowed, lower


def pair_masks(rows):
    lane = lax.broadcasted_iota(jnp.int32, (rows, LANES), 1)
    return (lane < HALF).astype(F32), (lane >= HALF).astype(F32)


def ahead_kernel(heads, proj, bc, aux, seg_row, conv_w, conv_b, dt_bias, neg_rate, skip, *rest):
    outs_ref, gated_ref, square_ref = rest[-3:]
    rows = proj.shape[0]
    inner = heads * HALF
    aux_v = aux[...]
    values_mixed, _ = conv_mixed(proj[:, inner : 2 * inner], aux_v, conv_w[:, :inner], conv_b[:, :inner])
    _, values = silu_parts(values_mixed)
    state_mixed, _ = conv_mixed(bc[...], aux_v, conv_w[:, inner:], conv_b[:, inner:])
    _, state = silu_parts(state_mixed)
    in_state, out_state = state[:, :LANES].astype(BF16), state[:, LANES:].astype(BF16)
    step, log_decay, allowed, _ = decays(
        proj[:, 2 * inner :], dt_bias[...], neg_rate[...], aux_v, seg_row[0]
    )
    step_t, log_t = step.T, log_decay.T
    inter = dot(out_state, in_state, ((1,), (1,)))
    first, second = pair_masks(rows)
    squares = jnp.zeros((rows, 1), F32)
    for pair in range(heads // 2):
        weights = []
        for h in (2 * pair, 2 * pair + 1):
            gap = log_decay[:, h : h + 1] - log_t[h : h + 1]
            decay = jnp.exp(jnp.where(allowed, gap, -1e30))
            weights.append((inter * decay * step_t[h : h + 1]).astype(BF16))
        at = slice(pair * LANES, (pair + 1) * LANES)
        own = values[:, at]
        low = own.astype(BF16).astype(F32)
        both = jnp.concatenate([low * first, low * second], axis=0).astype(BF16)
        carried = dot(jnp.concatenate(weights, axis=1), both)
        outs = carried + skip[:, at] * own
        _, gate = silu_parts(proj[:, at])
        gated = outs * gate
        outs_ref[:, at] = outs
        gated_ref[:, at] = gated
        squares = squares + jnp.sum(gated * gated, axis=1, keepdims=True)
    square_ref[...] = jnp.broadcast_to(squares, square_ref.shape)


def back_kernel(
    heads, proj, bc, aux, seg_row, conv_w, conv_b, dt_bias, neg_rate, skip, out_gain, outs, d_normed, scale, *rest
):
    d_main_ref, d_dt_ref, d_state_ref, d_wide_ref, d_narrow_ref = rest[-5:]
    rows = proj.shape[0]
    inner = heads * HALF
    aux_v = aux[...]
    values_in = proj[:, inner : 2 * inner]
    values_mixed, values_shifted = conv_mixed(values_in, aux_v, conv_w[:, :inner], conv_b[:, :inner])
    values_gate, values = silu_parts(values_mixed)
    state_mixed, _ = conv_mixed(bc[...], aux_v, conv_w[:, inner:], conv_b[:, inner:])
    _, state = silu_parts(state_mixed)
    in_state, out_state = state[:, :LANES].astype(BF16), state[:, LANES:].astype(BF16)
    last = proj[:, 2 * inner :]
    step, log_decay, allowed, lower = decays(last, dt_bias[...], neg_rate[...], aux_v, seg_row[0])
    step_t, log_t = step.T, log_decay.T
    inter = dot(out_state, in_state, ((1,), (1,)))
    first, second = pair_masks(rows)
    lane = lax.broadcasted_iota(jnp.int32, (rows, LANES), 1)
    sub = lax.broadcasted_iota(jnp.int32, (LANES, rows), 0)
    inverse, shrink = scale[:, 0:1], scale[:, 1:2]
    d_inter = jnp.zeros((rows, rows), F32)
    row_sums = jnp.zeros((rows, LANES), F32)
    col_sums = jnp.zeros((LANES, rows), F32)
    d_skip, d_gain, d_values = [], [], []
    for pair in range(heads // 2):
        at = slice(pair * LANES, (pair + 1) * LANES)
        own = values[:, at]
        low = own.astype(BF16)
        gate_in = proj[:, at]
        sig, gate = silu_parts(gate_in)
        outs_at = outs[:, at]
        gated = outs_at * gate
        dn = d_normed[:, at]
        d_gain.append(jnp.sum(gated * inverse * dn, axis=0, keepdims=True))
        d_gated = inverse * (out_gain[:, at] * dn) - gated * shrink
        d_outs = d_gated * gate
        d_main_ref[:, at] = (d_gated * outs_at * (sig * (1.0 + gate_in * (1.0 - sig)))).astype(BF16)
        d_skip.append(jnp.sum(d_outs * own, axis=0, keepdims=True))
        d_both = jnp.concatenate([d_outs * first, d_outs * second], axis=0).astype(BF16)
        d_weights = dot(d_both, low, ((1,), (1,)))
        weights = []
        for k, h in enumerate((2 * pair, 2 * pair + 1)):
            gap = log_decay[:, h : h + 1] - log_t[h : h + 1]
            decay = jnp.exp(jnp.where(allowed, gap, -1e30))
            step_row = step_t[h : h + 1]
            weights.append((inter * decay * step_row).astype(BF16))
            part = d_weights[k * rows : (k + 1) * rows] * decay
            d_inter = d_inter + part * step_row
            part = part * inter
            col = jnp.sum(part, axis=0, keepdims=True)
            col_sums = jnp.where(sub == h, col, col_sums)
            row_sum = jnp.sum(part * step_row, axis=1, keepdims=True)
            row_sums = jnp.where(lane == h, row_sum, row_sums)
        d_low = dot(jnp.concatenate(weights, axis=0), d_both, ((0,), (0,)))
        d_values.append(skip[:, at] * d_outs + d_low)
    d_values = jnp.concatenate(d_values, axis=1)
    d_mixed = d_values * (values_gate * (1.0 + values_mixed * (1.0 - values_gate)))
    d_in, d_w, d_b = conv_back(d_mixed, values_in, values_shifted, aux_v, conv_w[:, :inner])
    d_main_ref[:, inner : 2 * inner] = d_in.astype(BF16)
    low_inter = d_inter.astype(BF16)
    d_state_ref[:, :LANES] = dot(low_inter, out_state, ((0,), (0,)))
    d_state_ref[:, LANES:] = dot(low_inter, in_state)
    direct = col_sums.T
    d_log = row_sums - direct * step
    d_pace = dot_exact(lower.astype(F32), d_log, ((0,), (0,)))
    d_step = direct + d_pace * neg_rate[...]
    d_last = jnp.where(lane < heads, d_step * (1.0 / (1.0 + jnp.exp(-(last + dt_bias[...])))), 0.0)
    d_dt_ref[...] = d_last
    wide = d_w + [d_b, jnp.concatenate(d_skip, axis=1), jnp.concatenate(d_gain, axis=1)]
    wide.append(jnp.zeros((d_wide_ref.shape[1] - len(wide), inner), F32))
    d_wide_ref[0] = jnp.concatenate(wide, axis=0)
    d_rate = jnp.sum(d_pace * neg_rate[...] * step, axis=0, keepdims=True)
    narrow = [
        jnp.sum(d_last, axis=0, keepdims=True),
        jnp.where(lane[:1] < heads, d_rate, 0.0),
        jnp.zeros((d_narrow_ref.shape[1] - 2, LANES), F32),
    ]
    d_narrow_ref[0] = jnp.concatenate(narrow, axis=0)


def state_back_kernel(d_act, last, aux, conv_w, conv_b, d_dt, proj_ref, d_proj_ref, d_sums_ref):
    aux_v = aux[...]
    last_v = last[...]
    mixed, shifted = conv_mixed(last_v, aux_v, conv_w[...], conv_b[...])
    sig, _ = silu_parts(mixed)
    d_mixed = d_act[...] * (sig * (1.0 + mixed * (1.0 - sig)))
    d_in, d_w, d_b = conv_back(d_mixed, last_v, shifted, aux_v, conv_w[...])
    lane = lax.broadcasted_iota(jnp.int32, last_v.shape, 1)
    d_proj_ref[...] = jnp.where(lane < HALF, d_dt[...], d_in).astype(BF16)
    sums = d_w + [d_b]
    sums.append(jnp.zeros((d_sums_ref.shape[0] - len(sums), LANES), F32))
    d_sums_ref[...] = jnp.concatenate(sums, axis=0)


def rows_spec(rows, width, at):
    return pl.BlockSpec((rows, width), lambda i: (i + at, 0))


def whole_spec(shape):
    return pl.BlockSpec(shape, lambda i: (0,) * len(shape))


def ahead_call(heads, rows, at, count, proj, bc, aux, seg_rows, params, previous):
    conv_w, conv_b, dt_bias, neg_rate, skip = params
    total = proj.shape[0]
    inner = heads * HALF
    ins = [
        rows_spec(rows, proj.shape[1], at),
        rows_spec(rows, bc.shape[1], at),
        rows_spec(rows, aux.shape[1], at),
        pl.BlockSpec((1, 1, rows), lambda i: (i + at, 0, 0)),
    ] + [whole_spec(p.shape) for p in params]
    args = [proj, bc, aux, seg_rows, conv_w, conv_b, dt_bias, neg_rate, skip]
    aliases = {}
    if previous is not None:
        aliases = {len(args) + k: k for k in range(3)}
        ins += [pl.BlockSpec(memory_space=pl.ANY)] * 3
        args += list(previous)
    return pl.pallas_call(
        functools.partial(ahead_kernel, heads),
        grid=(count,),
        in_specs=ins,
        out_specs=[rows_spec(rows, inner, at), rows_spec(rows, inner, at), rows_spec(rows, LANES, at)],
        out_shape=[
            jax.ShapeDtypeStruct((total, inner), F32),
            jax.ShapeDtypeStruct((total, inner), F32),
            jax.ShapeDtypeStruct((total, LANES), F32),
        ],
        input_output_aliases=aliases,
        compiler_params=pltpu.CompilerParams(vmem_limit_bytes=VMEM_LIMIT),
        cost_estimate=pl.CostEstimate(
            flops=count * 2_000_000_000, bytes_accessed=count * 2_000_000, transcendentals=count * 400_000
        ),
    )(*args)


def back_call(heads, rows, at, count, proj, bc, aux, seg_rows, params, out_gain, outs, d_normed, scale, previous):
    total = proj.shape[0]
    inner = heads * HALF
    ins = [
        rows_spec(rows, proj.shape[1], at),
        rows_spec(rows, bc.shape[1], at),
        rows_spec(rows, aux.shape[1], at),
        pl.BlockSpec((1, 1, rows), lambda i: (i + at, 0, 0)),
    ] + [whole_spec(p.shape) for p in params]
    ins += [
        whole_spec(out_gain.shape),
        rows_spec(rows, inner, at),
        rows_spec(rows, inner, at),
        rows_spec(rows, scale.shape[1], at),
    ]
    args = [proj, bc, aux, seg_rows, *params, out_gain, outs, d_normed, scale]
    aliases = {}
    if previous is not None:
        aliases = {len(args) + k: k for k in range(5)}
        ins += [pl.BlockSpec(memory_space=pl.ANY)] * 5
        args += list(previous)
    blocks = total // rows
    return pl.pallas_call(
        functools.partial(back_kernel, heads),
        grid=(count,),
        in_specs=ins,
        out_specs=[
            rows_spec(rows, 2 * inner, at),
            rows_spec(rows, LANES, at),
            rows_spec(rows, bc.shape[1], at),
            pl.BlockSpec((1, 8, inner), lambda i: (i + at, 0, 0)),
            pl.BlockSpec((1, 8, LANES), lambda i: (i + at, 0, 0)),
        ],
        out_shape=[
            jax.ShapeDtypeStruct((total, 2 * inner + LANES), BF16),
            jax.ShapeDtypeStruct((total, LANES), F32),
            jax.ShapeDtypeStruct((total, bc.shape[1]), F32),
            jax.ShapeDtypeStruct((blocks, 8, inner), F32),
            jax.ShapeDtypeStruct((blocks, 8, LANES), F32),
        ],
        input_output_aliases=aliases,
        compiler_params=pltpu.CompilerParams(vmem_limit_bytes=VMEM_LIMIT),
        cost_estimate=pl.CostEstimate(
            flops=count * 4_000_000_000, bytes_accessed=count * 3_000_000, transcendentals=count * 600_000
        ),
    )(*args)


def state_back_call(d_act, proj, aux, conv_w, conv_b, d_dt, d_proj):
    total = proj.shape[0]
    column = proj.shape[1] // LANES - 1
    last_spec = pl.BlockSpec((total, LANES), lambda i: (0, column))
    return pl.pallas_call(
        state_back_kernel,
        grid=(1,),
        in_specs=[
            whole_spec(d_act.shape),
            last_spec,
            whole_spec(aux.shape),
            whole_spec(conv_w.shape),
            whole_spec(conv_b.shape),
            whole_spec(d_dt.shape),
            pl.BlockSpec(memory_space=pl.ANY),
        ],
        out_specs=[last_spec, whole_spec((8, LANES))],
        out_shape=[jax.ShapeDtypeStruct(d_proj.shape, BF16), jax.ShapeDtypeStruct((8, LANES), F32)],
        input_output_aliases={6: 0},
        compiler_params=pltpu.CompilerParams(vmem_limit_bytes=VMEM_LIMIT),
        cost_estimate=pl.CostEstimate(flops=1_000_000_000, bytes_accessed=1_500_000, transcendentals=70_000),
    )(d_act, proj, aux, conv_w, conv_b, d_dt, d_proj)


def make_aux(seg, rows, taps):
    blocks = seg.shape[0]
    columns = [seg.astype(F32)]
    for k in range(1, taps):
        before = jnp.pad(seg, ((0, 0), (k, 0)), constant_values=-1)[:, :rows]
        columns.append((before == seg).astype(F32))
    for k in range(1, taps):
        after = jnp.pad(seg, ((0, 0), (0, k)), constant_values=-1)[:, k:]
        columns.append((after == seg).astype(F32))
    columns += [jnp.zeros_like(columns[0])] * (8 - len(columns))
    return jnp.stack(columns, axis=-1).reshape(blocks * rows, 8)


def assemble_kernel(shard_rows, line, both, *refs):
    place_ref, sources, out, sems = refs[0], refs[1:-2], refs[-2], refs[-1]
    mine, side = place_ref[0], place_ref[1]

    def copies(run):
        count = 0
        for hop in range(-(line - 1), line):
            for other in range(2):
                source = sources[hop + line - 1] if both else sources[(hop + line - 1) * 2 + other]
                owner = mine + hop
                chunk = 2 * owner + (1 - side if other else side)
                chunk = jnp.clip(chunk, 0, 2 * line - 1)
                start = pl.multiple_of(chunk * shard_rows, 16)
                copy = pltpu.make_async_copy(
                    source.at[other] if both else source, out.at[pl.ds(start, shard_rows)], sems.at[count]
                )
                pl.when((owner >= 0) & (owner < line))(functools.partial(run, copy))
                count += 1

    copies(lambda copy: copy.start())
    copies(lambda copy: copy.wait())


def assemble(place, sources, shard_rows, line, both):
    width = sources[0].shape[-1]
    return pl.pallas_call(
        functools.partial(assemble_kernel, shard_rows, line, both),
        in_specs=[pl.BlockSpec(memory_space=pltpu.SMEM)] + [pl.BlockSpec(memory_space=pl.ANY)] * len(sources),
        out_specs=pl.BlockSpec(memory_space=pltpu.VMEM),
        out_shape=jax.ShapeDtypeStruct((2 * line * shard_rows, width), BF16),
        scratch_shapes=[pltpu.SemaphoreType.DMA((2 * (2 * line - 1),))],
        compiler_params=pltpu.CompilerParams(vmem_limit_bytes=VMEM_LIMIT),
        cost_estimate=pl.CostEstimate(
            flops=0, bytes_accessed=4 * line * shard_rows * width * 2, transcendentals=0
        ),
    )(place, *sources)


class Links:
    def __init__(self, mesh_shape):
        self.line = mesh_shape["fsdp"] // 2
        self.at = lax.axis_index("fsdp")
        self.place, self.side = self.at // 2, self.at % 2
        self.row, self.core = lax.axis_index("dp"), lax.axis_index("section")

    def swap_core(self, x):
        return lax.ppermute(x, "section", [(0, 1), (1, 0)])

    def swap_row(self, x):
        return lax.ppermute(x, "dp", [(0, 1), (1, 0)])

    def swap_side(self, x, places=None):
        places = range(self.line) if places is None else places
        return lax.ppermute(x, "fsdp", [(2 * p + s, 2 * p + 1 - s) for p in places for s in range(2)])

    def along(self, x, places, by):
        return lax.ppermute(x, "fsdp", [(2 * p + s, 2 * (p + by) + s) for p in places for s in range(2)])

    def mine_of_core(self, first, second):
        return jnp.where(self.core == 0, first, second)

    def in_row_order(self, own, other, axis):
        return jnp.where(
            self.row == 0, jnp.concatenate([own, other], axis), jnp.concatenate([other, own], axis)
        )

    def in_core_order(self, own, other, axis):
        return jnp.where(
            self.core == 0, jnp.concatenate([own, other], axis), jnp.concatenate([other, own], axis)
        )

    def cut(self, x, axis, which, parts=2):
        size = x.shape[axis] // parts
        return lax.dynamic_slice_in_dim(x, which * size, size, axis)

    def reached(self, hop):
        return [p for p in range(self.line) if 0 <= p + hop < self.line]

    def gather(self, piece, after=None):
        line = self.line
        if after is not None:
            piece, _ = lax.optimization_barrier((piece, after))
        got = {0: (piece, self.swap_side(piece))}
        up = down = piece
        marks = []
        for hop in range(1, line):
            up = self.along(up, [p for p in range(line - 1) if p >= hop - 1], 1)
            down = self.along(down, [p for p in range(1, line) if p <= line - hop], -1)
            marks.append(up)
            if 2 * hop >= line:
                either = jnp.where(self.place >= hop, up, down)
                crossed = self.swap_side(either, sorted(self.reached(-hop) + self.reached(hop)))
                got[-hop], got[hop] = (either, crossed), (either, crossed)
            else:
                got[-hop] = (up, self.swap_side(up, self.reached(-hop)))
                got[hop] = (down, self.swap_side(down, self.reached(hop)))
        sources = [got[hop][k] for hop in range(-(line - 1), line) for k in range(2)]
        where = jnp.stack([self.place, self.side])
        return assemble(where, sources, piece.shape[0], line, False), marks

    def gather_pairs(self, piece, after=None):
        line = self.line
        if after is not None:
            piece, _ = lax.optimization_barrier((piece, after))
        pair = jnp.stack([piece, self.swap_side(piece)])
        got = {0: pair}
        up = down = pair
        for hop in range(1, line):
            up = self.along(up, [p for p in range(line - 1) if p >= hop - 1], 1)
            down = self.along(down, [p for p in range(1, line) if p <= line - hop], -1)
            got[-hop], got[hop] = up, down
        sources = [got[hop] for hop in range(-(line - 1), line)]
        where = jnp.stack([self.place, self.side])
        return assemble(where, sources, piece.shape[0], line, True)

    def scatter(self, parts, after=None):
        line = self.line
        if after is not None:
            parts, _ = lax.optimization_barrier((parts, after))

        def part(place, other):
            index = 2 * place + (1 - self.side if other else self.side)
            return lax.dynamic_index_in_dim(parts, index, 0, keepdims=False)

        def joined(place, places):
            place = jnp.clip(place, 0, line - 1)
            return part(place, False).astype(F32) + self.swap_side(part(place, True), places).astype(F32)

        up = down = 0.0
        for hop in range(line - 1, 0, -1):
            if 2 * hop >= line:
                place = jnp.where(self.place >= hop, self.place - hop, self.place + hop)
                own_up = own_down = joined(place, sorted(self.reached(-hop) + self.reached(hop)))
            else:
                own_down = joined(self.place - hop, self.reached(-hop))
                own_up = joined(self.place + hop, self.reached(hop))
            down = self.along((own_down + down).astype(BF16), self.reached(-hop), -1).astype(F32)
            up = self.along((own_up + up).astype(BF16), self.reached(hop), 1).astype(F32)
        return joined(self.place, range(line)) + up + down

    def scatter_pairs(self, parts, after=None):
        line = self.line
        if after is not None:
            parts, _ = lax.optimization_barrier((parts, after))

        def pair(place):
            place = jnp.clip(place, 0, line - 1)
            return lax.dynamic_slice_in_dim(parts, 2 * place, 2, 0).astype(F32)

        up = down = 0.0
        for hop in range(line - 1, 0, -1):
            down = self.along((pair(self.place - hop) + down).astype(BF16), self.reached(-hop), -1).astype(F32)
            up = self.along((pair(self.place + hop) + up).astype(BF16), self.reached(hop), 1).astype(F32)
        total = pair(self.place) + up + down
        own = lax.dynamic_index_in_dim(total, self.side, 0, keepdims=False)
        sent = lax.dynamic_index_in_dim(total, 1 - self.side, 0, keepdims=False)
        return own + self.swap_side(sent.astype(BF16)).astype(F32)

    def sum_fsdp(self, x):
        x = x + self.swap_side(x)
        size = self.line
        if size & (size - 1):
            return lax.psum(x, "fsdp") / 2
        by = 1
        while by < size:
            pairs = [(2 * p + s, 2 * (p ^ by) + s) for p in range(size) for s in range(2)]
            x = x + lax.ppermute(x, "fsdp", pairs)
            by *= 2
        return x


def body(mesh_shape, inputs, seq_lengths, norm_gain, in_w, conv_w, conv_b, dt_bias, a_log, skip, out_gain, out_w, cotangent):
    links = Links(mesh_shape)
    core, row = links.core, links.row
    shards = mesh_shape["fsdp"]
    width = inputs.shape[1]
    half_width = width // 2
    own_tokens = inputs.shape[0]
    tokens = 2 * own_tokens
    rows = own_tokens // seq_lengths.shape[0]
    inner_all = out_gain.shape[1]
    heads_all = a_log.shape[1]
    head_dim = inner_all // heads_all
    taps, channels = conv_w.shape[1:]
    state_all = channels - inner_all
    state = state_all // 2
    heads = heads_all // 4
    inner = inner_all // 4
    shard_rows = in_w.shape[1]
    direct = (heads_all // shards) % 2 == 0 and heads_all % shards == 0
    groups = shards // 2 if direct else 1
    each = heads // groups
    span = each * head_dim

    def of_row(x, axis):
        return lax.index_in_dim(x, 0, axis, False), lax.index_in_dim(x, 1, axis, False)

    def pick_row(x, axis):
        first, second = of_row(x, axis)
        return jnp.where(row == 0, first, second)

    def wide_part(x, part):
        lead = x.shape[:-1]
        x = x.reshape(lead + (2, groups, 2, span))
        x = lax.index_in_dim(x, part, len(lead), False)
        return pick_row(x, len(lead) + 1).reshape(lead + (inner,))

    def head_part(x, part):
        lead = x.shape[:-1]
        x = x.reshape(lead + (2, groups, 2, each))
        x = lax.index_in_dim(x, part, len(lead), False)
        return pick_row(x, len(lead) + 1).reshape(lead + (heads,))

    def state_part(x, part):
        lead = x.shape[:-1]
        x = x.reshape(lead + (2, 2, state_all // 4))
        x = lax.index_in_dim(x, part, len(lead), False)
        return pick_row(x, len(lead))

    def columns_of(w, part):
        spare = jnp.zeros(w.shape[:-1] + (LANES - heads - state_all // 4,), w.dtype)
        return jnp.concatenate(
            [
                wide_part(w[:, :inner_all], part),
                wide_part(w[:, inner_all : 2 * inner_all], part),
                head_part(w[:, inner_all + channels :], part),
                spare,
                state_part(w[:, 2 * inner_all : inner_all + channels], part),
            ],
            axis=1,
        )

    def both_layers(own_part, other_part):
        came = links.swap_core(other_part)
        return links.mine_of_core(own_part, came), links.mine_of_core(came, own_part)

    in_first, in_second = columns_of(in_w[0], 0), columns_of(in_w[0], 1)
    in_pieces = both_layers(links.mine_of_core(in_first, in_second), links.mine_of_core(in_second, in_first))

    if direct:
        out_rows = pick_row(out_w[0].reshape(2, out_w.shape[1] // 2, width), 0)
    else:
        out_rows = out_w[0]
    out_first, out_second = out_rows[:, :half_width], out_rows[:, half_width:]
    out_pieces = both_layers(
        links.mine_of_core(out_first, out_second), links.mine_of_core(out_second, out_first)
    )

    def wide_row(x):
        return jnp.pad(x, ((0, 0), (0, channels - x.shape[1])))

    packed = jnp.concatenate(
        [conv_w[0], conv_b, wide_row(out_gain), wide_row(norm_gain), wide_row(dt_bias), wide_row(a_log), wide_row(skip)],
        axis=0,
    )
    packed_other = links.swap_core(packed)
    own_core_inner = lambda x: links.mine_of_core(wide_part(x, 0), wide_part(x, 1))
    own_core_heads = lambda x: links.mine_of_core(head_part(x, 0), head_part(x, 1))
    own_core_state = lambda x: links.mine_of_core(state_part(x, 0), state_part(x, 1))
    pad_lanes = lambda x: jnp.pad(x, ((0, 0), (0, LANES - x.shape[1])))

    def layer_params(pack):
        cw, cb = pack[:taps], pack[taps : taps + 1]
        og, ng = pack[taps + 1 : taps + 2, :inner_all], pack[taps + 2 : taps + 3, :width]
        dt, al, sk = (pack[taps + 3 + k : taps + 4 + k, :heads_all] for k in range(3))
        conv_full = jnp.concatenate([own_core_inner(cw[:, :inner_all]), cw[:, inner_all:]], axis=1)
        bias_full = jnp.concatenate([own_core_inner(cb[:, :inner_all]), cb[:, inner_all:]], axis=1)
        al = own_core_heads(al)
        lanes = (
            conv_full,
            bias_full,
            pad_lanes(own_core_heads(dt)),
            pad_lanes(-jnp.exp(al)),
            jnp.repeat(own_core_heads(sk), head_dim, axis=1),
        )
        front = lambda x: jnp.pad(x, ((0, 0), (LANES - x.shape[1], 0)))
        return {
            "lanes": lanes,
            "out_gain": own_core_inner(og),
            "norm_gain": ng,
            "state_w": front(own_core_state(cw[:, inner_all:])),
            "state_b": front(own_core_state(cb[:, inner_all:])),
        }

    params = (
        layer_params(links.mine_of_core(packed, packed_other)),
        layer_params(links.mine_of_core(packed_other, packed)),
    )

    all_tokens = links.in_row_order(inputs, links.swap_row(inputs), 0)
    all_lengths = links.in_row_order(seq_lengths, links.swap_row(seq_lengths), 0)
    ends = jnp.cumsum(all_lengths, axis=1)
    positions = jnp.arange(rows, dtype=jnp.int32)
    segments = jnp.sum((positions[None, :, None] >= ends[:, None, :]).astype(jnp.int32), axis=2)
    aux = make_aux(segments, rows, taps)
    seg_rows = segments.astype(F32)[:, None, :]
    blocks = tokens // rows
    per_call = 2 if blocks % 2 == 0 else 1

    def out_whole(pieces):
        kept = links.cut(pieces, 0, core)
        came = links.swap_core(links.cut(pieces, 0, 1 - core))
        return links.in_core_order(kept, came, 1)

    def gather_out(piece, pairs, after):
        if direct:
            full = links.gather_pairs(piece, after) if pairs else links.gather(piece, after)[0]
        else:
            full = lax.all_gather(piece, "fsdp", axis=0, tiled=True)
            full = pick_row(full.reshape(2, 2, inner, half_width), 1).reshape(2 * inner, half_width)
        return out_whole(full)

    in_weight, out_weight = [None, None], [None, None]
    in_weight[0], marks = links.gather(in_pieces[0])
    out_weight[0] = gather_out(out_pieces[0], False, marks[0])
    in_weight[1], marks = links.gather(in_pieces[1], marks[-1])
    out_weight[1] = gather_out(out_pieces[1], True, marks[-1])

    def to_rows(x):
        return x.reshape(-1, LANES)

    def total_of(x):
        x = to_rows(x)
        x = x + links.swap_core(x)
        x = x + links.swap_row(x)
        return x.reshape(-1)

    def norm_of(u):
        return lax.rsqrt(jnp.mean(u * u, axis=-1, keepdims=True) + 1e-05)

    def ahead(layer, u):
        own = params[layer]
        u = u.astype(F32)
        scaled = (u * norm_of(u) * own["norm_gain"]).astype(BF16)
        proj = dot(scaled, in_weight[layer])
        part = proj[:, 2 * inner + LANES - state_all // 4 :]
        part = links.in_row_order(part, links.swap_row(part), 1)
        bc = links.in_core_order(part, links.swap_core(part), 1)
        done = None
        for at in range(0, blocks, per_call):
            done = ahead_call(heads, rows, at, per_call, proj, bc, aux, seg_rows, own["lanes"], done)
        outs, gated, squares = done
        inverse = lax.rsqrt(total_of(squares[:, 0]) / inner_all + 1e-05)[:, None]
        normed = (gated * inverse * own["out_gain"]).astype(BF16)
        return {"scaled": scaled, "proj": proj, "bc": bc, "outs": outs, "gated": gated, "inverse": inverse, "normed": normed}

    def over_cores(x):
        kept = links.cut(x, 1, core)
        return kept + links.swap_core(links.cut(x, 1, 1 - core))

    def over_rows(x):
        x = x.astype(BF16)
        return x.astype(F32) + links.swap_row(x).astype(F32)

    def over_rows_own(x):
        kept = links.cut(x, 0, row)
        return kept + links.swap_row(links.cut(x, 0, 1 - row).astype(BF16)).astype(F32)

    def own_rows(x):
        return links.cut(x, 0, row)

    saved = [None, None]
    saved[0] = ahead(0, all_tokens)
    branch = over_rows(over_cores(dot(saved[0]["normed"], out_weight[0])))
    first = (links.cut(all_tokens, 1, core).astype(F32) + branch).astype(BF16)
    first = links.in_core_order(first, links.swap_core(first), 1)
    saved[1] = ahead(1, first)
    last_partial = dot(saved[1]["normed"], out_weight[1])
    branch = over_rows_own(over_cores(last_partial))
    second = (links.cut(own_rows(first), 1, core).astype(F32) + branch).astype(BF16)
    second = links.in_core_order(second, links.swap_core(second), 1)
    phase_out = jnp.where(core == 0, own_rows(first), second)[None]

    def out_parts(d_out):
        kept = links.cut(d_out, 1, core)
        came = links.swap_core(links.cut(d_out, 1, 1 - core))
        return links.in_core_order(kept, came, 0)

    def scatter_out(d_out, pairs, after=None):
        parts = out_parts(d_out)
        if direct:
            parts = parts.reshape(shards, -1, half_width)
            return links.scatter_pairs(parts, after) if pairs else links.scatter(parts, after)
        parts = parts.reshape(2, 1, inner, half_width)
        empty = jnp.zeros_like(parts)
        parts = links.in_row_order(parts, empty, 1).reshape(4 * inner, half_width)
        mine = lax.psum_scatter(parts, "fsdp", scatter_dimension=0, tiled=True)
        return mine.astype(F32) + links.swap_row(mine).astype(F32)

    def back(layer, grad):
        own, kept = params[layer], saved[layer]
        d_out = dot(kept["normed"], grad, ((0,), (0,))).astype(BF16)
        d_normed = dot(grad, out_weight[layer], ((1,), (1,)))
        meet = total_of(jnp.sum(kept["gated"] * own["out_gain"] * d_normed, axis=1))[:, None]
        inverse = kept["inverse"]
        scale = jnp.concatenate(
            [inverse, inverse * inverse * inverse * meet / inner_all, jnp.zeros((tokens, 6), F32)], axis=1
        )
        done = None
        for at in range(0, blocks, per_call):
            done = back_call(
                heads, rows, at, per_call, kept["proj"], kept["bc"], aux, seg_rows, own["lanes"],
                own["out_gain"], kept["outs"], d_normed, scale, done,
            )
        d_proj, d_dt, d_bc, d_wide, d_narrow = done
        d_bc = over_cores(d_bc)
        d_bc = links.cut(d_bc, 1, row) + links.swap_row(links.cut(d_bc, 1, 1 - row))
        d_bc = jnp.pad(d_bc, ((0, 0), (LANES - d_bc.shape[1], 0)))
        d_proj, d_state = state_back_call(d_bc, kept["proj"], aux, own["state_w"], own["state_b"], d_dt, d_proj)
        d_in = dot(kept["scaled"], d_proj, ((0,), (0,))).astype(BF16).reshape(shards, shard_rows, -1)
        d_scaled = over_cores(dot(d_proj, in_weight[layer], ((1,), (1,))))
        return d_out, d_in, d_scaled, jnp.sum(d_wide, axis=0), jnp.sum(d_narrow, axis=0), d_state

    def norm_back(layer, u, d_scaled):
        u = u.astype(F32)
        inverse = norm_of(u)
        gain = params[layer]["norm_gain"]
        meet = jnp.mean(u * gain * d_scaled, axis=1, keepdims=True)
        return inverse * gain * d_scaled - u * (inverse * inverse * inverse * meet)

    def gain_back(u, d_scaled):
        u = u.astype(F32)
        return jnp.sum(u * norm_of(u) * d_scaled, axis=0, keepdims=True)

    all_cot = links.in_row_order(cotangent, links.swap_row(cotangent), 0)
    d_out, d_in, d_scaled, wide1, narrow1, state1 = back(1, all_cot)
    sums_out1 = scatter_out(d_out, True)
    sums_in1 = links.scatter(d_in)
    d_scaled = over_rows(d_scaled)
    d_scaled = links.in_core_order(d_scaled, links.swap_core(d_scaled), 1)
    grad = (all_cot.astype(F32) + norm_back(1, first, d_scaled)).astype(BF16)
    gain1 = gain_back(own_rows(first), own_rows(d_scaled))

    d_out, d_in, d_scaled, wide0, narrow0, state0 = back(0, grad)
    sums_out0 = scatter_out(d_out, False)
    sums_in0 = links.scatter(d_in)
    d_scaled = over_rows_own(d_scaled)
    d_scaled = links.in_core_order(d_scaled, links.swap_core(d_scaled), 1)
    own_grad = own_rows(grad)
    grad_in = (own_grad.astype(F32) + norm_back(0, inputs, d_scaled)).astype(BF16)
    gain0 = gain_back(inputs, d_scaled)
    input_grad = jnp.where(core == 0, grad_in, own_grad)[None]

    def pack_small(wide, narrow, gain, d_state):
        gain = gain.reshape(-1, inner)
        narrow_rows = jnp.concatenate([narrow[:2], d_state[: taps + 1]], axis=0)
        narrow_rows = jnp.pad(narrow_rows.reshape(1, -1), ((0, 0), (0, 2 * inner - narrow_rows.size)))
        return jnp.concatenate([wide[: taps + 3], gain, narrow_rows.reshape(2, inner)], axis=0)

    gain_rows = width // inner
    small = jnp.concatenate([pack_small(wide0, narrow0, gain0, state0), pack_small(wide1, narrow1, gain1, state1)], axis=0)
    small = links.sum_fsdp(small)
    per = small.shape[0] // 2
    small_other = links.swap_row(small)
    mine = links.mine_of_core(small[:per], small[per:])
    mine_other = links.mine_of_core(small_other[:per], small_other[per:])
    theirs = links.mine_of_core(small[per:], small[:per])
    theirs_other = links.mine_of_core(small_other[per:], small_other[:per])
    came = links.swap_core(jnp.stack([theirs, theirs_other]))
    by_row = lambda a, b: jnp.where(row == 0, jnp.stack([a, b]), jnp.stack([b, a]))
    own_parts, came_parts = by_row(mine, mine_other), by_row(came[0], came[1])
    quarters = jnp.where(core == 0, jnp.stack([own_parts, came_parts]), jnp.stack([came_parts, own_parts]))

    def spread_wide(x):
        lead = x.shape[2:-1]
        x = x.reshape((2, 2) + lead + (groups, span))
        x = jnp.moveaxis(x, (0, 1), (len(lead), len(lead) + 2))
        return x.reshape(lead + (inner_all,))

    def spread_heads(x):
        x = x.reshape((2, 2, groups, each))
        return jnp.moveaxis(x, 1, 2).reshape(1, heads_all)

    wide = quarters[:, :, : taps + 3]
    grad_norm = mine[taps + 3 : taps + 3 + gain_rows] + mine_other[taps + 3 : taps + 3 + gain_rows]
    grad_norm = grad_norm.reshape(1, width)
    narrow = quarters[:, :, taps + 3 + gain_rows :].reshape(2, 2, -1)
    narrow = narrow[:, :, : (taps + 3) * LANES].reshape(2, 2, taps + 3, LANES)
    states = narrow[:, :, 2:, LANES - state_all // 4 :]
    states = jnp.moveaxis(states, 2, 0).reshape(taps + 1, state_all)
    wide_full = spread_wide(wide)
    grad_conv_w = jnp.concatenate([wide_full[:taps], states[:taps]], axis=1)[None]
    grad_conv_b = jnp.concatenate([wide_full[taps : taps + 1], states[taps:]], axis=1)
    grad_skip = wide_full[taps + 1].reshape(1, heads_all, head_dim).sum(axis=-1)
    grad_out_gain = wide_full[taps + 2 : taps + 3]
    grad_dt = spread_heads(narrow[:, :, 0, :heads])
    grad_a = spread_heads(narrow[:, :, 1, :heads])

    def own_layer(x0, x1):
        low0, low1 = x0.astype(BF16), x1.astype(BF16)
        far0, far1 = links.swap_row(low0), links.swap_row(low1)
        mine, far = links.mine_of_core(low0, low1), links.mine_of_core(far0, far1)
        came = links.swap_core(jnp.stack([links.mine_of_core(low1, low0), links.mine_of_core(far1, far0)]))
        own_rows_, came_rows = by_row(mine, far), by_row(came[0], came[1])
        return jnp.where(core == 0, jnp.stack([own_rows_, came_rows]), jnp.stack([came_rows, own_rows_]))

    whole_in = own_layer(sums_in0, sums_in1).astype(F32)

    def spread_columns(x):
        x = x.reshape(2, 2, shard_rows, groups, span)
        return x.transpose(2, 0, 3, 1, 4).reshape(shard_rows, inner_all)

    tail = whole_in[..., 2 * inner :]
    grad_in_w = jnp.concatenate(
        [
            spread_columns(whole_in[..., :inner]),
            spread_columns(whole_in[..., inner : 2 * inner]),
            tail[..., LANES - state_all // 4 :].transpose(2, 0, 1, 3).reshape(shard_rows, state_all),
            tail[..., :heads].reshape(2, 2, shard_rows, groups, each).transpose(2, 0, 3, 1, 4).reshape(shard_rows, heads_all),
        ],
        axis=1,
    )[None]
    if direct:
        whole_out = own_layer(sums_out0, sums_out1).astype(F32)
        grad_out_w = whole_out.transpose(1, 2, 0, 3).reshape(1, out_w.shape[1], width)
    else:
        came = links.swap_core(links.mine_of_core(sums_out1, sums_out0).astype(BF16)).astype(F32)
        grad_out_w = links.in_core_order(links.mine_of_core(sums_out0, sums_out1), came, 1)[None]

    return (
        phase_out, input_grad, grad_norm, grad_in_w, grad_conv_w, grad_conv_b,
        grad_dt, grad_a, grad_skip, grad_out_gain, grad_out_w,
    )


def solution(mesh):
    return jax.shard_map(
        functools.partial(body, dict(mesh.shape)),
        mesh=mesh,
        in_specs=(
            P(("fsdp", "dp"), None),
            P(("fsdp", "dp"), None),
            P("section", None),
            P("section", "fsdp", None),
            P("section", None, None),
            P("section", None),
            P("section", None),
            P("section", None),
            P("section", None),
            P("section", None),
            P("section", "fsdp", None),
            P(("fsdp", "dp"), None),
        ),
        out_specs=(
            P("section", ("fsdp", "dp"), None),
            P("section", ("fsdp", "dp"), None),
            P("section", None),
            P("section", "fsdp", None),
            P("section", None, None),
            P("section", None),
            P("section", None),
            P("section", None),
            P("section", None),
            P("section", None),
            P("section", "fsdp", None),
        ),
        check_vma=False,
    )
```

time: 2400 us -> 786 us (0.33)
  waiting for transfers between devices: 1540 us -> 253 us
  local copies, waits for them, and re-layouts: 440 us -> 124 us
  starting transfers between devices: 7.25 us -> 227 us
  matrix products: 243 us -> 39.8 us
  other arithmetic: 138 us -> 83.3 us
  Pallas kernels: 0 us -> 42.6 us
    unnamed x13 -> x0, waiting for transfers between devices: 845 us -> none
    all_gather x2 -> x0, waiting for transfers between devices: 502 us -> none  [the longest x1 385 us: body(): lax.all_gather(in_w, 'fsdp', axis=1, tiled=True)]
    unnamed x374 -> x392, local copies, waits for them, and re-layouts: 421 us -> 44.2 us
    ppermute x4 -> x129, waiting for transfers between devices: 1.42 us -> 253 us  [the longest x33 107 us: swap_side(): lax.ppermute(x, 'fsdp', [(2 * p + s, 2 * p + 1 - s) for p in places for s...]
    ppermute x4 -> x129, starting transfers between devices: 6.84 us -> 227 us  [the longest x48 137 us: along(): lax.ppermute(x, 'fsdp', [(2 * p + s, 2 * (p + by) + s) for p in places fo...]
    dot_general x45 -> x12, matrix products: 243 us -> 39.8 us  [dot(): lax.dot_general(a, b, (dims, ((), ())), precision=precision, preferred_el...]
    psum x2 -> x0, waiting for transfers between devices: 187 us -> none  [the longest x1 108 us: body(): small_total = lax.psum(small_terms, ('fsdp', 'dp'))]
    pallas_call x0 -> x14, Pallas kernels: none -> 42.6 us  [the longest x4 21.8 us: back_call(): pl.pallas_call(functools.partial(back_kernel, heads), grid=(count,), in_s...]
  transfers between devices with their start and end apart: 14 -> 129, of which waited for: 9 -> 44; matrix products, arithmetic and copies ran while one was open for 30% -> 22% of each run, Pallas kernels for 0% -> 4%
where the time goes in v1:
time: 786 us; the launch traced here: 775 us
  waiting for transfers between devices  253 us (32%)
  starting transfers between devices  227 us (29%)
  local copies, waits for them, and re-layouts  124 us (16%)
  other arithmetic  83.3 us (11%)
  Pallas kernels  42.6 us (5%)
  matrix products  39.8 us (5%)
    ppermute x48, starting transfers between devices, along(): lax.ppermute(x, 'fsdp', [(2 * p + s, 2 * (p + by) + s) for p in places fo...  137 us
    ppermute x33, waiting for transfers between devices, swap_side(): lax.ppermute(x, 'fsdp', [(2 * p + s, 2 * p + 1 - s) for p in places for s...  107 us
    ppermute x48, waiting for transfers between devices, along(): lax.ppermute(x, 'fsdp', [(2 * p + s, 2 * (p + by) + s) for p in places fo...  98.3 us
    ppermute x33, starting transfers between devices, swap_side(): lax.ppermute(x, 'fsdp', [(2 * p + s, 2 * p + 1 - s) for p in places for s...  58.6 us
    ppermute x20, waiting for transfers between devices, swap_row(): return lax.ppermute(x, 'dp', [(0, 1), (1, 0)])  46.6 us
    unnamed x392, local copies, waits for them, and re-layouts  44.2 us
    dot_general x12, matrix products, dot(): lax.dot_general(a, b, (dims, ((), ())), precision=precision, preferred_el...  39.8 us
    pallas_call x4, Pallas kernels, back_call(): pl.pallas_call(functools.partial(back_kernel, heads), grid=(count,), in_s...  21.8 us
  transfers between devices with their start and end apart: 129, of which 44 were waited for; matrix products, arithmetic and copies ran while one was open for 22% of the time, Pallas kernels for 4%

profile of v1, /device:TPU:0, one launch (start us, length us, event | category | flops | bytes accessed | tf_op | source)
XLA Modules:
  0.0 774.7 jit_solution(18087439378745934641)
XLA Ops:
  3.3 3.8 copy.304
  28.1 14.7 %collective-permute-done.16 = s32[2,3]{1,0:T(2,128)S(1)} collective-permute-done((s32[2,3]{1,0:T(2,128)S(1)}, s32[2,3]{1,0:T(2,128)S(1)}, u32[]{:S(2)}, u32[]{:S(2)}) %collective-permute-start.16) | collective-permute-done | bytes 56 | tf_op jit(solution)/shard_map/ppermute | solution.py:382
  49.7 3.8 collective-permute-start.3
  56.0 10.5 %collective-permute-done.3.refs_5_ = bf16[192,1664]{1,0:T(8,128)(2,1)S(1)} collective-permute-done((bf16[192,1664]{1,0:T(8,128)(2,1)S(1)}, bf16[192,1664]{1,0:T(8,128)(2,1)S(1)}, u32[]{:S(2)}, u32[]{:S(2)}) %collective-permute-start.3) | collective-permute-done | bytes 639008 | tf_op jit(solution)/shard_map/ppermute | solution.py:389
  77.2 10.7 %collective-permute-done.7 = bf16[192,1664]{1,0:T(8,128)(2,1)} collective-permute-done((bf16[192,1664]{1,0:T(8,128)(2,1)S(1)}, bf16[192,1664]{1,0:T(8,128)(2,1)}, u32[]{:S(2)}, u32[]{:S(2)}) %collective-permute-start.7) | collective-permute-done | bytes 639008 | tf_op jit(solution)/shard_map/ppermute | solution.py:389
  91.1 4.6 collective-permute-start.20
  101.5 8.6 %collective-permute-done.23.refs_9_ = bf16[192,768]{1,0:T(8,128)(2,1)S(1)} collective-permute-done((bf16[192,768]{1,0:T(8,128)(2,1)S(1)}, bf16[192,768]{1,0:T(8,128)(2,1)S(1)}, u32[]{:S(2)}, u32[]{:S(2)}) %collective-permute-start.23) | collective-permute-done | bytes 294944 | tf_op jit(solution)/shard_map/ppermute | solution.py:389
  112.8 3.4 collective-permute-start.13
  116.8 4.1 collective-permute-done.24
  120.9 3.3 collective-permute-start.9
  128.2 3.8 collective-permute-done.13.refs_10_
  132.0 3.4 collective-permute-start.30
  135.5 10.3 %collective-permute-done.10.refs_4_.refs_12_ = bf16[192,1664]{1,0:T(8,128)(2,1)S(1)} collective-permute-done((bf16[192,1664]{1,0:T(8,128)(2,1)S(1)}, bf16[192,1664]{1,0:T(8,128)(2,1)S(1)}, u32[]{:S(2)}, u32[]{:S(2)}) %collective-permute-start.10) | collective-permute-done | bytes 639008 | tf_op jit(solution)/shard_map/ppermute | solution.py:386
  146.4 13.0 %collective-permute-done.9.refs_2_.refs_14_ = bf16[192,1664]{1,0:T(8,128)(2,1)S(1)} collective-permute-done((bf16[192,1664]{1,0:T(8,128)(2,1)S(1)}, bf16[192,1664]{1,0:T(8,128)(2,1)S(1)}, u32[]{:S(2)}, u32[]{:S(2)}) %collective-permute-start.9) | collective-permute-done | bytes 639008 | tf_op jit(solution)/shard_map/ppermute | solution.py:386
  169.9 4.8 collective-permute-done.14
  178.2 5.2 collective-permute-done.26.refs_2_.refs_14_
  199.6 4.3 fusion.63
  206.7 6.9 collective-permute-done.35.refs_5_
  215.6 11.4 %collective-permute-done.38.refs_9_ = bf16[192,1664]{1,0:T(8,128)(2,1)S(1)} collective-permute-done((bf16[192,1664]{1,0:T(8,128)(2,1)S(1)}, bf16[192,1664]{1,0:T(8,128)(2,1)S(1)}, u32[]{:S(2)}, u32[]{:S(2)}) %collective-permute-start.38) | collective-permute-done | bytes 639008 | tf_op jit(solution)/shard_map/ppermute | solution.py:389
  233.1 15.2 %collective-permute-done.39 = bf16[192,1664]{1,0:T(8,128)(2,1)S(1)} collective-permute-done((bf16[192,1664]{1,0:T(8,128)(2,1)S(1)}, bf16[192,1664]{1,0:T(8,128)(2,1)S(1)}, u32[]{:S(2)}, u32[]{:S(2)}) %collective-permute-start.39) | collective-permute-done | bytes 639008 | tf_op jit(solution)/shard_map/ppermute | solution.py:389
  250.2 7.7 collective-permute-done.50
  260.4 18.5 %collective-permute-start.51 = (bf16[2,192,768]{2,1,0:T(8,128)(2,1)S(1)}, bf16[2,192,768]{2,1,0:T(8,128)(2,1)}, u32[]{:S(2)}, u32[]{:S(2)}) collective-permute-start(bf16[2,192,768]{2,1,0:T(8,128)(2,1)S(1)} %pad_maximum_fusion.1.refs_4_), channel_id=1, source_target_pairs={{0,4},{2,6},{4,8},{6,10},{8,12},{10,14},{1,5},{3,7},{5,9},{7,11},{... | collective-permute-start | bytes 1769480 | tf_op jit(solution)/shard_map/ppermute | solution.py:389
  289.5 6.7 collective-permute-done.54.refs_5_
  300.3 12.8 %collective-permute-done.41.refs_2_.refs_14_ = bf16[192,1664]{1,0:T(8,128)(2,1)S(1)} collective-permute-done((bf16[192,1664]{1,0:T(8,128)(2,1)S(1)}, bf16[192,1664]{1,0:T(8,128)(2,1)S(1)}, u32[]{:S(2)}, u32[]{:S(2)}) %collective-permute-start.41) | collective-permute-done | bytes 639008 | tf_op jit(solution)/shard_map/ppermute | solution.py:386
  336.3 3.7 collective-permute-done.56.refs_7_
  353.2 5.3 multiply_reduce_fusion.1
  374.0 5.3 shard_map.211
  379.4 5.8 shard_map.212
  391.5 5.9 collective-permute-done.65
  410.0 3.5 convolution_convert_fusion
  414.8 3.4 collective-permute-start.94
  424.7 9.2 %collective-permute-done.94 = bf16[192,1664]{1,0:T(8,128)(2,1)S(1)} collective-permute-done((bf16[192,1664]{1,0:T(8,128)(2,1)S(1)}, bf16[192,1664]{1,0:T(8,128)(2,1)S(1)}, u32[]{:S(2)}, u32[]{:S(2)}) %collective-permute-start.94) | collective-permute-done | bytes 639008 | tf_op jit(solution)/shard_map/ppermute | solution.py:386
  435.0 4.0 collective-permute-start.95
  441.8 9.6 %collective-permute-done.67 = bf16[512,768]{1,0:T(8,128)(2,1)S(1)} collective-permute-done((bf16[512,768]{1,0:T(8,128)(2,1)S(1)}, bf16[512,768]{1,0:T(8,128)(2,1)S(1)}, u32[]{:S(2)}, u32[]{:S(2)}) %collective-permute-start.67) | collective-permute-done | bytes 786464 | tf_op jit(solution)/shard_map/ppermute | solution.py:382
  452.9 3.4 collective-permute-start.92
  460.4 3.9 collective-permute-done.120
  464.2 5.2 collective-permute-start.96
  475.7 7.9 %collective-permute-start.121 = (bf16[2,192,768]{2,1,0:T(8,128)(2,1)}, bf16[2,192,768]{2,1,0:T(8,128)(2,1)}, u32[]{:S(2)}, u32[]{:S(2)}) collective-permute-start(bf16[2,192,768]{2,1,0:T(8,128)(2,1)} %get-tuple-element.139), channel_id=1, source_target_pairs={{0,4},{2,6},{4,8},{6,10},{8,12},{10,14},{1,5},{3,7},{5,9},{7,11},{... | collective-permute-start | bytes 1769480 | tf_op jit(solution)/shard_map/ppermute | solution.py:389
  483.6 3.6 fusion.28
  489.8 3.5 fusion.10
  493.4 4.9 multiply_reduce_fusion
  512.6 5.3 shard_map.214
  518.0 5.4 shard_map.215
  528.6 5.6 collective-permute-done.72
  536.0 3.5 convolution_convert_fusion.1
  541.1 3.4 collective-permute-start.110
  549.7 3.4 collective-permute-done.110
  560.9 10.4 %collective-permute-done.109 = bf16[192,768]{1,0:T(8,128)(2,1)S(1)} collective-permute-done((bf16[192,768]{1,0:T(8,128)(2,1)S(1)}, bf16[192,768]{1,0:T(8,128)(2,1)S(1)}, u32[]{:S(2)}, u32[]{:S(2)}) %collective-permute-start.109) | collective-permute-done | bytes 294944 | tf_op jit(solution)/shard_map/ppermute | solution.py:386
  579.4 13.1 %collective-permute-done.108 = bf16[192,768]{1,0:T(8,128)(2,1)S(1)} collective-permute-done((bf16[192,768]{1,0:T(8,128)(2,1)S(1)}, bf16[192,768]{1,0:T(8,128)(2,1)S(1)}, u32[]{:S(2)}, u32[]{:S(2)}) %collective-permute-start.108) | collective-permute-done | bytes 294944 | tf_op jit(solution)/shard_map/ppermute | solution.py:386
  610.9 13.9 %collective-permute-done.107 = bf16[192,768]{1,0:T(8,128)(2,1)S(1)} collective-permute-done((bf16[192,768]{1,0:T(8,128)(2,1)S(1)}, bf16[192,768]{1,0:T(8,128)(2,1)S(1)}, u32[]{:S(2)}, u32[]{:S(2)}) %collective-permute-start.107) | collective-permute-done | bytes 294944 | tf_op jit(solution)/shard_map/ppermute | solution.py:386
  624.8 7.3 collective-permute-start.85
  632.9 22.0 %collective-permute-start.113 = (bf16[192,768]{1,0:T(8,128)(2,1)S(1)}, bf16[192,768]{1,0:T(8,128)(2,1)S(1)}, u32[]{:S(2)}, u32[]{:S(2)}) collective-permute-start(bf16[192,768]{1,0:T(8,128)(2,1)S(1)} %get-tuple-element.150), channel_id=1, source_target_pairs={{0,4},{2,6},{4,8},{6,10},{8,12},{10,14},{1,5},{3,7},{5,9},{7,11},{... | collective-permute-start | bytes 884744 | tf_op jit(solution)/shard_map/ppermute | solution.py:389
  669.5 9.4 %collective-permute-start.97 = (bf16[192,1664]{1,0:T(8,128)(2,1)S(1)}, bf16[192,1664]{1,0:T(8,128)(2,1)S(1)}, u32[]{:S(2)}, u32[]{:S(2)}) collective-permute-start(bf16[192,1664]{1,0:T(8,128)(2,1)S(1)} %copy-done.109), channel_id=1, source_target_pairs={{0,4},{2,6},{4,8},{6,10},{8,12},{10,14},{1,5},{3,7},{5,9},{7,11},{... | collective-permute-start | bytes 1916936 | tf_op jit(solution)/shard_map/ppermute | solution.py:389
  681.4 7.6 collective-permute-start.86
  691.5 3.5 collective-permute-done.90
  695.0 3.3 collective-permute-done.86
  717.0 4.0 collective-permute-start.78
  744.2 3.8 reshape.1458
  748.1 4.1 copy.362
  752.1 5.1 reshape.1459
  757.2 3.6 reshape.1456
  760.9 4.1 copy.361
  765.0 5.3 reshape.1457
  770.2 4.3 maximum_bitcast_fusion
  (955 shorter events, 338.4 us)
Async XLA Ops:
  2.9 86.3 %collective-permute-start.19 = (bf16[192,768]{1,0:T(8,128)(2,1)}, bf16[192,768]{1,0:T(8,128)(2,1)}, u32[]{:S(2)}, u32[]{:S(2)}) collective-permute-start(bf16[192,768]{1,0:T(8,128)(2,1)} %broadcast_select_fusion.11), channel_id=1, source_target_pairs={{0,16},{16,0},{1,17},{17,1},{2,18},{18,2},{3,19},{19,3},{4,20},{20... | collective-permute-start | bytes 884744 | tf_op jit(solution)/shard_map/ppermute | solution.py:379
  21.7 26.8 %collective-permute-start.2 = (bf16[192,1664]{1,0:T(8,128)(2,1)S(1)}, bf16[192,1664]{1,0:T(8,128)(2,1)}, u32[]{:S(2)}, u32[]{:S(2)}) collective-permute-start(bf16[192,1664]{1,0:T(8,128)(2,1)S(1)} %broadcast_select_fusion.4), channel_id=1, source_target_pairs={{0,16},{16,0},{1,17},{17,1},{2,18},{18,2},{3,19},{19,3},{4,20},{20... | collective-permute-start | bytes 1916936 | tf_op jit(solution)/shard_map/ppermute | solution.py:379
  21.8 91.0 %collective-permute-start = (bf16[256,1536]{1,0:T(8,128)(2,1)}, bf16[256,1536]{1,0:T(8,128)(2,1)}, u32[]{:S(2)}, u32[]{:S(2)}) collective-permute-start(bf16[256,1536]{1,0:T(8,128)(2,1)} %param.12), channel_id=1, source_target_pairs={{0,1},{1,0},{2,3},{3,2},{4,5},{5,4},{6,7},{7,6},{8,9},{9,8},{10,11... | collective-permute-start | bytes 2359304 | tf_op jit(solution)/shard_map/ppermute | solution.py:382
  25.0 18.5 %collective-permute-start.1 = (f32[10,3328]{1,0:T(8,128)S(1)}, f32[10,3328]{1,0:T(8,128)S(1)}, u32[]{:S(2)}, u32[]{:S(2)}) collective-permute-start(f32[10,3328]{1,0:T(8,128)S(1)} %concatenate.188), channel_id=1, source_target_pairs={{0,16},{16,0},{1,17},{17,1},{2,18},{18,2},{3,19},{19,3},{4,20},{20... | collective-permute-start | bytes 399368 | tf_op jit(solution)/shard_map/ppermute | solution.py:379
  76.5 34.2 %collective-permute-start.5 = (bf16[192,1664]{1,0:T(8,128)(2,1)}, bf16[192,1664]{1,0:T(8,128)(2,1)S(1)}, u32[]{:S(2)}, u32[]{:S(2)}) collective-permute-start(bf16[192,1664]{1,0:T(8,128)(2,1)} %collective-permute-done.4), channel_id=1, source_target_pairs={{8,12},{10,14},{9,13},{11,15},{24,28},{26,30},{25,29},{27,31}} | collective-permute-start | bytes 1916936 | tf_op jit(solution)/shard_map/ppermute | solution.py:389
  87.9 23.5 %collective-permute-start.8 = (bf16[192,1664]{1,0:T(8,128)(2,1)}, bf16[192,1664]{1,0:T(8,128)(2,1)S(1)}, u32[]{:S(2)}, u32[]{:S(2)}) collective-permute-start(bf16[192,1664]{1,0:T(8,128)(2,1)} %collective-permute-done.7), channel_id=1, source_target_pairs={{4,0},{6,2},{5,1},{7,3},{20,16},{22,18},{21,17},{23,19}} | collective-permute-start | bytes 1916936 | tf_op jit(solution)/shard_map/ppermute | solution.py:389
  99.9 26.9 %collective-permute-start.12 = (bf16[192,1664]{1,0:T(8,128)(2,1)S(1)}, bf16[192,1664]{1,0:T(8,128)(2,1)S(1)}, u32[]{:S(2)}, u32[]{:S(2)}) collective-permute-start(bf16[192,1664]{1,0:T(8,128)(2,1)S(1)} %get-tuple-element.158.refs_7_), channel_id=1, source_target_pairs={{0,2},{2,0},{4,6},{6,4},{8,10},{10,8},{12,14},{14,12},{1,3},{3,1},... | collective-permute-start | bytes 1916936 | tf_op jit(solution)/shard_map/ppermute | solution.py:386
  112.8 19.2 %collective-permute-start.13 = (bf16[192,1664]{1,0:T(8,128)(2,1)S(1)}, bf16[192,1664]{1,0:T(8,128)(2,1)S(1)}, u32[]{:S(2)}, u32[]{:S(2)}) collective-permute-start(bf16[192,1664]{1,0:T(8,128)(2,1)S(1)} %collective-permute-done.6.refs_9_), channel_id=1, source_target_pairs={{0,2},{2,0},{4,6},{6,4},{8,10},{10,8},{1,3},{3,1},{5,7},{7,5},{9,1... | collective-permute-start | bytes 1916936 | tf_op jit(solution)/shard_map/ppermute | solution.py:386
  116.3 29.5 %collective-permute-start.10 = (bf16[192,1664]{1,0:T(8,128)(2,1)S(1)}, bf16[192,1664]{1,0:T(8,128)(2,1)S(1)}, u32[]{:S(2)}, u32[]{:S(2)}) collective-permute-start(bf16[192,1664]{1,0:T(8,128)(2,1)S(1)} %broadcast_select_fusion.1.refs_3_.refs_11_), channel_id=1, source_target_pairs={{0,2},{2,0},{4,6},{6,4},{8,10},{10,8},{12,14},{14,12},{1,3},{3,1},... | collective-permute-start | bytes 1916936 | tf_op jit(solution)/shard_map/ppermute | solution.py:386
  120.9 38.5 %collective-permute-start.9 = (bf16[192,1664]{1,0:T(8,128)(2,1)S(1)}, bf16[192,1664]{1,0:T(8,128)(2,1)S(1)}, u32[]{:S(2)}, u32[]{:S(2)}) collective-permute-start(bf16[192,1664]{1,0:T(8,128)(2,1)S(1)} %broadcast_select_fusion.7.refs_1_.refs_13_), channel_id=1, source_target_pairs={{0,2},{2,0},{12,14},{14,12},{1,3},{3,1},{13,15},{15,13},{16,18},{1... | collective-permute-start | bytes 1916936 | tf_op jit(solution)/shard_map/ppermute | solution.py:386
  126.9 51.2 %collective-permute-start.29 = (bf16[192,768]{1,0:T(8,128)(2,1)S(1)}, bf16[192,768]{1,0:T(8,128)(2,1)S(1)}, u32[]{:S(2)}, u32[]{:S(2)}) collective-permute-start(bf16[192,768]{1,0:T(8,128)(2,1)S(1)} %get-tuple-element.55.refs_7_), channel_id=1, source_target_pairs={{0,2},{2,0},{4,6},{6,4},{8,10},{10,8},{12,14},{14,12},{1,3},{3,1},... | collective-permute-start | bytes 884744 | tf_op jit(solution)/shard_map/ppermute | solution.py:386
  127.5 50.6 %collective-permute-start.28 = (bf16[192,768]{1,0:T(8,128)(2,1)S(1)}, bf16[192,768]{1,0:T(8,128)(2,1)S(1)}, u32[]{:S(2)}, u32[]{:S(2)}) collective-permute-start(bf16[192,768]{1,0:T(8,128)(2,1)S(1)} %collective-permute-done.20.refs_5_), channel_id=1, source_target_pairs={{4,6},{6,4},{8,10},{10,8},{12,14},{14,12},{5,7},{7,5},{9,11},{11,9... | collective-permute-start | bytes 884744 | tf_op jit(solution)/shard_map/ppermute | solution.py:386
  132.0 46.1 %collective-permute-start.30 = (bf16[192,768]{1,0:T(8,128)(2,1)S(1)}, bf16[192,768]{1,0:T(8,128)(2,1)S(1)}, u32[]{:S(2)}, u32[]{:S(2)}) collective-permute-start(bf16[192,768]{1,0:T(8,128)(2,1)S(1)} %collective-permute-done.23.refs_9_), channel_id=1, source_target_pairs={{0,2},{2,0},{4,6},{6,4},{8,10},{10,8},{1,3},{3,1},{5,7},{7,5},{9,1... | collective-permute-start | bytes 884744 | tf_op jit(solution)/shard_map/ppermute | solution.py:386
  145.7 21.1 %collective-permute-start.22 = (bf16[192,768]{1,0:T(8,128)(2,1)S(1)}, bf16[192,768]{1,0:T(8,128)(2,1)S(1)}, u32[]{:S(2)}, u32[]{:S(2)}) collective-permute-start(bf16[192,768]{1,0:T(8,128)(2,1)S(1)} %collective-permute-done.21), channel_id=1, source_target_pairs={{8,12},{10,14},{9,13},{11,15},{24,28},{26,30},{25,29},{27,31}} | collective-permute-start | bytes 884744 | tf_op jit(solution)/shard_map/ppermute | solution.py:389
  204.1 26.9 %collective-permute-start.32 = (f32[512,768]{1,0:T(8,128)S(1)}, f32[512,768]{1,0:T(8,128)S(1)}, u32[]{:S(2)}, u32[]{:S(2)}) collective-permute-start(f32[512,768]{1,0:T(8,128)S(1)} %constant_dynamic-slice_fusion.15), channel_id=1, source_target_pairs={{0,16},{16,0},{1,17},{17,1},{2,18},{18,2},{3,19},{19,3},{4,20},{20... | collective-permute-start | bytes 4718600 | tf_op jit(solution)/shard_map/ppermute | solution.py:379
  205.4 21.5 %collective-permute-start.38 = (bf16[192,1664]{1,0:T(8,128)(2,1)S(1)}, bf16[192,1664]{1,0:T(8,128)(2,1)S(1)}, u32[]{:S(2)}, u32[]{:S(2)}) collective-permute-start(bf16[192,1664]{1,0:T(8,128)(2,1)S(1)} %get-tuple-element.56.refs_7_), channel_id=1, source_target_pairs={{4,0},{6,2},{8,4},{10,6},{12,8},{14,10},{5,1},{7,3},{9,5},{11,7},{... | collective-permute-start | bytes 1916936 | tf_op jit(solution)/shard_map/ppermute | solution.py:389
  227.0 21.3 %collective-permute-start.39 = (bf16[192,1664]{1,0:T(8,128)(2,1)S(1)}, bf16[192,1664]{1,0:T(8,128)(2,1)S(1)}, u32[]{:S(2)}, u32[]{:S(2)}) collective-permute-start(bf16[192,1664]{1,0:T(8,128)(2,1)S(1)} %collective-permute-done.38.refs_9_), channel_id=1, source_target_pairs={{4,0},{6,2},{8,4},{10,6},{5,1},{7,3},{9,5},{11,7},{20,16},{22,18},... | collective-permute-start | bytes 1916936 | tf_op jit(solution)/shard_map/ppermute | solution.py:389
  228.3 21.3 %collective-permute-start.37 = (bf16[192,1664]{1,0:T(8,128)(2,1)S(1)}, bf16[192,1664]{1,0:T(8,128)(2,1)S(1)}, u32[]{:S(2)}, u32[]{:S(2)}) collective-permute-start(bf16[192,1664]{1,0:T(8,128)(2,1)S(1)} %collective-permute-done.36), channel_id=1, source_target_pairs={{8,12},{10,14},{9,13},{11,15},{24,28},{26,30},{25,29},{27,31}} | collective-permute-start | bytes 1916936 | tf_op jit(solution)/shard_map/ppermute | solution.py:389
  229.4 31.0 %collective-permute-start.44 = (bf16[192,1664]{1,0:T(8,128)(2,1)S(1)}, bf16[192,1664]{1,0:T(8,128)(2,1)S(1)}, u32[]{:S(2)}, u32[]{:S(2)}) collective-permute-start(bf16[192,1664]{1,0:T(8,128)(2,1)S(1)} %get-tuple-element.56.refs_7_), channel_id=1, source_target_pairs={{0,2},{2,0},{4,6},{6,4},{8,10},{10,8},{12,14},{14,12},{1,3},{3,1},... | collective-permute-start | bytes 1916936 | tf_op jit(solution)/shard_map/ppermute | solution.py:386
  231.2 47.8 %collective-permute-start.33 = (bf16[512,768]{1,0:T(8,128)(2,1)S(1)}, bf16[512,768]{1,0:T(8,128)(2,1)S(1)}, u32[]{:S(2)}, u32[]{:S(2)}) collective-permute-start(bf16[512,768]{1,0:T(8,128)(2,1)S(1)} %add_convert_fusion.2), channel_id=1, source_target_pairs={{0,1},{1,0},{2,3},{3,2},{4,5},{5,4},{6,7},{7,6},{8,9},{9,8},{10,11... | collective-permute-start | bytes 2359304 | tf_op jit(solution)/shard_map/ppermute | solution.py:382
  232.4 49.4 %collective-permute-start.43 = (bf16[192,1664]{1,0:T(8,128)(2,1)S(1)}, bf16[192,1664]{1,0:T(8,128)(2,1)S(1)}, u32[]{:S(2)}, u32[]{:S(2)}) collective-permute-start(bf16[192,1664]{1,0:T(8,128)(2,1)S(1)} %collective-permute-done.35.refs_5_), channel_id=1, source_target_pairs={{4,6},{6,4},{8,10},{10,8},{12,14},{14,12},{5,7},{7,5},{9,11},{11,9... | collective-permute-start | bytes 1916936 | tf_op jit(solution)/shard_map/ppermute | solution.py:386
  248.3 33.3 %collective-permute-start.40 = (bf16[192,1664]{1,0:T(8,128)(2,1)S(1)}, bf16[192,1664]{1,0:T(8,128)(2,1)S(1)}, u32[]{:S(2)}, u32[]{:S(2)}) collective-permute-start(bf16[192,1664]{1,0:T(8,128)(2,1)S(1)} %collective-permute-done.39), channel_id=1, source_target_pairs={{4,0},{6,2},{5,1},{7,3},{20,16},{22,18},{21,17},{23,19}} | collective-permute-start | bytes 1916936 | tf_op jit(solution)/shard_map/ppermute | solution.py:389
  257.9 26.1 %collective-permute-start.45 = (bf16[192,1664]{1,0:T(8,128)(2,1)S(1)}, bf16[192,1664]{1,0:T(8,128)(2,1)S(1)}, u32[]{:S(2)}, u32[]{:S(2)}) collective-permute-start(bf16[192,1664]{1,0:T(8,128)(2,1)S(1)} %collective-permute-done.38.refs_9_), channel_id=1, source_target_pairs={{0,2},{2,0},{4,6},{6,4},{8,10},{10,8},{1,3},{3,1},{5,7},{7,5},{9,1... | collective-permute-start | bytes 1916936 | tf_op jit(solution)/shard_map/ppermute | solution.py:386
  260.4 27.5 %collective-permute-start.51 = (bf16[2,192,768]{2,1,0:T(8,128)(2,1)S(1)}, bf16[2,192,768]{2,1,0:T(8,128)(2,1)}, u32[]{:S(2)}, u32[]{:S(2)}) collective-permute-start(bf16[2,192,768]{2,1,0:T(8,128)(2,1)S(1)} %pad_maximum_fusion.1.refs_4_), channel_id=1, source_target_pairs={{0,4},{2,6},{4,8},{6,10},{8,12},{10,14},{1,5},{3,7},{5,9},{7,11},{... | collective-permute-start | bytes 1769480 | tf_op jit(solution)/shard_map/ppermute | solution.py:389
  281.6 42.7 %collective-permute-start.34 = (bf16[512,768]{1,0:T(8,128)(2,1)}, bf16[512,768]{1,0:T(8,128)(2,1)}, u32[]{:S(2)}, u32[]{:S(2)}) collective-permute-start(bf16[512,768]{1,0:T(8,128)(2,1)} %add_convert_fusion.1), channel_id=1, source_target_pairs={{0,16},{16,0},{1,17},{17,1},{2,18},{18,2},{3,19},{19,3},{4,20},{20... | collective-permute-start | bytes 2359304 | tf_op jit(solution)/shard_map/ppermute | solution.py:379
  285.0 28.1 %collective-permute-start.41 = (bf16[192,1664]{1,0:T(8,128)(2,1)S(1)}, bf16[192,1664]{1,0:T(8,128)(2,1)S(1)}, u32[]{:S(2)}, u32[]{:S(2)}) collective-permute-start(bf16[192,1664]{1,0:T(8,128)(2,1)S(1)} %broadcast_select_fusion.6.refs_1_.refs_13_), channel_id=1, source_target_pairs={{0,2},{2,0},{12,14},{14,12},{1,3},{3,1},{13,15},{15,13},{16,18},{1... | collective-permute-start | bytes 1916936 | tf_op jit(solution)/shard_map/ppermute | solution.py:386
  288.0 32.8 %collective-permute-start.52 = (bf16[2,192,768]{2,1,0:T(8,128)(2,1)}, bf16[2,192,768]{2,1,0:T(8,128)(2,1)}, u32[]{:S(2)}, u32[]{:S(2)}) collective-permute-start(bf16[2,192,768]{2,1,0:T(8,128)(2,1)} %collective-permute-done.51.refs_3_), channel_id=1, source_target_pairs={{4,8},{6,10},{8,12},{10,14},{5,9},{7,11},{9,13},{11,15},{20,24},{2... | collective-permute-start | bytes 1769480 | tf_op jit(solution)/shard_map/ppermute | solution.py:389
  296.1 26.6 %collective-permute-start.55 = (bf16[2,192,768]{2,1,0:T(8,128)(2,1)}, bf16[2,192,768]{2,1,0:T(8,128)(2,1)}, u32[]{:S(2)}, u32[]{:S(2)}) collective-permute-start(bf16[2,192,768]{2,1,0:T(8,128)(2,1)} %collective-permute-done.54.refs_5_), channel_id=1, source_target_pairs={{4,0},{6,2},{8,4},{10,6},{5,1},{7,3},{9,5},{11,7},{20,16},{22,18},... | collective-permute-start | bytes 1769480 | tf_op jit(solution)/shard_map/ppermute | solution.py:389
  299.7 53.4 %collective-permute-start.61 = (bf16[256,1536]{1,0:T(8,128)(2,1)}, bf16[256,1536]{1,0:T(8,128)(2,1)}, u32[]{:S(2)}, u32[]{:S(2)}) collective-permute-start(bf16[256,1536]{1,0:T(8,128)(2,1)} %param.23), channel_id=1, source_target_pairs={{0,1},{1,0},{2,3},{3,2},{4,5},{5,4},{6,7},{7,6},{8,9},{9,8},{10,11... | collective-permute-start | bytes 2359304 | tf_op jit(solution)/shard_map/ppermute | solution.py:382
  391.3 27.4 %collective-permute-start.118 = (bf16[768,768]{1,0:T(8,128)(2,1)}, bf16[768,768]{1,0:T(8,128)(2,1)}, u32[]{:S(2)}, u32[]{:S(2)}) collective-permute-start(bf16[768,768]{1,0:T(8,128)(2,1)} %get-tuple-element.144), channel_id=1, source_target_pairs={{0,16},{16,0},{1,17},{17,1},{2,18},{18,2},{3,19},{19,3},{4,20},{20... | collective-permute-start | bytes 3538952 | tf_op jit(solution)/shard_map/ppermute | solution.py:379
  403.9 18.4 %collective-permute-start.66 = (f32[512,768]{1,0:T(8,128)}, f32[512,768]{1,0:T(8,128)}, u32[]{:S(2)}, u32[]{:S(2)}) collective-permute-start(f32[512,768]{1,0:T(8,128)} %constant_dynamic-slice_fusion.9), channel_id=1, source_target_pairs={{0,16},{16,0},{1,17},{17,1},{2,18},{18,2},{3,19},{19,3},{4,20},{20... | collective-permute-start | bytes 4718600 | tf_op jit(solution)/shard_map/ppermute | solution.py:379
  408.7 30.5 %collective-permute-start.58 = (f32[512,768]{1,0:T(8,128)}, f32[512,768]{1,0:T(8,128)}, u32[]{:S(2)}, u32[]{:S(2)}) collective-permute-start(f32[512,768]{1,0:T(8,128)} %constant_dynamic-slice_fusion.12), channel_id=1, source_target_pairs={{0,16},{16,0},{1,17},{17,1},{2,18},{18,2},{3,19},{19,3},{4,20},{20... | collective-permute-start | bytes 4718600 | tf_op jit(solution)/shard_map/ppermute | solution.py:379
  414.8 19.1 %collective-permute-start.94 = (bf16[192,1664]{1,0:T(8,128)(2,1)S(1)}, bf16[192,1664]{1,0:T(8,128)(2,1)S(1)}, u32[]{:S(2)}, u32[]{:S(2)}) collective-permute-start(bf16[192,1664]{1,0:T(8,128)(2,1)S(1)} %get-tuple-element.123), channel_id=1, source_target_pairs={{0,2},{2,0},{12,14},{14,12},{1,3},{3,1},{13,15},{15,13},{16,18},{1... | collective-permute-start | bytes 1916936 | tf_op jit(solution)/shard_map/ppermute | solution.py:386
  418.2 34.7 %collective-permute-start.93 = (bf16[192,1664]{1,0:T(8,128)(2,1)S(1)}, bf16[192,1664]{1,0:T(8,128)(2,1)S(1)}, u32[]{:S(2)}, u32[]{:S(2)}) collective-permute-start(bf16[192,1664]{1,0:T(8,128)(2,1)S(1)} %get-tuple-element.124), channel_id=1, source_target_pairs={{0,2},{2,0},{4,6},{6,4},{8,10},{10,8},{12,14},{14,12},{1,3},{3,1},... | collective-permute-start | bytes 1916936 | tf_op jit(solution)/shard_map/ppermute | solution.py:386
  422.3 36.5 %collective-permute-start.122 = (bf16[2,192,768]{2,1,0:T(8,128)(2,1)S(1)}, bf16[2,192,768]{2,1,0:T(8,128)(2,1)S(1)}, u32[]{:S(2)}, u32[]{:S(2)}) collective-permute-start(bf16[2,192,768]{2,1,0:T(8,128)(2,1)S(1)} %get-tuple-element.142), channel_id=1, source_target_pairs={{12,8},{14,10},{13,9},{15,11},{28,24},{30,26},{29,25},{31,27}} | collective-permute-start | bytes 1769480 | tf_op jit(solution)/shard_map/ppermute | solution.py:389
  435.0 21.3 %collective-permute-start.95 = (bf16[192,1664]{1,0:T(8,128)(2,1)S(1)}, bf16[192,1664]{1,0:T(8,128)(2,1)S(1)}, u32[]{:S(2)}, u32[]{:S(2)}) collective-permute-start(bf16[192,1664]{1,0:T(8,128)(2,1)S(1)} %fusion.26), channel_id=1, source_target_pairs={{0,4},{2,6},{1,5},{3,7},{16,20},{18,22},{17,21},{19,23}} | collective-permute-start | bytes 1916936 | tf_op jit(solution)/shard_map/ppermute | solution.py:389
  439.3 18.1 %collective-permute-start.99 = (bf16[192,1664]{1,0:T(8,128)(2,1)S(1)}, bf16[192,1664]{1,0:T(8,128)(2,1)S(1)}, u32[]{:S(2)}, u32[]{:S(2)}) collective-permute-start(bf16[192,1664]{1,0:T(8,128)(2,1)S(1)} %fusion.26), channel_id=1, source_target_pairs={{12,8},{14,10},{13,9},{15,11},{28,24},{30,26},{29,25},{31,27}} | collective-permute-start | bytes 1916936 | tf_op jit(solution)/shard_map/ppermute | solution.py:389
  452.9 22.0 %collective-permute-start.92 = (bf16[192,1664]{1,0:T(8,128)(2,1)}, bf16[192,1664]{1,0:T(8,128)(2,1)}, u32[]{:S(2)}, u32[]{:S(2)}) collective-permute-start(bf16[192,1664]{1,0:T(8,128)(2,1)} %get-tuple-element.125), channel_id=1, source_target_pairs={{0,2},{2,0},{4,6},{6,4},{8,10},{10,8},{1,3},{3,1},{5,7},{7,5},{9,1... | collective-permute-start | bytes 1916936 | tf_op jit(solution)/shard_map/ppermute | solution.py:386
  457.4 29.8 %collective-permute-start.68 = (f32[512,768]{1,0:T(8,128)S(1)}, f32[512,768]{1,0:T(8,128)}, u32[]{:S(2)}, u32[]{:S(2)}) collective-permute-start(f32[512,768]{1,0:T(8,128)S(1)} %convert_add_fusion), channel_id=1, source_target_pairs={{0,16},{16,0},{1,17},{17,1},{2,18},{18,2},{3,19},{19,3},{4,20},{20... | collective-permute-start | bytes 4718600 | tf_op jit(solution)/shard_map/ppermute | solution.py:379
  464.2 19.4 %collective-permute-start.96 = (bf16[192,1664]{1,0:T(8,128)(2,1)}, bf16[192,1664]{1,0:T(8,128)(2,1)}, u32[]{:S(2)}, u32[]{:S(2)}) collective-permute-start(bf16[192,1664]{1,0:T(8,128)(2,1)} %get-tuple-element.115), channel_id=1, source_target_pairs={{0,4},{2,6},{4,8},{6,10},{1,5},{3,7},{5,9},{7,11},{16,20},{18,22},... | collective-permute-start | bytes 1916936 | tf_op jit(solution)/shard_map/ppermute | solution.py:389
  475.0 26.3 %collective-permute-start.123 = (bf16[2,192,768]{2,1,0:T(8,128)(2,1)S(1)}, bf16[2,192,768]{2,1,0:T(8,128)(2,1)S(1)}, u32[]{:S(2)}, u32[]{:S(2)}) collective-permute-start(bf16[2,192,768]{2,1,0:T(8,128)(2,1)S(1)} %get-tuple-element.140), channel_id=1, source_target_pairs={{8,4},{10,6},{12,8},{14,10},{9,5},{11,7},{13,9},{15,11},{24,20},{2... | collective-permute-start | bytes 1769480 | tf_op jit(solution)/shard_map/ppermute | solution.py:389
  475.7 51.3 %collective-permute-start.121 = (bf16[2,192,768]{2,1,0:T(8,128)(2,1)}, bf16[2,192,768]{2,1,0:T(8,128)(2,1)}, u32[]{:S(2)}, u32[]{:S(2)}) collective-permute-start(bf16[2,192,768]{2,1,0:T(8,128)(2,1)} %get-tuple-element.139), channel_id=1, source_target_pairs={{0,4},{2,6},{4,8},{6,10},{8,12},{10,14},{1,5},{3,7},{5,9},{7,11},{... | collective-permute-start | bytes 1769480 | tf_op jit(solution)/shard_map/ppermute | solution.py:389
  503.2 23.7 %collective-permute-start.124 = (bf16[2,192,768]{2,1,0:T(8,128)(2,1)}, bf16[2,192,768]{2,1,0:T(8,128)(2,1)}, u32[]{:S(2)}, u32[]{:S(2)}) collective-permute-start(bf16[2,192,768]{2,1,0:T(8,128)(2,1)} %add_convert_fusion.7), channel_id=1, source_target_pairs={{4,0},{6,2},{8,4},{10,6},{12,8},{14,10},{5,1},{7,3},{9,5},{11,7},{... | collective-permute-start | bytes 1769480 | tf_op jit(solution)/shard_map/ppermute | solution.py:389
  545.8 31.1 %collective-permute-start.83 = (bf16[192,1664]{1,0:T(8,128)(2,1)S(1)}, bf16[192,1664]{1,0:T(8,128)(2,1)S(1)}, u32[]{:S(2)}, u32[]{:S(2)}) collective-permute-start(bf16[192,1664]{1,0:T(8,128)(2,1)S(1)} %get-tuple-element.130), channel_id=1, source_target_pairs={{0,2},{2,0},{12,14},{14,12},{1,3},{3,1},{13,15},{15,13},{16,18},{1... | collective-permute-start | bytes 1916936 | tf_op jit(solution)/shard_map/ppermute | solution.py:386
  548.5 22.8 %collective-permute-start.109 = (bf16[192,768]{1,0:T(8,128)(2,1)S(1)}, bf16[192,768]{1,0:T(8,128)(2,1)S(1)}, u32[]{:S(2)}, u32[]{:S(2)}) collective-permute-start(bf16[192,768]{1,0:T(8,128)(2,1)S(1)} %get-tuple-element.148), channel_id=1, source_target_pairs={{0,2},{2,0},{4,6},{6,4},{8,10},{10,8},{12,14},{14,12},{1,3},{3,1},... | collective-permute-start | bytes 884744 | tf_op jit(solution)/shard_map/ppermute | solution.py:386
  553.2 19.3 %collective-permute-start.111 = (bf16[192,768]{1,0:T(8,128)(2,1)S(1)}, bf16[192,768]{1,0:T(8,128)(2,1)S(1)}, u32[]{:S(2)}, u32[]{:S(2)}) collective-permute-start(bf16[192,768]{1,0:T(8,128)(2,1)S(1)} %fusion.47), channel_id=1, source_target_pairs={{0,4},{2,6},{1,5},{3,7},{16,20},{18,22},{17,21},{19,23}} | collective-permute-start | bytes 884744 | tf_op jit(solution)/shard_map/ppermute | solution.py:389
  554.6 20.7 %collective-permute-start.115 = (bf16[192,768]{1,0:T(8,128)(2,1)S(1)}, bf16[192,768]{1,0:T(8,128)(2,1)S(1)}, u32[]{:S(2)}, u32[]{:S(2)}) collective-permute-start(bf16[192,768]{1,0:T(8,128)(2,1)S(1)} %fusion.47), channel_id=1, source_target_pairs={{12,8},{14,10},{13,9},{15,11},{28,24},{30,26},{29,25},{31,27}} | collective-permute-start | bytes 884744 | tf_op jit(solution)/shard_map/ppermute | solution.py:389
  560.9 71.2 %collective-permute-start.73 = (f32[512,768]{1,0:T(8,128)}, f32[512,768]{1,0:T(8,128)}, u32[]{:S(2)}, u32[]{:S(2)}) collective-permute-start(f32[512,768]{1,0:T(8,128)} %constant_dynamic-slice_fusion.6), channel_id=1, source_target_pairs={{0,16},{16,0},{1,17},{17,1},{2,18},{18,2},{3,19},{19,3},{4,20},{20... | collective-permute-start | bytes 4718600 | tf_op jit(solution)/shard_map/ppermute | solution.py:379
  571.3 29.4 %collective-permute-start.82 = (bf16[192,1664]{1,0:T(8,128)(2,1)}, bf16[192,1664]{1,0:T(8,128)(2,1)}, u32[]{:S(2)}, u32[]{:S(2)}) collective-permute-start(bf16[192,1664]{1,0:T(8,128)(2,1)} %get-tuple-element.131), channel_id=1, source_target_pairs={{0,2},{2,0},{4,6},{6,4},{8,10},{10,8},{12,14},{14,12},{1,3},{3,1},... | collective-permute-start | bytes 1916936 | tf_op jit(solution)/shard_map/ppermute | solution.py:386
  572.5 19.9 %collective-permute-start.108 = (bf16[192,768]{1,0:T(8,128)(2,1)S(1)}, bf16[192,768]{1,0:T(8,128)(2,1)S(1)}, u32[]{:S(2)}, u32[]{:S(2)}) collective-permute-start(bf16[192,768]{1,0:T(8,128)(2,1)S(1)} %get-tuple-element.149), channel_id=1, source_target_pairs={{0,2},{2,0},{4,6},{6,4},{8,10},{10,8},{1,3},{3,1},{5,7},{7,5},{9,1... | collective-permute-start | bytes 884744 | tf_op jit(solution)/shard_map/ppermute | solution.py:386
  575.3 19.3 %collective-permute-start.114 = (bf16[192,768]{1,0:T(8,128)(2,1)S(1)}, bf16[192,768]{1,0:T(8,128)(2,1)S(1)}, u32[]{:S(2)}, u32[]{:S(2)}) collective-permute-start(bf16[192,768]{1,0:T(8,128)(2,1)S(1)} %get-tuple-element.146), channel_id=1, source_target_pairs={{4,6},{6,4},{8,10},{10,8},{12,14},{14,12},{5,7},{7,5},{9,11},{11,9... | collective-permute-start | bytes 884744 | tf_op jit(solution)/shard_map/ppermute | solution.py:386
  576.9 19.2 %collective-permute-start.112 = (bf16[192,768]{1,0:T(8,128)(2,1)S(1)}, bf16[192,768]{1,0:T(8,128)(2,1)S(1)}, u32[]{:S(2)}, u32[]{:S(2)}) collective-permute-start(bf16[192,768]{1,0:T(8,128)(2,1)S(1)} %get-tuple-element.137), channel_id=1, source_target_pairs={{0,4},{2,6},{4,8},{6,10},{1,5},{3,7},{5,9},{7,11},{16,20},{18,22},... | collective-permute-start | bytes 884744 | tf_op jit(solution)/shard_map/ppermute | solution.py:389
  600.7 59.7 %collective-permute-start.81 = (bf16[192,1664]{1,0:T(8,128)(2,1)S(1)}, bf16[192,1664]{1,0:T(8,128)(2,1)S(1)}, u32[]{:S(2)}, u32[]{:S(2)}) collective-permute-start(bf16[192,1664]{1,0:T(8,128)(2,1)S(1)} %copy-done.108), channel_id=1, source_target_pairs={{0,2},{2,0},{4,6},{6,4},{8,10},{10,8},{1,3},{3,1},{5,7},{7,5},{9,1... | collective-permute-start | bytes 1916936 | tf_op jit(solution)/shard_map/ppermute | solution.py:386
  605.4 19.4 %collective-permute-start.107 = (bf16[192,768]{1,0:T(8,128)(2,1)S(1)}, bf16[192,768]{1,0:T(8,128)(2,1)S(1)}, u32[]{:S(2)}, u32[]{:S(2)}) collective-permute-start(bf16[192,768]{1,0:T(8,128)(2,1)S(1)} %copy-done.118), channel_id=1, source_target_pairs={{0,2},{2,0},{4,6},{6,4},{8,10},{10,8},{12,14},{14,12},{1,3},{3,1},... | collective-permute-start | bytes 884744 | tf_op jit(solution)/shard_map/ppermute | solution.py:386
  606.6 26.2 %collective-permute-start.117 = (bf16[192,768]{1,0:T(8,128)(2,1)S(1)}, bf16[192,768]{1,0:T(8,128)(2,1)S(1)}, u32[]{:S(2)}, u32[]{:S(2)}) collective-permute-start(bf16[192,768]{1,0:T(8,128)(2,1)S(1)} %get-tuple-element.151), channel_id=1, source_target_pairs={{4,0},{6,2},{8,4},{10,6},{12,8},{14,10},{5,1},{7,3},{9,5},{11,7},{... | collective-permute-start | bytes 884744 | tf_op jit(solution)/shard_map/ppermute | solution.py:389
  610.2 51.6 %collective-permute-start.87 = (bf16[192,1664]{1,0:T(8,128)(2,1)S(1)}, bf16[192,1664]{1,0:T(8,128)(2,1)S(1)}, u32[]{:S(2)}, u32[]{:S(2)}) collective-permute-start(bf16[192,1664]{1,0:T(8,128)(2,1)S(1)} %get-tuple-element.129), channel_id=1, source_target_pairs={{4,6},{6,4},{8,10},{10,8},{12,14},{14,12},{5,7},{7,5},{9,11},{11,9... | collective-permute-start | bytes 1916936 | tf_op jit(solution)/shard_map/ppermute | solution.py:386
  624.8 38.1 %collective-permute-start.85 = (bf16[192,1664]{1,0:T(8,128)(2,1)S(1)}, bf16[192,1664]{1,0:T(8,128)(2,1)S(1)}, u32[]{:S(2)}, u32[]{:S(2)}) collective-permute-start(bf16[192,1664]{1,0:T(8,128)(2,1)S(1)} %get-tuple-element.117), channel_id=1, source_target_pairs={{0,4},{2,6},{4,8},{6,10},{1,5},{3,7},{5,9},{7,11},{16,20},{18,22},... | collective-permute-start | bytes 1916936 | tf_op jit(solution)/shard_map/ppermute | solution.py:389
  632.1 31.8 %collective-permute-start.89 = (bf16[192,1664]{1,0:T(8,128)(2,1)S(1)}, bf16[192,1664]{1,0:T(8,128)(2,1)S(1)}, u32[]{:S(2)}, u32[]{:S(2)}) collective-permute-start(bf16[192,1664]{1,0:T(8,128)(2,1)S(1)} %get-tuple-element.118), channel_id=1, source_target_pairs={{8,4},{10,6},{12,8},{14,10},{9,5},{11,7},{13,9},{15,11},{24,20},{2... | collective-permute-start | bytes 1916936 | tf_op jit(solution)/shard_map/ppermute | solution.py:389
  632.9 26.2 %collective-permute-start.113 = (bf16[192,768]{1,0:T(8,128)(2,1)S(1)}, bf16[192,768]{1,0:T(8,128)(2,1)S(1)}, u32[]{:S(2)}, u32[]{:S(2)}) collective-permute-start(bf16[192,768]{1,0:T(8,128)(2,1)S(1)} %get-tuple-element.150), channel_id=1, source_target_pairs={{0,4},{2,6},{4,8},{6,10},{8,12},{10,14},{1,5},{3,7},{5,9},{7,11},{... | collective-permute-start | bytes 884744 | tf_op jit(solution)/shard_map/ppermute | solution.py:389
  660.5 30.5 %collective-permute-start.101 = (bf16[192,1664]{1,0:T(8,128)(2,1)S(1)}, bf16[192,1664]{1,0:T(8,128)(2,1)S(1)}, u32[]{:S(2)}, u32[]{:S(2)}) collective-permute-start(bf16[192,1664]{1,0:T(8,128)(2,1)S(1)} %copy-done.110), channel_id=1, source_target_pairs={{4,0},{6,2},{8,4},{10,6},{12,8},{14,10},{5,1},{7,3},{9,5},{11,7},{... | collective-permute-start | bytes 1916936 | tf_op jit(solution)/shard_map/ppermute | solution.py:389
  669.5 22.0 %collective-permute-start.97 = (bf16[192,1664]{1,0:T(8,128)(2,1)S(1)}, bf16[192,1664]{1,0:T(8,128)(2,1)S(1)}, u32[]{:S(2)}, u32[]{:S(2)}) collective-permute-start(bf16[192,1664]{1,0:T(8,128)(2,1)S(1)} %copy-done.109), channel_id=1, source_target_pairs={{0,4},{2,6},{4,8},{6,10},{8,12},{10,14},{1,5},{3,7},{5,9},{7,11},{... | collective-permute-start | bytes 1916936 | tf_op jit(solution)/shard_map/ppermute | solution.py:389
  691.5 23.2 %collective-permute-start.128 = (bf16[2,192,768]{2,1,0:T(8,128)(2,1)}, bf16[2,192,768]{2,1,0:T(8,128)(2,1)}, u32[]{:S(2)}, u32[]{:S(2)}) collective-permute-start(bf16[2,192,768]{2,1,0:T(8,128)(2,1)} %pad_maximum_fusion.2), channel_id=1, source_target_pairs={{0,16},{16,0},{1,17},{17,1},{2,18},{18,2},{3,19},{19,3},{4,20},{20... | collective-permute-start | bytes 1769480 | tf_op jit(solution)/shard_map/ppermute | solution.py:379
  701.4 30.9 %collective-permute-start.102 = (bf16[192,1664]{1,0:T(8,128)(2,1)}, bf16[192,1664]{1,0:T(8,128)(2,1)}, u32[]{:S(2)}, u32[]{:S(2)}) collective-permute-start(bf16[192,1664]{1,0:T(8,128)(2,1)} %get-tuple-element.107), channel_id=1, source_target_pairs={{0,1},{1,0},{2,3},{3,2},{4,5},{5,4},{6,7},{7,6},{8,9},{9,8},{10,11... | collective-permute-start | bytes 1916936 | tf_op jit(solution)/shard_map/ppermute | solution.py:382
  702.4 29.9 %collective-permute-start.103 = (bf16[192,1664]{1,0:T(8,128)(2,1)}, bf16[192,1664]{1,0:T(8,128)(2,1)}, u32[]{:S(2)}, u32[]{:S(2)}) collective-permute-start(bf16[192,1664]{1,0:T(8,128)(2,1)} %get-tuple-element.108), channel_id=1, source_target_pairs={{0,1},{1,0},{2,3},{3,2},{4,5},{5,4},{6,7},{7,6},{8,9},{9,8},{10,11... | collective-permute-start | bytes 1916936 | tf_op jit(solution)/shard_map/ppermute | solution.py:382
  (253 other events, 3238.5 us)

commit v2 on v1

v2 whole, which is shorter than its diff:
```python
import functools

import jax
import jax.numpy as jnp
from jax import lax
from jax.experimental import pallas as pl
from jax.experimental.pallas import tpu as pltpu
from jax.sharding import PartitionSpec as P

F32 = jnp.float32
BF16 = jnp.bfloat16
LANES = 128
HALF = 64
VMEM_LIMIT = 40 * 1024 * 1024
VMEM_ALL = 60 * 1024 * 1024


def dot(a, b, dims=((1,), (0,)), precision=None):
    return lax.dot_general(a, b, (dims, ((), ())), precision=precision, preferred_element_type=F32)


def dot_exact(a, b, dims=((1,), (0,))):
    return dot(a, b, dims, lax.Precision.HIGHEST)


def silu_parts(x):
    gate = 1.0 / (1.0 + jnp.exp(-x))
    return gate, x * gate


def softplus(x):
    return jnp.maximum(x, 0.0) + jnp.log1p(jnp.exp(-jnp.abs(x)))


def conv_mixed(conv_in, aux, conv_w, conv_b):
    taps = conv_w.shape[0]
    mixed = conv_b + conv_w[taps - 1 : taps] * conv_in
    shifted = []
    for back in range(1, taps):
        moved = pltpu.roll(conv_in, back, 0) * aux[:, back : back + 1]
        shifted.append(moved)
        mixed = mixed + conv_w[taps - 1 - back : taps - back] * moved
    return mixed, shifted


def conv_back(d_mixed, conv_in, shifted, aux, conv_w):
    taps = conv_w.shape[0]
    rows = d_mixed.shape[0]
    d_in = conv_w[taps - 1 : taps] * d_mixed
    d_w = [None] * taps
    d_w[taps - 1] = jnp.sum(d_mixed * conv_in, axis=0, keepdims=True)
    for back in range(1, taps):
        ahead = pltpu.roll(d_mixed, rows - back, 0) * aux[:, taps - 1 + back : taps + back]
        d_in = d_in + conv_w[taps - 1 - back : taps - back] * ahead
        d_w[taps - 1 - back] = jnp.sum(d_mixed * shifted[back - 1], axis=0, keepdims=True)
    return d_in, d_w, jnp.sum(d_mixed, axis=0, keepdims=True)


def decays(last, dt_bias, neg_rate, aux, seg_row):
    rows = last.shape[0]
    step = softplus(last + dt_bias)
    row = lax.broadcasted_iota(jnp.int32, (rows, rows), 0)
    col = lax.broadcasted_iota(jnp.int32, (rows, rows), 1)
    lower = row >= col
    log_decay = dot_exact(lower.astype(F32), neg_rate * step)
    allowed = lower & (aux[:, 0:1] == seg_row)
    return step, log_decay, allowed, lower


def pair_masks(rows):
    lane = lax.broadcasted_iota(jnp.int32, (rows, LANES), 1)
    return (lane < HALF).astype(F32), (lane >= HALF).astype(F32)


def unpack(packed, taps, heads):
    inner = heads * HALF
    conv_w, conv_b = packed[:taps, :], packed[taps : taps + 1, :]
    out_gain, skip = packed[taps + 1 : taps + 2, :inner], packed[taps + 2 : taps + 3, :inner]
    dt_bias, neg_rate = packed[taps + 3 : taps + 4, :LANES], packed[taps + 3 : taps + 4, LANES : 2 * LANES]
    return conv_w, conv_b, dt_bias, neg_rate, skip, out_gain


def ahead_kernel(heads, taps, proj, last, bc, aux, seg_row, packed, outs_ref, gated_ref, square_ref):
    rows = proj.shape[0]
    conv_w, conv_b, dt_bias, neg_rate, skip, _ = unpack(packed, taps, heads)
    inner = heads * HALF
    aux_v = aux[...]
    values_mixed, _ = conv_mixed(proj[:, inner : 2 * inner], aux_v, conv_w[:, :inner], conv_b[:, :inner])
    _, values = silu_parts(values_mixed)
    state_mixed, _ = conv_mixed(bc[...], aux_v, conv_w[:, inner:], conv_b[:, inner:])
    _, state = silu_parts(state_mixed)
    in_state, out_state = state[:, :LANES].astype(BF16), state[:, LANES:].astype(BF16)
    step, log_decay, allowed, _ = decays(
        last[...], dt_bias, neg_rate, aux_v, seg_row[0]
    )
    step_t, log_t = step.T, log_decay.T
    inter = dot(out_state, in_state, ((1,), (1,)))
    first, second = pair_masks(rows)
    squares = jnp.zeros((rows, 1), F32)
    for pair in range(heads // 2):
        weights = []
        for h in (2 * pair, 2 * pair + 1):
            gap = log_decay[:, h : h + 1] - log_t[h : h + 1]
            decay = jnp.exp(jnp.where(allowed, gap, -1e30))
            weights.append((inter * decay * step_t[h : h + 1]).astype(BF16))
        at = slice(pair * LANES, (pair + 1) * LANES)
        own = values[:, at]
        low = own.astype(BF16).astype(F32)
        both = jnp.concatenate([low * first, low * second], axis=0).astype(BF16)
        carried = dot(jnp.concatenate(weights, axis=1), both)
        outs = carried + skip[:, at] * own
        _, gate = silu_parts(proj[:, at])
        gated = outs * gate
        outs_ref[:, at] = outs
        gated_ref[:, at] = gated
        squares = squares + jnp.sum(gated * gated, axis=1, keepdims=True)
    square_ref[...] = jnp.broadcast_to(squares, square_ref.shape)


def back_kernel(
    heads, taps, proj, last_ref, bc, aux, seg_row, packed, outs, d_normed, inverse_ref, shrink_ref, *results
):
    d_main_ref, d_dt_ref, d_state_ref, d_wide_ref, d_narrow_ref = results
    rows = proj.shape[0]
    conv_w, conv_b, dt_bias, neg_rate, skip, out_gain = unpack(packed, taps, heads)
    inner = heads * HALF
    aux_v = aux[...]
    values_in = proj[:, inner : 2 * inner]
    values_mixed, values_shifted = conv_mixed(values_in, aux_v, conv_w[:, :inner], conv_b[:, :inner])
    values_gate, values = silu_parts(values_mixed)
    state_mixed, _ = conv_mixed(bc[...], aux_v, conv_w[:, inner:], conv_b[:, inner:])
    _, state = silu_parts(state_mixed)
    in_state, out_state = state[:, :LANES].astype(BF16), state[:, LANES:].astype(BF16)
    last = last_ref[...]
    step, log_decay, allowed, lower = decays(last, dt_bias, neg_rate, aux_v, seg_row[0])
    step_t, log_t = step.T, log_decay.T
    inter = dot(out_state, in_state, ((1,), (1,)))
    first, second = pair_masks(rows)
    lane = lax.broadcasted_iota(jnp.int32, (rows, LANES), 1)
    sub = lax.broadcasted_iota(jnp.int32, (LANES, rows), 0)
    inverse, shrink = inverse_ref[...], shrink_ref[...]
    d_inter = jnp.zeros((rows, rows), F32)
    row_sums = jnp.zeros((rows, LANES), F32)
    col_sums = jnp.zeros((LANES, rows), F32)
    d_skip, d_gain, d_values = [], [], []
    for pair in range(heads // 2):
        at = slice(pair * LANES, (pair + 1) * LANES)
        own = values[:, at]
        low = own.astype(BF16)
        gate_in = proj[:, at]
        sig, gate = silu_parts(gate_in)
        outs_at = outs[:, at]
        gated = outs_at * gate
        dn = d_normed[:, at]
        d_gain.append(jnp.sum(gated * inverse * dn, axis=0, keepdims=True))
        d_gated = inverse * (out_gain[:, at] * dn) - gated * shrink
        d_outs = d_gated * gate
        d_main_ref[:, at] = (d_gated * outs_at * (sig * (1.0 + gate_in * (1.0 - sig)))).astype(BF16)
        d_skip.append(jnp.sum(d_outs * own, axis=0, keepdims=True))
        d_both = jnp.concatenate([d_outs * first, d_outs * second], axis=0).astype(BF16)
        d_weights = dot(d_both, low, ((1,), (1,)))
        weights = []
        for k, h in enumerate((2 * pair, 2 * pair + 1)):
            gap = log_decay[:, h : h + 1] - log_t[h : h + 1]
            decay = jnp.exp(jnp.where(allowed, gap, -1e30))
            step_row = step_t[h : h + 1]
            weights.append((inter * decay * step_row).astype(BF16))
            part = d_weights[k * rows : (k + 1) * rows] * decay
            d_inter = d_inter + part * step_row
            part = part * inter
            col = jnp.sum(part, axis=0, keepdims=True)
            col_sums = jnp.where(sub == h, col, col_sums)
            row_sum = jnp.sum(part * step_row, axis=1, keepdims=True)
            row_sums = jnp.where(lane == h, row_sum, row_sums)
        d_low = dot(jnp.concatenate(weights, axis=0), d_both, ((0,), (0,)))
        d_values.append(skip[:, at] * d_outs + d_low)
    d_values = jnp.concatenate(d_values, axis=1)
    d_mixed = d_values * (values_gate * (1.0 + values_mixed * (1.0 - values_gate)))
    d_in, d_w, d_b = conv_back(d_mixed, values_in, values_shifted, aux_v, conv_w[:, :inner])
    d_main_ref[:, inner : 2 * inner] = d_in.astype(BF16)
    low_inter = d_inter.astype(BF16)
    d_state_ref[:, :LANES] = dot(low_inter, out_state, ((0,), (0,)))
    d_state_ref[:, LANES:] = dot(low_inter, in_state)
    direct = col_sums.T
    d_log = row_sums - direct * step
    d_pace = dot_exact(lower.astype(F32), d_log, ((0,), (0,)))
    d_step = direct + d_pace * neg_rate
    d_last = jnp.where(lane < heads, d_step * (1.0 / (1.0 + jnp.exp(-(last + dt_bias)))), 0.0)
    d_dt_ref[...] = d_last
    wide = d_w + [d_b, jnp.concatenate(d_skip, axis=1), jnp.concatenate(d_gain, axis=1)]
    wide.append(jnp.zeros((d_wide_ref.shape[1] - len(wide), inner), F32))
    d_wide_ref[0] = jnp.concatenate(wide, axis=0)
    d_rate = jnp.sum(d_pace * neg_rate * step, axis=0, keepdims=True)
    narrow = [
        jnp.sum(d_last, axis=0, keepdims=True),
        jnp.where(lane[:1] < heads, d_rate, 0.0),
        jnp.zeros((d_narrow_ref.shape[1] - 2, LANES), F32),
    ]
    d_narrow_ref[0] = jnp.concatenate(narrow, axis=0)


def state_back_kernel(taps, d_act, last, aux, packed, d_dt, d_proj_ref, d_sums_ref):
    aux_v = aux[...]
    last_v = last[...]
    conv_w, conv_b = packed[8 : 8 + taps, :LANES], packed[8 + taps : 9 + taps, :LANES]
    mixed, shifted = conv_mixed(last_v, aux_v, conv_w, conv_b)
    sig, _ = silu_parts(mixed)
    d_mixed = d_act[...] * (sig * (1.0 + mixed * (1.0 - sig)))
    d_in, d_w, d_b = conv_back(d_mixed, last_v, shifted, aux_v, conv_w)
    lane = lax.broadcasted_iota(jnp.int32, last_v.shape, 1)
    d_proj_ref[...] = jnp.where(lane < HALF, d_dt[...], d_in).astype(BF16)
    sums = d_w + [d_b]
    sums.append(jnp.zeros((d_sums_ref.shape[0] - len(sums), LANES), F32))
    d_sums_ref[...] = jnp.concatenate(sums, axis=0)


def rows_spec(rows, width):
    return pl.BlockSpec((rows, width), lambda i: (i, 0))


def whole_spec(shape):
    return pl.BlockSpec(shape, lambda i: (0,) * len(shape))


def ahead_call(heads, taps, rows, proj, last, bc, aux, seg_rows, packed):
    total = proj.shape[0]
    inner = heads * HALF
    count = total // rows
    return pl.pallas_call(
        functools.partial(ahead_kernel, heads, taps),
        grid=(count,),
        in_specs=[
            rows_spec(rows, proj.shape[1]),
            rows_spec(rows, LANES),
            rows_spec(rows, bc.shape[1]),
            rows_spec(rows, aux.shape[1]),
            pl.BlockSpec((1, 1, rows), lambda i: (i, 0, 0)),
            whole_spec(packed.shape),
        ],
        out_specs=[rows_spec(rows, inner), rows_spec(rows, inner), rows_spec(rows, LANES)],
        out_shape=[
            jax.ShapeDtypeStruct((total, inner), F32),
            jax.ShapeDtypeStruct((total, inner), F32),
            jax.ShapeDtypeStruct((total, LANES), F32),
        ],
        compiler_params=pltpu.CompilerParams(vmem_limit_bytes=VMEM_LIMIT),
        cost_estimate=pl.CostEstimate(
            flops=count * 1_000_000_000, bytes_accessed=count * 2_000_000, transcendentals=count * 400_000
        ),
    )(proj, last, bc, aux, seg_rows, packed)


def back_call(heads, taps, rows, proj, last, bc, aux, seg_rows, packed, outs, d_normed, inverse, shrink):
    total = proj.shape[0]
    inner = heads * HALF
    count = total // rows
    return pl.pallas_call(
        functools.partial(back_kernel, heads, taps),
        grid=(count,),
        in_specs=[
            rows_spec(rows, proj.shape[1]),
            rows_spec(rows, LANES),
            rows_spec(rows, bc.shape[1]),
            rows_spec(rows, aux.shape[1]),
            pl.BlockSpec((1, 1, rows), lambda i: (i, 0, 0)),
            whole_spec(packed.shape),
            rows_spec(rows, inner),
            rows_spec(rows, inner),
            rows_spec(rows, 1),
            rows_spec(rows, 1),
        ],
        out_specs=[
            rows_spec(rows, 2 * inner),
            rows_spec(rows, LANES),
            rows_spec(rows, bc.shape[1]),
            pl.BlockSpec((1, 8, inner), lambda i: (i, 0, 0)),
            pl.BlockSpec((1, 8, LANES), lambda i: (i, 0, 0)),
        ],
        out_shape=[
            jax.ShapeDtypeStruct((total, 2 * inner), BF16),
            jax.ShapeDtypeStruct((total, LANES), F32),
            jax.ShapeDtypeStruct((total, bc.shape[1]), F32),
            jax.ShapeDtypeStruct((count, 8, inner), F32),
            jax.ShapeDtypeStruct((count, 8, LANES), F32),
        ],
        compiler_params=pltpu.CompilerParams(vmem_limit_bytes=VMEM_LIMIT),
        cost_estimate=pl.CostEstimate(
            flops=count * 2_000_000_000, bytes_accessed=count * 3_000_000, transcendentals=count * 600_000
        ),
    )(proj, last, bc, aux, seg_rows, packed, outs, d_normed, inverse, shrink)


def state_back_call(taps, d_act, last, aux, packed, d_dt):
    args = (d_act, last, aux, packed, d_dt)
    return pl.pallas_call(
        functools.partial(state_back_kernel, taps),
        grid=(1,),
        in_specs=[whole_spec(x.shape) for x in args],
        out_specs=[whole_spec(last.shape), whole_spec((8, LANES))],
        out_shape=[jax.ShapeDtypeStruct(last.shape, BF16), jax.ShapeDtypeStruct((8, LANES), F32)],
        compiler_params=pltpu.CompilerParams(vmem_limit_bytes=VMEM_LIMIT),
        cost_estimate=pl.CostEstimate(flops=100_000_000, bytes_accessed=1_500_000, transcendentals=70_000),
    )(*args)


def make_aux(seg, rows, taps):
    blocks = seg.shape[0]
    columns = [seg.astype(F32)]
    for k in range(1, taps):
        before = jnp.pad(seg, ((0, 0), (k, 0)), constant_values=-1)[:, :rows]
        columns.append((before == seg).astype(F32))
    for k in range(1, taps):
        after = jnp.pad(seg, ((0, 0), (0, k)), constant_values=-1)[:, k:]
        columns.append((after == seg).astype(F32))
    columns += [jnp.zeros_like(columns[0])] * (8 - len(columns))
    return jnp.stack(columns, axis=-1).reshape(blocks * rows, 8)


def ring_owner(at, line):
    at = lax.rem(at + 2 * line, 2 * line)
    return jnp.where(at < line, 2 * at, 4 * line - 2 * at - 1)


def assemble_kernel(cuts, starts, *refs):
    outs, sems = refs[-1 - len(cuts) : -1], refs[-1]
    sources = refs[: -1 - len(cuts)]

    def copies(run):
        for k, source in enumerate(sources):
            start = pl.multiple_of(starts[k], 16)
            for n, (low, high) in enumerate(cuts):
                run(
                    pltpu.make_async_copy(
                        source.at[:, low:high],
                        outs[n].at[pl.ds(start, source.shape[0])],
                        sems.at[k * len(cuts) + n],
                    )
                )

    copies(lambda copy: copy.start())
    copies(lambda copy: copy.wait())


def assemble(starts, sources, cuts):
    total = sum(x.shape[0] for x in sources)
    return pl.pallas_call(
        functools.partial(assemble_kernel, cuts),
        in_specs=[pl.BlockSpec(memory_space=pltpu.SMEM)] + [pl.BlockSpec(memory_space=pl.ANY)] * len(sources),
        out_specs=[pl.BlockSpec(memory_space=pltpu.VMEM)] * len(cuts),
        out_shape=[jax.ShapeDtypeStruct((total, high - low), BF16) for low, high in cuts],
        scratch_shapes=[pltpu.SemaphoreType.DMA((len(sources) * len(cuts),))],
        compiler_params=pltpu.CompilerParams(vmem_limit_bytes=VMEM_ALL),
        cost_estimate=pl.CostEstimate(
            flops=0, bytes_accessed=4 * total * sources[0].shape[1], transcendentals=0
        ),
    )(jnp.stack(starts).astype(jnp.int32), *sources)


def quarter_kernel(sizes, where, in_w, out_w, own_ref, other_ref):
    inner_all, state_all, groups, each, heads_all = sizes
    span = each * HALF
    inner = inner_all // 4
    row, core = where[2], where[3]
    tail = in_w[:, 2 * inner_all :]
    spare, depth = LANES - state_all // 4, tail.shape[1]
    for part, ref in ((core, own_ref), (1 - core, other_ref)):
        for base in range(2):
            for group in range(groups):
                pieces = []
                for c in range(2):
                    at = base * inner_all + c * inner_all // 2 + group * 2 * span
                    both = in_w[:, at : at + 2 * span]
                    pieces.append(jnp.where(row == 0, both[:, :span], both[:, span:]))
                ref[:, base * inner + group * span : base * inner + (group + 1) * span] = jnp.where(
                    part == 0, pieces[0], pieces[1]
                )
        source = lax.broadcasted_iota(jnp.int32, (depth, LANES), 0)
        lane = lax.broadcasted_iota(jnp.int32, (depth, LANES), 1)
        group = sum((lane >= g * each).astype(jnp.int32) for g in range(1, groups))
        head = state_all + part * (heads_all // 2) + (2 * group + row) * each + lane - group * each
        state = part * (state_all // 2) + row * (state_all // 4) + lane - spare
        wanted = jnp.where(lane < groups * each, head, jnp.where(lane >= spare, state, -1))
        ref[:, 2 * inner : 2 * inner + LANES] = dot(tail, (source == wanted).astype(BF16)).astype(BF16)
        if out_w is not None:
            half_rows, half = out_w.shape[0] // 2, out_w.shape[1] // 2
            mine = jnp.where(row == 0, out_w[:half_rows, :], out_w[half_rows:, :])
            ref[:, 2 * inner + LANES :] = jnp.where(part == 0, mine[:, :half], mine[:, half:])


def quarters_of(where, in_w, out_w, sizes):
    inner = sizes[0] // 4
    width = 2 * inner + LANES + (0 if out_w is None else out_w.shape[1] // 2)
    spec = pl.BlockSpec(memory_space=pltpu.VMEM)
    kernel = functools.partial(quarter_kernel, sizes)
    args = [where, in_w, out_w]
    if out_w is None:
        args = args[:2]
        inner_kernel = kernel
        kernel = lambda a, b, c, d: inner_kernel(a, b, None, c, d)
    return pl.pallas_call(
        kernel,
        in_specs=[pl.BlockSpec(memory_space=pltpu.SMEM)] + [spec] * (len(args) - 1),
        out_specs=[spec, spec],
        out_shape=[jax.ShapeDtypeStruct((in_w.shape[0], width), BF16)] * 2,
        compiler_params=pltpu.CompilerParams(vmem_limit_bytes=VMEM_LIMIT),
        cost_estimate=pl.CostEstimate(flops=0, bytes_accessed=10_000_000, transcendentals=0),
    )(*args)


def join_kernel(sizes, where, *refs):
    inner_all, state_all, groups, each, heads_all = sizes
    span = each * HALF
    inner = inner_all // 4
    row, core = where[2], where[3]
    has_out = len(refs) > 5
    in_ref = refs[-2] if has_out else refs[-1]

    def quarter(sources, c, r, low, high):
        mine, far, came, came_far = sources
        own = jnp.where(row == r, mine[:, low:high], far[:, low:high])
        theirs = jnp.where(row == r, came[:, low:high], came_far[:, low:high])
        return jnp.where(core == c, own, theirs)

    tails = 0.0
    spare, depth = LANES - state_all // 4, state_all + heads_all
    lane = lax.broadcasted_iota(jnp.int32, (LANES, depth), 0)
    target = lax.broadcasted_iota(jnp.int32, (LANES, depth), 1)
    group = sum((lane >= g * each).astype(jnp.int32) for g in range(1, groups))
    for c in range(2):
        for base in range(2):
            for g in range(groups):
                low = base * inner + g * span
                both = [quarter(refs[:4], c, r, low, low + span).astype(F32) for r in range(2)]
                at = base * inner_all + c * inner_all // 2 + g * 2 * span
                in_ref[0, :, at : at + 2 * span] = jnp.concatenate(both, axis=1)
        for r in range(2):
            head = state_all + c * (heads_all // 2) + (2 * group + r) * each + lane - group * each
            state = c * (state_all // 2) + r * (state_all // 4) + lane - spare
            wanted = jnp.where(lane < groups * each, head, jnp.where(lane >= spare, state, -1))
            chosen = (target == wanted).astype(BF16)
            tails = tails + dot(quarter(refs[:4], c, r, 2 * inner, 2 * inner + LANES), chosen)
            if has_out:
                half_rows, half = refs[4].shape
                low = quarter(refs[4:8], c, r, 0, half).astype(F32)
                refs[-1][0, r * half_rows : (r + 1) * half_rows, c * half : (c + 1) * half] = low
    in_ref[0, :, 2 * inner_all :] = tails


def join(where, quarters, sizes):
    rows = quarters[0].shape[0]
    inner_all, state_all, groups, each, heads_all = sizes
    shapes = [jax.ShapeDtypeStruct((1, rows, 2 * inner_all + state_all + heads_all), F32)]
    if len(quarters) > 4:
        shapes.append(jax.ShapeDtypeStruct((1, 2 * quarters[4].shape[0], 2 * quarters[4].shape[1]), F32))
    spec = pl.BlockSpec(memory_space=pltpu.VMEM)
    return pl.pallas_call(
        functools.partial(join_kernel, sizes),
        in_specs=[pl.BlockSpec(memory_space=pltpu.SMEM)] + [spec] * len(quarters),
        out_specs=[spec] * len(shapes),
        out_shape=shapes,
        compiler_params=pltpu.CompilerParams(vmem_limit_bytes=VMEM_LIMIT),
        cost_estimate=pl.CostEstimate(flops=0, bytes_accessed=12_000_000, transcendentals=0),
    )(where, *quarters)


class Links:
    def __init__(self, mesh_shape):
        self.line = mesh_shape["fsdp"] // 2
        at = self.fsdp = lax.axis_index("fsdp")
        self.at = jnp.where(at % 2 == 0, at // 2, 2 * self.line - 1 - at // 2)
        ring = [2 * p for p in range(self.line)] + [2 * p + 1 for p in reversed(range(self.line))]
        self.ahead = [(ring[k - 1], ring[k]) for k in range(len(ring))]
        self.behind = [(after, before) for before, after in self.ahead]
        self.row, self.core = lax.axis_index("dp"), lax.axis_index("section")

    def swap_core(self, x):
        return lax.ppermute(x, "section", [(0, 1), (1, 0)])

    def swap_row(self, x):
        return lax.ppermute(x, "dp", [(0, 1), (1, 0)])

    def swap_side(self, x):
        return lax.ppermute(x, "fsdp", [(2 * p + s, 2 * p + 1 - s) for p in range(self.line) for s in range(2)])

    def mine_of_core(self, first, second):
        return jnp.where(self.core == 0, first, second)

    def in_row_order(self, own, other, axis):
        return jnp.where(
            self.row == 0, jnp.concatenate([own, other], axis), jnp.concatenate([other, own], axis)
        )

    def in_core_order(self, own, other, axis):
        return jnp.where(
            self.core == 0, jnp.concatenate([own, other], axis), jnp.concatenate([other, own], axis)
        )

    def cut(self, x, axis, which, parts=2):
        size = x.shape[axis] // parts
        return lax.dynamic_slice_in_dim(x, which * size, size, axis)

    def upper(self, shard_rows):
        return (shard_rows + 31) // 32 * 16

    def gather(self, piece):
        shard_rows = piece.shape[0]
        upper = self.upper(shard_rows)
        up, down = piece[:upper], piece[upper:]
        sources, starts = [piece], [ring_owner(self.at, self.line) * shard_rows]
        for hop in range(1, 2 * self.line):
            up, down = yield [lax.ppermute(up, "fsdp", self.ahead), lax.ppermute(down, "fsdp", self.behind)]
            sources += [up, down]
            starts.append(ring_owner(self.at - hop, self.line) * shard_rows)
            starts.append(ring_owner(self.at + hop, self.line) * shard_rows + upper)
        return starts, sources

    def shift(self, x, by):
        line = self.line
        return lax.ppermute(x, "fsdp", [(2 * p + s, 2 * ((p + by) % line) + s) for p in range(line) for s in range(2)])

    def gather_side(self, piece):
        line, shard_rows = self.line, piece.shape[0]
        place, side = self.fsdp // 2, self.fsdp % 2
        order = sorted(range(1, line), key=lambda by: min(by, line - by))
        sources, starts = [], []
        held = piece
        for turn in range(line):
            by = 0 if turn == 0 else order[turn - 1]
            parts = [self.swap_side(held)]
            if turn < line - 1:
                parts.append(self.shift(piece, order[turn]))
            crossed, *moved = yield parts
            owner = 2 * lax.rem(place - by + line, line)
            sources += [held, crossed]
            starts += [(owner + side) * shard_rows, (owner + 1 - side) * shard_rows]
            held = moved[0] if moved else None
        return starts, sources

    def scatter_side(self, parts):
        line = self.line
        place, side = self.fsdp // 2, self.fsdp % 2
        order = sorted(range(1, line), key=lambda by: -min(by, line - by)) + [0]

        def term(by, other):
            owner = 2 * lax.rem(place + by, line) + (1 - side if other else side)
            return lax.dynamic_index_in_dim(parts, owner, 0, keepdims=False)

        total, summed = 0.0, None
        for turn in range(line):
            moves = [self.swap_side(term(order[turn], True))]
            if turn > 0:
                moves.append(self.shift(summed, order[turn - 1]))
            crossed, *moved = yield moves
            summed = term(order[turn], False).astype(F32) + crossed.astype(F32)
            if turn < line - 1:
                summed = summed.astype(BF16)
            if moved:
                total = total + moved[0].astype(F32)
        return (total + summed).astype(BF16)

    def scatter(self, shard_rows, term):
        upper = self.upper(shard_rows)
        up = down = None
        for hop in range(1, 2 * self.line):
            own_up = term(ring_owner(self.at - hop, self.line), 0, upper)
            own_down = term(ring_owner(self.at + hop, self.line), upper, shard_rows)
            if hop > 1:
                own_up = (own_up.astype(F32) + up.astype(F32)).astype(BF16)
                own_down = (own_down.astype(F32) + down.astype(F32)).astype(BF16)
            up, down = yield [lax.ppermute(own_up, "fsdp", self.ahead), lax.ppermute(own_down, "fsdp", self.behind)]
        owner = ring_owner(self.at, self.line)
        up = up.astype(F32) + term(owner, 0, upper).astype(F32)
        down = down.astype(F32) + term(owner, upper, shard_rows).astype(F32)
        return jnp.concatenate([up.astype(BF16), down.astype(BF16)], axis=0)

    def sum_line(self, x):
        size = self.line
        if size & (size - 1):
            return lax.psum(x, "fsdp") / 2
        by = 1
        while by < size:
            pairs = [(2 * p + s, 2 * (p ^ by) + s) for p in range(size) for s in range(2)]
            x = x + lax.ppermute(x, "fsdp", pairs)
            by *= 2
        return x


RING = {('gb', 0): True, ('gb', 1): False, ('out', 1): False, ('in', 1): True, ('out', 0): False, ('in', 0): True}


class Schedule:
    def __init__(self, work):
        self.work, self.sent, self.sides = work, None, []

    def launch(self, moves, finish):
        self.sides.append([moves, None, finish])

    def round(self, parts):
        extra = []
        if self.work is not None:
            try:
                extra = list(self.work.send(self.sent))
            except StopIteration:
                self.work = None
        groups = [list(parts), extra]
        going = []
        for side in self.sides:
            try:
                groups.append(list(side[0].send(side[1])))
                going.append(side)
            except StopIteration as stop:
                side[2](stop.value)
        self.sides = going
        joined = list(lax.optimization_barrier(tuple(x for group in groups for x in group)))
        split = []
        for group in groups:
            split.append(joined[: len(group)])
            joined = joined[len(group) :]
        self.sent = split[1]
        for side, values in zip(going, split[2:]):
            side[1] = values
        return split[0]

    def run(self, moves):
        sent = None
        while True:
            try:
                parts = moves.send(sent)
            except StopIteration as stop:
                return stop.value
            sent = self.round(parts)


def body(mesh_shape, inputs, seq_lengths, norm_gain, in_w, conv_w, conv_b, dt_bias, a_log, skip, out_gain, out_w, cotangent):
    links = Links(mesh_shape)
    core, row = links.core, links.row
    shards = mesh_shape["fsdp"]
    width = inputs.shape[1]
    half_width = width // 2
    own_tokens = inputs.shape[0]
    tokens = 2 * own_tokens
    rows = own_tokens // seq_lengths.shape[0]
    inner_all = out_gain.shape[1]
    heads_all = a_log.shape[1]
    head_dim = inner_all // heads_all
    taps, channels = conv_w.shape[1:]
    state_all = channels - inner_all
    state_own = state_all // 4
    heads = heads_all // 4
    inner = inner_all // 4
    split = 2 * inner + LANES
    shard_rows = in_w.shape[1]
    direct = heads_all % shards == 0 and (heads_all // shards) % 2 == 0
    groups = shards // 2 if direct else 1
    each = heads // groups
    span = each * head_dim
    sizes = (inner_all, state_all, groups, each, heads_all)

    def pick_row(x, axis):
        return jnp.where(row == 0, lax.index_in_dim(x, 0, axis, False), lax.index_in_dim(x, 1, axis, False))

    def pick(x, axis):
        return links.mine_of_core(lax.index_in_dim(x, 0, axis, False), lax.index_in_dim(x, 1, axis, False))

    def wide_part(x):
        x = pick(x.reshape(x.shape[0], 2, groups, 2, span), 1)
        return pick_row(x, 2).reshape(x.shape[0], inner)

    def head_part(x):
        x = pick(x.reshape(x.shape[0], 2, groups, 2, each), 1)
        return pick_row(x, 2).reshape(x.shape[0], heads)

    def state_part(x):
        x = pick(x.reshape(x.shape[0], 2, 2, state_own), 1)
        return pick_row(x, 1)

    def wide_row(x):
        return jnp.pad(x, ((0, 0), (0, channels - x.shape[1])))

    zero = jnp.int32(0)
    where = jnp.stack([zero, zero, row, core]).astype(jnp.int32)
    own_part, other_part = quarters_of(where, in_w[0], out_w[0] if direct else None, sizes)
    came_part = links.swap_core(other_part)
    both = (links.mine_of_core(own_part, came_part), links.mine_of_core(came_part, own_part))
    if not direct:
        out_first, out_second = out_w[0][:, :half_width], out_w[0][:, half_width:]
        kept = links.mine_of_core(out_first, out_second)
        came = links.swap_core(links.mine_of_core(out_second, out_first))
        out_pieces = (links.mine_of_core(kept, came), links.mine_of_core(came, kept))
    pieces = list(both)

    packed = jnp.concatenate(
        [conv_w[0], conv_b, wide_row(out_gain), wide_row(norm_gain), wide_row(dt_bias), wide_row(a_log), wide_row(skip)],
        axis=0,
    )
    packed_other = links.swap_core(packed)
    all_lengths = links.in_row_order(seq_lengths, links.swap_row(seq_lengths), 0)
    sent_tokens, pieces[0], all_lengths, packed_other = lax.optimization_barrier(
        (inputs, pieces[0], all_lengths, packed_other)
    )

    def layer_params(pack):
        cw, cb = pack[:taps], pack[taps : taps + 1]
        og, ng = pack[taps + 1 : taps + 2, :inner_all], pack[taps + 2 : taps + 3, :width]
        dt, al, sk = (pack[taps + 3 + k : taps + 4 + k, :heads_all] for k in range(3))
        lanes = inner + state_all
        fill = lambda x: jnp.pad(x, ((0, 0), (0, lanes - x.shape[1])))
        conv = jnp.concatenate([cw, cb], axis=0)
        narrow = jnp.concatenate([head_part(dt), -jnp.exp(head_part(al))], axis=0)
        narrow = jnp.pad(narrow, ((0, 0), (0, LANES - heads))).reshape(1, 2 * LANES)
        own_state = jnp.pad(state_part(conv[:, inner_all:]), ((0, 0), (LANES - state_own, 0)))
        rows_ = [
            jnp.concatenate([wide_part(conv[:, :inner_all]), conv[:, inner_all:]], axis=1),
            fill(wide_part(og)),
            fill(jnp.repeat(head_part(sk), head_dim, axis=1)),
            fill(narrow),
            fill(own_state),
        ]
        return fill(jnp.concatenate([jnp.concatenate(rows_, axis=0), jnp.zeros((16 - 2 * taps - 5, lanes), F32)], axis=0)), ng

    blocks = tokens // rows
    big = {}

    def to_rows(x):
        return x.reshape(-1, LANES)

    def norm_of(u):
        return lax.rsqrt(jnp.mean(u * u, axis=-1, keepdims=True) + 1e-05)

    def over_cores(x):
        return links.cut(x, 1, core) + links.swap_core(links.cut(x, 1, 1 - core))

    def own_rows(x):
        return links.cut(x, 0, row)

    def norm_back(u, gain, d_scaled):
        u = u.astype(F32)
        inverse = norm_of(u)
        meet = jnp.mean(u * gain * d_scaled, axis=1, keepdims=True)
        return inverse * gain * d_scaled - u * (inverse * inverse * inverse * meet)

    def gain_back(u, d_scaled):
        u = u.astype(F32)
        return jnp.sum(u * norm_of(u) * d_scaled, axis=0, keepdims=True)

    def scaled_of(u, gain):
        u = u.astype(F32)
        return (u * norm_of(u) * gain).astype(BF16)

    def out_whole(pieces):
        kept = links.cut(pieces, 0, core)
        came = links.swap_core(links.cut(pieces, 0, 1 - core))
        return links.in_core_order(kept, came, 1)

    def ahead(layer, scaled):
        wide_w, last_w = big["in", layer]
        last = dot(scaled, last_w)
        came = links.swap_row(last[:, LANES - state_own :])
        proj = dot(scaled, wide_w)
        proj, last, came = yield [proj, last, came]
        part = links.in_row_order(last[:, LANES - state_own :], came, 1)
        bc = links.in_core_order(part, links.swap_core(part), 1)
        outs, gated, squares = ahead_call(heads, taps, rows, proj, last, bc, aux, seg_rows, big["pack", layer])
        bc, outs, gated, squares = yield [bc, outs, gated, squares]
        squares = to_rows(squares[:, 0])
        squares = squares + links.swap_core(squares)
        squares = squares + links.swap_row(squares)
        (squares,) = yield [squares]
        inverse = lax.rsqrt(squares.reshape(tokens, 1) / inner_all + 1e-05)
        gain = big["pack", layer][taps + 1 : taps + 2, :inner]
        normed = (gated * inverse * gain).astype(BF16)
        normed_all = links.in_core_order(normed, links.swap_core(normed), 1)
        return {"scaled": scaled, "proj": proj, "last": last, "bc": bc, "outs": outs, "gated": gated, "inverse": inverse, "normed": normed_all}

    def back_first(layer, kept, grad, meet=None):
        d_normed = dot(grad, big["out_whole", layer], ((1,), (1,)))
        gain = big["pack", layer][taps + 1 : taps + 2, :inner]
        if meet is None:
            meet = to_rows(jnp.sum(kept["gated"] * gain * d_normed, axis=1))
            d_normed, meet = yield [d_normed, meet]
            meet = meet + links.swap_core(meet)
            meet = (links.swap_row(meet) + meet) * to_rows(kept["inverse"][:, 0])
            (meet,) = yield [meet]
        else:
            meet = meet + links.swap_core(meet)
            d_normed, meet = yield [d_normed, meet]
        inverse = kept["inverse"]
        shrink = inverse * inverse * meet.reshape(tokens, 1) / inner_all
        d_main, d_dt, d_bc, d_wide, d_narrow = back_call(
            heads, taps, rows, kept["proj"], kept["last"], kept["bc"], aux, seg_rows, big["pack", layer],
            kept["outs"], d_normed, inverse, shrink,
        )
        d_main, d_dt, d_bc, d_wide, d_narrow = yield [d_main, d_dt, d_bc, d_wide, d_narrow]
        wide_w, last_w = big["in", layer]
        d_bc = over_cores(d_bc)
        d_bc = links.cut(d_bc, 1, row) + links.swap_row(links.cut(d_bc, 1, 1 - row))
        d_in = dot(kept["scaled"], d_main, ((0,), (0,))).astype(BF16)
        d_scaled = dot(d_main, wide_w, ((1,), (1,)))
        d_bc, d_in, d_scaled = yield [d_bc, d_in, d_scaled]
        d_bc = jnp.pad(d_bc, ((0, 0), (LANES - d_bc.shape[1], 0)))
        d_last, d_state = state_back_call(taps, d_bc, kept["last"], aux, big["pack", layer], d_dt)
        d_in_last = dot(kept["scaled"], d_last, ((0,), (0,))).astype(BF16)
        d_scaled = d_scaled + dot(d_last, last_w, ((1,), (1,)))
        d_scaled, d_in, d_in_last = yield [d_scaled, d_in, d_in_last]
        done["in", layer] = d_in, d_in_last
        return d_scaled, (jnp.sum(d_wide, axis=0), jnp.sum(d_narrow, axis=0), d_state)

    def out_grad(kept, grad):
        return dot(kept["normed"], links.cut(grad, 1, core), ((0,), (0,))).astype(BF16)

    def four(low0, low1, far0, far1, theirs):
        return [
            links.mine_of_core(low0, low1),
            links.mine_of_core(far0, far1),
            theirs,
            links.swap_core(links.mine_of_core(far1, far0)),
        ]

    aux = seg_rows = None
    done = {}

    def send_out(layer, d_out):
        done["out", layer] = d_out
        if direct and not RING["out", layer]:


            def finish(total):
                done["sum", ("out", layer)] = total

            schedule.launch(links.scatter_side(d_out.reshape(shards, shard_rows, half_width)), finish)

    def work():
        nonlocal aux, seg_rows
        pack0, gain0 = layer_params(links.mine_of_core(packed, packed_other))
        pack1, gain1 = layer_params(links.mine_of_core(packed_other, packed))
        ends = jnp.cumsum(all_lengths, axis=1)
        positions = jnp.arange(rows, dtype=jnp.int32)
        segments = jnp.sum((positions[None, :, None] >= ends[:, None, :]).astype(jnp.int32), axis=2)
        aux, seg_rows = make_aux(segments, rows, taps), segments.astype(F32)[:, None, :]
        came_tokens = links.swap_row(sent_tokens)
        pack0, pack1, gain0, gain1, aux, seg_rows = yield [pack0, pack1, gain0, gain1, aux, seg_rows]
        big["pack", 0], big["pack", 1] = pack0, pack1
        (came_tokens,) = yield [came_tokens]
        tokens_all = links.in_row_order(inputs, came_tokens, 0)
        scaled = scaled_of(tokens_all, gain0)
        sent_cot, _ = lax.optimization_barrier((cotangent, came_tokens))
        came_cot = links.swap_row(sent_cot)
        tokens_all, scaled = yield [tokens_all, scaled]
        yield [scaled]
        cot_all = links.in_row_order(cotangent, came_cot, 0)
        (cot_all,) = yield [cot_all]
        while ("in", 0) not in big:
            yield [scaled]
        kept0 = yield from ahead(0, scaled)
        while ("out", 0) not in big:
            yield [scaled]
        branch = dot(kept0["normed"], big["out", 0]).astype(BF16)
        kept0["normed"], kept0["inverse"], branch = yield [kept0["normed"], kept0["inverse"], branch]
        came = links.swap_row(branch)
        big["out_whole", 0] = out_whole(big["out", 0])
        branch, big["out_whole", 0] = yield [branch, big["out_whole", 0]]
        (came,) = yield [came]
        while ("in", 1) not in big:
            yield [came]
        branch = branch.astype(F32) + came.astype(F32)
        first = (links.cut(tokens_all, 1, core).astype(F32) + branch).astype(BF16)
        first = links.in_core_order(first, links.swap_core(first), 1)
        scaled = scaled_of(first, gain1)
        kept1 = yield from ahead(1, scaled)
        d_out = out_grad(kept1, cot_all)
        kept1["normed"], kept1["inverse"], d_out = yield [kept1["normed"], kept1["inverse"], d_out]
        send_out(1, d_out)
        while ("out", 1) not in big:
            yield [first]
        big["out_whole", 1] = out_whole(big["out", 1])
        d_scaled, small1 = yield from back_first(1, kept1, cot_all)
        d_scaled = over_cores(d_scaled).astype(BF16)
        (d_scaled,) = yield [d_scaled]
        came = links.swap_row(d_scaled)
        yield [d_scaled]
        (came,) = yield [came]
        d_scaled = d_scaled.astype(F32) + came.astype(F32)
        d_scaled = links.in_core_order(d_scaled, links.swap_core(d_scaled), 1)
        grad = (cot_all.astype(F32) + norm_back(first, gain1, d_scaled)).astype(BF16)
        gain_sum1 = gain_back(own_rows(first), own_rows(d_scaled))
        d_out = out_grad(kept0, grad)
        grad, d_out = yield [grad, d_out]
        send_out(0, d_out)
        meet = to_rows(jnp.sum(branch * links.cut(grad, 1, core).astype(F32), axis=1))
        d_scaled, small0 = yield from back_first(0, kept0, grad, meet)
        d_scaled = over_cores(d_scaled)
        (d_scaled,) = yield [d_scaled]
        came = links.swap_row(links.cut(d_scaled, 0, 1 - row).astype(BF16))
        (came,) = yield [came]
        d_scaled = own_rows(d_scaled) + came.astype(F32)
        d_scaled = links.in_core_order(d_scaled, links.swap_core(d_scaled), 1)
        own_grad = own_rows(grad)
        grad_in = (own_grad.astype(F32) + norm_back(inputs, gain0, d_scaled)).astype(BF16)
        gain_sum0 = gain_back(inputs, d_scaled)
        grad_in, gain_sum0 = yield [grad_in, gain_sum0]
        done["input_grad"] = jnp.where(core == 0, grad_in, own_grad)[None]
        while ("sum", ("in", 1)) not in done:
            yield [gain_sum0]
        far_in1 = links.swap_row(done["sum", ("in", 1)])
        small = jnp.concatenate([pack_small(*small0, gain_sum0), pack_small(*small1, gain_sum1)], axis=0)
        small = small + links.swap_side(small)
        if direct:
            while ("sum", ("out", 0)) not in done:
                yield [small]
            out0, out1 = done["sum", ("out", 0)], done["sum", ("out", 1)]
            far0, far1 = links.swap_row(out0), links.swap_row(out1)
            small, far0, far1 = yield [small, far0, far1]
            theirs = links.swap_core(links.mine_of_core(out1, out0))
            done["out_quarters"] = four(out0, out1, far0, far1, theirs)
        small = links.sum_line(small)
        (small,) = yield [small]
        small_other = links.swap_row(small)
        partial = dot(kept1["normed"], big["out", 1])
        small, small_other, partial = yield [small, small_other, partial]
        came = links.swap_row(links.cut(partial, 0, 1 - row).astype(BF16))
        done["small"] = spread_small(small, small_other)
        came, done["far", "in"], *done["small"] = yield [came, far_in1] + list(done["small"])
        second = own_rows(partial) + came.astype(F32) + links.cut(own_rows(first), 1, core).astype(F32)
        second = second.astype(BF16)
        second = links.in_core_order(second, links.swap_core(second), 1)
        done["phase_out"] = jnp.where(core == 0, own_rows(first), second)[None]
        (done["phase_out"],) = yield [done["phase_out"]]

    gain_rows = width // inner

    def pack_small(wide_, narrow, d_state, gain):
        gain = gain.reshape(-1, inner)
        narrow_rows = jnp.concatenate([narrow[:2], d_state[: taps + 1]], axis=0)
        narrow_rows = jnp.pad(narrow_rows.reshape(1, -1), ((0, 0), (0, 2 * inner - narrow_rows.size)))
        return jnp.concatenate([wide_[: taps + 3], gain, narrow_rows.reshape(2, inner)], axis=0)

    def by_row(a, b):
        return jnp.where(row == 0, jnp.stack([a, b]), jnp.stack([b, a]))

    def spread_small(small, small_other):
        per = small.shape[0] // 2
        mine = links.mine_of_core(small[:per], small[per:])
        mine_other = links.mine_of_core(small_other[:per], small_other[per:])
        theirs = links.mine_of_core(small[per:], small[:per])
        theirs_other = links.mine_of_core(small_other[per:], small_other[:per])
        came = links.swap_core(jnp.stack([theirs, theirs_other]))
        own_parts, came_parts = by_row(mine, mine_other), by_row(came[0], came[1])
        quarters = jnp.where(core == 0, jnp.stack([own_parts, came_parts]), jnp.stack([came_parts, own_parts]))

        def spread_wide(x):
            lead = x.shape[2:-1]
            x = x.reshape((2, 2) + lead + (groups, span))
            x = jnp.moveaxis(x, (0, 1), (len(lead), len(lead) + 2))
            return x.reshape(lead + (inner_all,))

        def spread_heads(x):
            x = x.reshape((2, 2, groups, each))
            return jnp.moveaxis(x, 1, 2).reshape(1, heads_all)

        grad_norm = mine[taps + 3 : taps + 3 + gain_rows] + mine_other[taps + 3 : taps + 3 + gain_rows]
        narrow = quarters[:, :, taps + 3 + gain_rows :].reshape(2, 2, -1)
        narrow = narrow[:, :, : (taps + 3) * LANES].reshape(2, 2, taps + 3, LANES)
        states = jnp.moveaxis(narrow[:, :, 2:, LANES - state_own :], 2, 0).reshape(taps + 1, state_all)
        wide_full = spread_wide(quarters[:, :, : taps + 3])
        return [
            grad_norm.reshape(1, width),
            jnp.concatenate([wide_full[:taps], states[:taps]], axis=1)[None],
            jnp.concatenate([wide_full[taps : taps + 1], states[taps:]], axis=1),
            spread_heads(narrow[:, :, 0, :heads]),
            spread_heads(narrow[:, :, 1, :heads]),
            wide_full[taps + 1].reshape(1, heads_all, head_dim).sum(axis=-1),
            wide_full[taps + 2 : taps + 3],
        ]

    schedule = Schedule(work())

    def gather(layer):
        cuts = [(0, 2 * inner), (2 * inner, split)]
        piece, side_piece = pieces[layer], None
        if direct and RING["gb", layer]:
            cuts.append((split, split + half_width))
        elif direct:
            piece, side_piece = piece[:, :split], piece[:, split:]
        if side_piece is not None:

            def finish(found):
                (big["out", layer],) = assemble(*found, [(0, half_width)])

            schedule.launch(links.gather_side(side_piece), finish)
        full = assemble(*schedule.run(links.gather(piece)), cuts)
        big["in", layer] = full[:2]
        if len(cuts) > 2:
            big["out", layer] = full[2]
        elif not direct:
            big["out", layer] = out_gathered(layer)

    def scatter(kind, layer):
        name = (kind, layer)
        while name not in done:
            schedule.round([])
        if kind == "out" and direct and not RING[name]:
            return
        if kind == "out" and not direct:
            parts = done[name].reshape(2, 1, inner, half_width)
            parts = links.in_row_order(parts, jnp.zeros_like(parts), 1).reshape(4 * inner, half_width)
            mine = lax.psum_scatter(parts, "fsdp", scatter_dimension=0, tiled=True)
            total = mine.astype(F32) + links.swap_row(mine).astype(F32)
            done["sum", name] = total.astype(BF16)
        elif RING[name]:
            parts = [x.reshape(shards, shard_rows, -1) for x in (done[name] if kind == "in" else [done[name]])]

            def term(owner, low, high):
                taken = [lax.dynamic_slice(x, (owner, low, 0), (1, high - low, x.shape[2]))[0] for x in parts]
                return taken[0] if len(taken) == 1 else jnp.concatenate(taken, axis=1)

            done["sum", name] = schedule.run(links.scatter(shard_rows, term))
        else:
            parts = jnp.concatenate(done[name], axis=1) if kind == "in" else done[name]
            done["sum", name] = lax.psum_scatter(parts, "fsdp", scatter_dimension=0, tiled=True)

    def out_gathered(layer):
        full = lax.all_gather(out_pieces[layer], "fsdp", axis=0, tiled=True)
        return pick_row(full.reshape(2, 2, inner, half_width), 1).reshape(2 * inner, half_width)

    gather(0)
    gather(1)
    scatter("out", 1)
    scatter("in", 1)
    scatter("out", 0)
    scatter("in", 0)
    while schedule.work is not None:
        schedule.round([])

    low0, low1, far1 = done["sum", ("in", 0)], done["sum", ("in", 1)], done["far", "in"]
    out0, out1 = done["sum", ("out", 0)], done["sum", ("out", 1)]
    theirs = links.swap_core(links.mine_of_core(low1, low0))
    quarters = four(low0, low1, links.swap_row(low0), far1, theirs)
    if direct:
        grad_in_w, grad_out_w = join(where, quarters + done["out_quarters"], sizes)
    else:
        (grad_in_w,) = join(where, quarters, sizes)
        theirs = links.swap_core(links.mine_of_core(out1, out0))
        grad_out_w = links.in_core_order(links.mine_of_core(out0, out1), theirs, 1).astype(F32)[None]
    grad_norm, grad_conv_w, grad_conv_b, grad_dt, grad_a, grad_skip, grad_out_gain = done["small"]
    return (
        done["phase_out"], done["input_grad"], grad_norm, grad_in_w, grad_conv_w, grad_conv_b,
        grad_dt, grad_a, grad_skip, grad_out_gain, grad_out_w,
    )


def solution(mesh):
    return jax.shard_map(
        functools.partial(body, dict(mesh.shape)),
        mesh=mesh,
        in_specs=(
            P(("fsdp", "dp"), None),
            P(("fsdp", "dp"), None),
            P("section", None),
            P("section", "fsdp", None),
            P("section", None, None),
            P("section", None),
            P("section", None),
            P("section", None),
            P("section", None),
            P("section", None),
            P("section", "fsdp", None),
            P(("fsdp", "dp"), None),
        ),
        out_specs=(
            P("section", ("fsdp", "dp"), None),
            P("section", ("fsdp", "dp"), None),
            P("section", None),
            P("section", "fsdp", None),
            P("section", None, None),
            P("section", None),
            P("section", None),
            P("section", None),
            P("section", None),
            P("section", None),
            P("section", "fsdp", None),
        ),
        check_vma=False,
    )
```

time: 786 us -> 600 us (0.76)
  starting transfers between devices: 227 us -> 120 us
  local copies, waits for them, and re-layouts: 124 us -> 55.2 us
  waiting for transfers between devices: 253 us -> 221 us
  Pallas kernels: 42.6 us -> 57.5 us
  matrix products: 39.8 us -> 53.5 us
    ppermute x83 -> x80, starting transfers between devices: 202 us -> 92.7 us  [the longest x14 19.3 us: gather(): lax.ppermute(up, 'fsdp', self.ahead)]
    ppermute x83 -> x80, waiting for transfers between devices: 205 us -> 172 us  [the longest x14 65.4 us: gather(): lax.ppermute(up, 'fsdp', self.ahead)]
    unnamed x392 -> x319, local copies, waits for them, and re-layouts: 44.2 us -> 19.3 us
    reshape x27 -> x14, local copies, waits for them, and re-layouts: 24.3 us -> 1.14 us  [the longest x6 0.55 us: head_part(): x = pick(x.reshape(x.shape[0], 2, groups, 2, each), 1)]
    pallas_call x14 -> x11, Pallas kernels: 42.6 us -> 57.5 us  [the longest x2 21.3 us: back_call(): pl.pallas_call(functools.partial(back_kernel, heads, taps), grid=(count,)...]
    dot_general x12 -> x18, matrix products: 39.8 us -> 53.5 us  [dot(): lax.dot_general(a, b, (dims, ((), ())), precision=precision, preferred_el...]
    slice x63 -> x39, local copies, waits for them, and re-layouts: 15.7 us -> 4.58 us  [the longest x2 1.74 us: gather(): up, down = (piece[:upper], piece[upper:])]
    another operation x17 -> x6, other arithmetic: 10.8 us -> 0.43 us  [the longest x1 0.18 us: work(): ends = jnp.cumsum(all_lengths, axis=1)]
  transfers between devices with their start and end apart: 129 -> 124, of which waited for: 44 -> 62; matrix products, arithmetic and copies ran while one was open for 22% -> 23% of each run, Pallas kernels for 4% -> 8%
where the time goes in v2:
time: 600 us; the launch traced here: 591 us
  waiting for transfers between devices  221 us (37%)
  starting transfers between devices  120 us (20%)
  other arithmetic  79 us (13%)
  Pallas kernels  57.5 us (10%)
  local copies, waits for them, and re-layouts  55.2 us (9%)
  matrix products  53.5 us (9%)
    ppermute x14, waiting for transfers between devices, gather(): lax.ppermute(up, 'fsdp', self.ahead)  65.4 us
    dot_general x18, matrix products, dot(): lax.dot_general(a, b, (dims, ((), ())), precision=precision, preferred_el...  53.5 us
    ppermute x19, waiting for transfers between devices, swap_row(): return lax.ppermute(x, 'dp', [(0, 1), (1, 0)])  44.3 us
    ppermute x19, starting transfers between devices, swap_row(): return lax.ppermute(x, 'dp', [(0, 1), (1, 0)])  23.9 us
    ppermute x13, waiting for transfers between devices, swap_side(): lax.ppermute(x, 'fsdp', [(2 * p + s, 2 * p + 1 - s) for p in range(self.l...  23.7 us
    ppermute x14, waiting for transfers between devices, scatter(): lax.ppermute(own_down, 'fsdp', self.behind)  21.5 us
    pallas_call x2, Pallas kernels, back_call(): pl.pallas_call(functools.partial(back_kernel, heads, taps), grid=(count,)...  21.3 us
    ppermute x9, waiting for transfers between devices, shift(): lax.ppermute(x, 'fsdp', [(2 * p + s, 2 * ((p + by) % line) + s) for p in...  19.4 us
  transfers between devices with their start and end apart: 124, of which 62 were waited for; matrix products, arithmetic and copies ran while one was open for 23% of the time, Pallas kernels for 8%

profile of v2, /device:TPU:0, one launch (start us, length us, event | category | flops | bytes accessed | tf_op | source)
XLA Modules:
  0.0 590.7 jit_solution(16360688706100038186)
XLA Ops:
  3.8 3.0 shard_map.203
  7.3 2.6 collective-permute-start.1
  26.5 6.3 %collective-permute-done.4.refs_2_ = bf16[96,2432]{1,0:T(8,128)(2,1)S(1)} collective-permute-done((bf16[96,2432]{1,0:T(8,128)(2,1)}, bf16[96,2432]{1,0:T(8,128)(2,1)S(1)}, u32[]{:S(2)}, u32[]{:S(2)}) %collective-permute-start.4) | collective-permute-done | bytes 466976 | tf_op jit(solution)/shard_map/ppermute | solution.py:511
  36.0 6.7 %collective-permute-done.7 = bf16[256,1536]{1,0:T(8,128)(2,1)S(1)} collective-permute-done((bf16[256,1536]{1,0:T(8,128)(2,1)S(1)}, bf16[256,1536]{1,0:T(8,128)(2,1)S(1)}, u32[]{:S(2)}, u32[]{:S(2)}) %collective-permute-start.7) | collective-permute-done | bytes 786464 | tf_op jit(solution)/shard_map/ppermute | solution.py:480
  50.1 6.1 %collective-permute-done.8.refs_5_ = bf16[96,2432]{1,0:T(8,128)(2,1)S(1)} collective-permute-done((bf16[96,2432]{1,0:T(8,128)(2,1)}, bf16[96,2432]{1,0:T(8,128)(2,1)S(1)}, u32[]{:S(2)}, u32[]{:S(2)}) %collective-permute-start.8) | collective-permute-done | bytes 466976 | tf_op jit(solution)/shard_map/ppermute | solution.py:511
  59.4 7.5 %collective-permute-done.12.refs_7_ = bf16[96,2432]{1,0:T(8,128)(2,1)S(1)} collective-permute-done((bf16[96,2432]{1,0:T(8,128)(2,1)S(1)}, bf16[96,2432]{1,0:T(8,128)(2,1)S(1)}, u32[]{:S(2)}, u32[]{:S(2)}) %collective-permute-start.12) | collective-permute-done | bytes 466976 | tf_op jit(solution)/shard_map/ppermute | solution.py:511
  67.0 2.6 collective-permute-done.13.refs_8_
  69.6 2.5 collective-permute-start.14
  73.9 7.1 %collective-permute-done.14.refs_9_ = bf16[96,2432]{1,0:T(8,128)(2,1)} collective-permute-done((bf16[96,2432]{1,0:T(8,128)(2,1)S(1)}, bf16[96,2432]{1,0:T(8,128)(2,1)}, u32[]{:S(2)}, u32[]{:S(2)}) %collective-permute-start.14) | collective-permute-done | bytes 466976 | tf_op jit(solution)/shard_map/ppermute | solution.py:511
  81.0 2.9 collective-permute-done.15.refs_10_
  88.3 8.8 %collective-permute-done.17.refs_11_ = bf16[96,2432]{1,0:T(8,128)(2,1)} collective-permute-done((bf16[96,2432]{1,0:T(8,128)(2,1)}, bf16[96,2432]{1,0:T(8,128)(2,1)}, u32[]{:S(2)}, u32[]{:S(2)}) %collective-permute-start.17) | collective-permute-done | bytes 466976 | tf_op jit(solution)/shard_map/ppermute | solution.py:511
  97.1 3.1 collective-permute-done.18.refs_12_
  103.1 8.0 %collective-permute-done.19.refs_13_ = bf16[96,2432]{1,0:T(8,128)(2,1)S(1)} collective-permute-done((bf16[96,2432]{1,0:T(8,128)(2,1)}, bf16[96,2432]{1,0:T(8,128)(2,1)S(1)}, u32[]{:S(2)}, u32[]{:S(2)}) %collective-permute-start.19) | collective-permute-done | bytes 466976 | tf_op jit(solution)/shard_map/ppermute | solution.py:511
  111.9 7.3 %shard_map.204 = (bf16[1536,1536]{1,0:T(8,128)(2,1)}, bf16[1536,128]{1,0:T(8,128)(2,1)}, bf16[1536,768]{1,0:T(8,128)(2,1)}) custom-call(s32[15]{0:T(128)} %stack.204.starts, bf16[192,2432]{1,0:T(8,128)(2,1)} %copy-done.34, bf16[96,2432]{1,0:T(8,128)(2,1)} %copy-done.82, bf16[96,2432]{1,0:T(8,128)(2,1)} %copy-done.81, ...), custom_call_target="tpu_custom_call" | custom-call | bytes 14942208 | tf_op jit(solution)/shard_map/pallas_call | solution.py:346
  122.6 6.6 %fusion.127.proj = f32[512,1536]{1,0:T(8,128)} fusion(bf16[512,1536]{1,0:T(8,128)(2,1)S(1)} %fusion.2, bf16[1536,1536]{1,0:T(8,128)(2,1)} %get-tuple-element.231), kind=kOutput, calls=%fused_computation.399 | convolution fusion | flops 2415919104 | bytes 9437184 | tf_op jit(solution)/shard_map/dot_general | solution.py:19
  136.0 5.3 shard_map.205
  141.4 5.1 collective-permute-done.24.refs_3_
  151.4 3.0 collective-permute-done.32
  154.4 8.4 %collective-permute-done.34.refs_6_ = bf16[192,768]{1,0:T(8,128)(2,1)S(1)} collective-permute-done((bf16[192,768]{1,0:T(8,128)(2,1)S(1)}, bf16[192,768]{1,0:T(8,128)(2,1)S(1)}, u32[]{:S(2)}, u32[]{:S(2)}) %collective-permute-start.34) | collective-permute-done | bytes 294944 | tf_op jit(solution)/shard_map/ppermute | solution.py:519
  169.8 6.1 %collective-permute-start.35 = (bf16[96,1664]{1,0:T(8,128)(2,1)S(1)}, bf16[96,1664]{1,0:T(8,128)(2,1)S(1)}, u32[]{:S(2)}, u32[]{:S(2)}) collective-permute-start(bf16[96,1664]{1,0:T(8,128)(2,1)S(1)} %collective-permute-done.29.refs_5_), channel_id=1, source_target_pairs={{2,0},{0,4},{4,8},{8,12},{12,14},{14,10},{10,6},{6,2},{3,1},{1,5},... | collective-permute-start | bytes 958472 | tf_op jit(solution)/shard_map/ppermute | solution.py:511
  179.6 6.0 %collective-permute-done.35.refs_7_ = bf16[96,1664]{1,0:T(8,128)(2,1)S(1)} collective-permute-done((bf16[96,1664]{1,0:T(8,128)(2,1)S(1)}, bf16[96,1664]{1,0:T(8,128)(2,1)S(1)}, u32[]{:S(2)}, u32[]{:S(2)}) %collective-permute-start.35) | collective-permute-done | bytes 319520 | tf_op jit(solution)/shard_map/ppermute | solution.py:511
  190.1 4.6 collective-permute-done.39.refs_9_
  196.7 5.6 collective-permute-done.42.refs_11_
  209.3 3.7 shard_map.208
  213.1 2.7 collective-permute-done.46.refs_13_
  217.2 5.7 shard_map.206
  223.0 3.7 fusion.3
  229.6 7.2 %fusion.115.proj = f32[512,1536]{1,0:T(8,128)} fusion(bf16[1536,1536]{1,0:T(8,128)(2,1)} %get-tuple-element.267, bf16[512,1536]{1,0:T(8,128)(2,1)} %get-tuple-element.417, f32[1536]{0:T(1024)S(1)} %reduce.14, f32[512]{0:T(512)S(1)} %add_rsqrt_fusion.1), kind=kOutput, calls=%fused_computation.390 | convolution fusion | flops 2419064832 | bytes 9445376 | tf_op jit(solution)/shard_map/dot_general | solution.py:19
  240.0 5.3 shard_map.207
  251.6 2.6 collective-permute-done.53
  256.7 2.9 convolution_convert_fusion.3
  263.8 8.1 %collective-permute-done.54 = bf16[192,768]{1,0:T(8,128)(2,1)} collective-permute-done((bf16[192,768]{1,0:T(8,128)(2,1)}, bf16[192,768]{1,0:T(8,128)(2,1)}, u32[]{:S(2)}, u32[]{:S(2)}) %collective-permute-start.54) | collective-permute-done | bytes 294944 | tf_op jit(solution)/shard_map/ppermute | solution.py:483
  280.3 8.5 %collective-permute-done.58 = bf16[192,768]{1,0:T(8,128)(2,1)} collective-permute-done((bf16[192,768]{1,0:T(8,128)(2,1)}, bf16[192,768]{1,0:T(8,128)(2,1)}, u32[]{:S(2)}, u32[]{:S(2)}) %collective-permute-start.58) | collective-permute-done | bytes 294944 | tf_op jit(solution)/shard_map/ppermute | solution.py:519
  296.9 10.7 %shard_map.209 = (bf16[512,1536]{1,0:T(8,128)(2,1)S(1)}, f32[512,128]{1,0:T(8,128)S(1)}, f32[512,256]{1,0:T(8,128)S(1)}, f32[4,8,768]{2,1,0:T(8,128)S(1)}, f32[4,8,128]{2,1,0:T(8,128)S(1)}) custom-call(f32[512,1536]{1,0:T(8,128)S(1)} %copy-done.14, f32[512,128]{1,0:T(8,128)S(1)} %copy.307.last.last_ref, f32[512,256]{1,0:T(8,128)S(1)} %maximum_select_fusion.12.bc, ...), custom_call_target="tpu_custom_call" | custom-call | flops 8000000000 | bytes 12000000 | tf_op jit(solution)/shard_map/pallas_call | solution.py:257
  307.8 4.6 fusion.129
  313.5 3.9 collective-permute-start.64
  318.7 5.9 convolution_convert_fusion.1
  333.3 4.0 dynamic-slice_bitcast_fusion.4
  342.3 5.0 collective-permute-done.65
  349.7 7.0 %collective-permute-done.69 = bf16[96,1664]{1,0:T(8,128)(2,1)S(1)} collective-permute-done((bf16[96,1664]{1,0:T(8,128)(2,1)S(1)}, bf16[96,1664]{1,0:T(8,128)(2,1)S(1)}, u32[]{:S(2)}, u32[]{:S(2)}) %collective-permute-start.69) | collective-permute-done | bytes 319520 | tf_op jit(solution)/shard_map/ppermute | solution.py:570
  358.1 2.5 collective-permute-done.70
  366.7 4.0 fusion.7
  370.8 3.4 fusion.10
  381.2 2.6 fusion.131.d_normed
  385.8 9.1 %collective-permute-done.77 = bf16[192,768]{1,0:T(8,128)(2,1)S(1)} collective-permute-done((bf16[192,768]{1,0:T(8,128)(2,1)S(1)}, bf16[192,768]{1,0:T(8,128)(2,1)S(1)}, u32[]{:S(2)}, u32[]{:S(2)}) %collective-permute-start.77) | collective-permute-done | bytes 294944 | tf_op jit(solution)/shard_map/ppermute | solution.py:483
  401.4 10.6 %shard_map.211 = (bf16[512,1536]{1,0:T(8,128)(2,1)S(1)}, f32[512,128]{1,0:T(8,128)S(1)}, f32[512,256]{1,0:T(8,128)S(1)}, f32[4,8,768]{2,1,0:T(8,128)S(1)}, f32[4,8,128]{2,1,0:T(8,128)S(1)}) custom-call(f32[512,1536]{1,0:T(8,128)S(1)} %copy-done.12, f32[512,128]{1,0:T(8,128)S(1)} %copy.299.last.last_ref, f32[512,256]{1,0:T(8,128)S(1)} %maximum_select_fusion.11.bc, ...), custom_call_target="tpu_custom_call" | custom-call | flops 8000000000 | bytes 12000000 | tf_op jit(solution)/shard_map/pallas_call | solution.py:257
  413.3 4.6 fusion.132
  419.2 4.7 collective-permute-start.87
  427.6 4.3 convolution_convert_fusion
  438.9 2.7 collective-permute-start.91
  446.8 2.5 collective-permute-done.91
  449.3 5.8 collective-permute-done.89
  459.0 4.5 dynamic-slice_bitcast_fusion.1
  471.0 2.9 broadcast_select_fusion.7
  477.0 4.8 collective-permute-done.95
  489.5 4.8 collective-permute-done.97
  503.4 6.4 %collective-permute-done.101 = f32[22,768]{1,0:T(8,128)S(1)} collective-permute-done((f32[22,768]{1,0:T(8,128)S(1)}, f32[22,768]{1,0:T(8,128)S(1)}, u32[]{:S(2)}, u32[]{:S(2)}) %collective-permute-start.101) | collective-permute-done | bytes 67616 | tf_op jit(solution)/shard_map/ppermute | solution.py:483
  515.2 2.9 fusion.134
  518.1 4.1 collective-permute-done.107
  522.4 4.5 collective-permute-start.109
  547.2 3.6 collective-permute-done.113
  560.4 4.9 collective-permute-done.116
  567.9 13.8 %collective-permute-done.119 = bf16[192,1664]{1,0:T(8,128)(2,1)S(1)} collective-permute-done((bf16[192,1664]{1,0:T(8,128)(2,1)S(1)}, bf16[192,1664]{1,0:T(8,128)(2,1)S(1)}, u32[]{:S(2)}, u32[]{:S(2)}) %collective-permute-start.119) | collective-permute-done | bytes 639008 | tf_op jit(solution)/shard_map/ppermute | solution.py:480
  585.9 4.6 shard_map.213
  (841 shorter events, 252.0 us)
Async XLA Ops:
  20.3 12.5 %collective-permute-start.4 = (bf16[96,2432]{1,0:T(8,128)(2,1)}, bf16[96,2432]{1,0:T(8,128)(2,1)S(1)}, u32[]{:S(2)}, u32[]{:S(2)}) collective-permute-start(bf16[96,2432]{1,0:T(8,128)(2,1)} %get-tuple-element.472), channel_id=1, source_target_pairs={{0,2},{4,0},{8,4},{12,8},{14,12},{10,14},{6,10},{2,6},{1,3},{5,1},... | collective-permute-start | bytes 1400840 | tf_op jit(solution)/shard_map/ppermute | solution.py:511
  22.3 11.6 %collective-permute-start.3 = (bf16[96,2432]{1,0:T(8,128)(2,1)S(1)}, bf16[96,2432]{1,0:T(8,128)(2,1)S(1)}, u32[]{:S(2)}, u32[]{:S(2)}) collective-permute-start(bf16[96,2432]{1,0:T(8,128)(2,1)S(1)} %get-tuple-element.473), channel_id=1, source_target_pairs={{2,0},{0,4},{4,8},{8,12},{12,14},{14,10},{10,6},{6,2},{3,1},{1,5},... | collective-permute-start | bytes 1400840 | tf_op jit(solution)/shard_map/ppermute | solution.py:511
  24.3 18.5 %collective-permute-start.7 = (bf16[256,1536]{1,0:T(8,128)(2,1)S(1)}, bf16[256,1536]{1,0:T(8,128)(2,1)S(1)}, u32[]{:S(2)}, u32[]{:S(2)}) collective-permute-start(bf16[256,1536]{1,0:T(8,128)(2,1)S(1)} %copy-done.27), channel_id=1, source_target_pairs={{0,1},{1,0},{2,3},{3,2},{4,5},{5,4},{6,7},{7,6},{8,9},{9,8},{10,11... | collective-permute-start | bytes 2359304 | tf_op jit(solution)/shard_map/ppermute | solution.py:480
  33.9 10.8 %collective-permute-start.5 = (bf16[96,2432]{1,0:T(8,128)(2,1)S(1)}, bf16[96,2432]{1,0:T(8,128)(2,1)}, u32[]{:S(2)}, u32[]{:S(2)}) collective-permute-start(bf16[96,2432]{1,0:T(8,128)(2,1)S(1)} %collective-permute-done.3.refs_1_), channel_id=1, source_target_pairs={{2,0},{0,4},{4,8},{8,12},{12,14},{14,10},{10,6},{6,2},{3,1},{1,5},... | collective-permute-start | bytes 1400840 | tf_op jit(solution)/shard_map/ppermute | solution.py:511
  34.5 10.8 %collective-permute-start.6 = (bf16[96,2432]{1,0:T(8,128)(2,1)S(1)}, bf16[96,2432]{1,0:T(8,128)(2,1)}, u32[]{:S(2)}, u32[]{:S(2)}) collective-permute-start(bf16[96,2432]{1,0:T(8,128)(2,1)S(1)} %collective-permute-done.4.refs_2_), channel_id=1, source_target_pairs={{0,2},{4,0},{8,4},{12,8},{14,12},{10,14},{6,10},{2,6},{1,3},{5,1},... | collective-permute-start | bytes 1400840 | tf_op jit(solution)/shard_map/ppermute | solution.py:511
  48.1 24.0 %collective-permute-start.16 = (bf16[256,1536]{1,0:T(8,128)(2,1)S(1)}, bf16[256,1536]{1,0:T(8,128)(2,1)S(1)}, u32[]{:S(2)}, u32[]{:S(2)}) collective-permute-start(bf16[256,1536]{1,0:T(8,128)(2,1)S(1)} %copy-done.80), channel_id=1, source_target_pairs={{0,1},{1,0},{2,3},{3,2},{4,5},{5,4},{6,7},{7,6},{8,9},{9,8},{10,11... | collective-permute-start | bytes 2359304 | tf_op jit(solution)/shard_map/ppermute | solution.py:480
  59.1 10.5 %collective-permute-start.13 = (bf16[96,2432]{1,0:T(8,128)(2,1)S(1)}, bf16[96,2432]{1,0:T(8,128)(2,1)S(1)}, u32[]{:S(2)}, u32[]{:S(2)}) collective-permute-start(bf16[96,2432]{1,0:T(8,128)(2,1)S(1)} %collective-permute-done.9.refs_6_), channel_id=1, source_target_pairs={{0,2},{4,0},{8,4},{12,8},{14,12},{10,14},{6,10},{2,6},{1,3},{5,1},... | collective-permute-start | bytes 1400840 | tf_op jit(solution)/shard_map/ppermute | solution.py:511
  69.6 11.5 %collective-permute-start.14 = (bf16[96,2432]{1,0:T(8,128)(2,1)S(1)}, bf16[96,2432]{1,0:T(8,128)(2,1)}, u32[]{:S(2)}, u32[]{:S(2)}) collective-permute-start(bf16[96,2432]{1,0:T(8,128)(2,1)S(1)} %collective-permute-done.12.refs_7_), channel_id=1, source_target_pairs={{2,0},{0,4},{4,8},{8,12},{12,14},{14,10},{10,6},{6,2},{3,1},{1,5},... | collective-permute-start | bytes 1400840 | tf_op jit(solution)/shard_map/ppermute | solution.py:511
  72.1 11.8 %collective-permute-start.15 = (bf16[96,2432]{1,0:T(8,128)(2,1)S(1)}, bf16[96,2432]{1,0:T(8,128)(2,1)}, u32[]{:S(2)}, u32[]{:S(2)}) collective-permute-start(bf16[96,2432]{1,0:T(8,128)(2,1)S(1)} %collective-permute-done.13.refs_8_), channel_id=1, source_target_pairs={{0,2},{4,0},{8,4},{12,8},{14,12},{10,14},{6,10},{2,6},{1,3},{5,1},... | collective-permute-start | bytes 1400840 | tf_op jit(solution)/shard_map/ppermute | solution.py:511
  83.9 13.2 %collective-permute-start.17 = (bf16[96,2432]{1,0:T(8,128)(2,1)}, bf16[96,2432]{1,0:T(8,128)(2,1)}, u32[]{:S(2)}, u32[]{:S(2)}) collective-permute-start(bf16[96,2432]{1,0:T(8,128)(2,1)} %collective-permute-done.14.refs_9_), channel_id=1, source_target_pairs={{2,0},{0,4},{4,8},{8,12},{12,14},{14,10},{10,6},{6,2},{3,1},{1,5},... | collective-permute-start | bytes 1400840 | tf_op jit(solution)/shard_map/ppermute | solution.py:511
  85.6 14.6 %collective-permute-start.18 = (bf16[96,2432]{1,0:T(8,128)(2,1)}, bf16[96,2432]{1,0:T(8,128)(2,1)}, u32[]{:S(2)}, u32[]{:S(2)}) collective-permute-start(bf16[96,2432]{1,0:T(8,128)(2,1)} %collective-permute-done.15.refs_10_), channel_id=1, source_target_pairs={{0,2},{4,0},{8,4},{12,8},{14,12},{10,14},{6,10},{2,6},{1,3},{5,1},... | collective-permute-start | bytes 1400840 | tf_op jit(solution)/shard_map/ppermute | solution.py:511
  86.6 42.6 %collective-permute-start.23 = (bf16[192,768]{1,0:T(8,128)(2,1)S(1)}, bf16[192,768]{1,0:T(8,128)(2,1)}, u32[]{:S(2)}, u32[]{:S(2)}) collective-permute-start(bf16[192,768]{1,0:T(8,128)(2,1)S(1)} %slice.538.refs_0_), channel_id=1, source_target_pairs={{0,4},{2,6},{4,8},{6,10},{8,12},{10,14},{12,0},{14,2},{1,5},{3,7},... | collective-permute-start | bytes 884744 | tf_op jit(solution)/shard_map/ppermute | solution.py:519
  88.3 40.9 %collective-permute-start.22 = (bf16[192,768]{1,0:T(8,128)(2,1)S(1)}, bf16[192,768]{1,0:T(8,128)(2,1)}, u32[]{:S(2)}, u32[]{:S(2)}) collective-permute-start(bf16[192,768]{1,0:T(8,128)(2,1)S(1)} %slice.538.refs_0_), channel_id=1, source_target_pairs={{0,2},{2,0},{4,6},{6,4},{8,10},{10,8},{12,14},{14,12},{1,3},{3,1},... | collective-permute-start | bytes 884744 | tf_op jit(solution)/shard_map/ppermute | solution.py:483
  100.2 11.0 %collective-permute-start.19 = (bf16[96,2432]{1,0:T(8,128)(2,1)}, bf16[96,2432]{1,0:T(8,128)(2,1)S(1)}, u32[]{:S(2)}, u32[]{:S(2)}) collective-permute-start(bf16[96,2432]{1,0:T(8,128)(2,1)} %collective-permute-done.17.refs_11_), channel_id=1, source_target_pairs={{2,0},{0,4},{4,8},{8,12},{12,14},{14,10},{10,6},{6,2},{3,1},{1,5},... | collective-permute-start | bytes 1400840 | tf_op jit(solution)/shard_map/ppermute | solution.py:511
  100.7 10.7 %collective-permute-start.20 = (bf16[96,2432]{1,0:T(8,128)(2,1)}, bf16[96,2432]{1,0:T(8,128)(2,1)}, u32[]{:S(2)}, u32[]{:S(2)}) collective-permute-start(bf16[96,2432]{1,0:T(8,128)(2,1)} %collective-permute-done.18.refs_12_), channel_id=1, source_target_pairs={{0,2},{4,0},{8,4},{12,8},{14,12},{10,14},{6,10},{2,6},{1,3},{5,1},... | collective-permute-start | bytes 1400840 | tf_op jit(solution)/shard_map/ppermute | solution.py:511
  103.1 26.1 %collective-permute-start.11 = (bf16[96,1664]{1,0:T(8,128)(2,1)}, bf16[96,1664]{1,0:T(8,128)(2,1)}, u32[]{:S(2)}, u32[]{:S(2)}) collective-permute-start(bf16[96,1664]{1,0:T(8,128)(2,1)} %get-tuple-element.474), channel_id=1, source_target_pairs={{0,2},{4,0},{8,4},{12,8},{14,12},{10,14},{6,10},{2,6},{1,3},{5,1},... | collective-permute-start | bytes 958472 | tf_op jit(solution)/shard_map/ppermute | solution.py:511
  111.1 18.1 %collective-permute-start.10 = (bf16[96,1664]{1,0:T(8,128)(2,1)}, bf16[96,1664]{1,0:T(8,128)(2,1)}, u32[]{:S(2)}, u32[]{:S(2)}) collective-permute-start(bf16[96,1664]{1,0:T(8,128)(2,1)} %get-tuple-element.475), channel_id=1, source_target_pairs={{2,0},{0,4},{4,8},{8,12},{12,14},{14,10},{10,6},{6,2},{3,1},{1,5},... | collective-permute-start | bytes 958472 | tf_op jit(solution)/shard_map/ppermute | solution.py:511
  130.1 11.2 %collective-permute-start.28 = (bf16[192,768]{1,0:T(8,128)(2,1)S(1)}, bf16[192,768]{1,0:T(8,128)(2,1)S(1)}, u32[]{:S(2)}, u32[]{:S(2)}) collective-permute-start(bf16[192,768]{1,0:T(8,128)(2,1)S(1)} %copy-done.55), channel_id=1, source_target_pairs={{0,12},{2,14},{4,0},{6,2},{8,4},{10,6},{12,8},{14,10},{1,13},{3,15... | collective-permute-start | bytes 884744 | tf_op jit(solution)/shard_map/ppermute | solution.py:519
  130.6 10.7 %collective-permute-start.27 = (bf16[192,768]{1,0:T(8,128)(2,1)}, bf16[192,768]{1,0:T(8,128)(2,1)S(1)}, u32[]{:S(2)}, u32[]{:S(2)}) collective-permute-start(bf16[192,768]{1,0:T(8,128)(2,1)} %collective-permute-done.23.refs_2_), channel_id=1, source_target_pairs={{0,2},{2,0},{4,6},{6,4},{8,10},{10,8},{12,14},{14,12},{1,3},{3,1},... | collective-permute-start | bytes 884744 | tf_op jit(solution)/shard_map/ppermute | solution.py:483
  131.6 14.9 %collective-permute-start.24 = (bf16[96,1664]{1,0:T(8,128)(2,1)}, bf16[96,1664]{1,0:T(8,128)(2,1)S(1)}, u32[]{:S(2)}, u32[]{:S(2)}) collective-permute-start(bf16[96,1664]{1,0:T(8,128)(2,1)} %collective-permute-done.10.refs_1_), channel_id=1, source_target_pairs={{2,0},{0,4},{4,8},{8,12},{12,14},{14,10},{10,6},{6,2},{3,1},{1,5},... | collective-permute-start | bytes 958472 | tf_op jit(solution)/shard_map/ppermute | solution.py:511
  133.6 12.9 %collective-permute-start.25 = (bf16[96,1664]{1,0:T(8,128)(2,1)}, bf16[96,1664]{1,0:T(8,128)(2,1)S(1)}, u32[]{:S(2)}, u32[]{:S(2)}) collective-permute-start(bf16[96,1664]{1,0:T(8,128)(2,1)} %collective-permute-done.11.refs_2_), channel_id=1, source_target_pairs={{0,2},{4,0},{8,4},{12,8},{14,12},{10,14},{6,10},{2,6},{1,3},{5,1},... | collective-permute-start | bytes 958472 | tf_op jit(solution)/shard_map/ppermute | solution.py:511
  146.7 16.1 %collective-permute-start.34 = (bf16[192,768]{1,0:T(8,128)(2,1)S(1)}, bf16[192,768]{1,0:T(8,128)(2,1)S(1)}, u32[]{:S(2)}, u32[]{:S(2)}) collective-permute-start(bf16[192,768]{1,0:T(8,128)(2,1)S(1)} %copy-done.55), channel_id=1, source_target_pairs={{0,8},{2,10},{4,12},{6,14},{8,0},{10,2},{12,4},{14,6},{1,9},{3,11}... | collective-permute-start | bytes 884744 | tf_op jit(solution)/shard_map/ppermute | solution.py:519
  147.6 15.3 %collective-permute-start.33 = (bf16[192,768]{1,0:T(8,128)(2,1)S(1)}, bf16[192,768]{1,0:T(8,128)(2,1)S(1)}, u32[]{:S(2)}, u32[]{:S(2)}) collective-permute-start(bf16[192,768]{1,0:T(8,128)(2,1)S(1)} %collective-permute-done.28.refs_4_), channel_id=1, source_target_pairs={{0,2},{2,0},{4,6},{6,4},{8,10},{10,8},{12,14},{14,12},{1,3},{3,1},... | collective-permute-start | bytes 884744 | tf_op jit(solution)/shard_map/ppermute | solution.py:483
  148.8 14.7 %collective-permute-start.29 = (bf16[96,1664]{1,0:T(8,128)(2,1)S(1)}, bf16[96,1664]{1,0:T(8,128)(2,1)S(1)}, u32[]{:S(2)}, u32[]{:S(2)}) collective-permute-start(bf16[96,1664]{1,0:T(8,128)(2,1)S(1)} %collective-permute-done.24.refs_3_), channel_id=1, source_target_pairs={{2,0},{0,4},{4,8},{8,12},{12,14},{14,10},{10,6},{6,2},{3,1},{1,5},... | collective-permute-start | bytes 958472 | tf_op jit(solution)/shard_map/ppermute | solution.py:511
  150.2 15.3 %collective-permute-start.30 = (bf16[96,1664]{1,0:T(8,128)(2,1)S(1)}, bf16[96,1664]{1,0:T(8,128)(2,1)S(1)}, u32[]{:S(2)}, u32[]{:S(2)}) collective-permute-start(bf16[96,1664]{1,0:T(8,128)(2,1)S(1)} %collective-permute-done.25.refs_4_), channel_id=1, source_target_pairs={{0,2},{4,0},{8,4},{12,8},{14,12},{10,14},{6,10},{2,6},{1,3},{5,1},... | collective-permute-start | bytes 958472 | tf_op jit(solution)/shard_map/ppermute | solution.py:511
  169.2 19.0 %collective-permute-start.41 = (bf16[768,768]{1,0:T(8,128)(2,1)S(1)}, bf16[768,768]{1,0:T(8,128)(2,1)S(1)}, u32[]{:S(2)}, u32[]{:S(2)}) collective-permute-start(bf16[768,768]{1,0:T(8,128)(2,1)S(1)} %get-tuple-element.463), channel_id=1, source_target_pairs={{0,16},{16,0},{1,17},{17,1},{2,18},{18,2},{3,19},{19,3},{4,20},{20... | collective-permute-start | bytes 3538952 | tf_op jit(solution)/shard_map/ppermute | solution.py:477
  169.8 15.8 %collective-permute-start.35 = (bf16[96,1664]{1,0:T(8,128)(2,1)S(1)}, bf16[96,1664]{1,0:T(8,128)(2,1)S(1)}, u32[]{:S(2)}, u32[]{:S(2)}) collective-permute-start(bf16[96,1664]{1,0:T(8,128)(2,1)S(1)} %collective-permute-done.29.refs_5_), channel_id=1, source_target_pairs={{2,0},{0,4},{4,8},{8,12},{12,14},{14,10},{10,6},{6,2},{3,1},{1,5},... | collective-permute-start | bytes 958472 | tf_op jit(solution)/shard_map/ppermute | solution.py:511
  185.6 18.7 %collective-permute-start.44 = (bf16[512,768]{1,0:T(8,128)(2,1)S(1)}, bf16[512,768]{1,0:T(8,128)(2,1)S(1)}, u32[]{:S(2)}, u32[]{:S(2)}) collective-permute-start(bf16[512,768]{1,0:T(8,128)(2,1)S(1)} %convolution_convert_fusion.6), channel_id=1, source_target_pairs={{0,1},{1,0},{2,3},{3,2},{4,5},{5,4},{6,7},{7,6},{8,9},{9,8},{10,11... | collective-permute-start | bytes 2359304 | tf_op jit(solution)/shard_map/ppermute | solution.py:480
  205.6 17.4 %collective-permute-start.45 = (bf16[512,768]{1,0:T(8,128)(2,1)}, bf16[512,768]{1,0:T(8,128)(2,1)}, u32[]{:S(2)}, u32[]{:S(2)}) collective-permute-start(bf16[512,768]{1,0:T(8,128)(2,1)} %add_convert_fusion.1), channel_id=1, source_target_pairs={{0,16},{16,0},{1,17},{17,1},{2,18},{18,2},{3,19},{19,3},{4,20},{20... | collective-permute-start | bytes 2359304 | tf_op jit(solution)/shard_map/ppermute | solution.py:477
  262.7 17.6 %collective-permute-start.57 = (bf16[192,768]{1,0:T(8,128)(2,1)}, bf16[192,768]{1,0:T(8,128)(2,1)}, u32[]{:S(2)}, u32[]{:S(2)}) collective-permute-start(bf16[192,768]{1,0:T(8,128)(2,1)} %get-tuple-element.458), channel_id=1, source_target_pairs={{0,2},{2,0},{4,6},{6,4},{8,10},{10,8},{12,14},{14,12},{1,3},{3,1},... | collective-permute-start | bytes 884744 | tf_op jit(solution)/shard_map/ppermute | solution.py:483
  273.8 15.0 %collective-permute-start.58 = (bf16[192,768]{1,0:T(8,128)(2,1)}, bf16[192,768]{1,0:T(8,128)(2,1)}, u32[]{:S(2)}, u32[]{:S(2)}) collective-permute-start(bf16[192,768]{1,0:T(8,128)(2,1)} %fusion.42), channel_id=1, source_target_pairs={{0,8},{2,10},{4,12},{6,14},{8,0},{10,2},{12,4},{14,6},{1,9},{3,11}... | collective-permute-start | bytes 884744 | tf_op jit(solution)/shard_map/ppermute | solution.py:519
  278.3 47.9 %collective-permute-start.63 = (bf16[192,768]{1,0:T(8,128)(2,1)}, bf16[192,768]{1,0:T(8,128)(2,1)}, u32[]{:S(2)}, u32[]{:S(2)}) collective-permute-start(bf16[192,768]{1,0:T(8,128)(2,1)} %get-tuple-element.456), channel_id=1, source_target_pairs={{0,2},{2,0},{4,6},{6,4},{8,10},{10,8},{12,14},{14,12},{1,3},{3,1},... | collective-permute-start | bytes 884744 | tf_op jit(solution)/shard_map/ppermute | solution.py:483
  279.0 28.6 %collective-permute-start.59 = (bf16[192,768]{1,0:T(8,128)(2,1)}, bf16[192,768]{1,0:T(8,128)(2,1)}, u32[]{:S(2)}, u32[]{:S(2)}) collective-permute-start(bf16[192,768]{1,0:T(8,128)(2,1)} %get-tuple-element.457), channel_id=1, source_target_pairs={{0,2},{2,0},{4,6},{6,4},{8,10},{10,8},{12,14},{14,12},{1,3},{3,1},... | collective-permute-start | bytes 884744 | tf_op jit(solution)/shard_map/ppermute | solution.py:483
  291.7 15.9 %collective-permute-start.60 = (bf16[192,768]{1,0:T(8,128)(2,1)S(1)}, bf16[192,768]{1,0:T(8,128)(2,1)S(1)}, u32[]{:S(2)}, u32[]{:S(2)}) collective-permute-start(bf16[192,768]{1,0:T(8,128)(2,1)S(1)} %fusion.41), channel_id=1, source_target_pairs={{0,4},{2,6},{4,8},{6,10},{8,12},{10,14},{12,0},{14,2},{1,5},{3,7},... | collective-permute-start | bytes 884744 | tf_op jit(solution)/shard_map/ppermute | solution.py:519
  313.5 12.7 %collective-permute-start.64 = (bf16[192,768]{1,0:T(8,128)(2,1)S(1)}, bf16[192,768]{1,0:T(8,128)(2,1)S(1)}, u32[]{:S(2)}, u32[]{:S(2)}) collective-permute-start(bf16[192,768]{1,0:T(8,128)(2,1)S(1)} %fusion.40), channel_id=1, source_target_pairs={{0,12},{2,14},{4,0},{6,2},{8,4},{10,6},{12,8},{14,10},{1,13},{3,15... | collective-permute-start | bytes 884744 | tf_op jit(solution)/shard_map/ppermute | solution.py:519
  341.1 19.4 %collective-permute-start.70 = (bf16[512,768]{1,0:T(8,128)(2,1)S(1)}, bf16[512,768]{1,0:T(8,128)(2,1)S(1)}, u32[]{:S(2)}, u32[]{:S(2)}) collective-permute-start(bf16[512,768]{1,0:T(8,128)(2,1)S(1)} %add_convert_fusion), channel_id=1, source_target_pairs={{0,1},{1,0},{2,3},{3,2},{4,5},{5,4},{6,7},{7,6},{8,9},{9,8},{10,11... | collective-permute-start | bytes 2359304 | tf_op jit(solution)/shard_map/ppermute | solution.py:480
  363.2 12.5 %collective-permute-start.72 = (bf16[96,1664]{1,0:T(8,128)(2,1)S(1)}, bf16[96,1664]{1,0:T(8,128)(2,1)S(1)}, u32[]{:S(2)}, u32[]{:S(2)}) collective-permute-start(bf16[96,1664]{1,0:T(8,128)(2,1)S(1)} %add_convert_fusion.27), channel_id=1, source_target_pairs={{0,2},{4,0},{8,4},{12,8},{14,12},{10,14},{6,10},{2,6},{1,3},{5,1},... | collective-permute-start | bytes 958472 | tf_op jit(solution)/shard_map/ppermute | solution.py:570
  377.1 17.8 %collective-permute-start.75 = (bf16[96,1664]{1,0:T(8,128)(2,1)S(1)}, bf16[96,1664]{1,0:T(8,128)(2,1)S(1)}, u32[]{:S(2)}, u32[]{:S(2)}) collective-permute-start(bf16[96,1664]{1,0:T(8,128)(2,1)S(1)} %add_convert_fusion.25), channel_id=1, source_target_pairs={{0,2},{4,0},{8,4},{12,8},{14,12},{10,14},{6,10},{2,6},{1,3},{5,1},... | collective-permute-start | bytes 958472 | tf_op jit(solution)/shard_map/ppermute | solution.py:570
  378.1 16.8 %collective-permute-start.74 = (bf16[96,1664]{1,0:T(8,128)(2,1)S(1)}, bf16[96,1664]{1,0:T(8,128)(2,1)S(1)}, u32[]{:S(2)}, u32[]{:S(2)}) collective-permute-start(bf16[96,1664]{1,0:T(8,128)(2,1)S(1)} %add_convert_fusion.26), channel_id=1, source_target_pairs={{2,0},{0,4},{4,8},{8,12},{12,14},{14,10},{10,6},{6,2},{3,1},{1,5},... | collective-permute-start | bytes 958472 | tf_op jit(solution)/shard_map/ppermute | solution.py:570
  380.3 14.7 %collective-permute-start.77 = (bf16[192,768]{1,0:T(8,128)(2,1)S(1)}, bf16[192,768]{1,0:T(8,128)(2,1)S(1)}, u32[]{:S(2)}, u32[]{:S(2)}) collective-permute-start(bf16[192,768]{1,0:T(8,128)(2,1)S(1)} %get-tuple-element.455), channel_id=1, source_target_pairs={{0,2},{2,0},{4,6},{6,4},{8,10},{10,8},{12,14},{14,12},{1,3},{3,1},... | collective-permute-start | bytes 884744 | tf_op jit(solution)/shard_map/ppermute | solution.py:483
  383.7 51.9 %collective-permute-start.86 = (bf16[192,768]{1,0:T(8,128)(2,1)}, bf16[192,768]{1,0:T(8,128)(2,1)}, u32[]{:S(2)}, u32[]{:S(2)}) collective-permute-start(bf16[192,768]{1,0:T(8,128)(2,1)} %get-tuple-element.453), channel_id=1, source_target_pairs={{0,2},{2,0},{4,6},{6,4},{8,10},{10,8},{12,14},{14,12},{1,3},{3,1},... | collective-permute-start | bytes 884744 | tf_op jit(solution)/shard_map/ppermute | solution.py:483
  384.9 27.1 %collective-permute-start.80 = (bf16[192,768]{1,0:T(8,128)(2,1)}, bf16[192,768]{1,0:T(8,128)(2,1)}, u32[]{:S(2)}, u32[]{:S(2)}) collective-permute-start(bf16[192,768]{1,0:T(8,128)(2,1)} %get-tuple-element.454), channel_id=1, source_target_pairs={{0,2},{2,0},{4,6},{6,4},{8,10},{10,8},{12,14},{14,12},{1,3},{3,1},... | collective-permute-start | bytes 884744 | tf_op jit(solution)/shard_map/ppermute | solution.py:483
  397.1 14.9 %collective-permute-start.81 = (bf16[192,768]{1,0:T(8,128)(2,1)S(1)}, bf16[192,768]{1,0:T(8,128)(2,1)S(1)}, u32[]{:S(2)}, u32[]{:S(2)}) collective-permute-start(bf16[192,768]{1,0:T(8,128)(2,1)S(1)} %fusion.39), channel_id=1, source_target_pairs={{0,8},{2,10},{4,12},{6,14},{8,0},{10,2},{12,4},{14,6},{1,9},{3,11}... | collective-permute-start | bytes 884744 | tf_op jit(solution)/shard_map/ppermute | solution.py:519
  397.3 14.7 %collective-permute-start.79 = (bf16[96,1664]{1,0:T(8,128)(2,1)S(1)}, bf16[96,1664]{1,0:T(8,128)(2,1)S(1)}, u32[]{:S(2)}, u32[]{:S(2)}) collective-permute-start(bf16[96,1664]{1,0:T(8,128)(2,1)S(1)} %add_convert_fusion.23), channel_id=1, source_target_pairs={{0,2},{4,0},{8,4},{12,8},{14,12},{10,14},{6,10},{2,6},{1,3},{5,1},... | collective-permute-start | bytes 958472 | tf_op jit(solution)/shard_map/ppermute | solution.py:570
  397.5 15.8 %collective-permute-start.78 = (bf16[96,1664]{1,0:T(8,128)(2,1)S(1)}, bf16[96,1664]{1,0:T(8,128)(2,1)S(1)}, u32[]{:S(2)}, u32[]{:S(2)}) collective-permute-start(bf16[96,1664]{1,0:T(8,128)(2,1)S(1)} %add_convert_fusion.24), channel_id=1, source_target_pairs={{2,0},{0,4},{4,8},{8,12},{12,14},{14,10},{10,6},{6,2},{3,1},{1,5},... | collective-permute-start | bytes 958472 | tf_op jit(solution)/shard_map/ppermute | solution.py:570
  419.2 16.5 %collective-permute-start.87 = (bf16[192,768]{1,0:T(8,128)(2,1)S(1)}, bf16[192,768]{1,0:T(8,128)(2,1)S(1)}, u32[]{:S(2)}, u32[]{:S(2)}) collective-permute-start(bf16[192,768]{1,0:T(8,128)(2,1)S(1)} %fusion.38), channel_id=1, source_target_pairs={{0,4},{2,6},{4,8},{6,10},{8,12},{10,14},{12,0},{14,2},{1,5},{3,7},... | collective-permute-start | bytes 884744 | tf_op jit(solution)/shard_map/ppermute | solution.py:519
  424.0 13.2 %collective-permute-start.83 = (bf16[96,1664]{1,0:T(8,128)(2,1)S(1)}, bf16[96,1664]{1,0:T(8,128)(2,1)S(1)}, u32[]{:S(2)}, u32[]{:S(2)}) collective-permute-start(bf16[96,1664]{1,0:T(8,128)(2,1)S(1)} %add_convert_fusion.21), channel_id=1, source_target_pairs={{0,2},{4,0},{8,4},{12,8},{14,12},{10,14},{6,10},{2,6},{1,3},{5,1},... | collective-permute-start | bytes 958472 | tf_op jit(solution)/shard_map/ppermute | solution.py:570
  425.3 12.3 %collective-permute-start.82 = (bf16[96,1664]{1,0:T(8,128)(2,1)S(1)}, bf16[96,1664]{1,0:T(8,128)(2,1)S(1)}, u32[]{:S(2)}, u32[]{:S(2)}) collective-permute-start(bf16[96,1664]{1,0:T(8,128)(2,1)S(1)} %add_convert_fusion.22), channel_id=1, source_target_pairs={{2,0},{0,4},{4,8},{8,12},{12,14},{14,10},{10,6},{6,2},{3,1},{1,5},... | collective-permute-start | bytes 958472 | tf_op jit(solution)/shard_map/ppermute | solution.py:570
  434.3 12.5 %collective-permute-start.90 = (bf16[192,768]{1,0:T(8,128)(2,1)S(1)}, bf16[192,768]{1,0:T(8,128)(2,1)S(1)}, u32[]{:S(2)}, u32[]{:S(2)}) collective-permute-start(bf16[192,768]{1,0:T(8,128)(2,1)S(1)} %copy-done.120), channel_id=1, source_target_pairs={{0,2},{2,0},{4,6},{6,4},{8,10},{10,8},{12,14},{14,12},{1,3},{3,1},... | collective-permute-start | bytes 884744 | tf_op jit(solution)/shard_map/ppermute | solution.py:483
  441.7 13.4 %collective-permute-start.89 = (bf16[96,1664]{1,0:T(8,128)(2,1)S(1)}, bf16[96,1664]{1,0:T(8,128)(2,1)S(1)}, u32[]{:S(2)}, u32[]{:S(2)}) collective-permute-start(bf16[96,1664]{1,0:T(8,128)(2,1)S(1)} %add_convert_fusion.19), channel_id=1, source_target_pairs={{0,2},{4,0},{8,4},{12,8},{14,12},{10,14},{6,10},{2,6},{1,3},{5,1},... | collective-permute-start | bytes 958472 | tf_op jit(solution)/shard_map/ppermute | solution.py:570
  442.3 12.8 %collective-permute-start.88 = (bf16[96,1664]{1,0:T(8,128)(2,1)S(1)}, bf16[96,1664]{1,0:T(8,128)(2,1)S(1)}, u32[]{:S(2)}, u32[]{:S(2)}) collective-permute-start(bf16[96,1664]{1,0:T(8,128)(2,1)S(1)} %add_convert_fusion.20), channel_id=1, source_target_pairs={{2,0},{0,4},{4,8},{8,12},{12,14},{14,10},{10,6},{6,2},{3,1},{1,5},... | collective-permute-start | bytes 958472 | tf_op jit(solution)/shard_map/ppermute | solution.py:570
  456.0 11.0 %collective-permute-start.94 = (f32[512,768]{1,0:T(8,128)S(1)}, f32[512,768]{1,0:T(8,128)}, u32[]{:S(2)}, u32[]{:S(2)}) collective-permute-start(f32[512,768]{1,0:T(8,128)S(1)} %constant_dynamic-slice_fusion.10), channel_id=1, source_target_pairs={{0,16},{16,0},{1,17},{17,1},{2,18},{18,2},{3,19},{19,3},{4,20},{20... | collective-permute-start | bytes 4718600 | tf_op jit(solution)/shard_map/ppermute | solution.py:477
  464.2 11.8 %collective-permute-start.92 = (bf16[96,1664]{1,0:T(8,128)(2,1)}, bf16[96,1664]{1,0:T(8,128)(2,1)}, u32[]{:S(2)}, u32[]{:S(2)}) collective-permute-start(bf16[96,1664]{1,0:T(8,128)(2,1)} %pad_maximum_fusion.4), channel_id=1, source_target_pairs={{2,0},{0,4},{4,8},{8,12},{12,14},{14,10},{10,6},{6,2},{3,1},{1,5},... | collective-permute-start | bytes 958472 | tf_op jit(solution)/shard_map/ppermute | solution.py:570
  469.5 12.3 %collective-permute-start.95 = (bf16[256,768]{1,0:T(8,128)(2,1)}, bf16[256,768]{1,0:T(8,128)(2,1)}, u32[]{:S(2)}, u32[]{:S(2)}) collective-permute-start(bf16[256,768]{1,0:T(8,128)(2,1)} %dynamic-slice_convert_fusion.1), channel_id=1, source_target_pairs={{0,1},{1,0},{2,3},{3,2},{4,5},{5,4},{6,7},{7,6},{8,9},{9,8},{10,11... | collective-permute-start | bytes 1179656 | tf_op jit(solution)/shard_map/ppermute | solution.py:480
  473.9 35.8 %collective-permute-start.103 = (bf16[192,768]{1,0:T(8,128)(2,1)S(1)}, bf16[192,768]{1,0:T(8,128)(2,1)}, u32[]{:S(2)}, u32[]{:S(2)}) collective-permute-start(bf16[192,768]{1,0:T(8,128)(2,1)S(1)} %get-tuple-element.412), channel_id=1, source_target_pairs={{0,1},{1,0},{2,3},{3,2},{4,5},{5,4},{6,7},{7,6},{8,9},{9,8},{10,11... | collective-permute-start | bytes 884744 | tf_op jit(solution)/shard_map/ppermute | solution.py:480
  474.5 35.2 %collective-permute-start.102 = (bf16[192,768]{1,0:T(8,128)(2,1)S(1)}, bf16[192,768]{1,0:T(8,128)(2,1)}, u32[]{:S(2)}, u32[]{:S(2)}) collective-permute-start(bf16[192,768]{1,0:T(8,128)(2,1)S(1)} %get-tuple-element.413), channel_id=1, source_target_pairs={{0,1},{1,0},{2,3},{3,2},{4,5},{5,4},{6,7},{7,6},{8,9},{9,8},{10,11... | collective-permute-start | bytes 884744 | tf_op jit(solution)/shard_map/ppermute | solution.py:480
  496.8 13.0 %collective-permute-start.100 = (bf16[96,1664]{1,0:T(8,128)(2,1)}, bf16[96,1664]{1,0:T(8,128)(2,1)S(1)}, u32[]{:S(2)}, u32[]{:S(2)}) collective-permute-start(bf16[96,1664]{1,0:T(8,128)(2,1)} %add_convert_fusion.15), channel_id=1, source_target_pairs={{0,2},{4,0},{8,4},{12,8},{14,12},{10,14},{6,10},{2,6},{1,3},{5,1},... | collective-permute-start | bytes 958472 | tf_op jit(solution)/shard_map/ppermute | solution.py:570
  510.0 12.3 %collective-permute-start.105 = (bf16[96,1664]{1,0:T(8,128)(2,1)S(1)}, bf16[96,1664]{1,0:T(8,128)(2,1)S(1)}, u32[]{:S(2)}, u32[]{:S(2)}) collective-permute-start(bf16[96,1664]{1,0:T(8,128)(2,1)S(1)} %add_convert_fusion.13), channel_id=1, source_target_pairs={{0,2},{4,0},{8,4},{12,8},{14,12},{10,14},{6,10},{2,6},{1,3},{5,1},... | collective-permute-start | bytes 958472 | tf_op jit(solution)/shard_map/ppermute | solution.py:570
  529.8 16.5 %collective-permute-start.114 = (bf16[192,1664]{1,0:T(8,128)(2,1)}, bf16[192,1664]{1,0:T(8,128)(2,1)}, u32[]{:S(2)}, u32[]{:S(2)}) collective-permute-start(bf16[192,1664]{1,0:T(8,128)(2,1)} %pad_maximum_fusion), channel_id=1, source_target_pairs={{0,1},{1,0},{2,3},{3,2},{4,5},{5,4},{6,7},{7,6},{8,9},{9,8},{10,11... | collective-permute-start | bytes 1916936 | tf_op jit(solution)/shard_map/ppermute | solution.py:480
  535.7 10.6 %collective-permute-start.112 = (bf16[96,1664]{1,0:T(8,128)(2,1)}, bf16[96,1664]{1,0:T(8,128)(2,1)}, u32[]{:S(2)}, u32[]{:S(2)}) collective-permute-start(bf16[96,1664]{1,0:T(8,128)(2,1)} %add_convert_fusion.9), channel_id=1, source_target_pairs={{0,2},{4,0},{8,4},{12,8},{14,12},{10,14},{6,10},{2,6},{1,3},{5,1},... | collective-permute-start | bytes 958472 | tf_op jit(solution)/shard_map/ppermute | solution.py:570
  539.5 11.3 %collective-permute-start.113 = (bf16[256,768]{1,0:T(8,128)(2,1)}, bf16[256,768]{1,0:T(8,128)(2,1)}, u32[]{:S(2)}, u32[]{:S(2)}) collective-permute-start(bf16[256,768]{1,0:T(8,128)(2,1)} %dynamic-slice_convert_fusion), channel_id=1, source_target_pairs={{0,1},{1,0},{2,3},{3,2},{4,5},{5,4},{6,7},{7,6},{8,9},{9,8},{10,11... | collective-permute-start | bytes 1179656 | tf_op jit(solution)/shard_map/ppermute | solution.py:480
  565.7 16.0 %collective-permute-start.119 = (bf16[192,1664]{1,0:T(8,128)(2,1)S(1)}, bf16[192,1664]{1,0:T(8,128)(2,1)S(1)}, u32[]{:S(2)}, u32[]{:S(2)}) collective-permute-start(bf16[192,1664]{1,0:T(8,128)(2,1)S(1)} %get-tuple-element.476), channel_id=1, source_target_pairs={{0,1},{1,0},{2,3},{3,2},{4,5},{5,4},{6,7},{7,6},{8,9},{9,8},{10,11... | collective-permute-start | bytes 1916936 | tf_op jit(solution)/shard_map/ppermute | solution.py:480
  567.3 18.5 %collective-permute-start.122 = (bf16[192,768]{1,0:T(8,128)(2,1)S(1)}, bf16[192,768]{1,0:T(8,128)(2,1)S(1)}, u32[]{:S(2)}, u32[]{:S(2)}) collective-permute-start(bf16[192,768]{1,0:T(8,128)(2,1)S(1)} %copy-done.108), channel_id=1, source_target_pairs={{0,16},{16,0},{1,17},{17,1},{2,18},{18,2},{3,19},{19,3},{4,20},{20... | collective-permute-start | bytes 884744 | tf_op jit(solution)/shard_map/ppermute | solution.py:477
  567.3 18.6 %collective-permute-start.120 = (bf16[192,1664]{1,0:T(8,128)(2,1)S(1)}, bf16[192,1664]{1,0:T(8,128)(2,1)S(1)}, u32[]{:S(2)}, u32[]{:S(2)}) collective-permute-start(bf16[192,1664]{1,0:T(8,128)(2,1)S(1)} %get-tuple-element.470), channel_id=1, source_target_pairs={{0,16},{16,0},{1,17},{17,1},{2,18},{18,2},{3,19},{19,3},{4,20},{20... | collective-permute-start | bytes 1916936 | tf_op jit(solution)/shard_map/ppermute | solution.py:477
  (218 other events, 1933.4 us)

commit v3 on v2

--- a/solution.py
+++ b/solution.py
@@ -13,6 +13,7 @@
 HALF = 64
 VMEM_LIMIT = 40 * 1024 * 1024
 VMEM_ALL = 60 * 1024 * 1024
+VMEM_ADD = 16 * 1024 * 1024
 
 
 def dot(a, b, dims=((1,), (0,)), precision=None):
@@ -118,7 +119,7 @@
 
 
 def back_kernel(
-    heads, taps, proj, last_ref, bc, aux, seg_row, packed, outs, d_normed, inverse_ref, shrink_ref, *results
+    heads, taps, proj, last_ref, bc, aux, seg_row, packed, outs, d_normed, scale, *results
 ):
     d_main_ref, d_dt_ref, d_state_ref, d_wide_ref, d_narrow_ref = results
     rows = proj.shape[0]
@@ -138,7 +139,7 @@
     first, second = pair_masks(rows)
     lane = lax.broadcasted_iota(jnp.int32, (rows, LANES), 1)
     sub = lax.broadcasted_iota(jnp.int32, (LANES, rows), 0)
-    inverse, shrink = inverse_ref[...], shrink_ref[...]
+    inverse, shrink = scale[:, 0:1], scale[:, 1:2]
     d_inter = jnp.zeros((rows, rows), F32)
     row_sums = jnp.zeros((rows, LANES), F32)
     col_sums = jnp.zeros((LANES, rows), F32)
@@ -250,7 +251,7 @@
     )(proj, last, bc, aux, seg_rows, packed)
 
 
-def back_call(heads, taps, rows, proj, last, bc, aux, seg_rows, packed, outs, d_normed, inverse, shrink):
+def back_call(heads, taps, rows, proj, last, bc, aux, seg_rows, packed, outs, d_normed, scale):
     total = proj.shape[0]
     inner = heads * HALF
     count = total // rows
@@ -266,8 +267,7 @@
             whole_spec(packed.shape),
             rows_spec(rows, inner),
             rows_spec(rows, inner),
-            rows_spec(rows, 1),
-            rows_spec(rows, 1),
+            rows_spec(rows, 2),
         ],
         out_specs=[
             rows_spec(rows, 2 * inner),
@@ -287,7 +287,7 @@
         cost_estimate=pl.CostEstimate(
             flops=count * 2_000_000_000, bytes_accessed=count * 3_000_000, transcendentals=count * 600_000
         ),
-    )(proj, last, bc, aux, seg_rows, packed, outs, d_normed, inverse, shrink)
+    )(proj, last, bc, aux, seg_rows, packed, outs, d_normed, scale)
 
 
 def state_back_call(taps, d_act, last, aux, packed, d_dt):
@@ -321,14 +321,79 @@
     return jnp.where(at < line, 2 * at, 4 * line - 2 * at - 1)
 
 
-def assemble_kernel(cuts, starts, *refs):
+def ring_add_kernel(count, upper, has_sums, owners, *refs):
+    ups, downs = refs[:count], refs[count : 2 * count]
+    sums = refs[2 * count : 2 * count + 2] if has_sums else None
+    outs = refs[2 * count + 2 * has_sums :]
+    low = 0
+    for up, down in zip(ups, downs):
+        high = low + up.shape[2]
+        for way, part in enumerate((up, down)):
+            value = part[0]
+            if has_sums:
+                value = (value.astype(F32) + sums[way][:, low:high].astype(F32)).astype(BF16)
+            if len(outs) == 2:
+                outs[way][:, low:high] = value
+            elif way == 0:
+                outs[0][:upper, low:high] = value
+            else:
+                outs[0][upper:, low:high] = value
+        low = high
+
+
+def ring_add(parts, owners, upper, sums, final):
+    shard_rows = parts[0].shape[1]
+    lower = shard_rows - upper
+    width = sum(x.shape[2] for x in parts)
+    count = len(parts)
+    specs = []
+    for k, x in enumerate(parts):
+        specs.append(pl.BlockSpec((1, upper, x.shape[2]), functools.partial(lambda k, i, own: (own[2 * k], 0, 0), k)))
+    for k, x in enumerate(parts):
+        at = upper // lower
+        specs.append(
+            pl.BlockSpec((1, lower, x.shape[2]), functools.partial(lambda k, at, i, own: (own[2 * k + 1], at, 0), k, at))
+        )
+    whole = lambda rows: pl.BlockSpec((rows, width), lambda i, own: (0, 0))
+    if sums is not None:
+        specs += [whole(upper), whole(lower)]
+    outs = [shard_rows] if final else [upper, lower]
+    return pl.pallas_call(
+        functools.partial(ring_add_kernel, count, upper, sums is not None),
+        grid_spec=pltpu.PrefetchScalarGridSpec(
+            num_scalar_prefetch=1, grid=(1,), in_specs=specs, out_specs=[whole(r) for r in outs]
+        ),
+        out_shape=[jax.ShapeDtypeStruct((r, width), BF16) for r in outs],
+        compiler_params=pltpu.CompilerParams(vmem_limit_bytes=VMEM_ADD),
+        cost_estimate=pl.CostEstimate(flops=0, bytes_accessed=1_000_000, transcendentals=0),
+    )(jnp.stack(owners).astype(jnp.int32), *parts, *parts, *(sums or ()))
+
+
+def outer_kernel(a, b, out):
+    out[...] = dot(a[...], b[...], ((0,), (0,))).astype(BF16)
+
+
+def outer(a, b, block):
+    rows, height = a.shape
+    return pl.pallas_call(
+        outer_kernel,
+        grid=(height // block,),
+        in_specs=[pl.BlockSpec((rows, block), lambda i: (0, i)), whole_spec(b.shape)],
+        out_specs=pl.BlockSpec((block, b.shape[1]), lambda i: (i, 0)),
+        out_shape=jax.ShapeDtypeStruct((height, b.shape[1]), BF16),
+        compiler_params=pltpu.CompilerParams(vmem_limit_bytes=VMEM_LIMIT),
+        cost_estimate=pl.CostEstimate(flops=0, bytes_accessed=1_000_000, transcendentals=0),
+    )(a, b)
+
+
+def assemble_kernel(cuts, turned, starts, *refs):
     outs, sems = refs[-1 - len(cuts) : -1], refs[-1]
     sources = refs[: -1 - len(cuts)]
 
     def copies(run):
         for k, source in enumerate(sources):
-            start = pl.multiple_of(starts[k], 16)
             for n, (low, high) in enumerate(cuts):
+                start = pl.multiple_of(starts[k + len(sources) * (n == turned)], 16)
                 run(
                     pltpu.make_async_copy(
                         source.at[:, low:high],
@@ -341,10 +406,11 @@
     copies(lambda copy: copy.wait())
 
 
-def assemble(starts, sources, cuts):
+def assemble(starts, sources, cuts, turned=None, turn=0):
     total = sum(x.shape[0] for x in sources)
+    starts = starts + [lax.rem(start + total - turn, total) for start in starts]
     return pl.pallas_call(
-        functools.partial(assemble_kernel, cuts),
+        functools.partial(assemble_kernel, cuts, turned),
         in_specs=[pl.BlockSpec(memory_space=pltpu.SMEM)] + [pl.BlockSpec(memory_space=pl.ANY)] * len(sources),
         out_specs=[pl.BlockSpec(memory_space=pltpu.VMEM)] * len(cuts),
         out_shape=[jax.ShapeDtypeStruct((total, high - low), BF16) for low, high in cuts],
@@ -413,7 +479,8 @@
     inner = inner_all // 4
     row, core = where[2], where[3]
     has_out = len(refs) > 5
-    in_ref = refs[-2] if has_out else refs[-1]
+    in_ref = refs[4]
+    split = 2 * inner + LANES
 
     def quarter(sources, c, r, low, high):
         mine, far, came, came_far = sources
@@ -440,18 +507,19 @@
             chosen = (target == wanted).astype(BF16)
             tails = tails + dot(quarter(refs[:4], c, r, 2 * inner, 2 * inner + LANES), chosen)
             if has_out:
-                half_rows, half = refs[4].shape
-                low = quarter(refs[4:8], c, r, 0, half).astype(F32)
-                refs[-1][0, r * half_rows : (r + 1) * half_rows, c * half : (c + 1) * half] = low
+                half_rows, half = refs[0].shape[0], refs[0].shape[1] - split
+                low = quarter(refs[:4], c, r, split, split + half).astype(F32)
+                refs[5][0, r * half_rows : (r + 1) * half_rows, c * half : (c + 1) * half] = low
     in_ref[0, :, 2 * inner_all :] = tails
 
 
 def join(where, quarters, sizes):
-    rows = quarters[0].shape[0]
+    rows, width = quarters[0].shape
     inner_all, state_all, groups, each, heads_all = sizes
+    split = inner_all // 2 + LANES
     shapes = [jax.ShapeDtypeStruct((1, rows, 2 * inner_all + state_all + heads_all), F32)]
-    if len(quarters) > 4:
-        shapes.append(jax.ShapeDtypeStruct((1, 2 * quarters[4].shape[0], 2 * quarters[4].shape[1]), F32))
+    if width > split:
+        shapes.append(jax.ShapeDtypeStruct((1, 2 * rows, 2 * (width - split)), F32))
     spec = pl.BlockSpec(memory_space=pltpu.VMEM)
     return pl.pallas_call(
         functools.partial(join_kernel, sizes),
@@ -514,64 +582,17 @@
             starts.append(ring_owner(self.at + hop, self.line) * shard_rows + upper)
         return starts, sources
 
-    def shift(self, x, by):
-        line = self.line
-        return lax.ppermute(x, "fsdp", [(2 * p + s, 2 * ((p + by) % line) + s) for p in range(line) for s in range(2)])
-
-    def gather_side(self, piece):
-        line, shard_rows = self.line, piece.shape[0]
-        place, side = self.fsdp // 2, self.fsdp % 2
-        order = sorted(range(1, line), key=lambda by: min(by, line - by))
-        sources, starts = [], []
-        held = piece
-        for turn in range(line):
-            by = 0 if turn == 0 else order[turn - 1]
-            parts = [self.swap_side(held)]
-            if turn < line - 1:
-                parts.append(self.shift(piece, order[turn]))
-            crossed, *moved = yield parts
-            owner = 2 * lax.rem(place - by + line, line)
-            sources += [held, crossed]
-            starts += [(owner + side) * shard_rows, (owner + 1 - side) * shard_rows]
-            held = moved[0] if moved else None
-        return starts, sources
-
-    def scatter_side(self, parts):
-        line = self.line
-        place, side = self.fsdp // 2, self.fsdp % 2
-        order = sorted(range(1, line), key=lambda by: -min(by, line - by)) + [0]
-
-        def term(by, other):
-            owner = 2 * lax.rem(place + by, line) + (1 - side if other else side)
-            return lax.dynamic_index_in_dim(parts, owner, 0, keepdims=False)
-
-        total, summed = 0.0, None
-        for turn in range(line):
-            moves = [self.swap_side(term(order[turn], True))]
-            if turn > 0:
-                moves.append(self.shift(summed, order[turn - 1]))
-            crossed, *moved = yield moves
-            summed = term(order[turn], False).astype(F32) + crossed.astype(F32)
-            if turn < line - 1:
-                summed = summed.astype(BF16)
-            if moved:
-                total = total + moved[0].astype(F32)
-        return (total + summed).astype(BF16)
-
-    def scatter(self, shard_rows, term):
+    def scatter(self, shard_rows, parts):
         upper = self.upper(shard_rows)
-        up = down = None
+        sums = None
         for hop in range(1, 2 * self.line):
-            own_up = term(ring_owner(self.at - hop, self.line), 0, upper)
-            own_down = term(ring_owner(self.at + hop, self.line), upper, shard_rows)
-            if hop > 1:
-                own_up = (own_up.astype(F32) + up.astype(F32)).astype(BF16)
-                own_down = (own_down.astype(F32) + down.astype(F32)).astype(BF16)
-            up, down = yield [lax.ppermute(own_up, "fsdp", self.ahead), lax.ppermute(own_down, "fsdp", self.behind)]
-        owner = ring_owner(self.at, self.line)
-        up = up.astype(F32) + term(owner, 0, upper).astype(F32)
-        down = down.astype(F32) + term(owner, upper, shard_rows).astype(F32)
-        return jnp.concatenate([up.astype(BF16), down.astype(BF16)], axis=0)
+            owners = []
+            for _, f in parts:
+                owners += [f(ring_owner(self.at - hop, self.line)), f(ring_owner(self.at + hop, self.line))]
+            up, down = ring_add([x for x, _ in parts], owners, upper, sums, False)
+            sums = yield [lax.ppermute(up, "fsdp", self.ahead), lax.ppermute(down, "fsdp", self.behind)]
+        owners = [f(ring_owner(self.at, self.line)) for _, f in parts for _ in range(2)]
+        return ring_add([x for x, _ in parts], owners, upper, sums, True)[0]
 
     def sum_line(self, x):
         size = self.line
@@ -582,18 +603,14 @@
             pairs = [(2 * p + s, 2 * (p ^ by) + s) for p in range(size) for s in range(2)]
             x = x + lax.ppermute(x, "fsdp", pairs)
             by *= 2
+            if by < size:
+                (x,) = yield [x]
         return x
-
-
-RING = {('gb', 0): True, ('gb', 1): False, ('out', 1): False, ('in', 1): True, ('out', 0): False, ('in', 0): True}
 
 
 class Schedule:
     def __init__(self, work):
-        self.work, self.sent, self.sides = work, None, []
-
-    def launch(self, moves, finish):
-        self.sides.append([moves, None, finish])
+        self.work, self.sent = work, None
 
     def round(self, parts):
         extra = []
@@ -602,24 +619,9 @@
                 extra = list(self.work.send(self.sent))
             except StopIteration:
                 self.work = None
-        groups = [list(parts), extra]
-        going = []
-        for side in self.sides:
-            try:
-                groups.append(list(side[0].send(side[1])))
-                going.append(side)
-            except StopIteration as stop:
-                side[2](stop.value)
-        self.sides = going
-        joined = list(lax.optimization_barrier(tuple(x for group in groups for x in group)))
-        split = []
-        for group in groups:
-            split.append(joined[: len(group)])
-            joined = joined[len(group) :]
-        self.sent = split[1]
-        for side, values in zip(going, split[2:]):
-            side[1] = values
-        return split[0]
+        joined = lax.optimization_barrier(tuple(parts) + tuple(extra))
+        self.sent = list(joined[len(parts) :])
+        return list(joined[: len(parts)])
 
     def run(self, moves):
         sent = None
@@ -748,11 +750,11 @@
         return (u * norm_of(u) * gain).astype(BF16)
 
     def out_whole(pieces):
-        kept = links.cut(pieces, 0, core)
-        came = links.swap_core(links.cut(pieces, 0, 1 - core))
-        return links.in_core_order(kept, came, 1)
-
-    def ahead(layer, scaled):
+        half = pieces.shape[0] // 2
+        kept, sent = (pieces[:half], pieces[half:]) if direct else (links.cut(pieces, 0, core), links.cut(pieces, 0, 1 - core))
+        return links.in_core_order(kept, links.swap_core(sent), 1)
+
+    def project(layer, scaled):
         wide_w, last_w = big["in", layer]
         last = dot(scaled, last_w)
         came = links.swap_row(last[:, LANES - state_own :])
@@ -760,74 +762,57 @@
         proj, last, came = yield [proj, last, came]
         part = links.in_row_order(last[:, LANES - state_own :], came, 1)
         bc = links.in_core_order(part, links.swap_core(part), 1)
+        return proj, last, bc
+
+    def mix(layer, proj, last, bc):
         outs, gated, squares = ahead_call(heads, taps, rows, proj, last, bc, aux, seg_rows, big["pack", layer])
-        bc, outs, gated, squares = yield [bc, outs, gated, squares]
-        squares = to_rows(squares[:, 0])
-        squares = squares + links.swap_core(squares)
-        squares = squares + links.swap_row(squares)
-        (squares,) = yield [squares]
-        inverse = lax.rsqrt(squares.reshape(tokens, 1) / inner_all + 1e-05)
+        return outs, gated, to_rows(squares[:, 0])
+
+    def over_all(x):
+        x = x + links.swap_core(x)
+        return x + links.swap_row(x)
+
+    def inverse_of(squares):
+        return lax.rsqrt(squares / inner_all + 1e-05)
+
+    def as_columns(*rows_):
+        return jnp.stack([x.reshape(tokens) for x in rows_]).T
+
+    def normed_of(layer, gated, inverse):
         gain = big["pack", layer][taps + 1 : taps + 2, :inner]
-        normed = (gated * inverse * gain).astype(BF16)
-        normed_all = links.in_core_order(normed, links.swap_core(normed), 1)
-        return {"scaled": scaled, "proj": proj, "last": last, "bc": bc, "outs": outs, "gated": gated, "inverse": inverse, "normed": normed_all}
-
-    def back_first(layer, kept, grad, meet=None):
-        d_normed = dot(grad, big["out_whole", layer], ((1,), (1,)))
-        gain = big["pack", layer][taps + 1 : taps + 2, :inner]
-        if meet is None:
-            meet = to_rows(jnp.sum(kept["gated"] * gain * d_normed, axis=1))
-            d_normed, meet = yield [d_normed, meet]
-            meet = meet + links.swap_core(meet)
-            meet = (links.swap_row(meet) + meet) * to_rows(kept["inverse"][:, 0])
-            (meet,) = yield [meet]
-        else:
-            meet = meet + links.swap_core(meet)
-            d_normed, meet = yield [d_normed, meet]
-        inverse = kept["inverse"]
-        shrink = inverse * inverse * meet.reshape(tokens, 1) / inner_all
-        d_main, d_dt, d_bc, d_wide, d_narrow = back_call(
+        normed = (gated * inverse.reshape(tokens, 1) * gain).astype(BF16)
+        other = links.swap_core(normed)
+        return jnp.concatenate([normed, other], axis=1) if direct else links.in_core_order(normed, other, 1)
+
+    def back_mix(layer, kept, d_normed, meet):
+        scale = as_columns(kept["inverse"], kept["inverse"] * meet / inner_all)
+        return back_call(
             heads, taps, rows, kept["proj"], kept["last"], kept["bc"], aux, seg_rows, big["pack", layer],
-            kept["outs"], d_normed, inverse, shrink,
+            kept["outs"], d_normed, scale,
         )
-        d_main, d_dt, d_bc, d_wide, d_narrow = yield [d_main, d_dt, d_bc, d_wide, d_narrow]
+
+    def back_project(layer, kept, d_main, d_dt, d_bc):
         wide_w, last_w = big["in", layer]
         d_bc = over_cores(d_bc)
+        d_scaled = dot(d_main, wide_w, ((1,), (1,)))
+        d_bc, d_scaled = yield [d_bc, d_scaled]
         d_bc = links.cut(d_bc, 1, row) + links.swap_row(links.cut(d_bc, 1, 1 - row))
-        d_in = dot(kept["scaled"], d_main, ((0,), (0,))).astype(BF16)
-        d_scaled = dot(d_main, wide_w, ((1,), (1,)))
-        d_bc, d_in, d_scaled = yield [d_bc, d_in, d_scaled]
+        d_in = outer(kept["scaled"], d_main, width // 3)
+        d_bc, d_in = yield [d_bc, d_in]
         d_bc = jnp.pad(d_bc, ((0, 0), (LANES - d_bc.shape[1], 0)))
         d_last, d_state = state_back_call(taps, d_bc, kept["last"], aux, big["pack", layer], d_dt)
         d_in_last = dot(kept["scaled"], d_last, ((0,), (0,))).astype(BF16)
         d_scaled = d_scaled + dot(d_last, last_w, ((1,), (1,)))
-        d_scaled, d_in, d_in_last = yield [d_scaled, d_in, d_in_last]
-        done["in", layer] = d_in, d_in_last
-        return d_scaled, (jnp.sum(d_wide, axis=0), jnp.sum(d_narrow, axis=0), d_state)
-
-    def out_grad(kept, grad):
-        return dot(kept["normed"], links.cut(grad, 1, core), ((0,), (0,))).astype(BF16)
-
-    def four(low0, low1, far0, far1, theirs):
-        return [
-            links.mine_of_core(low0, low1),
-            links.mine_of_core(far0, far1),
-            theirs,
-            links.swap_core(links.mine_of_core(far1, far0)),
-        ]
+        return d_scaled, d_in, d_in_last, d_state
+
+    def out_grad(normed, grad_half):
+        return dot(normed, grad_half, ((0,), (0,))).astype(BF16)
 
     aux = seg_rows = None
     done = {}
 
     def send_out(layer, d_out):
         done["out", layer] = d_out
-        if direct and not RING["out", layer]:
-
-
-            def finish(total):
-                done["sum", ("out", layer)] = total
-
-            schedule.launch(links.scatter_side(d_out.reshape(shards, shard_rows, half_width)), finish)
 
     def work():
         nonlocal aux, seg_rows
@@ -848,83 +833,109 @@
         tokens_all, scaled = yield [tokens_all, scaled]
         yield [scaled]
         cot_all = links.in_row_order(cotangent, came_cot, 0)
-        (cot_all,) = yield [cot_all]
+        cot_half = links.cut(cot_all, 1, core)
+        cot_all, cot_half = yield [cot_all, cot_half]
         while ("in", 0) not in big:
             yield [scaled]
-        kept0 = yield from ahead(0, scaled)
+        wide_w, last_w = big["in", 0]
+        if direct:
+            wide_w, last_w, big["out", 0] = yield [wide_w, last_w, big["out", 0]]
+        else:
+            wide_w, last_w = yield [wide_w, last_w]
+        big["in", 0] = wide_w, last_w
+        proj, last, bc = yield from project(0, scaled)
+        outs, gated, squares = mix(0, proj, last, bc)
+        bc, outs, gated, squares = yield [bc, outs, gated, squares]
+        (squares,) = yield [over_all(squares)]
+        inverse = inverse_of(squares)
+        normed = normed_of(0, gated, inverse)
         while ("out", 0) not in big:
-            yield [scaled]
-        branch = dot(kept0["normed"], big["out", 0]).astype(BF16)
-        kept0["normed"], kept0["inverse"], branch = yield [kept0["normed"], kept0["inverse"], branch]
+            yield [normed]
+        branch = dot(normed, big["out", 0]).astype(BF16)
         came = links.swap_row(branch)
+        normed, inverse, branch = yield [normed, inverse, branch]
+        kept0 = {"scaled": scaled, "proj": proj, "last": last, "bc": bc, "outs": outs, "inverse": inverse}
         big["out_whole", 0] = out_whole(big["out", 0])
-        branch, big["out_whole", 0] = yield [branch, big["out_whole", 0]]
-        (came,) = yield [came]
-        while ("in", 1) not in big:
+        came, big["out_whole", 0] = yield [came, big["out_whole", 0]]
+        normed0 = normed
+        while ("in", 1) not in big or ("out", 1) not in big:
             yield [came]
         branch = branch.astype(F32) + came.astype(F32)
         first = (links.cut(tokens_all, 1, core).astype(F32) + branch).astype(BF16)
         first = links.in_core_order(first, links.swap_core(first), 1)
         scaled = scaled_of(first, gain1)
-        kept1 = yield from ahead(1, scaled)
-        d_out = out_grad(kept1, cot_all)
-        kept1["normed"], kept1["inverse"], d_out = yield [kept1["normed"], kept1["inverse"], d_out]
+        big["out_whole", 1] = out_whole(big["out", 1])
+        proj, last, bc = yield from project(1, scaled)
+        d_normed = dot(cot_all, big["out_whole", 1], ((1,), (1,)))
+        outs, gated, squares = mix(1, proj, last, bc)
+        gain = big["pack", 1][taps + 1 : taps + 2, :inner]
+        meet = to_rows(jnp.sum(gated * gain * d_normed, axis=1))
+        both_sums = over_all(jnp.concatenate([squares, meet], axis=0))
+        bc, outs, gated, d_normed, both_sums = yield [bc, outs, gated, d_normed, both_sums]
+        squares, meet = both_sums[: squares.shape[0]], both_sums[squares.shape[0] :]
+        inverse = inverse_of(squares)
+        kept1 = {"scaled": scaled, "proj": proj, "last": last, "bc": bc, "outs": outs, "inverse": inverse}
+        found = back_mix(1, kept1, d_normed, inverse * inverse * meet)
+        d_main, d_dt, d_bc, d_wide1, d_narrow1 = yield list(found)
+        normed1 = normed_of(1, gated, inverse)
+        d_out = out_grad(normed1, cot_half)
+        d_scaled, d_in, d_in_last, d_state1 = yield from back_project(1, kept1, d_main, d_dt, d_bc)
+        d_scaled, d_in, d_in_last, d_out = yield [d_scaled, d_in, d_in_last, d_out]
+        done["in", 1] = d_in, d_in_last
         send_out(1, d_out)
-        while ("out", 1) not in big:
-            yield [first]
-        big["out_whole", 1] = out_whole(big["out", 1])
-        d_scaled, small1 = yield from back_first(1, kept1, cot_all)
+        small1 = jnp.sum(d_wide1, axis=0), jnp.sum(d_narrow1, axis=0), d_state1
         d_scaled = over_cores(d_scaled).astype(BF16)
+        came = links.swap_row(d_scaled)
         (d_scaled,) = yield [d_scaled]
-        came = links.swap_row(d_scaled)
-        yield [d_scaled]
         (came,) = yield [came]
         d_scaled = d_scaled.astype(F32) + came.astype(F32)
         d_scaled = links.in_core_order(d_scaled, links.swap_core(d_scaled), 1)
         grad = (cot_all.astype(F32) + norm_back(first, gain1, d_scaled)).astype(BF16)
         gain_sum1 = gain_back(own_rows(first), own_rows(d_scaled))
-        d_out = out_grad(kept0, grad)
-        grad, d_out = yield [grad, d_out]
+        grad, gain_sum1 = yield [grad, gain_sum1]
+        grad_half = links.cut(grad, 1, core)
+        meet = to_rows(jnp.sum(branch * grad_half.astype(F32), axis=1))
+        meet = meet + links.swap_core(meet)
+        d_normed = dot(grad, big["out_whole", 0], ((1,), (1,)))
+        d_normed, meet, grad_half = yield [d_normed, meet, grad_half]
+        found = back_mix(0, kept0, d_normed, kept0["inverse"] * meet)
+        d_main, d_dt, d_bc, d_wide0, d_narrow0 = yield list(found)
+        d_out = out_grad(normed0, grad_half)
+        d_scaled, d_in, d_in_last, d_state0 = yield from back_project(0, kept0, d_main, d_dt, d_bc)
+        d_scaled, d_in, d_in_last, d_out = yield [d_scaled, d_in, d_in_last, d_out]
+        done["in", 0] = d_in, d_in_last
         send_out(0, d_out)
-        meet = to_rows(jnp.sum(branch * links.cut(grad, 1, core).astype(F32), axis=1))
-        d_scaled, small0 = yield from back_first(0, kept0, grad, meet)
+        small0 = jnp.sum(d_wide0, axis=0), jnp.sum(d_narrow0, axis=0), d_state0
+        while ("sum", 1) not in done:
+            yield [d_scaled]
+        far_upper = links.swap_row(done["sum", 1][: shard_rows // 2])
         d_scaled = over_cores(d_scaled)
-        (d_scaled,) = yield [d_scaled]
+        d_scaled, far_upper = yield [d_scaled, far_upper]
         came = links.swap_row(links.cut(d_scaled, 0, 1 - row).astype(BF16))
-        (came,) = yield [came]
+        partial = dot(normed1, big["out", 1])
+        came, partial = yield [came, partial]
+        far_lower = links.swap_row(done["sum", 1][shard_rows // 2 :])
         d_scaled = own_rows(d_scaled) + came.astype(F32)
         d_scaled = links.in_core_order(d_scaled, links.swap_core(d_scaled), 1)
         own_grad = own_rows(grad)
         grad_in = (own_grad.astype(F32) + norm_back(inputs, gain0, d_scaled)).astype(BF16)
         gain_sum0 = gain_back(inputs, d_scaled)
-        grad_in, gain_sum0 = yield [grad_in, gain_sum0]
         done["input_grad"] = jnp.where(core == 0, grad_in, own_grad)[None]
-        while ("sum", ("in", 1)) not in done:
-            yield [gain_sum0]
-        far_in1 = links.swap_row(done["sum", ("in", 1)])
+        done["input_grad"], gain_sum0, far_lower = yield [done["input_grad"], gain_sum0, far_lower]
+        done["far", 1] = jnp.concatenate([far_upper, far_lower], axis=0)
+        came = links.swap_row(links.cut(partial, 0, 1 - row).astype(BF16))
         small = jnp.concatenate([pack_small(*small0, gain_sum0), pack_small(*small1, gain_sum1)], axis=0)
         small = small + links.swap_side(small)
-        if direct:
-            while ("sum", ("out", 0)) not in done:
-                yield [small]
-            out0, out1 = done["sum", ("out", 0)], done["sum", ("out", 1)]
-            far0, far1 = links.swap_row(out0), links.swap_row(out1)
-            small, far0, far1 = yield [small, far0, far1]
-            theirs = links.swap_core(links.mine_of_core(out1, out0))
-            done["out_quarters"] = four(out0, out1, far0, far1, theirs)
-        small = links.sum_line(small)
-        (small,) = yield [small]
-        small_other = links.swap_row(small)
-        partial = dot(kept1["normed"], big["out", 1])
-        small, small_other, partial = yield [small, small_other, partial]
-        came = links.swap_row(links.cut(partial, 0, 1 - row).astype(BF16))
-        done["small"] = spread_small(small, small_other)
-        came, done["far", "in"], *done["small"] = yield [came, far_in1] + list(done["small"])
+        came, small = yield [came, small]
         second = own_rows(partial) + came.astype(F32) + links.cut(own_rows(first), 1, core).astype(F32)
         second = second.astype(BF16)
         second = links.in_core_order(second, links.swap_core(second), 1)
         done["phase_out"] = jnp.where(core == 0, own_rows(first), second)[None]
-        (done["phase_out"],) = yield [done["phase_out"]]
+        small = yield from links.sum_line(small)
+        done["phase_out"], small = yield [done["phase_out"], small]
+        small_other = links.swap_row(small)
+        done["small"] = spread_small(small, small_other)
+        done["small"] = yield list(done["small"])
 
     gain_rows = width // inner
 
@@ -975,48 +986,29 @@
     schedule = Schedule(work())
 
     def gather(layer):
-        cuts = [(0, 2 * inner), (2 * inner, split)]
-        piece, side_piece = pieces[layer], None
-        if direct and RING["gb", layer]:
-            cuts.append((split, split + half_width))
-        elif direct:
-            piece, side_piece = piece[:, :split], piece[:, split:]
-        if side_piece is not None:
-
-            def finish(found):
-                (big["out", layer],) = assemble(*found, [(0, half_width)])
-
-            schedule.launch(links.gather_side(side_piece), finish)
-        full = assemble(*schedule.run(links.gather(piece)), cuts)
+        cuts = [(0, 2 * inner), (2 * inner, split)] + ([(split, split + half_width)] if direct else [])
+        full = assemble(*schedule.run(links.gather(pieces[layer])), cuts, 2, core * (shards // 2 * shard_rows))
+        if direct:
+            big["out", layer] = full[2]
+        else:
+            big["out", layer] = out_gathered(layer)
         big["in", layer] = full[:2]
-        if len(cuts) > 2:
-            big["out", layer] = full[2]
-        elif not direct:
-            big["out", layer] = out_gathered(layer)
-
-    def scatter(kind, layer):
-        name = (kind, layer)
-        while name not in done:
+
+    def scatter(layer):
+        while ("in", layer) not in done:
             schedule.round([])
-        if kind == "out" and direct and not RING[name]:
-            return
-        if kind == "out" and not direct:
-            parts = done[name].reshape(2, 1, inner, half_width)
-            parts = links.in_row_order(parts, jnp.zeros_like(parts), 1).reshape(4 * inner, half_width)
-            mine = lax.psum_scatter(parts, "fsdp", scatter_dimension=0, tiled=True)
-            total = mine.astype(F32) + links.swap_row(mine).astype(F32)
-            done["sum", name] = total.astype(BF16)
-        elif RING[name]:
-            parts = [x.reshape(shards, shard_rows, -1) for x in (done[name] if kind == "in" else [done[name]])]
-
-            def term(owner, low, high):
-                taken = [lax.dynamic_slice(x, (owner, low, 0), (1, high - low, x.shape[2]))[0] for x in parts]
-                return taken[0] if len(taken) == 1 else jnp.concatenate(taken, axis=1)
-
-            done["sum", name] = schedule.run(links.scatter(shard_rows, term))
+        parts = list(done["in", layer])
+        if direct:
+            parts.append(done["out", layer])
         else:
-            parts = jnp.concatenate(done[name], axis=1) if kind == "in" else done[name]
-            done["sum", name] = lax.psum_scatter(parts, "fsdp", scatter_dimension=0, tiled=True)
+            sums = done["out", layer].reshape(2, 1, inner, half_width)
+            sums = links.in_row_order(sums, jnp.zeros_like(sums), 1).reshape(4 * inner, half_width)
+            sums = lax.psum_scatter(sums, "fsdp", scatter_dimension=0, tiled=True)
+            done["out_sum", layer] = (sums.astype(F32) + links.swap_row(sums).astype(F32)).astype(BF16)
+        by_core = (lambda f: jnp.where(core == 0, f, (f + shards // 2) % shards)) if direct else (lambda f: f)
+        laid = [lambda f: f, lambda f: f, by_core]
+        parts = [(x.reshape(shards, shard_rows, -1), f) for x, f in zip(parts, laid)]
+        done["sum", layer] = schedule.run(links.scatter(shard_rows, parts))
 
     def out_gathered(layer):
         full = lax.all_gather(out_pieces[layer], "fsdp", axis=0, tiled=True)
@@ -1024,21 +1016,21 @@
 
     gather(0)
     gather(1)
-    scatter("out", 1)
-    scatter("in", 1)
-    scatter("out", 0)
-    scatter("in", 0)
+    scatter(1)
+    scatter(0)
     while schedule.work is not None:
         schedule.round([])
 
-    low0, low1, far1 = done["sum", ("in", 0)], done["sum", ("in", 1)], done["far", "in"]
-    out0, out1 = done["sum", ("out", 0)], done["sum", ("out", 1)]
+    low0, low1, far1 = done["sum", 0], done["sum", 1], done["far", 1]
     theirs = links.swap_core(links.mine_of_core(low1, low0))
-    quarters = four(low0, low1, links.swap_row(low0), far1, theirs)
+    far0 = links.swap_row(low0)
+    quarters = [links.mine_of_core(low0, low1), links.mine_of_core(far0, far1)]
+    quarters += [theirs, links.swap_core(links.mine_of_core(far1, far0))]
     if direct:
-        grad_in_w, grad_out_w = join(where, quarters + done["out_quarters"], sizes)
+        grad_in_w, grad_out_w = join(where, quarters, sizes)
     else:
         (grad_in_w,) = join(where, quarters, sizes)
+        out0, out1 = done["out_sum", 0], done["out_sum", 1]
         theirs = links.swap_core(links.mine_of_core(out1, out0))
         grad_out_w = links.in_core_order(links.mine_of_core(out0, out1), theirs, 1).astype(F32)[None]
     grad_norm, grad_conv_w, grad_conv_b, grad_dt, grad_a, grad_skip, grad_out_gain = done["small"]

time: 600 us -> 571 us (0.952)
  other arithmetic: 79 us -> 32.5 us
  starting transfers between devices: 120 us -> 85 us
  waiting for transfers between devices: 221 us -> 249 us
  Pallas kernels: 57.5 us -> 80.2 us
  local copies, waits for them, and re-layouts: 55.2 us -> 70.3 us
  matrix products: 53.5 us -> 40.2 us
    unnamed x319 -> x288, local copies, waits for them, and re-layouts: 19.3 us -> 49 us
    convert_element_type x36 -> x2, other arithmetic: 23.7 us -> 0.39 us  [normed_of(): normed = (gated * inverse.reshape(tokens, 1) * gain).astype(BF16)]
    pallas_call x3 -> x20, Pallas kernels: 16.7 us -> 39.3 us  [the longest x16 18.2 us: ring_add(): pl.pallas_call(functools.partial(ring_add_kernel, count, upper, sums is n...]
    ppermute x37 -> x28, starting transfers between devices: 48.7 us -> 29.6 us  [the longest x14 16.5 us: scatter(): lax.ppermute(down, 'fsdp', self.behind)]
    ppermute x13 -> x1, waiting for transfers between devices: 23.7 us -> 9.15 us  [swap_side(): lax.ppermute(x, 'fsdp', [(2 * p + s, 2 * p + 1 - s) for p in range(self.l...]
    dot_general x18 -> x16, matrix products: 53.5 us -> 40.2 us  [dot(): lax.dot_general(a, b, (dims, ((), ())), precision=precision, preferred_el...]
    squeeze x6 -> x0, local copies, waits for them, and re-layouts: 13.2 us -> none  [the longest x4 9.97 us: term(): lax.dynamic_slice(x, (owner, low, 0), (1, high - low, x.shape[2]))[0]]
    ppermute x2, waiting for transfers between devices: 5.99 us -> 17.4 us  [sum_line(): x = x + lax.ppermute(x, 'fsdp', pairs)]
  transfers between devices with their start and end apart: 124 -> 98, of which waited for: 62 -> 66; matrix products, arithmetic and copies ran while one was open for 23% -> 13% of each run, Pallas kernels for 8% -> 10%
where the time goes in v3:
time: 571 us; the launch traced here: 561 us
  waiting for transfers between devices  249 us (44%)
  starting transfers between devices  85 us (15%)
  Pallas kernels  80.2 us (14%)
  local copies, waits for them, and re-layouts  70.3 us (12%)
  matrix products  40.2 us (7%)
  other arithmetic  32.5 us (6%)
    ppermute x14, waiting for transfers between devices, gather(): lax.ppermute(up, 'fsdp', self.ahead)  72.4 us
    ppermute x14, waiting for transfers between devices, scatter(): lax.ppermute(up, 'fsdp', self.ahead)  56.9 us
    ppermute x17, waiting for transfers between devices, swap_row(): return lax.ppermute(x, 'dp', [(0, 1), (1, 0)])  55.1 us
    unnamed x288, local copies, waits for them, and re-layouts  49 us
    dot_general x16, matrix products, dot(): lax.dot_general(a, b, (dims, ((), ())), precision=precision, preferred_el...  40.2 us
    ppermute x14, waiting for transfers between devices, gather(): lax.ppermute(down, 'fsdp', self.behind)  22.5 us
    pallas_call x2, Pallas kernels, back_call(): pl.pallas_call(functools.partial(back_kernel, heads, taps), grid=(count,)...  21.1 us
    pallas_call x16, Pallas kernels, ring_add(): pl.pallas_call(functools.partial(ring_add_kernel, count, upper, sums is n...  18.2 us
  transfers between devices with their start and end apart: 98, of which 66 were waited for; matrix products, arithmetic and copies ran while one was open for 13% of the time, Pallas kernels for 10%

profile of v3, /device:TPU:0, one launch (start us, length us, event | category | flops | bytes accessed | tf_op | source)
XLA Modules:
  0.0 561.1 jit_solution(9084205853677071392)
XLA Ops:
  3.8 3.0 shard_map.203
  7.3 2.6 collective-permute-start.1
  22.5 6.8 %collective-permute-done.4.refs_2_ = bf16[96,2432]{1,0:T(8,128)(2,1)} collective-permute-done((bf16[96,2432]{1,0:T(8,128)(2,1)}, bf16[96,2432]{1,0:T(8,128)(2,1)}, u32[]{:S(2)}, u32[]{:S(2)}) %collective-permute-start.4) | collective-permute-done | bytes 466976 | tf_op jit(solution)/shard_map/ppermute | solution.py:579
  32.6 6.2 %collective-permute-done.7 = bf16[256,1536]{1,0:T(8,128)(2,1)S(1)} collective-permute-done((bf16[256,1536]{1,0:T(8,128)(2,1)S(1)}, bf16[256,1536]{1,0:T(8,128)(2,1)S(1)}, u32[]{:S(2)}, u32[]{:S(2)}) %collective-permute-start.7) | collective-permute-done | bytes 786464 | tf_op jit(solution)/shard_map/ppermute | solution.py:548
  38.8 2.7 collective-permute-done.5.refs_3_
  46.8 5.8 %collective-permute-done.8.refs_5_ = bf16[96,2432]{1,0:T(8,128)(2,1)S(1)} collective-permute-done((bf16[96,2432]{1,0:T(8,128)(2,1)S(1)}, bf16[96,2432]{1,0:T(8,128)(2,1)S(1)}, u32[]{:S(2)}, u32[]{:S(2)}) %collective-permute-start.8) | collective-permute-done | bytes 466976 | tf_op jit(solution)/shard_map/ppermute | solution.py:579
  56.1 7.4 %collective-permute-done.12.refs_7_ = bf16[96,2432]{1,0:T(8,128)(2,1)S(1)} collective-permute-done((bf16[96,2432]{1,0:T(8,128)(2,1)S(1)}, bf16[96,2432]{1,0:T(8,128)(2,1)S(1)}, u32[]{:S(2)}, u32[]{:S(2)}) %collective-permute-start.12) | collective-permute-done | bytes 466976 | tf_op jit(solution)/shard_map/ppermute | solution.py:579
  70.3 5.0 collective-permute-done.14.refs_9_
  75.3 3.3 collective-permute-done.15.refs_10_
  78.6 2.4 collective-permute-start.17
  81.0 10.5 %collective-permute-done.17.refs_11_ = bf16[96,2432]{1,0:T(8,128)(2,1)} collective-permute-done((bf16[96,2432]{1,0:T(8,128)(2,1)}, bf16[96,2432]{1,0:T(8,128)(2,1)}, u32[]{:S(2)}, u32[]{:S(2)}) %collective-permute-start.17) | collective-permute-done | bytes 466976 | tf_op jit(solution)/shard_map/ppermute | solution.py:579
  91.5 2.8 collective-permute-done.18.refs_12_
  99.1 4.1 collective-permute-done.19.refs_13_
  104.9 7.3 %shard_map.204 = (bf16[1536,1536]{1,0:T(8,128)(2,1)}, bf16[1536,128]{1,0:T(8,128)(2,1)}, bf16[1536,768]{1,0:T(8,128)(2,1)}) custom-call(s32[30]{0:T(128)} %stack.456.starts, bf16[192,2432]{1,0:T(8,128)(2,1)} %copy-done.83, bf16[96,2432]{1,0:T(8,128)(2,1)} %collective-permute-done.3.refs_1_, bf16[96,2432]{1,0:T(8,128)(2,1)} %collective-permute-done.4.refs_2_, ...), custom_call_target="tpu_custom_call" | custom-call | bytes 14942208 | tf_op jit(solution)/shard_map/pallas_call | solution.py:412
  118.0 6.7 %fusion.83.proj = f32[512,1536]{1,0:T(8,128)} fusion(bf16[512,1536]{1,0:T(8,128)(2,1)S(1)} %fusion.2.a, bf16[1536,1536]{1,0:T(8,128)(2,1)} %get-tuple-element.241), kind=kOutput, calls=%fused_computation.238 | convolution fusion | flops 2415919104 | bytes 9437184 | tf_op jit(solution)/shard_map/dot_general | solution.py:20
  129.9 5.3 shard_map.205
  135.3 3.7 collective-permute-done.24.refs_5_
  143.4 3.3 collective-permute-done.30
  146.7 5.2 collective-permute-done.27.refs_7_
  158.1 7.8 %collective-permute-done.31.refs_9_ = bf16[96,2432]{1,0:T(8,128)(2,1)S(1)} collective-permute-done((bf16[96,2432]{1,0:T(8,128)(2,1)S(1)}, bf16[96,2432]{1,0:T(8,128)(2,1)S(1)}, u32[]{:S(2)}, u32[]{:S(2)}) %collective-permute-start.31) | collective-permute-done | bytes 466976 | tf_op jit(solution)/shard_map/ppermute | solution.py:579
  170.1 7.8 %collective-permute-done.34.refs_11_ = bf16[96,2432]{1,0:T(8,128)(2,1)S(1)} collective-permute-done((bf16[96,2432]{1,0:T(8,128)(2,1)S(1)}, bf16[96,2432]{1,0:T(8,128)(2,1)S(1)}, u32[]{:S(2)}, u32[]{:S(2)}) %collective-permute-start.34) | collective-permute-done | bytes 466976 | tf_op jit(solution)/shard_map/ppermute | solution.py:579
  181.8 11.2 %collective-permute-done.39.refs_13_ = bf16[96,2432]{1,0:T(8,128)(2,1)} collective-permute-done((bf16[96,2432]{1,0:T(8,128)(2,1)S(1)}, bf16[96,2432]{1,0:T(8,128)(2,1)}, u32[]{:S(2)}, u32[]{:S(2)}) %collective-permute-start.39) | collective-permute-done | bytes 466976 | tf_op jit(solution)/shard_map/ppermute | solution.py:579
  194.4 7.3 %shard_map.206 = (bf16[1536,1536]{1,0:T(8,128)(2,1)}, bf16[1536,128]{1,0:T(8,128)(2,1)}, bf16[1536,768]{1,0:T(8,128)(2,1)}) custom-call(s32[30]{0:T(128)} %stack.456.starts, bf16[192,2432]{1,0:T(8,128)(2,1)} %get-tuple-element.438.refs_0_, bf16[96,2432]{1,0:T(8,128)(2,1)} %collective-permute-done.10.refs_1_, ...), custom_call_target="tpu_custom_call" | custom-call | bytes 14942208 | tf_op jit(solution)/shard_map/pallas_call | solution.py:412
  201.7 3.2 fusion.72
  208.5 6.7 %fusion.85.proj = f32[512,1536]{1,0:T(8,128)} fusion(bf16[512,1536]{1,0:T(8,128)(2,1)S(1)} %fusion.5.a, bf16[1536,1536]{1,0:T(8,128)(2,1)} %get-tuple-element.271), kind=kOutput, calls=%fused_computation.240 | convolution fusion | flops 2415919104 | bytes 9437184 | tf_op jit(solution)/shard_map/dot_general | solution.py:20
  221.1 5.7 %shard_map.207 = (f32[512,768]{1,0:T(8,128)S(1)}, f32[512,768]{1,0:T(8,128)S(1)}, f32[512,128]{1,0:T(8,128)S(1)}) custom-call(f32[512,1536]{1,0:T(8,128)S(1)} %copy-done.63, f32[512,128]{1,0:T(8,128)S(1)} %copy.243.last.last_ref, f32[512,256]{1,0:T(8,128)S(1)} %maximum_select_fusion.10.bc, f32[512,8]{1,0:T(8,128)S(1)} %copy.237.aux, ...), custom_call_target="tpu_custom_call" | custom-call | flops 4000000000 | bytes 8000000 | tf_op jit(solution)/shard_map/pallas_call | solution.py:230
  227.0 5.2 multiply_reduce_fusion.1
  233.8 3.3 collective-permute-done.45
  242.1 10.6 %shard_map.208 = (bf16[512,1536]{1,0:T(8,128)(2,1)S(1)}, f32[512,128]{1,0:T(8,128)S(1)}, f32[512,256]{1,0:T(8,128)S(1)}, f32[4,8,768]{2,1,0:T(8,128)S(1)}, f32[4,8,128]{2,1,0:T(8,128)S(1)}) custom-call(f32[512,1536]{1,0:T(8,128)S(1)} %copy-done.64, f32[512,128]{1,0:T(8,128)S(1)} %copy.243.last.last_ref, f32[512,256]{1,0:T(8,128)S(1)} %maximum_select_fusion.10.bc, ...), custom_call_target="tpu_custom_call" | custom-call | flops 8000000000 | bytes 12000000 | tf_op jit(solution)/shard_map/pallas_call | solution.py:258
  252.8 4.7 fusion.87
  258.2 3.2 shard_map.209
  261.8 4.6 collective-permute-done.47
  271.3 3.4 collective-permute-done.51
  276.1 2.3 copy-done.1
  281.3 10.3 %collective-permute-done.49.refs_6_ = bf16[96,2432]{1,0:T(8,128)(2,1)S(1)} collective-permute-done((bf16[96,2432]{1,0:T(8,128)(2,1)S(1)}, bf16[96,2432]{1,0:T(8,128)(2,1)S(1)}, u32[]{:S(2)}, u32[]{:S(2)}) %collective-permute-start.49) | collective-permute-done | bytes 466976 | tf_op jit(solution)/shard_map/ppermute | solution.py:593
  295.7 2.7 convert_add_fusion
  309.2 3.7 fusion.7
  315.3 5.0 collective-permute-done.53.refs_6_
  325.9 2.6 fusion.89.d_normed
  328.5 8.5 %collective-permute-done.56.refs_6_ = bf16[96,2432]{1,0:T(8,128)(2,1)S(1)} collective-permute-done((bf16[96,2432]{1,0:T(8,128)(2,1)S(1)}, bf16[96,2432]{1,0:T(8,128)(2,1)S(1)}, u32[]{:S(2)}, u32[]{:S(2)}) %collective-permute-start.56) | collective-permute-done | bytes 466976 | tf_op jit(solution)/shard_map/ppermute | solution.py:593
  339.7 2.3 copy-done.3
  347.2 10.5 %shard_map.215 = (bf16[512,1536]{1,0:T(8,128)(2,1)S(1)}, f32[512,128]{1,0:T(8,128)S(1)}, f32[512,256]{1,0:T(8,128)S(1)}, f32[4,8,768]{2,1,0:T(8,128)S(1)}, f32[4,8,128]{2,1,0:T(8,128)S(1)}) custom-call(f32[512,1536]{1,0:T(8,128)S(1)} %copy-done.62, f32[512,128]{1,0:T(8,128)S(1)} %copy.235.last.last_ref, f32[512,256]{1,0:T(8,128)S(1)} %copy-done.22, ...), custom_call_target="tpu_custom_call" | custom-call | flops 8000000000 | bytes 12000000 | tf_op jit(solution)/shard_map/pallas_call | solution.py:258
  361.1 2.6 fusion.90
  363.8 8.4 %collective-permute-done.61.refs_6_ = bf16[96,2432]{1,0:T(8,128)(2,1)S(1)} collective-permute-done((bf16[96,2432]{1,0:T(8,128)(2,1)S(1)}, bf16[96,2432]{1,0:T(8,128)(2,1)S(1)}, u32[]{:S(2)}, u32[]{:S(2)}) %collective-permute-start.61) | collective-permute-done | bytes 466976 | tf_op jit(solution)/shard_map/ppermute | solution.py:593
  376.2 2.9 convolution_convert_fusion
  379.0 3.2 shard_map.218
  382.5 3.2 collective-permute-done.64.refs_6_
  391.7 6.0 %collective-permute-done.67.refs_6_ = bf16[96,2432]{1,0:T(8,128)(2,1)S(1)} collective-permute-done((bf16[96,2432]{1,0:T(8,128)(2,1)S(1)}, bf16[96,2432]{1,0:T(8,128)(2,1)S(1)}, u32[]{:S(2)}, u32[]{:S(2)}) %collective-permute-start.67) | collective-permute-done | bytes 466976 | tf_op jit(solution)/shard_map/ppermute | solution.py:593
  399.6 2.3 copy-done.4
  408.3 2.3 copy-done.6
  416.7 3.0 collective-permute-done.72
  422.9 2.8 collective-permute-done.69.refs_6_
  426.3 4.2 collective-permute-done.73
  437.7 6.5 %collective-permute-done.77 = bf16[96,2432]{1,0:T(8,128)(2,1)S(1)} collective-permute-done((bf16[96,2432]{1,0:T(8,128)(2,1)}, bf16[96,2432]{1,0:T(8,128)(2,1)S(1)}, u32[]{:S(2)}, u32[]{:S(2)}) %collective-permute-start.77) | collective-permute-done | bytes 466976 | tf_op jit(solution)/shard_map/ppermute | solution.py:548
  452.9 9.1 %collective-permute-done.81 = f32[22,768]{1,0:T(8,128)S(1)} collective-permute-done((f32[22,768]{1,0:T(8,128)S(1)}, f32[22,768]{1,0:T(8,128)S(1)}, u32[]{:S(2)}, u32[]{:S(2)}) %collective-permute-start.81) | collective-permute-done | bytes 67616 | tf_op jit(solution)/shard_map/ppermute | solution.py:551
  464.4 2.8 shard_map.225
  471.6 8.3 %collective-permute-done.84 = f32[22,768]{1,0:T(8,128)S(1)} collective-permute-done((f32[22,768]{1,0:T(8,128)S(1)}, f32[22,768]{1,0:T(8,128)S(1)}, u32[]{:S(2)}, u32[]{:S(2)}) %collective-permute-start.84) | collective-permute-done | bytes 67616 | tf_op jit(solution)/shard_map/ppermute | solution.py:604
  486.6 3.8 collective-permute-start.88
  491.5 9.1 %collective-permute-done.88 = f32[22,768]{1,0:T(8,128)S(1)} collective-permute-done((f32[22,768]{1,0:T(8,128)S(1)}, f32[22,768]{1,0:T(8,128)S(1)}, u32[]{:S(2)}, u32[]{:S(2)}) %collective-permute-start.88) | collective-permute-done | bytes 67616 | tf_op jit(solution)/shard_map/ppermute | solution.py:604
  514.1 2.3 copy-done.10
  520.5 10.3 %collective-permute-done.93.refs_6_ = bf16[96,2432]{1,0:T(8,128)(2,1)S(1)} collective-permute-done((bf16[96,2432]{1,0:T(8,128)(2,1)S(1)}, bf16[96,2432]{1,0:T(8,128)(2,1)S(1)}, u32[]{:S(2)}, u32[]{:S(2)}) %collective-permute-start.93) | collective-permute-done | bytes 466976 | tf_op jit(solution)/shard_map/ppermute | solution.py:593
  533.8 19.5 %collective-permute-done.95 = bf16[192,2432]{1,0:T(8,128)(2,1)S(1)} collective-permute-done((bf16[192,2432]{1,0:T(8,128)(2,1)S(1)}, bf16[192,2432]{1,0:T(8,128)(2,1)S(1)}, u32[]{:S(2)}, u32[]{:S(2)}) %collective-permute-start.95) | collective-permute-done | bytes 933920 | tf_op jit(solution)/shard_map/ppermute | solution.py:548
  553.6 2.5 collective-permute-done.97.refs_3_
  556.1 4.6 shard_map.230
  (729 shorter events, 211.2 us)
Async XLA Ops:
  16.8 12.6 %collective-permute-start.4 = (bf16[96,2432]{1,0:T(8,128)(2,1)}, bf16[96,2432]{1,0:T(8,128)(2,1)}, u32[]{:S(2)}, u32[]{:S(2)}) collective-permute-start(bf16[96,2432]{1,0:T(8,128)(2,1)} %get-tuple-element.441), channel_id=1, source_target_pairs={{0,2},{4,0},{8,4},{12,8},{14,12},{10,14},{6,10},{2,6},{1,3},{5,1},... | collective-permute-start | bytes 1400840 | tf_op jit(solution)/shard_map/ppermute | solution.py:579
  18.8 11.7 %collective-permute-start.3 = (bf16[96,2432]{1,0:T(8,128)(2,1)S(1)}, bf16[96,2432]{1,0:T(8,128)(2,1)}, u32[]{:S(2)}, u32[]{:S(2)}) collective-permute-start(bf16[96,2432]{1,0:T(8,128)(2,1)S(1)} %get-tuple-element.442), channel_id=1, source_target_pairs={{2,0},{0,4},{4,8},{8,12},{12,14},{14,10},{10,6},{6,2},{3,1},{1,5},... | collective-permute-start | bytes 1400840 | tf_op jit(solution)/shard_map/ppermute | solution.py:579
  20.3 18.5 %collective-permute-start.7 = (bf16[256,1536]{1,0:T(8,128)(2,1)S(1)}, bf16[256,1536]{1,0:T(8,128)(2,1)S(1)}, u32[]{:S(2)}, u32[]{:S(2)}) collective-permute-start(bf16[256,1536]{1,0:T(8,128)(2,1)S(1)} %copy-done.75), channel_id=1, source_target_pairs={{0,1},{1,0},{2,3},{3,2},{4,5},{5,4},{6,7},{7,6},{8,9},{9,8},{10,11... | collective-permute-start | bytes 2359304 | tf_op jit(solution)/shard_map/ppermute | solution.py:548
  30.5 10.9 %collective-permute-start.5 = (bf16[96,2432]{1,0:T(8,128)(2,1)}, bf16[96,2432]{1,0:T(8,128)(2,1)S(1)}, u32[]{:S(2)}, u32[]{:S(2)}) collective-permute-start(bf16[96,2432]{1,0:T(8,128)(2,1)} %collective-permute-done.3.refs_1_), channel_id=1, source_target_pairs={{2,0},{0,4},{4,8},{8,12},{12,14},{14,10},{10,6},{6,2},{3,1},{1,5},... | collective-permute-start | bytes 1400840 | tf_op jit(solution)/shard_map/ppermute | solution.py:579
  31.1 11.0 %collective-permute-start.6 = (bf16[96,2432]{1,0:T(8,128)(2,1)}, bf16[96,2432]{1,0:T(8,128)(2,1)}, u32[]{:S(2)}, u32[]{:S(2)}) collective-permute-start(bf16[96,2432]{1,0:T(8,128)(2,1)} %collective-permute-done.4.refs_2_), channel_id=1, source_target_pairs={{0,2},{4,0},{8,4},{12,8},{14,12},{10,14},{6,10},{2,6},{1,3},{5,1},... | collective-permute-start | bytes 1400840 | tf_op jit(solution)/shard_map/ppermute | solution.py:579
  44.8 22.6 %collective-permute-start.16 = (bf16[256,1536]{1,0:T(8,128)(2,1)S(1)}, bf16[256,1536]{1,0:T(8,128)(2,1)}, u32[]{:S(2)}, u32[]{:S(2)}) collective-permute-start(bf16[256,1536]{1,0:T(8,128)(2,1)S(1)} %copy-done.103), channel_id=1, source_target_pairs={{0,1},{1,0},{2,3},{3,2},{4,5},{5,4},{6,7},{7,6},{8,9},{9,8},{10,11... | collective-permute-start | bytes 2359304 | tf_op jit(solution)/shard_map/ppermute | solution.py:548
  67.5 11.1 %collective-permute-start.15 = (bf16[96,2432]{1,0:T(8,128)(2,1)}, bf16[96,2432]{1,0:T(8,128)(2,1)}, u32[]{:S(2)}, u32[]{:S(2)}) collective-permute-start(bf16[96,2432]{1,0:T(8,128)(2,1)} %collective-permute-done.13.refs_8_), channel_id=1, source_target_pairs={{0,2},{4,0},{8,4},{12,8},{14,12},{10,14},{6,10},{2,6},{1,3},{5,1},... | collective-permute-start | bytes 1400840 | tf_op jit(solution)/shard_map/ppermute | solution.py:579
  78.6 12.9 %collective-permute-start.17 = (bf16[96,2432]{1,0:T(8,128)(2,1)}, bf16[96,2432]{1,0:T(8,128)(2,1)}, u32[]{:S(2)}, u32[]{:S(2)}) collective-permute-start(bf16[96,2432]{1,0:T(8,128)(2,1)} %collective-permute-done.14.refs_9_), channel_id=1, source_target_pairs={{2,0},{0,4},{4,8},{8,12},{12,14},{14,10},{10,6},{6,2},{3,1},{1,5},... | collective-permute-start | bytes 1400840 | tf_op jit(solution)/shard_map/ppermute | solution.py:579
  81.0 13.3 %collective-permute-start.18 = (bf16[96,2432]{1,0:T(8,128)(2,1)}, bf16[96,2432]{1,0:T(8,128)(2,1)}, u32[]{:S(2)}, u32[]{:S(2)}) collective-permute-start(bf16[96,2432]{1,0:T(8,128)(2,1)} %collective-permute-done.15.refs_10_), channel_id=1, source_target_pairs={{0,2},{4,0},{8,4},{12,8},{14,12},{10,14},{6,10},{2,6},{1,3},{5,1},... | collective-permute-start | bytes 1400840 | tf_op jit(solution)/shard_map/ppermute | solution.py:579
  94.3 10.6 %collective-permute-start.20 = (bf16[96,2432]{1,0:T(8,128)(2,1)}, bf16[96,2432]{1,0:T(8,128)(2,1)}, u32[]{:S(2)}, u32[]{:S(2)}) collective-permute-start(bf16[96,2432]{1,0:T(8,128)(2,1)} %collective-permute-done.18.refs_12_), channel_id=1, source_target_pairs={{0,2},{4,0},{8,4},{12,8},{14,12},{10,14},{6,10},{2,6},{1,3},{5,1},... | collective-permute-start | bytes 1400840 | tf_op jit(solution)/shard_map/ppermute | solution.py:579
  96.4 15.8 %collective-permute-start.11 = (bf16[96,2432]{1,0:T(8,128)(2,1)S(1)}, bf16[96,2432]{1,0:T(8,128)(2,1)}, u32[]{:S(2)}, u32[]{:S(2)}) collective-permute-start(bf16[96,2432]{1,0:T(8,128)(2,1)S(1)} %get-tuple-element.443), channel_id=1, source_target_pairs={{0,2},{4,0},{8,4},{12,8},{14,12},{10,14},{6,10},{2,6},{1,3},{5,1},... | collective-permute-start | bytes 1400840 | tf_op jit(solution)/shard_map/ppermute | solution.py:579
  96.5 15.8 %collective-permute-start.10 = (bf16[96,2432]{1,0:T(8,128)(2,1)S(1)}, bf16[96,2432]{1,0:T(8,128)(2,1)}, u32[]{:S(2)}, u32[]{:S(2)}) collective-permute-start(bf16[96,2432]{1,0:T(8,128)(2,1)S(1)} %get-tuple-element.444), channel_id=1, source_target_pairs={{2,0},{0,4},{4,8},{8,12},{12,14},{14,10},{10,6},{6,2},{3,1},{1,5},... | collective-permute-start | bytes 1400840 | tf_op jit(solution)/shard_map/ppermute | solution.py:579
  114.0 10.7 %collective-permute-start.23 = (f32[512,64]{1,0:T(8,128)S(1)}, f32[512,64]{1,0:T(8,128)S(1)}, u32[]{:S(2)}, u32[]{:S(2)}) collective-permute-start(f32[512,64]{1,0:T(8,128)S(1)} %copy.272), channel_id=1, source_target_pairs={{0,1},{1,0},{2,3},{3,2},{4,5},{5,4},{6,7},{7,6},{8,9},{9,8},{10,11... | collective-permute-start | bytes 393224 | tf_op jit(solution)/shard_map/ppermute | solution.py:548
  125.6 13.4 %collective-permute-start.24 = (bf16[96,2432]{1,0:T(8,128)(2,1)S(1)}, bf16[96,2432]{1,0:T(8,128)(2,1)S(1)}, u32[]{:S(2)}, u32[]{:S(2)}) collective-permute-start(bf16[96,2432]{1,0:T(8,128)(2,1)S(1)} %collective-permute-done.21.refs_3_), channel_id=1, source_target_pairs={{2,0},{0,4},{4,8},{8,12},{12,14},{14,10},{10,6},{6,2},{3,1},{1,5},... | collective-permute-start | bytes 1400840 | tf_op jit(solution)/shard_map/ppermute | solution.py:579
  126.7 13.2 %collective-permute-start.25 = (bf16[96,2432]{1,0:T(8,128)(2,1)}, bf16[96,2432]{1,0:T(8,128)(2,1)S(1)}, u32[]{:S(2)}, u32[]{:S(2)}) collective-permute-start(bf16[96,2432]{1,0:T(8,128)(2,1)} %collective-permute-done.22.refs_4_), channel_id=1, source_target_pairs={{0,2},{4,0},{8,4},{12,8},{14,12},{10,14},{6,10},{2,6},{1,3},{5,1},... | collective-permute-start | bytes 1400840 | tf_op jit(solution)/shard_map/ppermute | solution.py:579
  139.9 12.0 %collective-permute-start.27 = (bf16[96,2432]{1,0:T(8,128)(2,1)S(1)}, bf16[96,2432]{1,0:T(8,128)(2,1)S(1)}, u32[]{:S(2)}, u32[]{:S(2)}) collective-permute-start(bf16[96,2432]{1,0:T(8,128)(2,1)S(1)} %collective-permute-done.24.refs_5_), channel_id=1, source_target_pairs={{2,0},{0,4},{4,8},{8,12},{12,14},{14,10},{10,6},{6,2},{3,1},{1,5},... | collective-permute-start | bytes 1400840 | tf_op jit(solution)/shard_map/ppermute | solution.py:579
  140.5 11.7 %collective-permute-start.28 = (bf16[96,2432]{1,0:T(8,128)(2,1)S(1)}, bf16[96,2432]{1,0:T(8,128)(2,1)S(1)}, u32[]{:S(2)}, u32[]{:S(2)}) collective-permute-start(bf16[96,2432]{1,0:T(8,128)(2,1)S(1)} %collective-permute-done.25.refs_6_), channel_id=1, source_target_pairs={{0,2},{4,0},{8,4},{12,8},{14,12},{10,14},{6,10},{2,6},{1,3},{5,1},... | collective-permute-start | bytes 1400840 | tf_op jit(solution)/shard_map/ppermute | solution.py:579
  152.7 15.7 %collective-permute-start.37 = (bf16[768,768]{1,0:T(8,128)(2,1)S(1)}, bf16[768,768]{1,0:T(8,128)(2,1)S(1)}, u32[]{:S(2)}, u32[]{:S(2)}) collective-permute-start(bf16[768,768]{1,0:T(8,128)(2,1)S(1)} %get-tuple-element.432), channel_id=1, source_target_pairs={{0,16},{16,0},{1,17},{17,1},{2,18},{18,2},{3,19},{19,3},{4,20},{20... | collective-permute-start | bytes 3538952 | tf_op jit(solution)/shard_map/ppermute | solution.py:545
  153.3 12.7 %collective-permute-start.31 = (bf16[96,2432]{1,0:T(8,128)(2,1)S(1)}, bf16[96,2432]{1,0:T(8,128)(2,1)S(1)}, u32[]{:S(2)}, u32[]{:S(2)}) collective-permute-start(bf16[96,2432]{1,0:T(8,128)(2,1)S(1)} %collective-permute-done.27.refs_7_), channel_id=1, source_target_pairs={{2,0},{0,4},{4,8},{8,12},{12,14},{14,10},{10,6},{6,2},{3,1},{1,5},... | collective-permute-start | bytes 1400840 | tf_op jit(solution)/shard_map/ppermute | solution.py:579
  154.0 12.4 %collective-permute-start.32 = (bf16[96,2432]{1,0:T(8,128)(2,1)S(1)}, bf16[96,2432]{1,0:T(8,128)(2,1)S(1)}, u32[]{:S(2)}, u32[]{:S(2)}) collective-permute-start(bf16[96,2432]{1,0:T(8,128)(2,1)S(1)} %collective-permute-done.28.refs_8_), channel_id=1, source_target_pairs={{0,2},{4,0},{8,4},{12,8},{14,12},{10,14},{6,10},{2,6},{1,3},{5,1},... | collective-permute-start | bytes 1400840 | tf_op jit(solution)/shard_map/ppermute | solution.py:579
  156.7 22.2 %collective-permute-start.36 = (bf16[512,768]{1,0:T(8,128)(2,1)S(1)}, bf16[512,768]{1,0:T(8,128)(2,1)S(1)}, u32[]{:S(2)}, u32[]{:S(2)}) collective-permute-start(bf16[512,768]{1,0:T(8,128)(2,1)S(1)} %convolution_convert_fusion.4), channel_id=1, source_target_pairs={{0,1},{1,0},{2,3},{3,2},{4,5},{5,4},{6,7},{7,6},{8,9},{9,8},{10,11... | collective-permute-start | bytes 2359304 | tf_op jit(solution)/shard_map/ppermute | solution.py:548
  166.4 11.5 %collective-permute-start.34 = (bf16[96,2432]{1,0:T(8,128)(2,1)S(1)}, bf16[96,2432]{1,0:T(8,128)(2,1)S(1)}, u32[]{:S(2)}, u32[]{:S(2)}) collective-permute-start(bf16[96,2432]{1,0:T(8,128)(2,1)S(1)} %collective-permute-done.31.refs_9_), channel_id=1, source_target_pairs={{2,0},{0,4},{4,8},{8,12},{12,14},{14,10},{10,6},{6,2},{3,1},{1,5},... | collective-permute-start | bytes 1400840 | tf_op jit(solution)/shard_map/ppermute | solution.py:579
  167.2 11.7 %collective-permute-start.35 = (bf16[96,2432]{1,0:T(8,128)(2,1)S(1)}, bf16[96,2432]{1,0:T(8,128)(2,1)}, u32[]{:S(2)}, u32[]{:S(2)}) collective-permute-start(bf16[96,2432]{1,0:T(8,128)(2,1)S(1)} %collective-permute-done.32.refs_10_), channel_id=1, source_target_pairs={{0,2},{4,0},{8,4},{12,8},{14,12},{10,14},{6,10},{2,6},{1,3},{5,1},... | collective-permute-start | bytes 1400840 | tf_op jit(solution)/shard_map/ppermute | solution.py:579
  179.8 25.0 %collective-permute-start.38 = (bf16[512,768]{1,0:T(8,128)(2,1)S(1)}, bf16[512,768]{1,0:T(8,128)(2,1)S(1)}, u32[]{:S(2)}, u32[]{:S(2)}) collective-permute-start(bf16[512,768]{1,0:T(8,128)(2,1)S(1)} %add_convert_fusion.1), channel_id=1, source_target_pairs={{0,16},{16,0},{1,17},{17,1},{2,18},{18,2},{3,19},{19,3},{4,20},{20... | collective-permute-start | bytes 2359304 | tf_op jit(solution)/shard_map/ppermute | solution.py:545
  179.8 13.2 %collective-permute-start.39 = (bf16[96,2432]{1,0:T(8,128)(2,1)S(1)}, bf16[96,2432]{1,0:T(8,128)(2,1)}, u32[]{:S(2)}, u32[]{:S(2)}) collective-permute-start(bf16[96,2432]{1,0:T(8,128)(2,1)S(1)} %collective-permute-done.34.refs_11_), channel_id=1, source_target_pairs={{2,0},{0,4},{4,8},{8,12},{12,14},{14,10},{10,6},{6,2},{3,1},{1,5},... | collective-permute-start | bytes 1400840 | tf_op jit(solution)/shard_map/ppermute | solution.py:579
  181.2 13.1 %collective-permute-start.40 = (bf16[96,2432]{1,0:T(8,128)(2,1)}, bf16[96,2432]{1,0:T(8,128)(2,1)}, u32[]{:S(2)}, u32[]{:S(2)}) collective-permute-start(bf16[96,2432]{1,0:T(8,128)(2,1)} %collective-permute-done.35.refs_12_), channel_id=1, source_target_pairs={{0,2},{4,0},{8,4},{12,8},{14,12},{10,14},{6,10},{2,6},{1,3},{5,1},... | collective-permute-start | bytes 1400840 | tf_op jit(solution)/shard_map/ppermute | solution.py:579
  204.8 22.1 %collective-permute-start.43 = (bf16[768,768]{1,0:T(8,128)(2,1)}, bf16[768,768]{1,0:T(8,128)(2,1)}, u32[]{:S(2)}, u32[]{:S(2)}) collective-permute-start(bf16[768,768]{1,0:T(8,128)(2,1)} %get-tuple-element.430), channel_id=1, source_target_pairs={{0,16},{16,0},{1,17},{17,1},{2,18},{18,2},{3,19},{19,3},{4,20},{20... | collective-permute-start | bytes 3538952 | tf_op jit(solution)/shard_map/ppermute | solution.py:545
  275.8 20.0 %collective-permute-start.52 = (bf16[512,768]{1,0:T(8,128)(2,1)}, bf16[512,768]{1,0:T(8,128)(2,1)}, u32[]{:S(2)}, u32[]{:S(2)}) collective-permute-start(bf16[512,768]{1,0:T(8,128)(2,1)} %add_convert_fusion), channel_id=1, source_target_pairs={{0,1},{1,0},{2,3},{3,2},{4,5},{5,4},{6,7},{7,6},{8,9},{9,8},{10,11... | collective-permute-start | bytes 2359304 | tf_op jit(solution)/shard_map/ppermute | solution.py:548
  279.1 12.6 %collective-permute-start.49 = (bf16[96,2432]{1,0:T(8,128)(2,1)S(1)}, bf16[96,2432]{1,0:T(8,128)(2,1)S(1)}, u32[]{:S(2)}, u32[]{:S(2)}) collective-permute-start(bf16[96,2432]{1,0:T(8,128)(2,1)S(1)} %get-tuple-element.299), channel_id=1, source_target_pairs={{2,0},{0,4},{4,8},{8,12},{12,14},{14,10},{10,6},{6,2},{3,1},{1,5},... | collective-permute-start | bytes 1400840 | tf_op jit(solution)/shard_map/ppermute | solution.py:593
  280.9 12.4 %collective-permute-start.50 = (bf16[96,2432]{1,0:T(8,128)(2,1)S(1)}, bf16[96,2432]{1,0:T(8,128)(2,1)S(1)}, u32[]{:S(2)}, u32[]{:S(2)}) collective-permute-start(bf16[96,2432]{1,0:T(8,128)(2,1)S(1)} %get-tuple-element.300), channel_id=1, source_target_pairs={{0,2},{4,0},{8,4},{12,8},{14,12},{10,14},{6,10},{2,6},{1,3},{5,1},... | collective-permute-start | bytes 1400840 | tf_op jit(solution)/shard_map/ppermute | solution.py:593
  298.4 10.8 %collective-permute-start.55 = (f32[512,768]{1,0:T(8,128)}, f32[512,768]{1,0:T(8,128)}, u32[]{:S(2)}, u32[]{:S(2)}) collective-permute-start(f32[512,768]{1,0:T(8,128)} %convert_add_fusion), channel_id=1, source_target_pairs={{0,16},{16,0},{1,17},{17,1},{2,18},{18,2},{3,19},{19,3},{4,20},{20... | collective-permute-start | bytes 4718600 | tf_op jit(solution)/shard_map/ppermute | solution.py:545
  307.1 13.2 %collective-permute-start.53 = (bf16[96,2432]{1,0:T(8,128)(2,1)S(1)}, bf16[96,2432]{1,0:T(8,128)(2,1)S(1)}, u32[]{:S(2)}, u32[]{:S(2)}) collective-permute-start(bf16[96,2432]{1,0:T(8,128)(2,1)S(1)} %get-tuple-element.304), channel_id=1, source_target_pairs={{2,0},{0,4},{4,8},{8,12},{12,14},{14,10},{10,6},{6,2},{3,1},{1,5},... | collective-permute-start | bytes 1400840 | tf_op jit(solution)/shard_map/ppermute | solution.py:593
  308.9 12.8 %collective-permute-start.54 = (bf16[96,2432]{1,0:T(8,128)(2,1)S(1)}, bf16[96,2432]{1,0:T(8,128)(2,1)S(1)}, u32[]{:S(2)}, u32[]{:S(2)}) collective-permute-start(bf16[96,2432]{1,0:T(8,128)(2,1)S(1)} %get-tuple-element.305), channel_id=1, source_target_pairs={{0,2},{4,0},{8,4},{12,8},{14,12},{10,14},{6,10},{2,6},{1,3},{5,1},... | collective-permute-start | bytes 1400840 | tf_op jit(solution)/shard_map/ppermute | solution.py:593
  323.8 13.1 %collective-permute-start.56 = (bf16[96,2432]{1,0:T(8,128)(2,1)S(1)}, bf16[96,2432]{1,0:T(8,128)(2,1)S(1)}, u32[]{:S(2)}, u32[]{:S(2)}) collective-permute-start(bf16[96,2432]{1,0:T(8,128)(2,1)S(1)} %get-tuple-element.309), channel_id=1, source_target_pairs={{2,0},{0,4},{4,8},{8,12},{12,14},{14,10},{10,6},{6,2},{3,1},{1,5},... | collective-permute-start | bytes 1400840 | tf_op jit(solution)/shard_map/ppermute | solution.py:593
  325.3 12.8 %collective-permute-start.57 = (bf16[96,2432]{1,0:T(8,128)(2,1)S(1)}, bf16[96,2432]{1,0:T(8,128)(2,1)S(1)}, u32[]{:S(2)}, u32[]{:S(2)}) collective-permute-start(bf16[96,2432]{1,0:T(8,128)(2,1)S(1)} %get-tuple-element.310), channel_id=1, source_target_pairs={{0,2},{4,0},{8,4},{12,8},{14,12},{10,14},{6,10},{2,6},{1,3},{5,1},... | collective-permute-start | bytes 1400840 | tf_op jit(solution)/shard_map/ppermute | solution.py:593
  344.9 12.8 %collective-permute-start.59 = (bf16[96,2432]{1,0:T(8,128)(2,1)S(1)}, bf16[96,2432]{1,0:T(8,128)(2,1)S(1)}, u32[]{:S(2)}, u32[]{:S(2)}) collective-permute-start(bf16[96,2432]{1,0:T(8,128)(2,1)S(1)} %get-tuple-element.315), channel_id=1, source_target_pairs={{2,0},{0,4},{4,8},{8,12},{12,14},{14,10},{10,6},{6,2},{3,1},{1,5},... | collective-permute-start | bytes 1400840 | tf_op jit(solution)/shard_map/ppermute | solution.py:593
  346.0 12.0 %collective-permute-start.60 = (bf16[96,2432]{1,0:T(8,128)(2,1)S(1)}, bf16[96,2432]{1,0:T(8,128)(2,1)S(1)}, u32[]{:S(2)}, u32[]{:S(2)}) collective-permute-start(bf16[96,2432]{1,0:T(8,128)(2,1)S(1)} %get-tuple-element.316), channel_id=1, source_target_pairs={{0,2},{4,0},{8,4},{12,8},{14,12},{10,14},{6,10},{2,6},{1,3},{5,1},... | collective-permute-start | bytes 1400840 | tf_op jit(solution)/shard_map/ppermute | solution.py:593
  359.0 13.1 %collective-permute-start.61 = (bf16[96,2432]{1,0:T(8,128)(2,1)S(1)}, bf16[96,2432]{1,0:T(8,128)(2,1)S(1)}, u32[]{:S(2)}, u32[]{:S(2)}) collective-permute-start(bf16[96,2432]{1,0:T(8,128)(2,1)S(1)} %get-tuple-element.329), channel_id=1, source_target_pairs={{2,0},{0,4},{4,8},{8,12},{12,14},{14,10},{10,6},{6,2},{3,1},{1,5},... | collective-permute-start | bytes 1400840 | tf_op jit(solution)/shard_map/ppermute | solution.py:593
  359.8 12.8 %collective-permute-start.62 = (bf16[96,2432]{1,0:T(8,128)(2,1)S(1)}, bf16[96,2432]{1,0:T(8,128)(2,1)S(1)}, u32[]{:S(2)}, u32[]{:S(2)}) collective-permute-start(bf16[96,2432]{1,0:T(8,128)(2,1)S(1)} %get-tuple-element.330), channel_id=1, source_target_pairs={{0,2},{4,0},{8,4},{12,8},{14,12},{10,14},{6,10},{2,6},{1,3},{5,1},... | collective-permute-start | bytes 1400840 | tf_op jit(solution)/shard_map/ppermute | solution.py:593
  373.9 11.8 %collective-permute-start.64 = (bf16[96,2432]{1,0:T(8,128)(2,1)S(1)}, bf16[96,2432]{1,0:T(8,128)(2,1)S(1)}, u32[]{:S(2)}, u32[]{:S(2)}) collective-permute-start(bf16[96,2432]{1,0:T(8,128)(2,1)S(1)} %get-tuple-element.335), channel_id=1, source_target_pairs={{2,0},{0,4},{4,8},{8,12},{12,14},{14,10},{10,6},{6,2},{3,1},{1,5},... | collective-permute-start | bytes 1400840 | tf_op jit(solution)/shard_map/ppermute | solution.py:593
  374.6 11.6 %collective-permute-start.65 = (bf16[96,2432]{1,0:T(8,128)(2,1)S(1)}, bf16[96,2432]{1,0:T(8,128)(2,1)S(1)}, u32[]{:S(2)}, u32[]{:S(2)}) collective-permute-start(bf16[96,2432]{1,0:T(8,128)(2,1)S(1)} %get-tuple-element.336), channel_id=1, source_target_pairs={{0,2},{4,0},{8,4},{12,8},{14,12},{10,14},{6,10},{2,6},{1,3},{5,1},... | collective-permute-start | bytes 1400840 | tf_op jit(solution)/shard_map/ppermute | solution.py:593
  387.2 10.6 %collective-permute-start.67 = (bf16[96,2432]{1,0:T(8,128)(2,1)S(1)}, bf16[96,2432]{1,0:T(8,128)(2,1)S(1)}, u32[]{:S(2)}, u32[]{:S(2)}) collective-permute-start(bf16[96,2432]{1,0:T(8,128)(2,1)S(1)} %get-tuple-element.340), channel_id=1, source_target_pairs={{2,0},{0,4},{4,8},{8,12},{12,14},{14,10},{10,6},{6,2},{3,1},{1,5},... | collective-permute-start | bytes 1400840 | tf_op jit(solution)/shard_map/ppermute | solution.py:593
  399.4 15.5 %collective-permute-start.71 = (f32[512,768]{1,0:T(8,128)}, f32[512,768]{1,0:T(8,128)}, u32[]{:S(2)}, u32[]{:S(2)}) collective-permute-start(f32[512,768]{1,0:T(8,128)} %constant_dynamic-slice_fusion), channel_id=1, source_target_pairs={{0,16},{16,0},{1,17},{17,1},{2,18},{18,2},{3,19},{19,3},{4,20},{20... | collective-permute-start | bytes 4718600 | tf_op jit(solution)/shard_map/ppermute | solution.py:545
  406.5 13.1 %collective-permute-start.72 = (bf16[96,2432]{1,0:T(8,128)(2,1)S(1)}, bf16[96,2432]{1,0:T(8,128)(2,1)S(1)}, u32[]{:S(2)}, u32[]{:S(2)}) collective-permute-start(bf16[96,2432]{1,0:T(8,128)(2,1)S(1)} %get-tuple-element.440), channel_id=1, source_target_pairs={{0,1},{1,0},{2,3},{3,2},{4,5},{5,4},{6,7},{7,6},{8,9},{9,8},{10,11... | collective-permute-start | bytes 1400840 | tf_op jit(solution)/shard_map/ppermute | solution.py:548
  412.9 12.8 %collective-permute-start.69 = (bf16[96,2432]{1,0:T(8,128)(2,1)S(1)}, bf16[96,2432]{1,0:T(8,128)(2,1)S(1)}, u32[]{:S(2)}, u32[]{:S(2)}) collective-permute-start(bf16[96,2432]{1,0:T(8,128)(2,1)S(1)} %get-tuple-element.352), channel_id=1, source_target_pairs={{2,0},{0,4},{4,8},{8,12},{12,14},{14,10},{10,6},{6,2},{3,1},{1,5},... | collective-permute-start | bytes 1400840 | tf_op jit(solution)/shard_map/ppermute | solution.py:593
  413.8 12.5 %collective-permute-start.70 = (bf16[96,2432]{1,0:T(8,128)(2,1)S(1)}, bf16[96,2432]{1,0:T(8,128)(2,1)S(1)}, u32[]{:S(2)}, u32[]{:S(2)}) collective-permute-start(bf16[96,2432]{1,0:T(8,128)(2,1)S(1)} %get-tuple-element.353), channel_id=1, source_target_pairs={{0,2},{4,0},{8,4},{12,8},{14,12},{10,14},{6,10},{2,6},{1,3},{5,1},... | collective-permute-start | bytes 1400840 | tf_op jit(solution)/shard_map/ppermute | solution.py:593
  419.7 10.8 %collective-permute-start.73 = (bf16[256,768]{1,0:T(8,128)(2,1)S(1)}, bf16[256,768]{1,0:T(8,128)(2,1)S(1)}, u32[]{:S(2)}, u32[]{:S(2)}) collective-permute-start(bf16[256,768]{1,0:T(8,128)(2,1)S(1)} %dynamic-slice_convert_fusion.1), channel_id=1, source_target_pairs={{0,1},{1,0},{2,3},{3,2},{4,5},{5,4},{6,7},{7,6},{8,9},{9,8},{10,11... | collective-permute-start | bytes 1179656 | tf_op jit(solution)/shard_map/ppermute | solution.py:548
  430.9 13.4 %collective-permute-start.77 = (bf16[96,2432]{1,0:T(8,128)(2,1)}, bf16[96,2432]{1,0:T(8,128)(2,1)S(1)}, u32[]{:S(2)}, u32[]{:S(2)}) collective-permute-start(bf16[96,2432]{1,0:T(8,128)(2,1)} %get-tuple-element.439), channel_id=1, source_target_pairs={{0,1},{1,0},{2,3},{3,2},{4,5},{5,4},{6,7},{7,6},{8,9},{9,8},{10,11... | collective-permute-start | bytes 1400840 | tf_op jit(solution)/shard_map/ppermute | solution.py:548
  433.4 12.9 %collective-permute-start.74 = (bf16[96,2432]{1,0:T(8,128)(2,1)S(1)}, bf16[96,2432]{1,0:T(8,128)(2,1)S(1)}, u32[]{:S(2)}, u32[]{:S(2)}) collective-permute-start(bf16[96,2432]{1,0:T(8,128)(2,1)S(1)} %get-tuple-element.360), channel_id=1, source_target_pairs={{2,0},{0,4},{4,8},{8,12},{12,14},{14,10},{10,6},{6,2},{3,1},{1,5},... | collective-permute-start | bytes 1400840 | tf_op jit(solution)/shard_map/ppermute | solution.py:593
  434.3 12.5 %collective-permute-start.75 = (bf16[96,2432]{1,0:T(8,128)(2,1)S(1)}, bf16[96,2432]{1,0:T(8,128)(2,1)S(1)}, u32[]{:S(2)}, u32[]{:S(2)}) collective-permute-start(bf16[96,2432]{1,0:T(8,128)(2,1)S(1)} %get-tuple-element.361), channel_id=1, source_target_pairs={{0,2},{4,0},{8,4},{12,8},{14,12},{10,14},{6,10},{2,6},{1,3},{5,1},... | collective-permute-start | bytes 1400840 | tf_op jit(solution)/shard_map/ppermute | solution.py:593
  448.6 13.5 %collective-permute-start.78 = (bf16[96,2432]{1,0:T(8,128)(2,1)}, bf16[96,2432]{1,0:T(8,128)(2,1)}, u32[]{:S(2)}, u32[]{:S(2)}) collective-permute-start(bf16[96,2432]{1,0:T(8,128)(2,1)} %get-tuple-element.365), channel_id=1, source_target_pairs={{2,0},{0,4},{4,8},{8,12},{12,14},{14,10},{10,6},{6,2},{3,1},{1,5},... | collective-permute-start | bytes 1400840 | tf_op jit(solution)/shard_map/ppermute | solution.py:593
  449.2 12.9 %collective-permute-start.79 = (bf16[96,2432]{1,0:T(8,128)(2,1)}, bf16[96,2432]{1,0:T(8,128)(2,1)}, u32[]{:S(2)}, u32[]{:S(2)}) collective-permute-start(bf16[96,2432]{1,0:T(8,128)(2,1)} %get-tuple-element.366), channel_id=1, source_target_pairs={{0,2},{4,0},{8,4},{12,8},{14,12},{10,14},{6,10},{2,6},{1,3},{5,1},... | collective-permute-start | bytes 1400840 | tf_op jit(solution)/shard_map/ppermute | solution.py:593
  450.6 11.4 %collective-permute-start.80 = (bf16[256,768]{1,0:T(8,128)(2,1)S(1)}, bf16[256,768]{1,0:T(8,128)(2,1)}, u32[]{:S(2)}, u32[]{:S(2)}) collective-permute-start(bf16[256,768]{1,0:T(8,128)(2,1)S(1)} %dynamic-slice_convert_fusion), channel_id=1, source_target_pairs={{0,1},{1,0},{2,3},{3,2},{4,5},{5,4},{6,7},{7,6},{8,9},{9,8},{10,11... | collective-permute-start | bytes 1179656 | tf_op jit(solution)/shard_map/ppermute | solution.py:548
  451.6 10.4 %collective-permute-start.81 = (f32[22,768]{1,0:T(8,128)S(1)}, f32[22,768]{1,0:T(8,128)S(1)}, u32[]{:S(2)}, u32[]{:S(2)}) collective-permute-start(f32[22,768]{1,0:T(8,128)S(1)} %concatenate.179), channel_id=1, source_target_pairs={{0,2},{2,0},{4,6},{6,4},{8,10},{10,8},{12,14},{14,12},{1,3},{3,1},... | collective-permute-start | bytes 202760 | tf_op jit(solution)/shard_map/ppermute | solution.py:551
  467.3 12.7 %collective-permute-start.82 = (bf16[96,2432]{1,0:T(8,128)(2,1)}, bf16[96,2432]{1,0:T(8,128)(2,1)}, u32[]{:S(2)}, u32[]{:S(2)}) collective-permute-start(bf16[96,2432]{1,0:T(8,128)(2,1)} %get-tuple-element.378), channel_id=1, source_target_pairs={{2,0},{0,4},{4,8},{8,12},{12,14},{14,10},{10,6},{6,2},{3,1},{1,5},... | collective-permute-start | bytes 1400840 | tf_op jit(solution)/shard_map/ppermute | solution.py:593
  467.8 12.1 %collective-permute-start.83 = (bf16[96,2432]{1,0:T(8,128)(2,1)}, bf16[96,2432]{1,0:T(8,128)(2,1)}, u32[]{:S(2)}, u32[]{:S(2)}) collective-permute-start(bf16[96,2432]{1,0:T(8,128)(2,1)} %get-tuple-element.379), channel_id=1, source_target_pairs={{0,2},{4,0},{8,4},{12,8},{14,12},{10,14},{6,10},{2,6},{1,3},{5,1},... | collective-permute-start | bytes 1400840 | tf_op jit(solution)/shard_map/ppermute | solution.py:593
  470.9 19.4 %collective-permute-start.87 = (bf16[256,768]{1,0:T(8,128)(2,1)S(1)}, bf16[256,768]{1,0:T(8,128)(2,1)S(1)}, u32[]{:S(2)}, u32[]{:S(2)}) collective-permute-start(bf16[256,768]{1,0:T(8,128)(2,1)S(1)} %add_convert_fusion.2), channel_id=1, source_target_pairs={{0,16},{16,0},{1,17},{17,1},{2,18},{18,2},{3,19},{19,3},{4,20},{20... | collective-permute-start | bytes 1179656 | tf_op jit(solution)/shard_map/ppermute | solution.py:545
  484.2 16.4 %collective-permute-start.85 = (bf16[96,2432]{1,0:T(8,128)(2,1)S(1)}, bf16[96,2432]{1,0:T(8,128)(2,1)S(1)}, u32[]{:S(2)}, u32[]{:S(2)}) collective-permute-start(bf16[96,2432]{1,0:T(8,128)(2,1)S(1)} %get-tuple-element.383), channel_id=1, source_target_pairs={{2,0},{0,4},{4,8},{8,12},{12,14},{14,10},{10,6},{6,2},{3,1},{1,5},... | collective-permute-start | bytes 1400840 | tf_op jit(solution)/shard_map/ppermute | solution.py:593
  485.6 15.1 %collective-permute-start.86 = (bf16[96,2432]{1,0:T(8,128)(2,1)S(1)}, bf16[96,2432]{1,0:T(8,128)(2,1)S(1)}, u32[]{:S(2)}, u32[]{:S(2)}) collective-permute-start(bf16[96,2432]{1,0:T(8,128)(2,1)S(1)} %get-tuple-element.384), channel_id=1, source_target_pairs={{0,2},{4,0},{8,4},{12,8},{14,12},{10,14},{6,10},{2,6},{1,3},{5,1},... | collective-permute-start | bytes 1400840 | tf_op jit(solution)/shard_map/ppermute | solution.py:593
  486.6 14.1 %collective-permute-start.88 = (f32[22,768]{1,0:T(8,128)S(1)}, f32[22,768]{1,0:T(8,128)S(1)}, u32[]{:S(2)}, u32[]{:S(2)}) collective-permute-start(f32[22,768]{1,0:T(8,128)S(1)} %add.828), channel_id=1, source_target_pairs={{0,8},{2,10},{4,12},{6,14},{8,0},{10,2},{12,4},{14,6},{1,9},{3,11}... | collective-permute-start | bytes 202760 | tf_op jit(solution)/shard_map/ppermute | solution.py:604
  518.3 12.5 %collective-permute-start.93 = (bf16[96,2432]{1,0:T(8,128)(2,1)S(1)}, bf16[96,2432]{1,0:T(8,128)(2,1)S(1)}, u32[]{:S(2)}, u32[]{:S(2)}) collective-permute-start(bf16[96,2432]{1,0:T(8,128)(2,1)S(1)} %get-tuple-element.397), channel_id=1, source_target_pairs={{2,0},{0,4},{4,8},{8,12},{12,14},{14,10},{10,6},{6,2},{3,1},{1,5},... | collective-permute-start | bytes 1400840 | tf_op jit(solution)/shard_map/ppermute | solution.py:593
  518.7 12.3 %collective-permute-start.94 = (bf16[96,2432]{1,0:T(8,128)(2,1)S(1)}, bf16[96,2432]{1,0:T(8,128)(2,1)S(1)}, u32[]{:S(2)}, u32[]{:S(2)}) collective-permute-start(bf16[96,2432]{1,0:T(8,128)(2,1)S(1)} %get-tuple-element.398), channel_id=1, source_target_pairs={{0,2},{4,0},{8,4},{12,8},{14,12},{10,14},{6,10},{2,6},{1,3},{5,1},... | collective-permute-start | bytes 1400840 | tf_op jit(solution)/shard_map/ppermute | solution.py:593
  531.7 21.6 %collective-permute-start.95 = (bf16[192,2432]{1,0:T(8,128)(2,1)S(1)}, bf16[192,2432]{1,0:T(8,128)(2,1)S(1)}, u32[]{:S(2)}, u32[]{:S(2)}) collective-permute-start(bf16[192,2432]{1,0:T(8,128)(2,1)S(1)} %shard_map.229), channel_id=1, source_target_pairs={{0,1},{1,0},{2,3},{3,2},{4,5},{5,4},{6,7},{7,6},{8,9},{9,8},{10,11... | collective-permute-start | bytes 2801672 | tf_op jit(solution)/shard_map/ppermute | solution.py:548
  533.7 19.9 %collective-permute-start.96 = (bf16[192,2432]{1,0:T(8,128)(2,1)S(1)}, bf16[192,2432]{1,0:T(8,128)(2,1)S(1)}, u32[]{:S(2)}, u32[]{:S(2)}) collective-permute-start(bf16[192,2432]{1,0:T(8,128)(2,1)S(1)} %get-tuple-element.435), channel_id=1, source_target_pairs={{0,16},{16,0},{1,17},{17,1},{2,18},{18,2},{3,19},{19,3},{4,20},{20... | collective-permute-start | bytes 2801672 | tf_op jit(solution)/shard_map/ppermute | solution.py:545
  (175 other events, 1405.1 us)

commit v4 on v3

--- a/solution.py
+++ b/solution.py
@@ -14,6 +14,7 @@
 VMEM_LIMIT = 40 * 1024 * 1024
 VMEM_ALL = 60 * 1024 * 1024
 VMEM_ADD = 16 * 1024 * 1024
+ROOM = 12
 
 
 def dot(a, b, dims=((1,), (0,)), precision=None):
@@ -373,14 +374,14 @@
     out[...] = dot(a[...], b[...], ((0,), (0,))).astype(BF16)
 
 
-def outer(a, b, block):
+def outer(a, b, block, room):
     rows, height = a.shape
     return pl.pallas_call(
         outer_kernel,
         grid=(height // block,),
         in_specs=[pl.BlockSpec((rows, block), lambda i: (0, i)), whole_spec(b.shape)],
         out_specs=pl.BlockSpec((block, b.shape[1]), lambda i: (i, 0)),
-        out_shape=jax.ShapeDtypeStruct((height, b.shape[1]), BF16),
+        out_shape=jax.ShapeDtypeStruct((room * height, b.shape[1]), BF16),
         compiler_params=pltpu.CompilerParams(vmem_limit_bytes=VMEM_LIMIT),
         cost_estimate=pl.CostEstimate(flops=0, bytes_accessed=1_000_000, transcendentals=0),
     )(a, b)
@@ -570,13 +571,25 @@
     def upper(self, shard_rows):
         return (shard_rows + 31) // 32 * 16
 
-    def gather(self, piece):
+    def gather(self, piece, apart):
         shard_rows = piece.shape[0]
         upper = self.upper(shard_rows)
         up, down = piece[:upper], piece[upper:]
         sources, starts = [piece], [ring_owner(self.at, self.line) * shard_rows]
+        mark = None
+        sent_up, sent_down = lax.ppermute(up, "fsdp", self.ahead), lax.ppermute(down, "fsdp", self.behind)
         for hop in range(1, 2 * self.line):
-            up, down = yield [lax.ppermute(up, "fsdp", self.ahead), lax.ppermute(down, "fsdp", self.behind)]
+            last = hop == 2 * self.line - 1
+            if apart:
+                up, mark = yield [sent_up, sent_up if mark is None else mark]
+                sent_up = None if last else lax.ppermute(up, "fsdp", self.ahead)
+                down, mark = lax.optimization_barrier((sent_down, mark))
+                sent_down = None if last else lax.ppermute(down, "fsdp", self.behind)
+            else:
+                up, down = yield [sent_up, sent_down]
+                if not last:
+                    sent_up = lax.ppermute(up, "fsdp", self.ahead)
+                    sent_down = lax.ppermute(down, "fsdp", self.behind)
             sources += [up, down]
             starts.append(ring_owner(self.at - hop, self.line) * shard_rows)
             starts.append(ring_owner(self.at + hop, self.line) * shard_rows + upper)
@@ -797,7 +810,7 @@
         d_scaled = dot(d_main, wide_w, ((1,), (1,)))
         d_bc, d_scaled = yield [d_bc, d_scaled]
         d_bc = links.cut(d_bc, 1, row) + links.swap_row(links.cut(d_bc, 1, 1 - row))
-        d_in = outer(kept["scaled"], d_main, width // 3)
+        d_in = outer(kept["scaled"], d_main, width // 3, ROOM)
         d_bc, d_in = yield [d_bc, d_in]
         d_bc = jnp.pad(d_bc, ((0, 0), (LANES - d_bc.shape[1], 0)))
         d_last, d_state = state_back_call(taps, d_bc, kept["last"], aux, big["pack", layer], d_dt)
@@ -987,7 +1000,7 @@
 
     def gather(layer):
         cuts = [(0, 2 * inner), (2 * inner, split)] + ([(split, split + half_width)] if direct else [])
-        full = assemble(*schedule.run(links.gather(pieces[layer])), cuts, 2, core * (shards // 2 * shard_rows))
+        full = assemble(*schedule.run(links.gather(pieces[layer], layer == 0)), cuts, 2, core * (shards // 2 * shard_rows))
         if direct:
             big["out", layer] = full[2]
         else:
@@ -1007,7 +1020,7 @@
             done["out_sum", layer] = (sums.astype(F32) + links.swap_row(sums).astype(F32)).astype(BF16)
         by_core = (lambda f: jnp.where(core == 0, f, (f + shards // 2) % shards)) if direct else (lambda f: f)
         laid = [lambda f: f, lambda f: f, by_core]
-        parts = [(x.reshape(shards, shard_rows, -1), f) for x, f in zip(parts, laid)]
+        parts = [(x.reshape(-1, shard_rows, x.shape[-1]), f) for x, f in zip(parts, laid)]
         done["sum", layer] = schedule.run(links.scatter(shard_rows, parts))
 
     def out_gathered(layer):

time: 571 us -> 557 us (0.975)
  local copies, waits for them, and re-layouts: 70.3 us -> 44.9 us
  Pallas kernels: 80.2 us -> 98 us
    ppermute x0 -> x24, waiting for transfers between devices: none -> 89.6 us  [the longest x6 36.9 us: gather(): sent_down = None if last else lax.ppermute(down, 'fsdp', self.behind)]
    ppermute x14 -> x2, waiting for transfers between devices: 72.4 us -> 0.01 us  [gather(): lax.ppermute(up, 'fsdp', self.ahead)]
    ppermute x0 -> x24, starting transfers between devices: none -> 25.4 us  [the longest x6 10.4 us: gather(): sent_down = None if last else lax.ppermute(down, 'fsdp', self.behind)]
    unnamed x288 -> x246, local copies, waits for them, and re-layouts: 49 us -> 25.1 us
    ppermute x14 -> x2, waiting for transfers between devices: 22.5 us -> 6.81 us  [gather(): lax.ppermute(down, 'fsdp', self.behind)]
    pallas_call x16, Pallas kernels: 18.2 us -> 33.5 us  [ring_add(): pl.pallas_call(functools.partial(ring_add_kernel, count, upper, sums is n...]
    ppermute x14 -> x2, starting transfers between devices: 15.2 us -> 0.48 us  [gather(): lax.ppermute(up, 'fsdp', self.ahead)]
    ppermute x14 -> x2, starting transfers between devices: 14.2 us -> 4.08 us  [gather(): lax.ppermute(down, 'fsdp', self.behind)]
  transfers between devices with their start and end apart: 98 -> 98, of which waited for: 66 -> 61; matrix products, arithmetic and copies ran while one was open for 13% -> 13% of each run, Pallas kernels for 10% -> 12%
where the time goes in v4:
time: 557 us; the launch traced here: 548 us
  waiting for transfers between devices  244 us (44%)
  Pallas kernels  98 us (18%)
  starting transfers between devices  83.7 us (15%)
  local copies, waits for them, and re-layouts  44.9 us (8%)
  matrix products  40.1 us (7%)
  other arithmetic  33.8 us (6%)
    ppermute x14, waiting for transfers between devices, scatter(): lax.ppermute(up, 'fsdp', self.ahead)  54.8 us
    ppermute x17, waiting for transfers between devices, swap_row(): return lax.ppermute(x, 'dp', [(0, 1), (1, 0)])  49.6 us
    dot_general x16, matrix products, dot(): lax.dot_general(a, b, (dims, ((), ())), precision=precision, preferred_el...  40.1 us
    ppermute x6, waiting for transfers between devices, gather(): sent_down = None if last else lax.ppermute(down, 'fsdp', self.behind)  36.9 us
    ppermute x6, waiting for transfers between devices, gather(): sent_up = lax.ppermute(up, 'fsdp', self.ahead)  35.1 us
    pallas_call x16, Pallas kernels, ring_add(): pl.pallas_call(functools.partial(ring_add_kernel, count, upper, sums is n...  33.5 us
    unnamed x246, local copies, waits for them, and re-layouts  25.1 us
    pallas_call x2, Pallas kernels, back_call(): pl.pallas_call(functools.partial(back_kernel, heads, taps), grid=(count,)...  21.1 us
  transfers between devices with their start and end apart: 98, of which 61 were waited for; matrix products, arithmetic and copies ran while one was open for 13% of the time, Pallas kernels for 12%

profile of v4, /device:TPU:0, one launch (start us, length us, event | category | flops | bytes accessed | tf_op | source)
XLA Modules:
  0.0 547.8 jit_solution(798441996705625279)
XLA Ops:
  3.8 3.0 shard_map.203
  7.3 2.6 collective-permute-start.1
  16.8 2.0 collective-permute-start.9
  22.6 6.8 %collective-permute-done.9.refs_2_ = bf16[96,2432]{1,0:T(8,128)(2,1)} collective-permute-done((bf16[96,2432]{1,0:T(8,128)(2,1)}, bf16[96,2432]{1,0:T(8,128)(2,1)}, u32[]{:S(2)}, u32[]{:S(2)}) %collective-permute-start.9) | collective-permute-done | bytes 466976 | tf_op jit(solution)/shard_map/ppermute | solution.py:580
  31.4 9.4 %collective-permute-done.10.refs_4_ = bf16[96,2432]{1,0:T(8,128)(2,1)S(1)} collective-permute-done((bf16[96,2432]{1,0:T(8,128)(2,1)}, bf16[96,2432]{1,0:T(8,128)(2,1)S(1)}, u32[]{:S(2)}, u32[]{:S(2)}) %collective-permute-start.10) | collective-permute-done | bytes 466976 | tf_op jit(solution)/shard_map/ppermute | solution.py:587
  45.5 6.1 %collective-permute-done.11.refs_6_ = bf16[96,2432]{1,0:T(8,128)(2,1)S(1)} collective-permute-done((bf16[96,2432]{1,0:T(8,128)(2,1)S(1)}, bf16[96,2432]{1,0:T(8,128)(2,1)S(1)}, u32[]{:S(2)}, u32[]{:S(2)}) %collective-permute-start.11) | collective-permute-done | bytes 466976 | tf_op jit(solution)/shard_map/ppermute | solution.py:587
  54.4 7.9 %collective-permute-done.13.refs_8_ = bf16[96,2432]{1,0:T(8,128)(2,1)S(1)} collective-permute-done((bf16[96,2432]{1,0:T(8,128)(2,1)S(1)}, bf16[96,2432]{1,0:T(8,128)(2,1)S(1)}, u32[]{:S(2)}, u32[]{:S(2)}) %collective-permute-start.13) | collective-permute-done | bytes 466976 | tf_op jit(solution)/shard_map/ppermute | solution.py:587
  65.1 2.4 maximum_select_fusion.5
  68.5 4.5 collective-permute-done.16.refs_10_
  75.7 8.9 %collective-permute-done.18.refs_12_ = bf16[96,2432]{1,0:T(8,128)(2,1)} collective-permute-done((bf16[96,2432]{1,0:T(8,128)(2,1)}, bf16[96,2432]{1,0:T(8,128)(2,1)}, u32[]{:S(2)}, u32[]{:S(2)}) %collective-permute-start.18) | collective-permute-done | bytes 466976 | tf_op jit(solution)/shard_map/ppermute | solution.py:587
  84.7 2.5 collective-permute-start.20
  87.4 2.0 collective-permute-start.8
  90.6 8.7 %collective-permute-done.19.refs_13_ = bf16[96,2432]{1,0:T(8,128)(2,1)} collective-permute-done((bf16[96,2432]{1,0:T(8,128)(2,1)}, bf16[96,2432]{1,0:T(8,128)(2,1)}, u32[]{:S(2)}, u32[]{:S(2)}) %collective-permute-start.19) | collective-permute-done | bytes 466976 | tf_op jit(solution)/shard_map/ppermute | solution.py:585
  99.3 7.3 %shard_map.204 = (bf16[1536,1536]{1,0:T(8,128)(2,1)}, bf16[1536,128]{1,0:T(8,128)(2,1)}, bf16[1536,768]{1,0:T(8,128)(2,1)}) custom-call(s32[30]{0:T(128)} %stack.456.starts, bf16[192,2432]{1,0:T(8,128)(2,1)} %copy-done.65, bf16[96,2432]{1,0:T(8,128)(2,1)} %collective-permute-done.3.refs_1_, bf16[96,2432]{1,0:T(8,128)(2,1)} %collective-permute-done.9.refs_2_, ...), custom_call_target="tpu_custom_call" | custom-call | bytes 14942208 | tf_op jit(solution)/shard_map/pallas_call | solution.py:413
  112.0 6.5 %fusion.83.proj = f32[512,1536]{1,0:T(8,128)} fusion(bf16[512,1536]{1,0:T(8,128)(2,1)S(1)} %fusion.2.a, bf16[1536,1536]{1,0:T(8,128)(2,1)} %get-tuple-element.227), kind=kOutput, calls=%fused_computation.238 | convolution fusion | flops 2415919104 | bytes 9437184 | tf_op jit(solution)/shard_map/dot_general | solution.py:21
  124.3 5.3 shard_map.205
  129.8 3.5 collective-permute-done.24.refs_5_
  138.7 3.0 collective-permute-done.30
  141.7 5.2 collective-permute-done.27.refs_7_
  155.2 7.3 %collective-permute-done.31.refs_9_ = bf16[96,2432]{1,0:T(8,128)(2,1)S(1)} collective-permute-done((bf16[96,2432]{1,0:T(8,128)(2,1)S(1)}, bf16[96,2432]{1,0:T(8,128)(2,1)S(1)}, u32[]{:S(2)}, u32[]{:S(2)}) %collective-permute-start.31) | collective-permute-done | bytes 466976 | tf_op jit(solution)/shard_map/ppermute | solution.py:591
  167.6 7.8 %collective-permute-done.34.refs_11_ = bf16[96,2432]{1,0:T(8,128)(2,1)S(1)} collective-permute-done((bf16[96,2432]{1,0:T(8,128)(2,1)S(1)}, bf16[96,2432]{1,0:T(8,128)(2,1)S(1)}, u32[]{:S(2)}, u32[]{:S(2)}) %collective-permute-start.34) | collective-permute-done | bytes 466976 | tf_op jit(solution)/shard_map/ppermute | solution.py:591
  179.7 11.1 %collective-permute-done.39.refs_13_ = bf16[96,2432]{1,0:T(8,128)(2,1)S(1)} collective-permute-done((bf16[96,2432]{1,0:T(8,128)(2,1)S(1)}, bf16[96,2432]{1,0:T(8,128)(2,1)S(1)}, u32[]{:S(2)}, u32[]{:S(2)}) %collective-permute-start.39) | collective-permute-done | bytes 466976 | tf_op jit(solution)/shard_map/ppermute | solution.py:591
  191.6 7.3 %shard_map.206 = (bf16[1536,1536]{1,0:T(8,128)(2,1)}, bf16[1536,128]{1,0:T(8,128)(2,1)}, bf16[1536,768]{1,0:T(8,128)(2,1)}) custom-call(s32[30]{0:T(128)} %stack.456.starts, bf16[192,2432]{1,0:T(8,128)(2,1)} %get-tuple-element.424.refs_0_, bf16[96,2432]{1,0:T(8,128)(2,1)} %collective-permute-done.7.refs_1_, bf16[96,2432]{1,0:T(8,128)(2,1)} %collective-permute-done.8.refs_2_, ...), custom_call_target="tpu_custom_call" | custom-call | bytes 14942208 | tf_op jit(solution)/shard_map/pallas_call | solution.py:413
  198.9 3.2 fusion.72
  206.2 6.6 %fusion.85.proj = f32[512,1536]{1,0:T(8,128)} fusion(bf16[512,1536]{1,0:T(8,128)(2,1)S(1)} %fusion.5.a, bf16[1536,1536]{1,0:T(8,128)(2,1)} %get-tuple-element.257), kind=kOutput, calls=%fused_computation.240 | convolution fusion | flops 2415919104 | bytes 9437184 | tf_op jit(solution)/shard_map/dot_general | solution.py:21
  218.4 5.7 %shard_map.207 = (f32[512,768]{1,0:T(8,128)S(1)}, f32[512,768]{1,0:T(8,128)S(1)}, f32[512,128]{1,0:T(8,128)S(1)}) custom-call(f32[512,1536]{1,0:T(8,128)S(1)} %copy-done.45, f32[512,128]{1,0:T(8,128)S(1)} %copy.243.last.last_ref, f32[512,256]{1,0:T(8,128)S(1)} %maximum_select_fusion.10.bc, f32[512,8]{1,0:T(8,128)S(1)} %copy.237.aux, ...), custom_call_target="tpu_custom_call" | custom-call | flops 4000000000 | bytes 8000000 | tf_op jit(solution)/shard_map/pallas_call | solution.py:231
  224.3 5.3 multiply_reduce_fusion.1
  231.5 3.1 collective-permute-done.45
  239.4 10.5 %shard_map.208 = (bf16[512,1536]{1,0:T(8,128)(2,1)S(1)}, f32[512,128]{1,0:T(8,128)S(1)}, f32[512,256]{1,0:T(8,128)S(1)}, f32[4,8,768]{2,1,0:T(8,128)S(1)}, f32[4,8,128]{2,1,0:T(8,128)S(1)}) custom-call(f32[512,1536]{1,0:T(8,128)S(1)} %copy-done.46, f32[512,128]{1,0:T(8,128)S(1)} %copy.243.last.last_ref, f32[512,256]{1,0:T(8,128)S(1)} %maximum_select_fusion.10.bc, ...), custom_call_target="tpu_custom_call" | custom-call | flops 8000000000 | bytes 12000000 | tf_op jit(solution)/shard_map/pallas_call | solution.py:259
  250.1 4.7 fusion.87
  255.8 4.5 shard_map.209
  260.5 3.2 collective-permute-done.47
  268.6 3.4 collective-permute-done.51
  277.7 10.3 %collective-permute-done.49.refs_6_ = bf16[96,2432]{1,0:T(8,128)(2,1)S(1)} collective-permute-done((bf16[96,2432]{1,0:T(8,128)(2,1)S(1)}, bf16[96,2432]{1,0:T(8,128)(2,1)S(1)}, u32[]{:S(2)}, u32[]{:S(2)}) %collective-permute-start.49) | collective-permute-done | bytes 466976 | tf_op jit(solution)/shard_map/ppermute | solution.py:606
  289.3 3.8 collective-permute-done.52
  293.1 2.7 convert_add_fusion
  302.6 3.5 fusion.7
  308.5 5.2 collective-permute-done.53.refs_6_
  319.3 2.6 fusion.89.d_normed
  321.9 8.4 %collective-permute-done.56.refs_6_ = bf16[96,2432]{1,0:T(8,128)(2,1)S(1)} collective-permute-done((bf16[96,2432]{1,0:T(8,128)(2,1)S(1)}, bf16[96,2432]{1,0:T(8,128)(2,1)S(1)}, u32[]{:S(2)}, u32[]{:S(2)}) %collective-permute-start.56) | collective-permute-done | bytes 466976 | tf_op jit(solution)/shard_map/ppermute | solution.py:606
  332.4 2.1 shard_map.214
  336.7 10.6 %shard_map.215 = (bf16[512,1536]{1,0:T(8,128)(2,1)S(1)}, f32[512,128]{1,0:T(8,128)S(1)}, f32[512,256]{1,0:T(8,128)S(1)}, f32[4,8,768]{2,1,0:T(8,128)S(1)}, f32[4,8,128]{2,1,0:T(8,128)S(1)}) custom-call(f32[512,1536]{1,0:T(8,128)S(1)} %copy-done.44, f32[512,128]{1,0:T(8,128)S(1)} %copy-done.10, f32[512,256]{1,0:T(8,128)S(1)} %copy-done.15, ...), custom_call_target="tpu_custom_call" | custom-call | flops 8000000000 | bytes 12000000 | tf_op jit(solution)/shard_map/pallas_call | solution.py:259
  347.4 2.2 shard_map.216
  351.7 2.6 fusion.90
  354.4 8.0 %collective-permute-done.61.refs_6_ = bf16[96,2432]{1,0:T(8,128)(2,1)S(1)} collective-permute-done((bf16[96,2432]{1,0:T(8,128)(2,1)S(1)}, bf16[96,2432]{1,0:T(8,128)(2,1)S(1)}, u32[]{:S(2)}, u32[]{:S(2)}) %collective-permute-start.61) | collective-permute-done | bytes 466976 | tf_op jit(solution)/shard_map/ppermute | solution.py:606
  367.5 2.8 convolution_convert_fusion
  370.3 4.5 shard_map.218
  384.5 5.7 %collective-permute-done.67.refs_6_ = bf16[96,2432]{1,0:T(8,128)(2,1)S(1)} collective-permute-done((bf16[96,2432]{1,0:T(8,128)(2,1)S(1)}, bf16[96,2432]{1,0:T(8,128)(2,1)S(1)}, u32[]{:S(2)}, u32[]{:S(2)}) %collective-permute-start.67) | collective-permute-done | bytes 466976 | tf_op jit(solution)/shard_map/ppermute | solution.py:606
  408.3 3.9 collective-permute-done.72
  418.4 4.7 collective-permute-done.73
  431.2 5.5 %collective-permute-done.77 = bf16[96,2432]{1,0:T(8,128)(2,1)S(1)} collective-permute-done((bf16[96,2432]{1,0:T(8,128)(2,1)S(1)}, bf16[96,2432]{1,0:T(8,128)(2,1)S(1)}, u32[]{:S(2)}, u32[]{:S(2)}) %collective-permute-start.77) | collective-permute-done | bytes 466976 | tf_op jit(solution)/shard_map/ppermute | solution.py:549
  436.7 3.1 collective-permute-done.74.refs_6_
  441.0 2.7 shard_map.224
  448.2 9.0 %collective-permute-done.81 = f32[22,768]{1,0:T(8,128)S(1)} collective-permute-done((f32[22,768]{1,0:T(8,128)S(1)}, f32[22,768]{1,0:T(8,128)S(1)}, u32[]{:S(2)}, u32[]{:S(2)}) %collective-permute-start.81) | collective-permute-done | bytes 67616 | tf_op jit(solution)/shard_map/ppermute | solution.py:552
  457.2 3.0 shard_map.225
  464.3 8.6 %collective-permute-done.84 = f32[22,768]{1,0:T(8,128)S(1)} collective-permute-done((f32[22,768]{1,0:T(8,128)S(1)}, f32[22,768]{1,0:T(8,128)S(1)}, u32[]{:S(2)}, u32[]{:S(2)}) %collective-permute-start.84) | collective-permute-done | bytes 67616 | tf_op jit(solution)/shard_map/ppermute | solution.py:617
  472.9 2.1 shard_map.226
  480.4 9.1 %collective-permute-done.88 = f32[22,768]{1,0:T(8,128)S(1)} collective-permute-done((f32[22,768]{1,0:T(8,128)S(1)}, f32[22,768]{1,0:T(8,128)S(1)}, u32[]{:S(2)}, u32[]{:S(2)}) %collective-permute-start.88) | collective-permute-done | bytes 67616 | tf_op jit(solution)/shard_map/ppermute | solution.py:617
  490.2 2.7 shard_map.227
  501.9 2.1 shard_map.228
  506.2 10.4 %collective-permute-done.93.refs_6_ = bf16[96,2432]{1,0:T(8,128)(2,1)S(1)} collective-permute-done((bf16[96,2432]{1,0:T(8,128)(2,1)S(1)}, bf16[96,2432]{1,0:T(8,128)(2,1)S(1)}, u32[]{:S(2)}, u32[]{:S(2)}) %collective-permute-start.93) | collective-permute-done | bytes 466976 | tf_op jit(solution)/shard_map/ppermute | solution.py:606
  520.3 19.7 %collective-permute-done.95 = bf16[192,2432]{1,0:T(8,128)(2,1)S(1)} collective-permute-done((bf16[192,2432]{1,0:T(8,128)(2,1)S(1)}, bf16[192,2432]{1,0:T(8,128)(2,1)S(1)}, u32[]{:S(2)}, u32[]{:S(2)}) %collective-permute-start.95) | collective-permute-done | bytes 933920 | tf_op jit(solution)/shard_map/ppermute | solution.py:549
  540.3 2.5 collective-permute-done.97.refs_3_
  542.8 4.6 shard_map.230
  (684 shorter events, 194.4 us)
Async XLA Ops:
  16.8 12.6 %collective-permute-start.9 = (bf16[96,2432]{1,0:T(8,128)(2,1)}, bf16[96,2432]{1,0:T(8,128)(2,1)}, u32[]{:S(2)}, u32[]{:S(2)}) collective-permute-start(bf16[96,2432]{1,0:T(8,128)(2,1)} %get-tuple-element.427), channel_id=1, source_target_pairs={{0,2},{4,0},{8,4},{12,8},{14,12},{10,14},{6,10},{2,6},{1,3},{5,1},... | collective-permute-start | bytes 1400840 | tf_op jit(solution)/shard_map/ppermute | solution.py:580
  18.8 12.2 %collective-permute-start.3 = (bf16[96,2432]{1,0:T(8,128)(2,1)S(1)}, bf16[96,2432]{1,0:T(8,128)(2,1)}, u32[]{:S(2)}, u32[]{:S(2)}) collective-permute-start(bf16[96,2432]{1,0:T(8,128)(2,1)S(1)} %get-tuple-element.428), channel_id=1, source_target_pairs={{2,0},{0,4},{4,8},{8,12},{12,14},{14,10},{10,6},{6,2},{3,1},{1,5},... | collective-permute-start | bytes 1400840 | tf_op jit(solution)/shard_map/ppermute | solution.py:580
  20.3 21.9 %collective-permute-start.5 = (bf16[256,1536]{1,0:T(8,128)(2,1)S(1)}, bf16[256,1536]{1,0:T(8,128)(2,1)S(1)}, u32[]{:S(2)}, u32[]{:S(2)}) collective-permute-start(bf16[256,1536]{1,0:T(8,128)(2,1)S(1)} %copy-done.57), channel_id=1, source_target_pairs={{0,1},{1,0},{2,3},{3,2},{4,5},{5,4},{6,7},{7,6},{8,9},{9,8},{10,11... | collective-permute-start | bytes 2359304 | tf_op jit(solution)/shard_map/ppermute | solution.py:549
  29.4 11.5 %collective-permute-start.10 = (bf16[96,2432]{1,0:T(8,128)(2,1)}, bf16[96,2432]{1,0:T(8,128)(2,1)S(1)}, u32[]{:S(2)}, u32[]{:S(2)}) collective-permute-start(bf16[96,2432]{1,0:T(8,128)(2,1)} %collective-permute-done.9.refs_2_), channel_id=1, source_target_pairs={{0,2},{4,0},{8,4},{12,8},{14,12},{10,14},{6,10},{2,6},{1,3},{5,1},... | collective-permute-start | bytes 1400840 | tf_op jit(solution)/shard_map/ppermute | solution.py:587
  31.0 11.2 %collective-permute-start.4 = (bf16[96,2432]{1,0:T(8,128)(2,1)}, bf16[96,2432]{1,0:T(8,128)(2,1)S(1)}, u32[]{:S(2)}, u32[]{:S(2)}) collective-permute-start(bf16[96,2432]{1,0:T(8,128)(2,1)} %collective-permute-done.3.refs_1_), channel_id=1, source_target_pairs={{2,0},{0,4},{4,8},{8,12},{12,14},{14,10},{10,6},{6,2},{3,1},{1,5},... | collective-permute-start | bytes 1400840 | tf_op jit(solution)/shard_map/ppermute | solution.py:585
  43.0 10.8 %collective-permute-start.6 = (bf16[96,2432]{1,0:T(8,128)(2,1)S(1)}, bf16[96,2432]{1,0:T(8,128)(2,1)S(1)}, u32[]{:S(2)}, u32[]{:S(2)}) collective-permute-start(bf16[96,2432]{1,0:T(8,128)(2,1)S(1)} %collective-permute-done.4.refs_3_), channel_id=1, source_target_pairs={{2,0},{0,4},{4,8},{8,12},{12,14},{14,10},{10,6},{6,2},{3,1},{1,5},... | collective-permute-start | bytes 1400840 | tf_op jit(solution)/shard_map/ppermute | solution.py:585
  43.6 21.5 %collective-permute-start.15 = (bf16[256,1536]{1,0:T(8,128)(2,1)}, bf16[256,1536]{1,0:T(8,128)(2,1)}, u32[]{:S(2)}, u32[]{:S(2)}) collective-permute-start(bf16[256,1536]{1,0:T(8,128)(2,1)} %param.23), channel_id=1, source_target_pairs={{0,1},{1,0},{2,3},{3,2},{4,5},{5,4},{6,7},{7,6},{8,9},{9,8},{10,11... | collective-permute-start | bytes 2359304 | tf_op jit(solution)/shard_map/ppermute | solution.py:549
  51.6 10.8 %collective-permute-start.13 = (bf16[96,2432]{1,0:T(8,128)(2,1)S(1)}, bf16[96,2432]{1,0:T(8,128)(2,1)S(1)}, u32[]{:S(2)}, u32[]{:S(2)}) collective-permute-start(bf16[96,2432]{1,0:T(8,128)(2,1)S(1)} %collective-permute-done.11.refs_6_), channel_id=1, source_target_pairs={{0,2},{4,0},{8,4},{12,8},{14,12},{10,14},{6,10},{2,6},{1,3},{5,1},... | collective-permute-start | bytes 1400840 | tf_op jit(solution)/shard_map/ppermute | solution.py:587
  53.8 10.8 %collective-permute-start.12 = (bf16[96,2432]{1,0:T(8,128)(2,1)S(1)}, bf16[96,2432]{1,0:T(8,128)(2,1)S(1)}, u32[]{:S(2)}, u32[]{:S(2)}) collective-permute-start(bf16[96,2432]{1,0:T(8,128)(2,1)S(1)} %collective-permute-done.6.refs_5_), channel_id=1, source_target_pairs={{2,0},{0,4},{4,8},{8,12},{12,14},{14,10},{10,6},{6,2},{3,1},{1,5},... | collective-permute-start | bytes 1400840 | tf_op jit(solution)/shard_map/ppermute | solution.py:585
  64.5 10.9 %collective-permute-start.14 = (bf16[96,2432]{1,0:T(8,128)(2,1)S(1)}, bf16[96,2432]{1,0:T(8,128)(2,1)}, u32[]{:S(2)}, u32[]{:S(2)}) collective-permute-start(bf16[96,2432]{1,0:T(8,128)(2,1)S(1)} %collective-permute-done.12.refs_7_), channel_id=1, source_target_pairs={{2,0},{0,4},{4,8},{8,12},{12,14},{14,10},{10,6},{6,2},{3,1},{1,5},... | collective-permute-start | bytes 1400840 | tf_op jit(solution)/shard_map/ppermute | solution.py:585
  73.0 11.7 %collective-permute-start.18 = (bf16[96,2432]{1,0:T(8,128)(2,1)}, bf16[96,2432]{1,0:T(8,128)(2,1)}, u32[]{:S(2)}, u32[]{:S(2)}) collective-permute-start(bf16[96,2432]{1,0:T(8,128)(2,1)} %collective-permute-done.16.refs_10_), channel_id=1, source_target_pairs={{0,2},{4,0},{8,4},{12,8},{14,12},{10,14},{6,10},{2,6},{1,3},{5,1},... | collective-permute-start | bytes 1400840 | tf_op jit(solution)/shard_map/ppermute | solution.py:587
  75.4 11.9 %collective-permute-start.17 = (bf16[96,2432]{1,0:T(8,128)(2,1)}, bf16[96,2432]{1,0:T(8,128)(2,1)}, u32[]{:S(2)}, u32[]{:S(2)}) collective-permute-start(bf16[96,2432]{1,0:T(8,128)(2,1)} %collective-permute-done.14.refs_9_), channel_id=1, source_target_pairs={{2,0},{0,4},{4,8},{8,12},{12,14},{14,10},{10,6},{6,2},{3,1},{1,5},... | collective-permute-start | bytes 1400840 | tf_op jit(solution)/shard_map/ppermute | solution.py:585
  84.7 14.6 %collective-permute-start.20 = (bf16[96,2432]{1,0:T(8,128)(2,1)}, bf16[96,2432]{1,0:T(8,128)(2,1)}, u32[]{:S(2)}, u32[]{:S(2)}) collective-permute-start(bf16[96,2432]{1,0:T(8,128)(2,1)} %collective-permute-done.18.refs_12_), channel_id=1, source_target_pairs={{0,2},{4,0},{8,4},{12,8},{14,12},{10,14},{6,10},{2,6},{1,3},{5,1},... | collective-permute-start | bytes 1400840 | tf_op jit(solution)/shard_map/ppermute | solution.py:587
  87.3 12.0 %collective-permute-start.19 = (bf16[96,2432]{1,0:T(8,128)(2,1)}, bf16[96,2432]{1,0:T(8,128)(2,1)}, u32[]{:S(2)}, u32[]{:S(2)}) collective-permute-start(bf16[96,2432]{1,0:T(8,128)(2,1)} %collective-permute-done.17.refs_11_), channel_id=1, source_target_pairs={{2,0},{0,4},{4,8},{8,12},{12,14},{14,10},{10,6},{6,2},{3,1},{1,5},... | collective-permute-start | bytes 1400840 | tf_op jit(solution)/shard_map/ppermute | solution.py:585
  87.4 19.2 %collective-permute-start.8 = (bf16[96,2432]{1,0:T(8,128)(2,1)S(1)}, bf16[96,2432]{1,0:T(8,128)(2,1)}, u32[]{:S(2)}, u32[]{:S(2)}) collective-permute-start(bf16[96,2432]{1,0:T(8,128)(2,1)S(1)} %get-tuple-element.429), channel_id=1, source_target_pairs={{0,2},{4,0},{8,4},{12,8},{14,12},{10,14},{6,10},{2,6},{1,3},{5,1},... | collective-permute-start | bytes 1400840 | tf_op jit(solution)/shard_map/ppermute | solution.py:580
  89.4 17.2 %collective-permute-start.7 = (bf16[96,2432]{1,0:T(8,128)(2,1)S(1)}, bf16[96,2432]{1,0:T(8,128)(2,1)}, u32[]{:S(2)}, u32[]{:S(2)}) collective-permute-start(bf16[96,2432]{1,0:T(8,128)(2,1)S(1)} %get-tuple-element.430), channel_id=1, source_target_pairs={{2,0},{0,4},{4,8},{8,12},{12,14},{14,10},{10,6},{6,2},{3,1},{1,5},... | collective-permute-start | bytes 1400840 | tf_op jit(solution)/shard_map/ppermute | solution.py:580
  120.1 13.1 %collective-permute-start.24 = (bf16[96,2432]{1,0:T(8,128)(2,1)S(1)}, bf16[96,2432]{1,0:T(8,128)(2,1)S(1)}, u32[]{:S(2)}, u32[]{:S(2)}) collective-permute-start(bf16[96,2432]{1,0:T(8,128)(2,1)S(1)} %collective-permute-done.21.refs_3_), channel_id=1, source_target_pairs={{2,0},{0,4},{4,8},{8,12},{12,14},{14,10},{10,6},{6,2},{3,1},{1,5},... | collective-permute-start | bytes 1400840 | tf_op jit(solution)/shard_map/ppermute | solution.py:591
  121.7 13.2 %collective-permute-start.25 = (bf16[96,2432]{1,0:T(8,128)(2,1)}, bf16[96,2432]{1,0:T(8,128)(2,1)S(1)}, u32[]{:S(2)}, u32[]{:S(2)}) collective-permute-start(bf16[96,2432]{1,0:T(8,128)(2,1)} %collective-permute-done.22.refs_4_), channel_id=1, source_target_pairs={{0,2},{4,0},{8,4},{12,8},{14,12},{10,14},{6,10},{2,6},{1,3},{5,1},... | collective-permute-start | bytes 1400840 | tf_op jit(solution)/shard_map/ppermute | solution.py:592
  134.9 12.0 %collective-permute-start.27 = (bf16[96,2432]{1,0:T(8,128)(2,1)S(1)}, bf16[96,2432]{1,0:T(8,128)(2,1)S(1)}, u32[]{:S(2)}, u32[]{:S(2)}) collective-permute-start(bf16[96,2432]{1,0:T(8,128)(2,1)S(1)} %collective-permute-done.24.refs_5_), channel_id=1, source_target_pairs={{2,0},{0,4},{4,8},{8,12},{12,14},{14,10},{10,6},{6,2},{3,1},{1,5},... | collective-permute-start | bytes 1400840 | tf_op jit(solution)/shard_map/ppermute | solution.py:591
  136.5 11.7 %collective-permute-start.28 = (bf16[96,2432]{1,0:T(8,128)(2,1)S(1)}, bf16[96,2432]{1,0:T(8,128)(2,1)S(1)}, u32[]{:S(2)}, u32[]{:S(2)}) collective-permute-start(bf16[96,2432]{1,0:T(8,128)(2,1)S(1)} %collective-permute-done.25.refs_6_), channel_id=1, source_target_pairs={{0,2},{4,0},{8,4},{12,8},{14,12},{10,14},{6,10},{2,6},{1,3},{5,1},... | collective-permute-start | bytes 1400840 | tf_op jit(solution)/shard_map/ppermute | solution.py:592
  149.3 16.6 %collective-permute-start.37 = (bf16[768,768]{1,0:T(8,128)(2,1)S(1)}, bf16[768,768]{1,0:T(8,128)(2,1)S(1)}, u32[]{:S(2)}, u32[]{:S(2)}) collective-permute-start(bf16[768,768]{1,0:T(8,128)(2,1)S(1)} %get-tuple-element.418), channel_id=1, source_target_pairs={{0,16},{16,0},{1,17},{17,1},{2,18},{18,2},{3,19},{19,3},{4,20},{20... | collective-permute-start | bytes 3538952 | tf_op jit(solution)/shard_map/ppermute | solution.py:546
  149.9 12.7 %collective-permute-start.31 = (bf16[96,2432]{1,0:T(8,128)(2,1)S(1)}, bf16[96,2432]{1,0:T(8,128)(2,1)S(1)}, u32[]{:S(2)}, u32[]{:S(2)}) collective-permute-start(bf16[96,2432]{1,0:T(8,128)(2,1)S(1)} %collective-permute-done.27.refs_7_), channel_id=1, source_target_pairs={{2,0},{0,4},{4,8},{8,12},{12,14},{14,10},{10,6},{6,2},{3,1},{1,5},... | collective-permute-start | bytes 1400840 | tf_op jit(solution)/shard_map/ppermute | solution.py:591
  151.5 12.4 %collective-permute-start.32 = (bf16[96,2432]{1,0:T(8,128)(2,1)S(1)}, bf16[96,2432]{1,0:T(8,128)(2,1)S(1)}, u32[]{:S(2)}, u32[]{:S(2)}) collective-permute-start(bf16[96,2432]{1,0:T(8,128)(2,1)S(1)} %collective-permute-done.28.refs_8_), channel_id=1, source_target_pairs={{0,2},{4,0},{8,4},{12,8},{14,12},{10,14},{6,10},{2,6},{1,3},{5,1},... | collective-permute-start | bytes 1400840 | tf_op jit(solution)/shard_map/ppermute | solution.py:592
  153.3 23.4 %collective-permute-start.36 = (bf16[512,768]{1,0:T(8,128)(2,1)S(1)}, bf16[512,768]{1,0:T(8,128)(2,1)S(1)}, u32[]{:S(2)}, u32[]{:S(2)}) collective-permute-start(bf16[512,768]{1,0:T(8,128)(2,1)S(1)} %convolution_convert_fusion.4), channel_id=1, source_target_pairs={{0,1},{1,0},{2,3},{3,2},{4,5},{5,4},{6,7},{7,6},{8,9},{9,8},{10,11... | collective-permute-start | bytes 2359304 | tf_op jit(solution)/shard_map/ppermute | solution.py:549
  163.9 11.5 %collective-permute-start.34 = (bf16[96,2432]{1,0:T(8,128)(2,1)S(1)}, bf16[96,2432]{1,0:T(8,128)(2,1)S(1)}, u32[]{:S(2)}, u32[]{:S(2)}) collective-permute-start(bf16[96,2432]{1,0:T(8,128)(2,1)S(1)} %collective-permute-done.31.refs_9_), channel_id=1, source_target_pairs={{2,0},{0,4},{4,8},{8,12},{12,14},{14,10},{10,6},{6,2},{3,1},{1,5},... | collective-permute-start | bytes 1400840 | tf_op jit(solution)/shard_map/ppermute | solution.py:591
  165.4 11.3 %collective-permute-start.35 = (bf16[96,2432]{1,0:T(8,128)(2,1)S(1)}, bf16[96,2432]{1,0:T(8,128)(2,1)}, u32[]{:S(2)}, u32[]{:S(2)}) collective-permute-start(bf16[96,2432]{1,0:T(8,128)(2,1)S(1)} %collective-permute-done.32.refs_10_), channel_id=1, source_target_pairs={{0,2},{4,0},{8,4},{12,8},{14,12},{10,14},{6,10},{2,6},{1,3},{5,1},... | collective-permute-start | bytes 1400840 | tf_op jit(solution)/shard_map/ppermute | solution.py:592
  177.7 24.4 %collective-permute-start.38 = (bf16[512,768]{1,0:T(8,128)(2,1)S(1)}, bf16[512,768]{1,0:T(8,128)(2,1)S(1)}, u32[]{:S(2)}, u32[]{:S(2)}) collective-permute-start(bf16[512,768]{1,0:T(8,128)(2,1)S(1)} %add_convert_fusion.1), channel_id=1, source_target_pairs={{0,16},{16,0},{1,17},{17,1},{2,18},{18,2},{3,19},{19,3},{4,20},{20... | collective-permute-start | bytes 2359304 | tf_op jit(solution)/shard_map/ppermute | solution.py:546
  177.7 13.1 %collective-permute-start.39 = (bf16[96,2432]{1,0:T(8,128)(2,1)S(1)}, bf16[96,2432]{1,0:T(8,128)(2,1)S(1)}, u32[]{:S(2)}, u32[]{:S(2)}) collective-permute-start(bf16[96,2432]{1,0:T(8,128)(2,1)S(1)} %collective-permute-done.34.refs_11_), channel_id=1, source_target_pairs={{2,0},{0,4},{4,8},{8,12},{12,14},{14,10},{10,6},{6,2},{3,1},{1,5},... | collective-permute-start | bytes 1400840 | tf_op jit(solution)/shard_map/ppermute | solution.py:591
  178.3 13.1 %collective-permute-start.40 = (bf16[96,2432]{1,0:T(8,128)(2,1)}, bf16[96,2432]{1,0:T(8,128)(2,1)}, u32[]{:S(2)}, u32[]{:S(2)}) collective-permute-start(bf16[96,2432]{1,0:T(8,128)(2,1)} %collective-permute-done.35.refs_12_), channel_id=1, source_target_pairs={{0,2},{4,0},{8,4},{12,8},{14,12},{10,14},{6,10},{2,6},{1,3},{5,1},... | collective-permute-start | bytes 1400840 | tf_op jit(solution)/shard_map/ppermute | solution.py:592
  202.1 22.2 %collective-permute-start.43 = (bf16[768,768]{1,0:T(8,128)(2,1)}, bf16[768,768]{1,0:T(8,128)(2,1)}, u32[]{:S(2)}, u32[]{:S(2)}) collective-permute-start(bf16[768,768]{1,0:T(8,128)(2,1)} %get-tuple-element.416), channel_id=1, source_target_pairs={{0,16},{16,0},{1,17},{17,1},{2,18},{18,2},{3,19},{19,3},{4,20},{20... | collective-permute-start | bytes 3538952 | tf_op jit(solution)/shard_map/ppermute | solution.py:546
  273.1 19.9 %collective-permute-start.52 = (bf16[512,768]{1,0:T(8,128)(2,1)}, bf16[512,768]{1,0:T(8,128)(2,1)}, u32[]{:S(2)}, u32[]{:S(2)}) collective-permute-start(bf16[512,768]{1,0:T(8,128)(2,1)} %add_convert_fusion), channel_id=1, source_target_pairs={{0,1},{1,0},{2,3},{3,2},{4,5},{5,4},{6,7},{7,6},{8,9},{9,8},{10,11... | collective-permute-start | bytes 2359304 | tf_op jit(solution)/shard_map/ppermute | solution.py:549
  275.4 12.5 %collective-permute-start.49 = (bf16[96,2432]{1,0:T(8,128)(2,1)S(1)}, bf16[96,2432]{1,0:T(8,128)(2,1)S(1)}, u32[]{:S(2)}, u32[]{:S(2)}) collective-permute-start(bf16[96,2432]{1,0:T(8,128)(2,1)S(1)} %get-tuple-element.285), channel_id=1, source_target_pairs={{2,0},{0,4},{4,8},{8,12},{12,14},{14,10},{10,6},{6,2},{3,1},{1,5},... | collective-permute-start | bytes 1400840 | tf_op jit(solution)/shard_map/ppermute | solution.py:606
  276.1 12.4 %collective-permute-start.50 = (bf16[96,2432]{1,0:T(8,128)(2,1)S(1)}, bf16[96,2432]{1,0:T(8,128)(2,1)S(1)}, u32[]{:S(2)}, u32[]{:S(2)}) collective-permute-start(bf16[96,2432]{1,0:T(8,128)(2,1)S(1)} %get-tuple-element.286), channel_id=1, source_target_pairs={{0,2},{4,0},{8,4},{12,8},{14,12},{10,14},{6,10},{2,6},{1,3},{5,1},... | collective-permute-start | bytes 1400840 | tf_op jit(solution)/shard_map/ppermute | solution.py:606
  300.5 13.2 %collective-permute-start.53 = (bf16[96,2432]{1,0:T(8,128)(2,1)S(1)}, bf16[96,2432]{1,0:T(8,128)(2,1)S(1)}, u32[]{:S(2)}, u32[]{:S(2)}) collective-permute-start(bf16[96,2432]{1,0:T(8,128)(2,1)S(1)} %get-tuple-element.290), channel_id=1, source_target_pairs={{2,0},{0,4},{4,8},{8,12},{12,14},{14,10},{10,6},{6,2},{3,1},{1,5},... | collective-permute-start | bytes 1400840 | tf_op jit(solution)/shard_map/ppermute | solution.py:606
  301.2 12.8 %collective-permute-start.54 = (bf16[96,2432]{1,0:T(8,128)(2,1)S(1)}, bf16[96,2432]{1,0:T(8,128)(2,1)S(1)}, u32[]{:S(2)}, u32[]{:S(2)}) collective-permute-start(bf16[96,2432]{1,0:T(8,128)(2,1)S(1)} %get-tuple-element.291), channel_id=1, source_target_pairs={{0,2},{4,0},{8,4},{12,8},{14,12},{10,14},{6,10},{2,6},{1,3},{5,1},... | collective-permute-start | bytes 1400840 | tf_op jit(solution)/shard_map/ppermute | solution.py:606
  317.2 13.0 %collective-permute-start.56 = (bf16[96,2432]{1,0:T(8,128)(2,1)S(1)}, bf16[96,2432]{1,0:T(8,128)(2,1)S(1)}, u32[]{:S(2)}, u32[]{:S(2)}) collective-permute-start(bf16[96,2432]{1,0:T(8,128)(2,1)S(1)} %get-tuple-element.295), channel_id=1, source_target_pairs={{2,0},{0,4},{4,8},{8,12},{12,14},{14,10},{10,6},{6,2},{3,1},{1,5},... | collective-permute-start | bytes 1400840 | tf_op jit(solution)/shard_map/ppermute | solution.py:606
  317.7 12.7 %collective-permute-start.57 = (bf16[96,2432]{1,0:T(8,128)(2,1)S(1)}, bf16[96,2432]{1,0:T(8,128)(2,1)S(1)}, u32[]{:S(2)}, u32[]{:S(2)}) collective-permute-start(bf16[96,2432]{1,0:T(8,128)(2,1)S(1)} %get-tuple-element.296), channel_id=1, source_target_pairs={{0,2},{4,0},{8,4},{12,8},{14,12},{10,14},{6,10},{2,6},{1,3},{5,1},... | collective-permute-start | bytes 1400840 | tf_op jit(solution)/shard_map/ppermute | solution.py:606
  334.6 12.7 %collective-permute-start.59 = (bf16[96,2432]{1,0:T(8,128)(2,1)S(1)}, bf16[96,2432]{1,0:T(8,128)(2,1)S(1)}, u32[]{:S(2)}, u32[]{:S(2)}) collective-permute-start(bf16[96,2432]{1,0:T(8,128)(2,1)S(1)} %get-tuple-element.301), channel_id=1, source_target_pairs={{2,0},{0,4},{4,8},{8,12},{12,14},{14,10},{10,6},{6,2},{3,1},{1,5},... | collective-permute-start | bytes 1400840 | tf_op jit(solution)/shard_map/ppermute | solution.py:606
  335.1 12.2 %collective-permute-start.60 = (bf16[96,2432]{1,0:T(8,128)(2,1)S(1)}, bf16[96,2432]{1,0:T(8,128)(2,1)S(1)}, u32[]{:S(2)}, u32[]{:S(2)}) collective-permute-start(bf16[96,2432]{1,0:T(8,128)(2,1)S(1)} %get-tuple-element.302), channel_id=1, source_target_pairs={{0,2},{4,0},{8,4},{12,8},{14,12},{10,14},{6,10},{2,6},{1,3},{5,1},... | collective-permute-start | bytes 1400840 | tf_op jit(solution)/shard_map/ppermute | solution.py:606
  349.7 12.8 %collective-permute-start.61 = (bf16[96,2432]{1,0:T(8,128)(2,1)S(1)}, bf16[96,2432]{1,0:T(8,128)(2,1)S(1)}, u32[]{:S(2)}, u32[]{:S(2)}) collective-permute-start(bf16[96,2432]{1,0:T(8,128)(2,1)S(1)} %get-tuple-element.315), channel_id=1, source_target_pairs={{2,0},{0,4},{4,8},{8,12},{12,14},{14,10},{10,6},{6,2},{3,1},{1,5},... | collective-permute-start | bytes 1400840 | tf_op jit(solution)/shard_map/ppermute | solution.py:606
  350.2 12.5 %collective-permute-start.62 = (bf16[96,2432]{1,0:T(8,128)(2,1)S(1)}, bf16[96,2432]{1,0:T(8,128)(2,1)S(1)}, u32[]{:S(2)}, u32[]{:S(2)}) collective-permute-start(bf16[96,2432]{1,0:T(8,128)(2,1)S(1)} %get-tuple-element.316), channel_id=1, source_target_pairs={{0,2},{4,0},{8,4},{12,8},{14,12},{10,14},{6,10},{2,6},{1,3},{5,1},... | collective-permute-start | bytes 1400840 | tf_op jit(solution)/shard_map/ppermute | solution.py:606
  362.8 12.1 %collective-permute-start.66 = (f32[512,64]{1,0:T(8,128)S(1)}, f32[512,64]{1,0:T(8,128)S(1)}, u32[]{:S(2)}, u32[]{:S(2)}) collective-permute-start(f32[512,64]{1,0:T(8,128)S(1)} %constant_dynamic-slice_fusion.1), channel_id=1, source_target_pairs={{0,1},{1,0},{2,3},{3,2},{4,5},{5,4},{6,7},{7,6},{8,9},{9,8},{10,11... | collective-permute-start | bytes 393224 | tf_op jit(solution)/shard_map/ppermute | solution.py:549
  365.2 11.5 %collective-permute-start.64 = (bf16[96,2432]{1,0:T(8,128)(2,1)S(1)}, bf16[96,2432]{1,0:T(8,128)(2,1)S(1)}, u32[]{:S(2)}, u32[]{:S(2)}) collective-permute-start(bf16[96,2432]{1,0:T(8,128)(2,1)S(1)} %get-tuple-element.321), channel_id=1, source_target_pairs={{2,0},{0,4},{4,8},{8,12},{12,14},{14,10},{10,6},{6,2},{3,1},{1,5},... | collective-permute-start | bytes 1400840 | tf_op jit(solution)/shard_map/ppermute | solution.py:606
  366.8 11.3 %collective-permute-start.65 = (bf16[96,2432]{1,0:T(8,128)(2,1)S(1)}, bf16[96,2432]{1,0:T(8,128)(2,1)S(1)}, u32[]{:S(2)}, u32[]{:S(2)}) collective-permute-start(bf16[96,2432]{1,0:T(8,128)(2,1)S(1)} %get-tuple-element.322), channel_id=1, source_target_pairs={{0,2},{4,0},{8,4},{12,8},{14,12},{10,14},{6,10},{2,6},{1,3},{5,1},... | collective-permute-start | bytes 1400840 | tf_op jit(solution)/shard_map/ppermute | solution.py:606
  392.7 13.6 %collective-permute-start.71 = (f32[512,768]{1,0:T(8,128)}, f32[512,768]{1,0:T(8,128)}, u32[]{:S(2)}, u32[]{:S(2)}) collective-permute-start(f32[512,768]{1,0:T(8,128)} %constant_dynamic-slice_fusion), channel_id=1, source_target_pairs={{0,16},{16,0},{1,17},{17,1},{2,18},{18,2},{3,19},{19,3},{4,20},{20... | collective-permute-start | bytes 4718600 | tf_op jit(solution)/shard_map/ppermute | solution.py:546
  399.2 13.1 %collective-permute-start.72 = (bf16[96,2432]{1,0:T(8,128)(2,1)S(1)}, bf16[96,2432]{1,0:T(8,128)(2,1)S(1)}, u32[]{:S(2)}, u32[]{:S(2)}) collective-permute-start(bf16[96,2432]{1,0:T(8,128)(2,1)S(1)} %get-tuple-element.426), channel_id=1, source_target_pairs={{0,1},{1,0},{2,3},{3,2},{4,5},{5,4},{6,7},{7,6},{8,9},{9,8},{10,11... | collective-permute-start | bytes 1400840 | tf_op jit(solution)/shard_map/ppermute | solution.py:549
  404.3 12.8 %collective-permute-start.69 = (bf16[96,2432]{1,0:T(8,128)(2,1)S(1)}, bf16[96,2432]{1,0:T(8,128)(2,1)S(1)}, u32[]{:S(2)}, u32[]{:S(2)}) collective-permute-start(bf16[96,2432]{1,0:T(8,128)(2,1)S(1)} %get-tuple-element.338), channel_id=1, source_target_pairs={{2,0},{0,4},{4,8},{8,12},{12,14},{14,10},{10,6},{6,2},{3,1},{1,5},... | collective-permute-start | bytes 1400840 | tf_op jit(solution)/shard_map/ppermute | solution.py:606
  405.9 12.5 %collective-permute-start.70 = (bf16[96,2432]{1,0:T(8,128)(2,1)S(1)}, bf16[96,2432]{1,0:T(8,128)(2,1)S(1)}, u32[]{:S(2)}, u32[]{:S(2)}) collective-permute-start(bf16[96,2432]{1,0:T(8,128)(2,1)S(1)} %get-tuple-element.339), channel_id=1, source_target_pairs={{0,2},{4,0},{8,4},{12,8},{14,12},{10,14},{6,10},{2,6},{1,3},{5,1},... | collective-permute-start | bytes 1400840 | tf_op jit(solution)/shard_map/ppermute | solution.py:606
  412.3 10.8 %collective-permute-start.73 = (bf16[256,768]{1,0:T(8,128)(2,1)S(1)}, bf16[256,768]{1,0:T(8,128)(2,1)S(1)}, u32[]{:S(2)}, u32[]{:S(2)}) collective-permute-start(bf16[256,768]{1,0:T(8,128)(2,1)S(1)} %dynamic-slice_convert_fusion.1), channel_id=1, source_target_pairs={{0,1},{1,0},{2,3},{3,2},{4,5},{5,4},{6,7},{7,6},{8,9},{9,8},{10,11... | collective-permute-start | bytes 1179656 | tf_op jit(solution)/shard_map/ppermute | solution.py:549
  423.5 13.2 %collective-permute-start.77 = (bf16[96,2432]{1,0:T(8,128)(2,1)S(1)}, bf16[96,2432]{1,0:T(8,128)(2,1)S(1)}, u32[]{:S(2)}, u32[]{:S(2)}) collective-permute-start(bf16[96,2432]{1,0:T(8,128)(2,1)S(1)} %copy-done.84), channel_id=1, source_target_pairs={{0,1},{1,0},{2,3},{3,2},{4,5},{5,4},{6,7},{7,6},{8,9},{9,8},{10,11... | collective-permute-start | bytes 1400840 | tf_op jit(solution)/shard_map/ppermute | solution.py:549
  426.9 12.9 %collective-permute-start.74 = (bf16[96,2432]{1,0:T(8,128)(2,1)S(1)}, bf16[96,2432]{1,0:T(8,128)(2,1)S(1)}, u32[]{:S(2)}, u32[]{:S(2)}) collective-permute-start(bf16[96,2432]{1,0:T(8,128)(2,1)S(1)} %get-tuple-element.346), channel_id=1, source_target_pairs={{2,0},{0,4},{4,8},{8,12},{12,14},{14,10},{10,6},{6,2},{3,1},{1,5},... | collective-permute-start | bytes 1400840 | tf_op jit(solution)/shard_map/ppermute | solution.py:606
  428.5 12.5 %collective-permute-start.75 = (bf16[96,2432]{1,0:T(8,128)(2,1)S(1)}, bf16[96,2432]{1,0:T(8,128)(2,1)S(1)}, u32[]{:S(2)}, u32[]{:S(2)}) collective-permute-start(bf16[96,2432]{1,0:T(8,128)(2,1)S(1)} %get-tuple-element.347), channel_id=1, source_target_pairs={{0,2},{4,0},{8,4},{12,8},{14,12},{10,14},{6,10},{2,6},{1,3},{5,1},... | collective-permute-start | bytes 1400840 | tf_op jit(solution)/shard_map/ppermute | solution.py:606
  443.7 13.5 %collective-permute-start.78 = (bf16[96,2432]{1,0:T(8,128)(2,1)}, bf16[96,2432]{1,0:T(8,128)(2,1)}, u32[]{:S(2)}, u32[]{:S(2)}) collective-permute-start(bf16[96,2432]{1,0:T(8,128)(2,1)} %get-tuple-element.351), channel_id=1, source_target_pairs={{2,0},{0,4},{4,8},{8,12},{12,14},{14,10},{10,6},{6,2},{3,1},{1,5},... | collective-permute-start | bytes 1400840 | tf_op jit(solution)/shard_map/ppermute | solution.py:606
  444.8 12.4 %collective-permute-start.79 = (bf16[96,2432]{1,0:T(8,128)(2,1)}, bf16[96,2432]{1,0:T(8,128)(2,1)}, u32[]{:S(2)}, u32[]{:S(2)}) collective-permute-start(bf16[96,2432]{1,0:T(8,128)(2,1)} %get-tuple-element.352), channel_id=1, source_target_pairs={{0,2},{4,0},{8,4},{12,8},{14,12},{10,14},{6,10},{2,6},{1,3},{5,1},... | collective-permute-start | bytes 1400840 | tf_op jit(solution)/shard_map/ppermute | solution.py:606
  460.2 12.7 %collective-permute-start.82 = (bf16[96,2432]{1,0:T(8,128)(2,1)}, bf16[96,2432]{1,0:T(8,128)(2,1)}, u32[]{:S(2)}, u32[]{:S(2)}) collective-permute-start(bf16[96,2432]{1,0:T(8,128)(2,1)} %get-tuple-element.364), channel_id=1, source_target_pairs={{2,0},{0,4},{4,8},{8,12},{12,14},{14,10},{10,6},{6,2},{3,1},{1,5},... | collective-permute-start | bytes 1400840 | tf_op jit(solution)/shard_map/ppermute | solution.py:606
  460.5 12.4 %collective-permute-start.83 = (bf16[96,2432]{1,0:T(8,128)(2,1)}, bf16[96,2432]{1,0:T(8,128)(2,1)}, u32[]{:S(2)}, u32[]{:S(2)}) collective-permute-start(bf16[96,2432]{1,0:T(8,128)(2,1)} %get-tuple-element.365), channel_id=1, source_target_pairs={{0,2},{4,0},{8,4},{12,8},{14,12},{10,14},{6,10},{2,6},{1,3},{5,1},... | collective-permute-start | bytes 1400840 | tf_op jit(solution)/shard_map/ppermute | solution.py:606
  463.9 15.4 %collective-permute-start.87 = (bf16[256,768]{1,0:T(8,128)(2,1)S(1)}, bf16[256,768]{1,0:T(8,128)(2,1)S(1)}, u32[]{:S(2)}, u32[]{:S(2)}) collective-permute-start(bf16[256,768]{1,0:T(8,128)(2,1)S(1)} %add_convert_fusion.2), channel_id=1, source_target_pairs={{0,16},{16,0},{1,17},{17,1},{2,18},{18,2},{3,19},{19,3},{4,20},{20... | collective-permute-start | bytes 1179656 | tf_op jit(solution)/shard_map/ppermute | solution.py:546
  475.0 14.5 %collective-permute-start.85 = (bf16[96,2432]{1,0:T(8,128)(2,1)S(1)}, bf16[96,2432]{1,0:T(8,128)(2,1)S(1)}, u32[]{:S(2)}, u32[]{:S(2)}) collective-permute-start(bf16[96,2432]{1,0:T(8,128)(2,1)S(1)} %get-tuple-element.369), channel_id=1, source_target_pairs={{2,0},{0,4},{4,8},{8,12},{12,14},{14,10},{10,6},{6,2},{3,1},{1,5},... | collective-permute-start | bytes 1400840 | tf_op jit(solution)/shard_map/ppermute | solution.py:606
  475.4 14.2 %collective-permute-start.86 = (bf16[96,2432]{1,0:T(8,128)(2,1)S(1)}, bf16[96,2432]{1,0:T(8,128)(2,1)S(1)}, u32[]{:S(2)}, u32[]{:S(2)}) collective-permute-start(bf16[96,2432]{1,0:T(8,128)(2,1)S(1)} %get-tuple-element.370), channel_id=1, source_target_pairs={{0,2},{4,0},{8,4},{12,8},{14,12},{10,14},{6,10},{2,6},{1,3},{5,1},... | collective-permute-start | bytes 1400840 | tf_op jit(solution)/shard_map/ppermute | solution.py:606
  477.4 12.2 %collective-permute-start.88 = (f32[22,768]{1,0:T(8,128)S(1)}, f32[22,768]{1,0:T(8,128)S(1)}, u32[]{:S(2)}, u32[]{:S(2)}) collective-permute-start(f32[22,768]{1,0:T(8,128)S(1)} %add.828), channel_id=1, source_target_pairs={{0,8},{2,10},{4,12},{6,14},{8,0},{10,2},{12,4},{14,6},{1,9},{3,11}... | collective-permute-start | bytes 202760 | tf_op jit(solution)/shard_map/ppermute | solution.py:617
  504.0 12.5 %collective-permute-start.93 = (bf16[96,2432]{1,0:T(8,128)(2,1)S(1)}, bf16[96,2432]{1,0:T(8,128)(2,1)S(1)}, u32[]{:S(2)}, u32[]{:S(2)}) collective-permute-start(bf16[96,2432]{1,0:T(8,128)(2,1)S(1)} %get-tuple-element.383), channel_id=1, source_target_pairs={{2,0},{0,4},{4,8},{8,12},{12,14},{14,10},{10,6},{6,2},{3,1},{1,5},... | collective-permute-start | bytes 1400840 | tf_op jit(solution)/shard_map/ppermute | solution.py:606
  504.1 12.5 %collective-permute-start.94 = (bf16[96,2432]{1,0:T(8,128)(2,1)S(1)}, bf16[96,2432]{1,0:T(8,128)(2,1)S(1)}, u32[]{:S(2)}, u32[]{:S(2)}) collective-permute-start(bf16[96,2432]{1,0:T(8,128)(2,1)S(1)} %get-tuple-element.384), channel_id=1, source_target_pairs={{0,2},{4,0},{8,4},{12,8},{14,12},{10,14},{6,10},{2,6},{1,3},{5,1},... | collective-permute-start | bytes 1400840 | tf_op jit(solution)/shard_map/ppermute | solution.py:606
  518.4 21.6 %collective-permute-start.95 = (bf16[192,2432]{1,0:T(8,128)(2,1)S(1)}, bf16[192,2432]{1,0:T(8,128)(2,1)S(1)}, u32[]{:S(2)}, u32[]{:S(2)}) collective-permute-start(bf16[192,2432]{1,0:T(8,128)(2,1)S(1)} %shard_map.229), channel_id=1, source_target_pairs={{0,1},{1,0},{2,3},{3,2},{4,5},{5,4},{6,7},{7,6},{8,9},{9,8},{10,11... | collective-permute-start | bytes 2801672 | tf_op jit(solution)/shard_map/ppermute | solution.py:549
  520.3 20.1 %collective-permute-start.96 = (bf16[192,2432]{1,0:T(8,128)(2,1)S(1)}, bf16[192,2432]{1,0:T(8,128)(2,1)S(1)}, u32[]{:S(2)}, u32[]{:S(2)}) collective-permute-start(bf16[192,2432]{1,0:T(8,128)(2,1)S(1)} %get-tuple-element.421), channel_id=1, source_target_pairs={{0,16},{16,0},{1,17},{17,1},{2,18},{18,2},{3,19},{19,3},{4,20},{20... | collective-permute-start | bytes 2801672 | tf_op jit(solution)/shard_map/ppermute | solution.py:546
  (154 other events, 1491.3 us)

commit v5 on v4

--- a/solution.py
+++ b/solution.py
@@ -388,20 +388,30 @@
 
 
 def assemble_kernel(cuts, turned, starts, *refs):
-    outs, sems = refs[-1 - len(cuts) : -1], refs[-1]
-    sources = refs[: -1 - len(cuts)]
+    made = len(cuts) + (turned is not None)
+    outs, sems = refs[-1 - made : -1], refs[-1]
+    sources = refs[: -1 - made]
 
     def copies(run):
         for k, source in enumerate(sources):
             for n, (low, high) in enumerate(cuts):
-                start = pl.multiple_of(starts[k + len(sources) * (n == turned)], 16)
-                run(
-                    pltpu.make_async_copy(
-                        source.at[:, low:high],
-                        outs[n].at[pl.ds(start, source.shape[0])],
-                        sems.at[k * len(cuts) + n],
-                    )
-                )
+                start = starts[k + len(sources) * (n == turned)]
+                sem = sems.at[k * len(cuts) + n]
+
+                def copy_to(out, at, condition):
+                    at = pl.multiple_of(jnp.clip(at, 0, out.shape[0] - source.shape[0]), 16)
+                    copy = pltpu.make_async_copy(source.at[:, low:high], out.at[pl.ds(at, source.shape[0])], sem)
+                    if condition is None:
+                        run(copy)
+                    else:
+                        pl.when(condition)(functools.partial(run, copy))
+
+                if n == turned:
+                    half = outs[n].shape[0]
+                    copy_to(outs[n], start, start < half)
+                    copy_to(outs[n + 1], start - half, start >= half)
+                else:
+                    copy_to(outs[n], start, None)
 
     copies(lambda copy: copy.start())
     copies(lambda copy: copy.wait())
@@ -410,11 +420,14 @@
 def assemble(starts, sources, cuts, turned=None, turn=0):
     total = sum(x.shape[0] for x in sources)
     starts = starts + [lax.rem(start + total - turn, total) for start in starts]
+    shapes = [(total, high - low) for low, high in cuts]
+    if turned is not None:
+        shapes[turned : turned + 1] = [(total // 2, shapes[turned][1])] * 2
     return pl.pallas_call(
         functools.partial(assemble_kernel, cuts, turned),
         in_specs=[pl.BlockSpec(memory_space=pltpu.SMEM)] + [pl.BlockSpec(memory_space=pl.ANY)] * len(sources),
-        out_specs=[pl.BlockSpec(memory_space=pltpu.VMEM)] * len(cuts),
-        out_shape=[jax.ShapeDtypeStruct((total, high - low), BF16) for low, high in cuts],
+        out_specs=[pl.BlockSpec(memory_space=pltpu.VMEM)] * len(shapes),
+        out_shape=[jax.ShapeDtypeStruct(shape, BF16) for shape in shapes],
         scratch_shapes=[pltpu.SemaphoreType.DMA((len(sources) * len(cuts),))],
         compiler_params=pltpu.CompilerParams(vmem_limit_bytes=VMEM_ALL),
         cost_estimate=pl.CostEstimate(
@@ -763,8 +776,7 @@
         return (u * norm_of(u) * gain).astype(BF16)
 
     def out_whole(pieces):
-        half = pieces.shape[0] // 2
-        kept, sent = (pieces[:half], pieces[half:]) if direct else (links.cut(pieces, 0, core), links.cut(pieces, 0, 1 - core))
+        kept, sent = pieces if direct else (links.cut(pieces, 0, core), links.cut(pieces, 0, 1 - core))
         return links.in_core_order(kept, links.swap_core(sent), 1)
 
     def project(layer, scaled):
@@ -796,6 +808,11 @@
         normed = (gated * inverse.reshape(tokens, 1) * gain).astype(BF16)
         other = links.swap_core(normed)
         return jnp.concatenate([normed, other], axis=1) if direct else links.in_core_order(normed, other, 1)
+
+    def out_project(normed, weights):
+        if direct:
+            return dot(normed[:, :inner], weights[0]) + dot(normed[:, inner:], weights[1])
+        return dot(normed, weights)
 
     def back_mix(layer, kept, d_normed, meet):
         scale = as_columns(kept["inverse"], kept["inverse"] * meet / inner_all)
@@ -852,7 +869,7 @@
             yield [scaled]
         wide_w, last_w = big["in", 0]
         if direct:
-            wide_w, last_w, big["out", 0] = yield [wide_w, last_w, big["out", 0]]
+            wide_w, last_w, *big["out", 0] = yield [wide_w, last_w, *big["out", 0]]
         else:
             wide_w, last_w = yield [wide_w, last_w]
         big["in", 0] = wide_w, last_w
@@ -864,7 +881,7 @@
         normed = normed_of(0, gated, inverse)
         while ("out", 0) not in big:
             yield [normed]
-        branch = dot(normed, big["out", 0]).astype(BF16)
+        branch = out_project(normed, big["out", 0]).astype(BF16)
         came = links.swap_row(branch)
         normed, inverse, branch = yield [normed, inverse, branch]
         kept0 = {"scaled": scaled, "proj": proj, "last": last, "bc": bc, "outs": outs, "inverse": inverse}
@@ -925,7 +942,7 @@
         d_scaled = over_cores(d_scaled)
         d_scaled, far_upper = yield [d_scaled, far_upper]
         came = links.swap_row(links.cut(d_scaled, 0, 1 - row).astype(BF16))
-        partial = dot(normed1, big["out", 1])
+        partial = out_project(normed1, big["out", 1])
         came, partial = yield [came, partial]
         far_lower = links.swap_row(done["sum", 1][shard_rows // 2 :])
         d_scaled = own_rows(d_scaled) + came.astype(F32)
@@ -1000,9 +1017,9 @@
 
     def gather(layer):
         cuts = [(0, 2 * inner), (2 * inner, split)] + ([(split, split + half_width)] if direct else [])
-        full = assemble(*schedule.run(links.gather(pieces[layer], layer == 0)), cuts, 2, core * (shards // 2 * shard_rows))
+        full = assemble(*schedule.run(links.gather(pieces[layer], layer == 0)), cuts, 2 if direct else None, core * (shards // 2 * shard_rows))
         if direct:
-            big["out", layer] = full[2]
+            big["out", layer] = full[2:]
         else:
             big["out", layer] = out_gathered(layer)
         big["in", layer] = full[:2]

time: 557 us -> 554 us (level)
    dot_general x16 -> x18, matrix products: 40.1 us -> 40.4 us  [dot(): lax.dot_general(a, b, (dims, ((), ())), precision=precision, preferred_el...]
    unnamed x246 -> x250, local copies, waits for them, and re-layouts: 25.1 us -> 25.1 us
where the time goes in v5:
time: 554 us; the launch traced here: 544 us
  waiting for transfers between devices  244 us (44%)
  Pallas kernels  97.9 us (18%)
  starting transfers between devices  83.7 us (15%)
  local copies, waits for them, and re-layouts  41.4 us (7%)
  matrix products  40.4 us (7%)
  other arithmetic  33.4 us (6%)
    ppermute x14, waiting for transfers between devices, scatter(): lax.ppermute(up, 'fsdp', self.ahead)  54.4 us
    ppermute x17, waiting for transfers between devices, swap_row(): return lax.ppermute(x, 'dp', [(0, 1), (1, 0)])  49.8 us
    dot_general x18, matrix products, dot(): lax.dot_general(a, b, (dims, ((), ())), precision=precision, preferred_el...  40.4 us
    ppermute x6, waiting for transfers between devices, gather(): sent_down = None if last else lax.ppermute(down, 'fsdp', self.behind)  37 us
    ppermute x6, waiting for transfers between devices, gather(): sent_up = lax.ppermute(up, 'fsdp', self.ahead)  35 us
    pallas_call x16, Pallas kernels, ring_add(): pl.pallas_call(functools.partial(ring_add_kernel, count, upper, sums is n...  33.5 us
    unnamed x250, local copies, waits for them, and re-layouts  25.1 us
    pallas_call x2, Pallas kernels, back_call(): pl.pallas_call(functools.partial(back_kernel, heads, taps), grid=(count,)...  21.1 us
  transfers between devices with their start and end apart: 98, of which 61 were waited for; matrix products, arithmetic and copies ran while one was open for 13% of the time, Pallas kernels for 12%

profile of v5, /device:TPU:0, one launch (start us, length us, event | category | flops | bytes accessed | tf_op | source)
XLA Modules:
  0.0 544.2 jit_solution(16827868490676515620)
XLA Ops:
  3.8 3.0 shard_map.203
  7.3 2.6 collective-permute-start.1
  16.8 2.0 collective-permute-start.9
  22.5 6.8 %collective-permute-done.9.refs_2_ = bf16[96,2432]{1,0:T(8,128)(2,1)} collective-permute-done((bf16[96,2432]{1,0:T(8,128)(2,1)}, bf16[96,2432]{1,0:T(8,128)(2,1)}, u32[]{:S(2)}, u32[]{:S(2)}) %collective-permute-start.9) | collective-permute-done | bytes 466976 | tf_op jit(solution)/shard_map/ppermute | solution.py:593
  31.4 9.4 %collective-permute-done.10.refs_4_ = bf16[96,2432]{1,0:T(8,128)(2,1)S(1)} collective-permute-done((bf16[96,2432]{1,0:T(8,128)(2,1)}, bf16[96,2432]{1,0:T(8,128)(2,1)S(1)}, u32[]{:S(2)}, u32[]{:S(2)}) %collective-permute-start.10) | collective-permute-done | bytes 466976 | tf_op jit(solution)/shard_map/ppermute | solution.py:600
  45.5 6.1 %collective-permute-done.11.refs_6_ = bf16[96,2432]{1,0:T(8,128)(2,1)S(1)} collective-permute-done((bf16[96,2432]{1,0:T(8,128)(2,1)S(1)}, bf16[96,2432]{1,0:T(8,128)(2,1)S(1)}, u32[]{:S(2)}, u32[]{:S(2)}) %collective-permute-start.11) | collective-permute-done | bytes 466976 | tf_op jit(solution)/shard_map/ppermute | solution.py:600
  54.4 7.9 %collective-permute-done.13.refs_8_ = bf16[96,2432]{1,0:T(8,128)(2,1)S(1)} collective-permute-done((bf16[96,2432]{1,0:T(8,128)(2,1)S(1)}, bf16[96,2432]{1,0:T(8,128)(2,1)S(1)}, u32[]{:S(2)}, u32[]{:S(2)}) %collective-permute-start.13) | collective-permute-done | bytes 466976 | tf_op jit(solution)/shard_map/ppermute | solution.py:600
  65.1 2.2 maximum_select_fusion.5
  68.4 4.6 collective-permute-done.16.refs_10_
  75.7 8.9 %collective-permute-done.18.refs_12_ = bf16[96,2432]{1,0:T(8,128)(2,1)} collective-permute-done((bf16[96,2432]{1,0:T(8,128)(2,1)}, bf16[96,2432]{1,0:T(8,128)(2,1)}, u32[]{:S(2)}, u32[]{:S(2)}) %collective-permute-start.18) | collective-permute-done | bytes 466976 | tf_op jit(solution)/shard_map/ppermute | solution.py:600
  84.7 2.5 collective-permute-start.20
  87.4 2.0 collective-permute-start.8
  90.5 8.8 %collective-permute-done.19.refs_13_ = bf16[96,2432]{1,0:T(8,128)(2,1)} collective-permute-done((bf16[96,2432]{1,0:T(8,128)(2,1)}, bf16[96,2432]{1,0:T(8,128)(2,1)}, u32[]{:S(2)}, u32[]{:S(2)}) %collective-permute-start.19) | collective-permute-done | bytes 466976 | tf_op jit(solution)/shard_map/ppermute | solution.py:598
  99.3 7.3 %shard_map.204 = (bf16[1536,1536]{1,0:T(8,128)(2,1)}, bf16[1536,128]{1,0:T(8,128)(2,1)}, bf16[768,768]{1,0:T(8,128)(2,1)}, bf16[768,768]{1,0:T(8,128)(2,1)}) custom-call(s32[30]{0:T(128)} %stack.456.starts, bf16[192,2432]{1,0:T(8,128)(2,1)} %copy-done.65, bf16[96,2432]{1,0:T(8,128)(2,1)} %collective-permute-done.3.refs_1_, ...), custom_call_target="tpu_custom_call" | custom-call | bytes 14942208 | tf_op jit(solution)/shard_map/pallas_call | solution.py:426
  112.0 6.6 %fusion.82.proj = f32[512,1536]{1,0:T(8,128)} fusion(bf16[512,1536]{1,0:T(8,128)(2,1)S(1)} %fusion.2.a, bf16[1536,1536]{1,0:T(8,128)(2,1)} %get-tuple-element.231), kind=kOutput, calls=%fused_computation.237 | convolution fusion | flops 2415919104 | bytes 9437184 | tf_op jit(solution)/shard_map/dot_general | solution.py:21
  124.3 5.3 shard_map.205
  129.7 3.5 collective-permute-done.24.refs_5_
  138.6 3.0 collective-permute-done.30
  141.7 5.2 collective-permute-done.27.refs_7_
  155.2 7.1 %collective-permute-done.31.refs_9_ = bf16[96,2432]{1,0:T(8,128)(2,1)S(1)} collective-permute-done((bf16[96,2432]{1,0:T(8,128)(2,1)S(1)}, bf16[96,2432]{1,0:T(8,128)(2,1)S(1)}, u32[]{:S(2)}, u32[]{:S(2)}) %collective-permute-start.31) | collective-permute-done | bytes 466976 | tf_op jit(solution)/shard_map/ppermute | solution.py:604
  167.3 7.8 %collective-permute-done.34.refs_11_ = bf16[96,2432]{1,0:T(8,128)(2,1)S(1)} collective-permute-done((bf16[96,2432]{1,0:T(8,128)(2,1)S(1)}, bf16[96,2432]{1,0:T(8,128)(2,1)S(1)}, u32[]{:S(2)}, u32[]{:S(2)}) %collective-permute-start.34) | collective-permute-done | bytes 466976 | tf_op jit(solution)/shard_map/ppermute | solution.py:604
  179.4 11.2 %collective-permute-done.39.refs_13_ = bf16[96,2432]{1,0:T(8,128)(2,1)} collective-permute-done((bf16[96,2432]{1,0:T(8,128)(2,1)S(1)}, bf16[96,2432]{1,0:T(8,128)(2,1)}, u32[]{:S(2)}, u32[]{:S(2)}) %collective-permute-start.39) | collective-permute-done | bytes 466976 | tf_op jit(solution)/shard_map/ppermute | solution.py:604
  191.0 7.2 %shard_map.206 = (bf16[1536,1536]{1,0:T(8,128)(2,1)}, bf16[1536,128]{1,0:T(8,128)(2,1)}, bf16[768,768]{1,0:T(8,128)(2,1)}, bf16[768,768]{1,0:T(8,128)(2,1)}) custom-call(s32[30]{0:T(128)} %stack.456.starts, bf16[192,2432]{1,0:T(8,128)(2,1)} %get-tuple-element.426.refs_0_, bf16[96,2432]{1,0:T(8,128)(2,1)} %collective-permute-done.7.refs_1_, ...), custom_call_target="tpu_custom_call" | custom-call | bytes 14942208 | tf_op jit(solution)/shard_map/pallas_call | solution.py:426
  202.4 6.7 %fusion.85.proj = f32[512,1536]{1,0:T(8,128)} fusion(bf16[512,1536]{1,0:T(8,128)(2,1)S(1)} %fusion.5.a, bf16[1536,1536]{1,0:T(8,128)(2,1)} %get-tuple-element.262), kind=kOutput, calls=%fused_computation.240 | convolution fusion | flops 2415919104 | bytes 9437184 | tf_op jit(solution)/shard_map/dot_general | solution.py:21
  214.6 5.7 %shard_map.207 = (f32[512,768]{1,0:T(8,128)S(1)}, f32[512,768]{1,0:T(8,128)S(1)}, f32[512,128]{1,0:T(8,128)S(1)}) custom-call(f32[512,1536]{1,0:T(8,128)S(1)} %copy-done.45, f32[512,128]{1,0:T(8,128)S(1)} %copy.243.last.last_ref, f32[512,256]{1,0:T(8,128)S(1)} %maximum_select_fusion.10.bc, f32[512,8]{1,0:T(8,128)S(1)} %copy.237.aux, ...), custom_call_target="tpu_custom_call" | custom-call | flops 4000000000 | bytes 8000000 | tf_op jit(solution)/shard_map/pallas_call | solution.py:231
  220.4 5.3 multiply_reduce_fusion.1
  227.6 3.1 collective-permute-done.45
  235.6 10.5 %shard_map.208 = (bf16[512,1536]{1,0:T(8,128)(2,1)S(1)}, f32[512,128]{1,0:T(8,128)S(1)}, f32[512,256]{1,0:T(8,128)S(1)}, f32[4,8,768]{2,1,0:T(8,128)S(1)}, f32[4,8,128]{2,1,0:T(8,128)S(1)}) custom-call(f32[512,1536]{1,0:T(8,128)S(1)} %copy-done.46, f32[512,128]{1,0:T(8,128)S(1)} %copy.243.last.last_ref, f32[512,256]{1,0:T(8,128)S(1)} %maximum_select_fusion.10.bc, ...), custom_call_target="tpu_custom_call" | custom-call | flops 8000000000 | bytes 12000000 | tf_op jit(solution)/shard_map/pallas_call | solution.py:259
  246.2 4.7 fusion.87
  251.9 4.5 shard_map.209
  256.6 3.3 collective-permute-done.47
  264.7 3.4 collective-permute-done.51
  273.7 10.3 %collective-permute-done.49.refs_6_ = bf16[96,2432]{1,0:T(8,128)(2,1)S(1)} collective-permute-done((bf16[96,2432]{1,0:T(8,128)(2,1)S(1)}, bf16[96,2432]{1,0:T(8,128)(2,1)S(1)}, u32[]{:S(2)}, u32[]{:S(2)}) %collective-permute-start.49) | collective-permute-done | bytes 466976 | tf_op jit(solution)/shard_map/ppermute | solution.py:619
  285.1 4.0 collective-permute-done.52
  289.1 2.7 convert_add_fusion
  298.7 3.6 fusion.7
  304.6 5.2 collective-permute-done.53.refs_6_
  315.2 2.6 fusion.89.d_normed
  317.8 8.3 %collective-permute-done.56.refs_6_ = bf16[96,2432]{1,0:T(8,128)(2,1)S(1)} collective-permute-done((bf16[96,2432]{1,0:T(8,128)(2,1)S(1)}, bf16[96,2432]{1,0:T(8,128)(2,1)S(1)}, u32[]{:S(2)}, u32[]{:S(2)}) %collective-permute-start.56) | collective-permute-done | bytes 466976 | tf_op jit(solution)/shard_map/ppermute | solution.py:619
  328.3 2.1 shard_map.214
  332.6 10.6 %shard_map.215 = (bf16[512,1536]{1,0:T(8,128)(2,1)S(1)}, f32[512,128]{1,0:T(8,128)S(1)}, f32[512,256]{1,0:T(8,128)S(1)}, f32[4,8,768]{2,1,0:T(8,128)S(1)}, f32[4,8,128]{2,1,0:T(8,128)S(1)}) custom-call(f32[512,1536]{1,0:T(8,128)S(1)} %copy-done.44, f32[512,128]{1,0:T(8,128)S(1)} %copy-done.10, f32[512,256]{1,0:T(8,128)S(1)} %copy-done.15, ...), custom_call_target="tpu_custom_call" | custom-call | flops 8000000000 | bytes 12000000 | tf_op jit(solution)/shard_map/pallas_call | solution.py:259
  343.4 2.2 shard_map.216
  347.6 2.6 fusion.90
  350.3 8.0 %collective-permute-done.61.refs_6_ = bf16[96,2432]{1,0:T(8,128)(2,1)S(1)} collective-permute-done((bf16[96,2432]{1,0:T(8,128)(2,1)S(1)}, bf16[96,2432]{1,0:T(8,128)(2,1)S(1)}, u32[]{:S(2)}, u32[]{:S(2)}) %collective-permute-start.61) | collective-permute-done | bytes 466976 | tf_op jit(solution)/shard_map/ppermute | solution.py:619
  363.6 2.8 convolution_convert_fusion
  366.5 4.5 shard_map.218
  380.7 5.7 %collective-permute-done.67.refs_6_ = bf16[96,2432]{1,0:T(8,128)(2,1)S(1)} collective-permute-done((bf16[96,2432]{1,0:T(8,128)(2,1)S(1)}, bf16[96,2432]{1,0:T(8,128)(2,1)S(1)}, u32[]{:S(2)}, u32[]{:S(2)}) %collective-permute-start.67) | collective-permute-done | bytes 466976 | tf_op jit(solution)/shard_map/ppermute | solution.py:619
  404.4 4.1 collective-permute-done.72
  414.6 4.7 collective-permute-done.73
  427.4 5.5 %collective-permute-done.77 = bf16[96,2432]{1,0:T(8,128)(2,1)S(1)} collective-permute-done((bf16[96,2432]{1,0:T(8,128)(2,1)S(1)}, bf16[96,2432]{1,0:T(8,128)(2,1)S(1)}, u32[]{:S(2)}, u32[]{:S(2)}) %collective-permute-start.77) | collective-permute-done | bytes 466976 | tf_op jit(solution)/shard_map/ppermute | solution.py:562
  432.9 3.1 collective-permute-done.74.refs_6_
  437.3 2.7 shard_map.224
  444.5 8.9 %collective-permute-done.81 = f32[22,768]{1,0:T(8,128)S(1)} collective-permute-done((f32[22,768]{1,0:T(8,128)S(1)}, f32[22,768]{1,0:T(8,128)S(1)}, u32[]{:S(2)}, u32[]{:S(2)}) %collective-permute-start.81) | collective-permute-done | bytes 67616 | tf_op jit(solution)/shard_map/ppermute | solution.py:565
  453.5 3.0 shard_map.225
  460.8 8.6 %collective-permute-done.84 = f32[22,768]{1,0:T(8,128)S(1)} collective-permute-done((f32[22,768]{1,0:T(8,128)S(1)}, f32[22,768]{1,0:T(8,128)S(1)}, u32[]{:S(2)}, u32[]{:S(2)}) %collective-permute-start.84) | collective-permute-done | bytes 67616 | tf_op jit(solution)/shard_map/ppermute | solution.py:630
  469.4 2.1 shard_map.226
  476.7 9.3 %collective-permute-done.88 = f32[22,768]{1,0:T(8,128)S(1)} collective-permute-done((f32[22,768]{1,0:T(8,128)S(1)}, f32[22,768]{1,0:T(8,128)S(1)}, u32[]{:S(2)}, u32[]{:S(2)}) %collective-permute-start.88) | collective-permute-done | bytes 67616 | tf_op jit(solution)/shard_map/ppermute | solution.py:630
  486.6 2.7 shard_map.227
  489.3 2.0 collective-permute-start.90
  498.2 2.1 shard_map.228
  502.5 10.4 %collective-permute-done.93.refs_6_ = bf16[96,2432]{1,0:T(8,128)(2,1)S(1)} collective-permute-done((bf16[96,2432]{1,0:T(8,128)(2,1)S(1)}, bf16[96,2432]{1,0:T(8,128)(2,1)S(1)}, u32[]{:S(2)}, u32[]{:S(2)}) %collective-permute-start.93) | collective-permute-done | bytes 466976 | tf_op jit(solution)/shard_map/ppermute | solution.py:619
  516.8 19.6 %collective-permute-done.95 = bf16[192,2432]{1,0:T(8,128)(2,1)S(1)} collective-permute-done((bf16[192,2432]{1,0:T(8,128)(2,1)S(1)}, bf16[192,2432]{1,0:T(8,128)(2,1)S(1)}, u32[]{:S(2)}, u32[]{:S(2)}) %collective-permute-start.95) | collective-permute-done | bytes 933920 | tf_op jit(solution)/shard_map/ppermute | solution.py:562
  536.7 2.5 collective-permute-done.97.refs_3_
  539.1 4.6 shard_map.230
  (688 shorter events, 191.4 us)
Async XLA Ops:
  16.8 12.6 %collective-permute-start.9 = (bf16[96,2432]{1,0:T(8,128)(2,1)}, bf16[96,2432]{1,0:T(8,128)(2,1)}, u32[]{:S(2)}, u32[]{:S(2)}) collective-permute-start(bf16[96,2432]{1,0:T(8,128)(2,1)} %get-tuple-element.429), channel_id=1, source_target_pairs={{0,2},{4,0},{8,4},{12,8},{14,12},{10,14},{6,10},{2,6},{1,3},{5,1},... | collective-permute-start | bytes 1400840 | tf_op jit(solution)/shard_map/ppermute | solution.py:593
  18.8 12.2 %collective-permute-start.3 = (bf16[96,2432]{1,0:T(8,128)(2,1)S(1)}, bf16[96,2432]{1,0:T(8,128)(2,1)}, u32[]{:S(2)}, u32[]{:S(2)}) collective-permute-start(bf16[96,2432]{1,0:T(8,128)(2,1)S(1)} %get-tuple-element.430), channel_id=1, source_target_pairs={{2,0},{0,4},{4,8},{8,12},{12,14},{14,10},{10,6},{6,2},{3,1},{1,5},... | collective-permute-start | bytes 1400840 | tf_op jit(solution)/shard_map/ppermute | solution.py:593
  20.3 21.9 %collective-permute-start.5 = (bf16[256,1536]{1,0:T(8,128)(2,1)S(1)}, bf16[256,1536]{1,0:T(8,128)(2,1)S(1)}, u32[]{:S(2)}, u32[]{:S(2)}) collective-permute-start(bf16[256,1536]{1,0:T(8,128)(2,1)S(1)} %copy-done.57), channel_id=1, source_target_pairs={{0,1},{1,0},{2,3},{3,2},{4,5},{5,4},{6,7},{7,6},{8,9},{9,8},{10,11... | collective-permute-start | bytes 2359304 | tf_op jit(solution)/shard_map/ppermute | solution.py:562
  29.3 11.5 %collective-permute-start.10 = (bf16[96,2432]{1,0:T(8,128)(2,1)}, bf16[96,2432]{1,0:T(8,128)(2,1)S(1)}, u32[]{:S(2)}, u32[]{:S(2)}) collective-permute-start(bf16[96,2432]{1,0:T(8,128)(2,1)} %collective-permute-done.9.refs_2_), channel_id=1, source_target_pairs={{0,2},{4,0},{8,4},{12,8},{14,12},{10,14},{6,10},{2,6},{1,3},{5,1},... | collective-permute-start | bytes 1400840 | tf_op jit(solution)/shard_map/ppermute | solution.py:600
  31.0 11.2 %collective-permute-start.4 = (bf16[96,2432]{1,0:T(8,128)(2,1)}, bf16[96,2432]{1,0:T(8,128)(2,1)S(1)}, u32[]{:S(2)}, u32[]{:S(2)}) collective-permute-start(bf16[96,2432]{1,0:T(8,128)(2,1)} %collective-permute-done.3.refs_1_), channel_id=1, source_target_pairs={{2,0},{0,4},{4,8},{8,12},{12,14},{14,10},{10,6},{6,2},{3,1},{1,5},... | collective-permute-start | bytes 1400840 | tf_op jit(solution)/shard_map/ppermute | solution.py:598
  40.8 10.8 %collective-permute-start.11 = (bf16[96,2432]{1,0:T(8,128)(2,1)S(1)}, bf16[96,2432]{1,0:T(8,128)(2,1)S(1)}, u32[]{:S(2)}, u32[]{:S(2)}) collective-permute-start(bf16[96,2432]{1,0:T(8,128)(2,1)S(1)} %collective-permute-done.10.refs_4_), channel_id=1, source_target_pairs={{0,2},{4,0},{8,4},{12,8},{14,12},{10,14},{6,10},{2,6},{1,3},{5,1},... | collective-permute-start | bytes 1400840 | tf_op jit(solution)/shard_map/ppermute | solution.py:600
  43.6 21.5 %collective-permute-start.15 = (bf16[256,1536]{1,0:T(8,128)(2,1)}, bf16[256,1536]{1,0:T(8,128)(2,1)}, u32[]{:S(2)}, u32[]{:S(2)}) collective-permute-start(bf16[256,1536]{1,0:T(8,128)(2,1)} %param.23), channel_id=1, source_target_pairs={{0,1},{1,0},{2,3},{3,2},{4,5},{5,4},{6,7},{7,6},{8,9},{9,8},{10,11... | collective-permute-start | bytes 2359304 | tf_op jit(solution)/shard_map/ppermute | solution.py:562
  51.6 10.8 %collective-permute-start.13 = (bf16[96,2432]{1,0:T(8,128)(2,1)S(1)}, bf16[96,2432]{1,0:T(8,128)(2,1)S(1)}, u32[]{:S(2)}, u32[]{:S(2)}) collective-permute-start(bf16[96,2432]{1,0:T(8,128)(2,1)S(1)} %collective-permute-done.11.refs_6_), channel_id=1, source_target_pairs={{0,2},{4,0},{8,4},{12,8},{14,12},{10,14},{6,10},{2,6},{1,3},{5,1},... | collective-permute-start | bytes 1400840 | tf_op jit(solution)/shard_map/ppermute | solution.py:600
  53.7 10.8 %collective-permute-start.12 = (bf16[96,2432]{1,0:T(8,128)(2,1)S(1)}, bf16[96,2432]{1,0:T(8,128)(2,1)S(1)}, u32[]{:S(2)}, u32[]{:S(2)}) collective-permute-start(bf16[96,2432]{1,0:T(8,128)(2,1)S(1)} %collective-permute-done.6.refs_5_), channel_id=1, source_target_pairs={{2,0},{0,4},{4,8},{8,12},{12,14},{14,10},{10,6},{6,2},{3,1},{1,5},... | collective-permute-start | bytes 1400840 | tf_op jit(solution)/shard_map/ppermute | solution.py:598
  64.5 10.9 %collective-permute-start.14 = (bf16[96,2432]{1,0:T(8,128)(2,1)S(1)}, bf16[96,2432]{1,0:T(8,128)(2,1)}, u32[]{:S(2)}, u32[]{:S(2)}) collective-permute-start(bf16[96,2432]{1,0:T(8,128)(2,1)S(1)} %collective-permute-done.12.refs_7_), channel_id=1, source_target_pairs={{2,0},{0,4},{4,8},{8,12},{12,14},{14,10},{10,6},{6,2},{3,1},{1,5},... | collective-permute-start | bytes 1400840 | tf_op jit(solution)/shard_map/ppermute | solution.py:598
  73.0 11.7 %collective-permute-start.18 = (bf16[96,2432]{1,0:T(8,128)(2,1)}, bf16[96,2432]{1,0:T(8,128)(2,1)}, u32[]{:S(2)}, u32[]{:S(2)}) collective-permute-start(bf16[96,2432]{1,0:T(8,128)(2,1)} %collective-permute-done.16.refs_10_), channel_id=1, source_target_pairs={{0,2},{4,0},{8,4},{12,8},{14,12},{10,14},{6,10},{2,6},{1,3},{5,1},... | collective-permute-start | bytes 1400840 | tf_op jit(solution)/shard_map/ppermute | solution.py:600
  75.4 11.9 %collective-permute-start.17 = (bf16[96,2432]{1,0:T(8,128)(2,1)}, bf16[96,2432]{1,0:T(8,128)(2,1)}, u32[]{:S(2)}, u32[]{:S(2)}) collective-permute-start(bf16[96,2432]{1,0:T(8,128)(2,1)} %collective-permute-done.14.refs_9_), channel_id=1, source_target_pairs={{2,0},{0,4},{4,8},{8,12},{12,14},{14,10},{10,6},{6,2},{3,1},{1,5},... | collective-permute-start | bytes 1400840 | tf_op jit(solution)/shard_map/ppermute | solution.py:598
  84.7 14.6 %collective-permute-start.20 = (bf16[96,2432]{1,0:T(8,128)(2,1)}, bf16[96,2432]{1,0:T(8,128)(2,1)}, u32[]{:S(2)}, u32[]{:S(2)}) collective-permute-start(bf16[96,2432]{1,0:T(8,128)(2,1)} %collective-permute-done.18.refs_12_), channel_id=1, source_target_pairs={{0,2},{4,0},{8,4},{12,8},{14,12},{10,14},{6,10},{2,6},{1,3},{5,1},... | collective-permute-start | bytes 1400840 | tf_op jit(solution)/shard_map/ppermute | solution.py:600
  87.3 12.0 %collective-permute-start.19 = (bf16[96,2432]{1,0:T(8,128)(2,1)}, bf16[96,2432]{1,0:T(8,128)(2,1)}, u32[]{:S(2)}, u32[]{:S(2)}) collective-permute-start(bf16[96,2432]{1,0:T(8,128)(2,1)} %collective-permute-done.17.refs_11_), channel_id=1, source_target_pairs={{2,0},{0,4},{4,8},{8,12},{12,14},{14,10},{10,6},{6,2},{3,1},{1,5},... | collective-permute-start | bytes 1400840 | tf_op jit(solution)/shard_map/ppermute | solution.py:598
  87.4 19.2 %collective-permute-start.8 = (bf16[96,2432]{1,0:T(8,128)(2,1)S(1)}, bf16[96,2432]{1,0:T(8,128)(2,1)}, u32[]{:S(2)}, u32[]{:S(2)}) collective-permute-start(bf16[96,2432]{1,0:T(8,128)(2,1)S(1)} %get-tuple-element.431), channel_id=1, source_target_pairs={{0,2},{4,0},{8,4},{12,8},{14,12},{10,14},{6,10},{2,6},{1,3},{5,1},... | collective-permute-start | bytes 1400840 | tf_op jit(solution)/shard_map/ppermute | solution.py:593
  89.4 17.2 %collective-permute-start.7 = (bf16[96,2432]{1,0:T(8,128)(2,1)S(1)}, bf16[96,2432]{1,0:T(8,128)(2,1)}, u32[]{:S(2)}, u32[]{:S(2)}) collective-permute-start(bf16[96,2432]{1,0:T(8,128)(2,1)S(1)} %get-tuple-element.432), channel_id=1, source_target_pairs={{2,0},{0,4},{4,8},{8,12},{12,14},{14,10},{10,6},{6,2},{3,1},{1,5},... | collective-permute-start | bytes 1400840 | tf_op jit(solution)/shard_map/ppermute | solution.py:593
  120.0 13.1 %collective-permute-start.24 = (bf16[96,2432]{1,0:T(8,128)(2,1)S(1)}, bf16[96,2432]{1,0:T(8,128)(2,1)S(1)}, u32[]{:S(2)}, u32[]{:S(2)}) collective-permute-start(bf16[96,2432]{1,0:T(8,128)(2,1)S(1)} %collective-permute-done.21.refs_3_), channel_id=1, source_target_pairs={{2,0},{0,4},{4,8},{8,12},{12,14},{14,10},{10,6},{6,2},{3,1},{1,5},... | collective-permute-start | bytes 1400840 | tf_op jit(solution)/shard_map/ppermute | solution.py:604
  121.7 13.2 %collective-permute-start.25 = (bf16[96,2432]{1,0:T(8,128)(2,1)}, bf16[96,2432]{1,0:T(8,128)(2,1)S(1)}, u32[]{:S(2)}, u32[]{:S(2)}) collective-permute-start(bf16[96,2432]{1,0:T(8,128)(2,1)} %collective-permute-done.22.refs_4_), channel_id=1, source_target_pairs={{0,2},{4,0},{8,4},{12,8},{14,12},{10,14},{6,10},{2,6},{1,3},{5,1},... | collective-permute-start | bytes 1400840 | tf_op jit(solution)/shard_map/ppermute | solution.py:605
  134.9 12.0 %collective-permute-start.27 = (bf16[96,2432]{1,0:T(8,128)(2,1)S(1)}, bf16[96,2432]{1,0:T(8,128)(2,1)S(1)}, u32[]{:S(2)}, u32[]{:S(2)}) collective-permute-start(bf16[96,2432]{1,0:T(8,128)(2,1)S(1)} %collective-permute-done.24.refs_5_), channel_id=1, source_target_pairs={{2,0},{0,4},{4,8},{8,12},{12,14},{14,10},{10,6},{6,2},{3,1},{1,5},... | collective-permute-start | bytes 1400840 | tf_op jit(solution)/shard_map/ppermute | solution.py:604
  136.5 11.7 %collective-permute-start.28 = (bf16[96,2432]{1,0:T(8,128)(2,1)S(1)}, bf16[96,2432]{1,0:T(8,128)(2,1)S(1)}, u32[]{:S(2)}, u32[]{:S(2)}) collective-permute-start(bf16[96,2432]{1,0:T(8,128)(2,1)S(1)} %collective-permute-done.25.refs_6_), channel_id=1, source_target_pairs={{0,2},{4,0},{8,4},{12,8},{14,12},{10,14},{6,10},{2,6},{1,3},{5,1},... | collective-permute-start | bytes 1400840 | tf_op jit(solution)/shard_map/ppermute | solution.py:605
  149.1 16.5 %collective-permute-start.37 = (bf16[768,768]{1,0:T(8,128)(2,1)S(1)}, bf16[768,768]{1,0:T(8,128)(2,1)S(1)}, u32[]{:S(2)}, u32[]{:S(2)}) collective-permute-start(bf16[768,768]{1,0:T(8,128)(2,1)S(1)} %copy-done.117), channel_id=1, source_target_pairs={{0,16},{16,0},{1,17},{17,1},{2,18},{18,2},{3,19},{19,3},{4,20},{20... | collective-permute-start | bytes 3538952 | tf_op jit(solution)/shard_map/ppermute | solution.py:559
  149.6 12.7 %collective-permute-start.31 = (bf16[96,2432]{1,0:T(8,128)(2,1)S(1)}, bf16[96,2432]{1,0:T(8,128)(2,1)S(1)}, u32[]{:S(2)}, u32[]{:S(2)}) collective-permute-start(bf16[96,2432]{1,0:T(8,128)(2,1)S(1)} %collective-permute-done.27.refs_7_), channel_id=1, source_target_pairs={{2,0},{0,4},{4,8},{8,12},{12,14},{14,10},{10,6},{6,2},{3,1},{1,5},... | collective-permute-start | bytes 1400840 | tf_op jit(solution)/shard_map/ppermute | solution.py:604
  151.2 12.4 %collective-permute-start.32 = (bf16[96,2432]{1,0:T(8,128)(2,1)S(1)}, bf16[96,2432]{1,0:T(8,128)(2,1)S(1)}, u32[]{:S(2)}, u32[]{:S(2)}) collective-permute-start(bf16[96,2432]{1,0:T(8,128)(2,1)S(1)} %collective-permute-done.28.refs_8_), channel_id=1, source_target_pairs={{0,2},{4,0},{8,4},{12,8},{14,12},{10,14},{6,10},{2,6},{1,3},{5,1},... | collective-permute-start | bytes 1400840 | tf_op jit(solution)/shard_map/ppermute | solution.py:605
  153.3 23.1 %collective-permute-start.36 = (bf16[512,768]{1,0:T(8,128)(2,1)S(1)}, bf16[512,768]{1,0:T(8,128)(2,1)S(1)}, u32[]{:S(2)}, u32[]{:S(2)}) collective-permute-start(bf16[512,768]{1,0:T(8,128)(2,1)S(1)} %add_convert_fusion.2), channel_id=1, source_target_pairs={{0,1},{1,0},{2,3},{3,2},{4,5},{5,4},{6,7},{7,6},{8,9},{9,8},{10,11... | collective-permute-start | bytes 2359304 | tf_op jit(solution)/shard_map/ppermute | solution.py:562
  163.6 11.5 %collective-permute-start.34 = (bf16[96,2432]{1,0:T(8,128)(2,1)S(1)}, bf16[96,2432]{1,0:T(8,128)(2,1)S(1)}, u32[]{:S(2)}, u32[]{:S(2)}) collective-permute-start(bf16[96,2432]{1,0:T(8,128)(2,1)S(1)} %collective-permute-done.31.refs_9_), channel_id=1, source_target_pairs={{2,0},{0,4},{4,8},{8,12},{12,14},{14,10},{10,6},{6,2},{3,1},{1,5},... | collective-permute-start | bytes 1400840 | tf_op jit(solution)/shard_map/ppermute | solution.py:604
  165.1 11.2 %collective-permute-start.35 = (bf16[96,2432]{1,0:T(8,128)(2,1)S(1)}, bf16[96,2432]{1,0:T(8,128)(2,1)S(1)}, u32[]{:S(2)}, u32[]{:S(2)}) collective-permute-start(bf16[96,2432]{1,0:T(8,128)(2,1)S(1)} %collective-permute-done.32.refs_10_), channel_id=1, source_target_pairs={{0,2},{4,0},{8,4},{12,8},{14,12},{10,14},{6,10},{2,6},{1,3},{5,1},... | collective-permute-start | bytes 1400840 | tf_op jit(solution)/shard_map/ppermute | solution.py:605
  177.4 20.9 %collective-permute-start.38 = (bf16[512,768]{1,0:T(8,128)(2,1)S(1)}, bf16[512,768]{1,0:T(8,128)(2,1)S(1)}, u32[]{:S(2)}, u32[]{:S(2)}) collective-permute-start(bf16[512,768]{1,0:T(8,128)(2,1)S(1)} %add_convert_fusion.1), channel_id=1, source_target_pairs={{0,16},{16,0},{1,17},{17,1},{2,18},{18,2},{3,19},{19,3},{4,20},{20... | collective-permute-start | bytes 2359304 | tf_op jit(solution)/shard_map/ppermute | solution.py:559
  177.4 13.2 %collective-permute-start.39 = (bf16[96,2432]{1,0:T(8,128)(2,1)S(1)}, bf16[96,2432]{1,0:T(8,128)(2,1)}, u32[]{:S(2)}, u32[]{:S(2)}) collective-permute-start(bf16[96,2432]{1,0:T(8,128)(2,1)S(1)} %collective-permute-done.34.refs_11_), channel_id=1, source_target_pairs={{2,0},{0,4},{4,8},{8,12},{12,14},{14,10},{10,6},{6,2},{3,1},{1,5},... | collective-permute-start | bytes 1400840 | tf_op jit(solution)/shard_map/ppermute | solution.py:604
  178.0 12.9 %collective-permute-start.40 = (bf16[96,2432]{1,0:T(8,128)(2,1)S(1)}, bf16[96,2432]{1,0:T(8,128)(2,1)}, u32[]{:S(2)}, u32[]{:S(2)}) collective-permute-start(bf16[96,2432]{1,0:T(8,128)(2,1)S(1)} %collective-permute-done.35.refs_12_), channel_id=1, source_target_pairs={{0,2},{4,0},{8,4},{12,8},{14,12},{10,14},{6,10},{2,6},{1,3},{5,1},... | collective-permute-start | bytes 1400840 | tf_op jit(solution)/shard_map/ppermute | solution.py:605
  198.2 22.2 %collective-permute-start.43 = (bf16[768,768]{1,0:T(8,128)(2,1)}, bf16[768,768]{1,0:T(8,128)(2,1)}, u32[]{:S(2)}, u32[]{:S(2)}) collective-permute-start(bf16[768,768]{1,0:T(8,128)(2,1)} %get-tuple-element.272), channel_id=1, source_target_pairs={{0,16},{16,0},{1,17},{17,1},{2,18},{18,2},{3,19},{19,3},{4,20},{20... | collective-permute-start | bytes 3538952 | tf_op jit(solution)/shard_map/ppermute | solution.py:559
  269.2 19.9 %collective-permute-start.52 = (bf16[512,768]{1,0:T(8,128)(2,1)}, bf16[512,768]{1,0:T(8,128)(2,1)}, u32[]{:S(2)}, u32[]{:S(2)}) collective-permute-start(bf16[512,768]{1,0:T(8,128)(2,1)} %add_convert_fusion), channel_id=1, source_target_pairs={{0,1},{1,0},{2,3},{3,2},{4,5},{5,4},{6,7},{7,6},{8,9},{9,8},{10,11... | collective-permute-start | bytes 2359304 | tf_op jit(solution)/shard_map/ppermute | solution.py:562
  271.5 12.5 %collective-permute-start.49 = (bf16[96,2432]{1,0:T(8,128)(2,1)S(1)}, bf16[96,2432]{1,0:T(8,128)(2,1)S(1)}, u32[]{:S(2)}, u32[]{:S(2)}) collective-permute-start(bf16[96,2432]{1,0:T(8,128)(2,1)S(1)} %get-tuple-element.291), channel_id=1, source_target_pairs={{2,0},{0,4},{4,8},{8,12},{12,14},{14,10},{10,6},{6,2},{3,1},{1,5},... | collective-permute-start | bytes 1400840 | tf_op jit(solution)/shard_map/ppermute | solution.py:619
  272.0 12.4 %collective-permute-start.50 = (bf16[96,2432]{1,0:T(8,128)(2,1)S(1)}, bf16[96,2432]{1,0:T(8,128)(2,1)S(1)}, u32[]{:S(2)}, u32[]{:S(2)}) collective-permute-start(bf16[96,2432]{1,0:T(8,128)(2,1)S(1)} %get-tuple-element.292), channel_id=1, source_target_pairs={{0,2},{4,0},{8,4},{12,8},{14,12},{10,14},{6,10},{2,6},{1,3},{5,1},... | collective-permute-start | bytes 1400840 | tf_op jit(solution)/shard_map/ppermute | solution.py:619
  296.6 13.2 %collective-permute-start.53 = (bf16[96,2432]{1,0:T(8,128)(2,1)S(1)}, bf16[96,2432]{1,0:T(8,128)(2,1)S(1)}, u32[]{:S(2)}, u32[]{:S(2)}) collective-permute-start(bf16[96,2432]{1,0:T(8,128)(2,1)S(1)} %get-tuple-element.296), channel_id=1, source_target_pairs={{2,0},{0,4},{4,8},{8,12},{12,14},{14,10},{10,6},{6,2},{3,1},{1,5},... | collective-permute-start | bytes 1400840 | tf_op jit(solution)/shard_map/ppermute | solution.py:619
  297.1 12.8 %collective-permute-start.54 = (bf16[96,2432]{1,0:T(8,128)(2,1)S(1)}, bf16[96,2432]{1,0:T(8,128)(2,1)S(1)}, u32[]{:S(2)}, u32[]{:S(2)}) collective-permute-start(bf16[96,2432]{1,0:T(8,128)(2,1)S(1)} %get-tuple-element.297), channel_id=1, source_target_pairs={{0,2},{4,0},{8,4},{12,8},{14,12},{10,14},{6,10},{2,6},{1,3},{5,1},... | collective-permute-start | bytes 1400840 | tf_op jit(solution)/shard_map/ppermute | solution.py:619
  313.1 13.0 %collective-permute-start.56 = (bf16[96,2432]{1,0:T(8,128)(2,1)S(1)}, bf16[96,2432]{1,0:T(8,128)(2,1)S(1)}, u32[]{:S(2)}, u32[]{:S(2)}) collective-permute-start(bf16[96,2432]{1,0:T(8,128)(2,1)S(1)} %get-tuple-element.301), channel_id=1, source_target_pairs={{2,0},{0,4},{4,8},{8,12},{12,14},{14,10},{10,6},{6,2},{3,1},{1,5},... | collective-permute-start | bytes 1400840 | tf_op jit(solution)/shard_map/ppermute | solution.py:619
  313.6 12.7 %collective-permute-start.57 = (bf16[96,2432]{1,0:T(8,128)(2,1)S(1)}, bf16[96,2432]{1,0:T(8,128)(2,1)S(1)}, u32[]{:S(2)}, u32[]{:S(2)}) collective-permute-start(bf16[96,2432]{1,0:T(8,128)(2,1)S(1)} %get-tuple-element.302), channel_id=1, source_target_pairs={{0,2},{4,0},{8,4},{12,8},{14,12},{10,14},{6,10},{2,6},{1,3},{5,1},... | collective-permute-start | bytes 1400840 | tf_op jit(solution)/shard_map/ppermute | solution.py:619
  330.5 12.7 %collective-permute-start.59 = (bf16[96,2432]{1,0:T(8,128)(2,1)S(1)}, bf16[96,2432]{1,0:T(8,128)(2,1)S(1)}, u32[]{:S(2)}, u32[]{:S(2)}) collective-permute-start(bf16[96,2432]{1,0:T(8,128)(2,1)S(1)} %get-tuple-element.307), channel_id=1, source_target_pairs={{2,0},{0,4},{4,8},{8,12},{12,14},{14,10},{10,6},{6,2},{3,1},{1,5},... | collective-permute-start | bytes 1400840 | tf_op jit(solution)/shard_map/ppermute | solution.py:619
  331.0 12.2 %collective-permute-start.60 = (bf16[96,2432]{1,0:T(8,128)(2,1)S(1)}, bf16[96,2432]{1,0:T(8,128)(2,1)S(1)}, u32[]{:S(2)}, u32[]{:S(2)}) collective-permute-start(bf16[96,2432]{1,0:T(8,128)(2,1)S(1)} %get-tuple-element.308), channel_id=1, source_target_pairs={{0,2},{4,0},{8,4},{12,8},{14,12},{10,14},{6,10},{2,6},{1,3},{5,1},... | collective-permute-start | bytes 1400840 | tf_op jit(solution)/shard_map/ppermute | solution.py:619
  345.6 12.8 %collective-permute-start.61 = (bf16[96,2432]{1,0:T(8,128)(2,1)S(1)}, bf16[96,2432]{1,0:T(8,128)(2,1)S(1)}, u32[]{:S(2)}, u32[]{:S(2)}) collective-permute-start(bf16[96,2432]{1,0:T(8,128)(2,1)S(1)} %get-tuple-element.321), channel_id=1, source_target_pairs={{2,0},{0,4},{4,8},{8,12},{12,14},{14,10},{10,6},{6,2},{3,1},{1,5},... | collective-permute-start | bytes 1400840 | tf_op jit(solution)/shard_map/ppermute | solution.py:619
  346.3 12.5 %collective-permute-start.62 = (bf16[96,2432]{1,0:T(8,128)(2,1)S(1)}, bf16[96,2432]{1,0:T(8,128)(2,1)S(1)}, u32[]{:S(2)}, u32[]{:S(2)}) collective-permute-start(bf16[96,2432]{1,0:T(8,128)(2,1)S(1)} %get-tuple-element.322), channel_id=1, source_target_pairs={{0,2},{4,0},{8,4},{12,8},{14,12},{10,14},{6,10},{2,6},{1,3},{5,1},... | collective-permute-start | bytes 1400840 | tf_op jit(solution)/shard_map/ppermute | solution.py:619
  358.9 12.0 %collective-permute-start.66 = (f32[512,64]{1,0:T(8,128)S(1)}, f32[512,64]{1,0:T(8,128)S(1)}, u32[]{:S(2)}, u32[]{:S(2)}) collective-permute-start(f32[512,64]{1,0:T(8,128)S(1)} %constant_dynamic-slice_fusion.1), channel_id=1, source_target_pairs={{0,1},{1,0},{2,3},{3,2},{4,5},{5,4},{6,7},{7,6},{8,9},{9,8},{10,11... | collective-permute-start | bytes 393224 | tf_op jit(solution)/shard_map/ppermute | solution.py:562
  361.3 11.4 %collective-permute-start.64 = (bf16[96,2432]{1,0:T(8,128)(2,1)S(1)}, bf16[96,2432]{1,0:T(8,128)(2,1)S(1)}, u32[]{:S(2)}, u32[]{:S(2)}) collective-permute-start(bf16[96,2432]{1,0:T(8,128)(2,1)S(1)} %get-tuple-element.327), channel_id=1, source_target_pairs={{2,0},{0,4},{4,8},{8,12},{12,14},{14,10},{10,6},{6,2},{3,1},{1,5},... | collective-permute-start | bytes 1400840 | tf_op jit(solution)/shard_map/ppermute | solution.py:619
  363.0 11.3 %collective-permute-start.65 = (bf16[96,2432]{1,0:T(8,128)(2,1)S(1)}, bf16[96,2432]{1,0:T(8,128)(2,1)S(1)}, u32[]{:S(2)}, u32[]{:S(2)}) collective-permute-start(bf16[96,2432]{1,0:T(8,128)(2,1)S(1)} %get-tuple-element.328), channel_id=1, source_target_pairs={{0,2},{4,0},{8,4},{12,8},{14,12},{10,14},{6,10},{2,6},{1,3},{5,1},... | collective-permute-start | bytes 1400840 | tf_op jit(solution)/shard_map/ppermute | solution.py:619
  389.0 13.6 %collective-permute-start.71 = (f32[512,768]{1,0:T(8,128)}, f32[512,768]{1,0:T(8,128)}, u32[]{:S(2)}, u32[]{:S(2)}) collective-permute-start(f32[512,768]{1,0:T(8,128)} %constant_dynamic-slice_fusion), channel_id=1, source_target_pairs={{0,16},{16,0},{1,17},{17,1},{2,18},{18,2},{3,19},{19,3},{4,20},{20... | collective-permute-start | bytes 4718600 | tf_op jit(solution)/shard_map/ppermute | solution.py:559
  395.4 13.1 %collective-permute-start.72 = (bf16[96,2432]{1,0:T(8,128)(2,1)S(1)}, bf16[96,2432]{1,0:T(8,128)(2,1)S(1)}, u32[]{:S(2)}, u32[]{:S(2)}) collective-permute-start(bf16[96,2432]{1,0:T(8,128)(2,1)S(1)} %get-tuple-element.428), channel_id=1, source_target_pairs={{0,1},{1,0},{2,3},{3,2},{4,5},{5,4},{6,7},{7,6},{8,9},{9,8},{10,11... | collective-permute-start | bytes 1400840 | tf_op jit(solution)/shard_map/ppermute | solution.py:562
  400.5 12.8 %collective-permute-start.69 = (bf16[96,2432]{1,0:T(8,128)(2,1)S(1)}, bf16[96,2432]{1,0:T(8,128)(2,1)S(1)}, u32[]{:S(2)}, u32[]{:S(2)}) collective-permute-start(bf16[96,2432]{1,0:T(8,128)(2,1)S(1)} %get-tuple-element.344), channel_id=1, source_target_pairs={{2,0},{0,4},{4,8},{8,12},{12,14},{14,10},{10,6},{6,2},{3,1},{1,5},... | collective-permute-start | bytes 1400840 | tf_op jit(solution)/shard_map/ppermute | solution.py:619
  402.1 12.5 %collective-permute-start.70 = (bf16[96,2432]{1,0:T(8,128)(2,1)S(1)}, bf16[96,2432]{1,0:T(8,128)(2,1)S(1)}, u32[]{:S(2)}, u32[]{:S(2)}) collective-permute-start(bf16[96,2432]{1,0:T(8,128)(2,1)S(1)} %get-tuple-element.345), channel_id=1, source_target_pairs={{0,2},{4,0},{8,4},{12,8},{14,12},{10,14},{6,10},{2,6},{1,3},{5,1},... | collective-permute-start | bytes 1400840 | tf_op jit(solution)/shard_map/ppermute | solution.py:619
  408.6 10.8 %collective-permute-start.73 = (bf16[256,768]{1,0:T(8,128)(2,1)S(1)}, bf16[256,768]{1,0:T(8,128)(2,1)S(1)}, u32[]{:S(2)}, u32[]{:S(2)}) collective-permute-start(bf16[256,768]{1,0:T(8,128)(2,1)S(1)} %dynamic-slice_convert_fusion.1), channel_id=1, source_target_pairs={{0,1},{1,0},{2,3},{3,2},{4,5},{5,4},{6,7},{7,6},{8,9},{9,8},{10,11... | collective-permute-start | bytes 1179656 | tf_op jit(solution)/shard_map/ppermute | solution.py:562
  419.8 13.2 %collective-permute-start.77 = (bf16[96,2432]{1,0:T(8,128)(2,1)S(1)}, bf16[96,2432]{1,0:T(8,128)(2,1)S(1)}, u32[]{:S(2)}, u32[]{:S(2)}) collective-permute-start(bf16[96,2432]{1,0:T(8,128)(2,1)S(1)} %copy-done.84), channel_id=1, source_target_pairs={{0,1},{1,0},{2,3},{3,2},{4,5},{5,4},{6,7},{7,6},{8,9},{9,8},{10,11... | collective-permute-start | bytes 1400840 | tf_op jit(solution)/shard_map/ppermute | solution.py:562
  423.2 12.9 %collective-permute-start.74 = (bf16[96,2432]{1,0:T(8,128)(2,1)S(1)}, bf16[96,2432]{1,0:T(8,128)(2,1)S(1)}, u32[]{:S(2)}, u32[]{:S(2)}) collective-permute-start(bf16[96,2432]{1,0:T(8,128)(2,1)S(1)} %get-tuple-element.352), channel_id=1, source_target_pairs={{2,0},{0,4},{4,8},{8,12},{12,14},{14,10},{10,6},{6,2},{3,1},{1,5},... | collective-permute-start | bytes 1400840 | tf_op jit(solution)/shard_map/ppermute | solution.py:619
  424.8 12.5 %collective-permute-start.75 = (bf16[96,2432]{1,0:T(8,128)(2,1)S(1)}, bf16[96,2432]{1,0:T(8,128)(2,1)S(1)}, u32[]{:S(2)}, u32[]{:S(2)}) collective-permute-start(bf16[96,2432]{1,0:T(8,128)(2,1)S(1)} %get-tuple-element.353), channel_id=1, source_target_pairs={{0,2},{4,0},{8,4},{12,8},{14,12},{10,14},{6,10},{2,6},{1,3},{5,1},... | collective-permute-start | bytes 1400840 | tf_op jit(solution)/shard_map/ppermute | solution.py:619
  440.0 13.5 %collective-permute-start.78 = (bf16[96,2432]{1,0:T(8,128)(2,1)}, bf16[96,2432]{1,0:T(8,128)(2,1)}, u32[]{:S(2)}, u32[]{:S(2)}) collective-permute-start(bf16[96,2432]{1,0:T(8,128)(2,1)} %get-tuple-element.357), channel_id=1, source_target_pairs={{2,0},{0,4},{4,8},{8,12},{12,14},{14,10},{10,6},{6,2},{3,1},{1,5},... | collective-permute-start | bytes 1400840 | tf_op jit(solution)/shard_map/ppermute | solution.py:619
  441.1 12.4 %collective-permute-start.79 = (bf16[96,2432]{1,0:T(8,128)(2,1)}, bf16[96,2432]{1,0:T(8,128)(2,1)}, u32[]{:S(2)}, u32[]{:S(2)}) collective-permute-start(bf16[96,2432]{1,0:T(8,128)(2,1)} %get-tuple-element.358), channel_id=1, source_target_pairs={{0,2},{4,0},{8,4},{12,8},{14,12},{10,14},{6,10},{2,6},{1,3},{5,1},... | collective-permute-start | bytes 1400840 | tf_op jit(solution)/shard_map/ppermute | solution.py:619
  456.5 12.9 %collective-permute-start.82 = (bf16[96,2432]{1,0:T(8,128)(2,1)}, bf16[96,2432]{1,0:T(8,128)(2,1)}, u32[]{:S(2)}, u32[]{:S(2)}) collective-permute-start(bf16[96,2432]{1,0:T(8,128)(2,1)} %get-tuple-element.370), channel_id=1, source_target_pairs={{2,0},{0,4},{4,8},{8,12},{12,14},{14,10},{10,6},{6,2},{3,1},{1,5},... | collective-permute-start | bytes 1400840 | tf_op jit(solution)/shard_map/ppermute | solution.py:619
  456.8 12.6 %collective-permute-start.83 = (bf16[96,2432]{1,0:T(8,128)(2,1)}, bf16[96,2432]{1,0:T(8,128)(2,1)}, u32[]{:S(2)}, u32[]{:S(2)}) collective-permute-start(bf16[96,2432]{1,0:T(8,128)(2,1)} %get-tuple-element.371), channel_id=1, source_target_pairs={{0,2},{4,0},{8,4},{12,8},{14,12},{10,14},{6,10},{2,6},{1,3},{5,1},... | collective-permute-start | bytes 1400840 | tf_op jit(solution)/shard_map/ppermute | solution.py:619
  460.4 15.2 %collective-permute-start.87 = (bf16[256,768]{1,0:T(8,128)(2,1)S(1)}, bf16[256,768]{1,0:T(8,128)(2,1)S(1)}, u32[]{:S(2)}, u32[]{:S(2)}) collective-permute-start(bf16[256,768]{1,0:T(8,128)(2,1)S(1)} %add_convert_fusion.3), channel_id=1, source_target_pairs={{0,16},{16,0},{1,17},{17,1},{2,18},{18,2},{3,19},{19,3},{4,20},{20... | collective-permute-start | bytes 1179656 | tf_op jit(solution)/shard_map/ppermute | solution.py:559
  471.5 14.5 %collective-permute-start.85 = (bf16[96,2432]{1,0:T(8,128)(2,1)S(1)}, bf16[96,2432]{1,0:T(8,128)(2,1)S(1)}, u32[]{:S(2)}, u32[]{:S(2)}) collective-permute-start(bf16[96,2432]{1,0:T(8,128)(2,1)S(1)} %get-tuple-element.375), channel_id=1, source_target_pairs={{2,0},{0,4},{4,8},{8,12},{12,14},{14,10},{10,6},{6,2},{3,1},{1,5},... | collective-permute-start | bytes 1400840 | tf_op jit(solution)/shard_map/ppermute | solution.py:619
  471.6 14.4 %collective-permute-start.86 = (bf16[96,2432]{1,0:T(8,128)(2,1)S(1)}, bf16[96,2432]{1,0:T(8,128)(2,1)S(1)}, u32[]{:S(2)}, u32[]{:S(2)}) collective-permute-start(bf16[96,2432]{1,0:T(8,128)(2,1)S(1)} %get-tuple-element.376), channel_id=1, source_target_pairs={{0,2},{4,0},{8,4},{12,8},{14,12},{10,14},{6,10},{2,6},{1,3},{5,1},... | collective-permute-start | bytes 1400840 | tf_op jit(solution)/shard_map/ppermute | solution.py:619
  473.6 12.4 %collective-permute-start.88 = (f32[22,768]{1,0:T(8,128)S(1)}, f32[22,768]{1,0:T(8,128)S(1)}, u32[]{:S(2)}, u32[]{:S(2)}) collective-permute-start(f32[22,768]{1,0:T(8,128)S(1)} %add.836), channel_id=1, source_target_pairs={{0,8},{2,10},{4,12},{6,14},{8,0},{10,2},{12,4},{14,6},{1,9},{3,11}... | collective-permute-start | bytes 202760 | tf_op jit(solution)/shard_map/ppermute | solution.py:630
  500.3 12.5 %collective-permute-start.93 = (bf16[96,2432]{1,0:T(8,128)(2,1)S(1)}, bf16[96,2432]{1,0:T(8,128)(2,1)S(1)}, u32[]{:S(2)}, u32[]{:S(2)}) collective-permute-start(bf16[96,2432]{1,0:T(8,128)(2,1)S(1)} %get-tuple-element.389), channel_id=1, source_target_pairs={{2,0},{0,4},{4,8},{8,12},{12,14},{14,10},{10,6},{6,2},{3,1},{1,5},... | collective-permute-start | bytes 1400840 | tf_op jit(solution)/shard_map/ppermute | solution.py:619
  500.6 12.3 %collective-permute-start.94 = (bf16[96,2432]{1,0:T(8,128)(2,1)S(1)}, bf16[96,2432]{1,0:T(8,128)(2,1)S(1)}, u32[]{:S(2)}, u32[]{:S(2)}) collective-permute-start(bf16[96,2432]{1,0:T(8,128)(2,1)S(1)} %get-tuple-element.390), channel_id=1, source_target_pairs={{0,2},{4,0},{8,4},{12,8},{14,12},{10,14},{6,10},{2,6},{1,3},{5,1},... | collective-permute-start | bytes 1400840 | tf_op jit(solution)/shard_map/ppermute | solution.py:619
  514.7 21.6 %collective-permute-start.95 = (bf16[192,2432]{1,0:T(8,128)(2,1)S(1)}, bf16[192,2432]{1,0:T(8,128)(2,1)S(1)}, u32[]{:S(2)}, u32[]{:S(2)}) collective-permute-start(bf16[192,2432]{1,0:T(8,128)(2,1)S(1)} %shard_map.229), channel_id=1, source_target_pairs={{0,1},{1,0},{2,3},{3,2},{4,5},{5,4},{6,7},{7,6},{8,9},{9,8},{10,11... | collective-permute-start | bytes 2801672 | tf_op jit(solution)/shard_map/ppermute | solution.py:562
  516.7 19.9 %collective-permute-start.96 = (bf16[192,2432]{1,0:T(8,128)(2,1)S(1)}, bf16[192,2432]{1,0:T(8,128)(2,1)S(1)}, u32[]{:S(2)}, u32[]{:S(2)}) collective-permute-start(bf16[192,2432]{1,0:T(8,128)(2,1)S(1)} %get-tuple-element.423), channel_id=1, source_target_pairs={{0,16},{16,0},{1,17},{17,1},{2,18},{18,2},{3,19},{19,3},{4,20},{20... | collective-permute-start | bytes 2801672 | tf_op jit(solution)/shard_map/ppermute | solution.py:559
  (156 other events, 1496.4 us)
